TPU v7x, 32 devices: a whole 2x2x4 slice. The times are simulated.
32 devices in a mesh: grp: 2 (over x), wide: 16 (over z, y, core).
Axes of the slice: x: 2, y: 2, z: 4, core: 2. Of those that a mesh axis runs over, the one named last changes fastest.
Arguments:
- residual_in: bfloat16 [6, 16, 5120], P('grp', None, 'wide'), parts along dimension 0, may hold values from -1.5 to 1.5
- norm_gain: bfloat16 [5120], replicated, may hold values from 0.099609375 to 1.8984375
- gate_weight: bfloat16 [5120, 16384], P('wide'), may hold values from -0.078125 to 0.078125
- up_weight: bfloat16 [5120, 16384], P('wide'), may hold values from -0.078125 to 0.078125
- down_weight: bfloat16 [16384, 5120], P(None, 'wide'), may hold values from -0.046875 to 0.046875
- out_weight: bfloat16 [8192, 5120], P('wide'), may hold values from -0.5 to 0.5
- queries: bfloat16 [6, 16, 8, 8, 128], P('grp', 'wide'), parts along dimension 0, may hold values from -6 to 6
- kv_cache: bfloat16 [2, 32, 8, 512, 128], P(None, ('grp', 'wide')), parts along dimension 1, may hold values from -6 to 6
- new_kv: bfloat16 [6, 2, 16, 8, 128], P('grp', None, 'wide'), parts along dimension 0, may hold values from -6 to 6
- cache_len: int32 [32], P('grp'), parts along dimension 0, may hold values from 1 to 512, 4096 in all
Outputs:
- ffn_out: bfloat16 [6, 16, 5120], P('grp', 'wide'), parts along dimension 0
- attn_out: bfloat16 [6, 16, 8, 8, 128], P('grp', 'wide'), parts along dimension 0
- hidden: bfloat16 [6, 16, 5120], P('grp', 'wide'), parts along dimension 0
There are 2 independent parts, one for each index of `grp`. A program takes and returns all parts, laid end to end along the dimension named above; an argument that names none is the same for every part. Nothing has to cross between parts.
All inputs are finite; a program needn't handle non-finite values. Where the computation divides by a largest or mean magnitude, that divisor is 1e-20 or more.
Results may differ from a plain program's by a relative error of at most 0.0095.
Values may be sent and summed in bfloat16 or wider, within the bound.
No kernel may reach another device: no remote copies, remote signals or barrier semaphores. Data moves between devices by JAX's collectives and lax.ppermute only.
A program may use at most 256 MiB of HBM per device.

v0:
```python
import jax
import jax.numpy as jnp
from jax import lax
from jax.sharding import PartitionSpec as P

BLOCK = 128
QMAX = 448


EPS_NORM = 1e-06
EPS_SCALE = 1e-06
NEG = -1e30


def float_grid(values):
    magnitude = jnp.abs(values)
    spacing = jnp.full_like(values, 2.0 ** (-9))
    for exponent in range(-5, 9):
        spacing = jnp.where(magnitude >= 2.0**exponent, spacing * 2.0, spacing)
    return jnp.floor(values / spacing + 0.5) * spacing


def quantize(weight):
    rows, cols = weight.shape
    blocks = weight.astype(jnp.float32).reshape(rows // BLOCK, BLOCK, cols // BLOCK, BLOCK)
    largest = jnp.max(jnp.abs(blocks), axis=(1, 3)) + EPS_SCALE
    levels = float_grid(blocks * QMAX / largest[:, None, :, None])
    return (levels.reshape(rows, cols).astype(jnp.bfloat16), largest / QMAX)


def scaled_product(left, levels, spread):
    count = left.shape[0]
    inner = levels.shape[0] // BLOCK
    width = levels.shape[1]
    part = jnp.einsum(
        "rki,kic->rkc",
        left.reshape(count, inner, BLOCK),
        levels.reshape(inner, BLOCK, width),
        preferred_element_type=jnp.float32,
    )
    return jnp.sum(part * spread[None], axis=1)


def local_product(left, levels, scale):
    return scaled_product(left, levels, jnp.repeat(scale, BLOCK, axis=1))


def reduce_rows(partial_value, dim):
    total = lax.psum(partial_value, "wide")
    share = partial_value.shape[dim] // lax.axis_size("wide")
    return lax.dynamic_slice_in_dim(total, lax.axis_index("wide") * share, share, dim)


def attention(queries, kv_cache, new_kv, live):
    steps = queries.shape[0]
    factor = queries.shape[-1] ** (-0.5)
    keys = kv_cache[0]
    values = kv_cache[1]
    new_keys = new_kv[:, 0]
    new_values = new_kv[:, 1]
    position = jnp.arange(keys.shape[2], dtype=jnp.int32)
    valid = position[None, None, None, :] < live[:, None, None, None]
    results = []
    for step in range(steps):
        query = queries[step]
        cached = (
            jnp.einsum("shqd,shcd->shqc", query, keys, preferred_element_type=jnp.float32) * factor
        )
        recent = (
            jnp.einsum("shqd,tshd->shqt", query, new_keys, preferred_element_type=jnp.float32)
            * factor
        )
        fresh = (jnp.arange(steps, dtype=jnp.int32) <= step)[None, None, None, :]
        top = jnp.maximum(
            jnp.max(jnp.where(valid, cached, NEG), axis=-1),
            jnp.max(jnp.where(fresh, recent, NEG), axis=-1),
        )[..., None]
        e_cached = jnp.where(valid, jnp.exp(cached - top), 0.0)
        e_recent = jnp.where(fresh, jnp.exp(recent - top), 0.0)
        total = jnp.sum(e_cached, axis=-1, keepdims=True) + jnp.sum(
            e_recent, axis=-1, keepdims=True
        )
        p_cached = (e_cached / total).astype(jnp.bfloat16)
        p_recent = (e_recent / total).astype(jnp.bfloat16)
        mixed = jnp.einsum("shqc,shcd->shqd", p_cached, values, preferred_element_type=jnp.float32)
        mixed = mixed + jnp.einsum(
            "shqt,tshd->shqd", p_recent, new_values, preferred_element_type=jnp.float32
        )
        results.append(mixed.astype(jnp.bfloat16))
    return jnp.stack(results)


def on_device(
    residual_in,
    norm_gain,
    gate_weight,
    up_weight,
    down_weight,
    out_weight,
    queries,
    kv_cache,
    new_kv,
    cache_len,
):
    gate_cols, up_cols = (
        lax.all_to_all(gate_weight, "wide", split_axis=1, concat_axis=0, tiled=True),
        lax.all_to_all(up_weight, "wide", split_axis=1, concat_axis=0, tiled=True),
    )
    down_rows = lax.all_to_all(down_weight, "wide", split_axis=0, concat_axis=1, tiled=True)
    owned_levels, owned_scale = quantize(out_weight)
    out_levels = lax.all_to_all(owned_levels, "wide", split_axis=1, concat_axis=0, tiled=True)
    out_scale = lax.all_gather(owned_scale, "wide", axis=0, tiled=True)
    seq_dev = kv_cache.shape[1]
    live = lax.dynamic_slice_in_dim(cache_len, lax.axis_index("wide") * seq_dev, seq_dev, 0)
    attn_out = attention(queries, kv_cache, new_kv, live)
    steps = attn_out.shape[0]
    flat_heads = attn_out.reshape(steps, seq_dev, -1)
    width_dev = out_levels.shape[1]
    out_spread = lax.dynamic_slice_in_dim(
        jnp.repeat(out_scale, BLOCK, axis=1), lax.axis_index("wide") * width_dev, width_dev, 1
    )
    piece = lax.all_gather(flat_heads, "wide", axis=1, tiled=True)
    rows_in = piece.reshape(-1, piece.shape[-1])
    projected = scaled_product(rows_in, out_levels, out_spread).reshape(
        steps, piece.shape[1], width_dev
    )
    hidden_cols = (residual_in.astype(jnp.float32) + projected).astype(jnp.bfloat16)
    hidden = lax.all_to_all(hidden_cols, "wide", split_axis=1, concat_axis=2, tiled=True)
    gate_levels, gate_scale = quantize(gate_cols)
    up_levels, up_scale = quantize(up_cols)
    down_levels, down_scale = quantize(down_rows)
    states = hidden.astype(jnp.float32)
    power = jnp.mean(states * states, axis=-1, keepdims=True)
    normed = (states * lax.rsqrt(power + EPS_NORM) * norm_gain.astype(jnp.float32)).astype(
        jnp.bfloat16
    )
    width = normed.shape[-1]
    piece = lax.all_gather(normed, "wide", axis=1, tiled=True)
    flat = piece.reshape(-1, width)
    gate = local_product(flat, gate_levels, gate_scale)
    up = local_product(flat, up_levels, up_scale)
    act = (jax.nn.silu(gate) * up).astype(jnp.bfloat16)
    partial_value = local_product(act, down_levels, down_scale).reshape(
        piece.shape[0], piece.shape[1], width
    )
    ffn_sum = reduce_rows(partial_value, 1)
    return (ffn_sum.astype(jnp.bfloat16), attn_out, hidden)


def solution(mesh):
    placed = (
        P("grp", None, "wide"),
        P(),
        P("wide", None),
        P("wide", None),
        P(None, "wide"),
        P("wide", None),
        P("grp", "wide", None, None, None),
        P(None, ("grp", "wide"), None, None, None),
        P("grp", None, "wide", None, None),
        P("grp"),
    )
    return jax.shard_map(
        on_device,
        mesh=mesh,
        in_specs=placed,
        out_specs=(
            P("grp", "wide", None),
            P("grp", "wide", None, None, None),
            P("grp", "wide", None),
        ),
        check_vma=False,
    )
```

profile of v0, /device:TPU:0, one launch (start us, length us, event | category | flops | bytes accessed | tf_op | source)
XLA Modules:
  0.0 1157.7 jit_solution(16056633360956368868)
XLA Ops:
  0.6 8.0 copy.72
  8.6 8.0 convert_abs_fusion.3
  16.7 12.2 %abs.61 = f32[4,128,40,128]{1,0,3,2:T(4,128)} reshape(f32[512,5120]{0,1:T(8,128)} %convert_abs_fusion.3) | data formatting | bytes 20971520 | tf_op jit(solution)/shard_map/abs | solution.py:26
  35.8 20.3 %fusion.13 = bf16[512,5120]{0,1:T(8,128)(2,1)} fusion(f32[640,8,4,128]{3,2,1,0:T(4,128)S(1)} %bitcast.209, bf16[512,5120]{0,1:T(8,128)(2,1)} %copy.72), kind=kLoop, calls=%fused_computation.85 | loop fusion | flops 133693440 | bytes 20971520 | tf_op jit(solution)/shard_map/convert_element_type | solution.py:28
  56.2 7.4 all-to-all-start.2
  69.1 104.3 %all_gather.9 = bf16[3,16,8192]{2,0,1:T(4,128)(2,1)S(1)} all-gather(bf16[3,1,8192]{2,0,1:T(4,128)(2,1)S(1)} %pad_maximum_fusion), channel_id=1, replica_groups=mesh['grp'=2,'wide'=16] {'wide'}, dimensions={1}, use_global_device_ids=true | all-gather | bytes 835584 | tf_op jit(solution)/shard_map/all_gather | solution.py:122
  174.3 39.1 %all-gather = f32[16,4,40]{2,1,0:T(4,128)S(1)} all-gather(f32[1,4,40]{2,1,0:T(4,128)S(1)} %copy.82), channel_id=1, replica_groups=mesh['grp'=2,'wide'=16] {'wide'}, dimensions={0}, use_global_device_ids=true | all-gather | bytes 10880 | tf_op jit(solution)/shard_map/all_gather | solution.py:112
  214.1 7.8 copy.73
  221.9 9.1 reshape.447
  231.0 12.8 %multiply_reduce_fusion.3 = f32[320,48]{0,1:T(8,128)S(1)} fusion(f32[64,320]{1,0:T(8,128)S(1)} %constant_dynamic-slice_fusion, bf16[64,128,320]{1,0,2:T(8,128)(2,1)} %reshape.447, bf16[48,64,128]{2,1,0:T(8,128)(2,1)S(1)} %bitcast.222), kind=kOutput, calls=%fused_computation.93 | convolution fusion | flops 253608960 | bytes 6172672 | tf_op jit(solution)/shard_map/rki,kic->rkc/dot_general | solution.py:35
  248.2 9.8 copy.154
  264.1 9.7 copy.153
  273.8 177.5 %all-to-all-done.1 = bf16[320,16,1024]{2,0,1:T(8,128)(2,1)} async-done(((bf16[320,16,1024]{2,0,1:T(8,128)(2,1)}), bf16[320,16,1024]{2,0,1:T(8,128)(2,1)}, u32[]{:S(2)}, u32[]{:S(2)}) %all-to-all-start.1) | async-done | bytes 10485792 | tf_op jit(solution)/shard_map/all_to_all | solution.py:106
  451.3 45.0 %all-to-all-start.4 = ((bf16[320,16,1024]{2,0,1:T(8,128)(2,1)}), bf16[320,16,1024]{2,0,1:T(8,128)(2,1)}, u32[]{:S(2)}, u32[]{:S(2)}) async-start(bf16[320,16,1024]{2,0,1:T(8,128)(2,1)} %bitcast.207), calls=%async_computation.4 | async-start | bytes 20971520 | tf_op jit(solution)/shard_map/all_to_all | solution.py:107
  496.3 9.7 copy.152
  507.1 196.2 %all_gather.11 = bf16[3,16,5120]{2,0,1:T(4,128)(2,1)S(1)} all-gather(bf16[3,1,5120]{2,0,1:T(4,128)(2,1)S(1)} %multiply_convert_fusion.8), channel_id=1, replica_groups=mesh['grp'=2,'wide'=16] {'wide'}, dimensions={1}, use_global_device_ids=true | all-gather | bytes 522240 | tf_op jit(solution)/shard_map/all_gather | solution.py:138
  703.6 12.5 %convert_multiply_fusion.1 = (f32[320,16,1024]{2,0,1:T(8,128)}, f32[320,16,1024]{2,0,1:T(8,128)S(1)}) fusion(bf16[320,16,1024]{2,0,1:T(8,128)(2,1)} %all-to-all-done.1), kind=kLoop, calls=%fused_computation.42 | loop fusion | flops 15728640 | bytes 52428800 | tf_op jit(solution)/shard_map/mul | solution.py:27
  716.1 10.0 copy.101
  726.1 8.1 bitcast_reduce_fusion.1
  734.5 37.1 %all-to-all-start = ((bf16[16,1024,320]{1,2,0:T(8,128)(2,1)}), bf16[16,1024,320]{1,2,0:T(8,128)(2,1)}, u32[]{:S(2)}, u32[]{:S(2)}) async-start(bf16[16,1024,320]{1,2,0:T(8,128)(2,1)} %bitcast.206), calls=%async_computation | async-start | bytes 20971520 | tf_op jit(solution)/shard_map/all_to_all | solution.py:109
  771.6 36.9 %multiply_reduce_fusion.2 = f32[1024,48]{0,1:T(8,128)S(1)} fusion(f32[40,1024]{1,0:T(8,128)S(1)} %get-tuple-element.47, f32[40,128,1024]{2,1,0:T(8,128)} %bitcast.210, f32[40,1024]{1,0:T(8,128)S(1)} %get-tuple-element.48, bf16[48,40,128]{2,1,0:T(8,128)(2,1)S(1)} %bitcast.227), kind=kOutput, calls=%fused_computation.90 | convolution fusion | flops 764100608 | bytes 21987328 | tf_op jit(solution)/shard_map/rki,kic->rkc/dot_general | solution.py:35
  809.3 12.5 %convert_multiply_fusion = (f32[320,16,1024]{2,0,1:T(8,128)}, f32[320,16,1024]{2,0,1:T(8,128)S(1)}) fusion(bf16[320,16,1024]{2,0,1:T(8,128)(2,1)} %all-to-all-done.4), kind=kLoop, calls=%fused_computation.40 | loop fusion | flops 15728640 | bytes 52428800 | tf_op jit(solution)/shard_map/mul | solution.py:27
  821.7 10.0 copy.105
  831.7 8.3 bitcast_reduce_fusion
  844.7 37.1 %multiply_reduce_fusion.1 = f32[1024,48]{0,1:T(8,128)S(1)} fusion(f32[40,1024]{1,0:T(8,128)S(1)} %get-tuple-element.45, f32[40,128,1024]{2,1,0:T(8,128)S(1)} %bitcast.211, f32[40,1024]{1,0:T(8,128)S(1)} %get-tuple-element.46, bf16[48,40,128]{2,1,0:T(8,128)(2,1)S(1)} %bitcast.228), kind=kOutput, calls=%fused_computation.89 | convolution fusion | flops 764100608 | bytes 21987328 | tf_op jit(solution)/shard_map/rki,kic->rkc/dot_general | solution.py:35
  881.9 76.9 %all-to-all-done = bf16[16,1024,320]{1,2,0:T(8,128)(2,1)} async-done(((bf16[16,1024,320]{1,2,0:T(8,128)(2,1)}), bf16[16,1024,320]{1,2,0:T(8,128)(2,1)}, u32[]{:S(2)}, u32[]{:S(2)}) %all-to-all-start) | async-done | bytes 10485792 | tf_op jit(solution)/shard_map/all_to_all | solution.py:109
  958.8 12.5 %convert_abs_fusion.2 = (f32[16,1024,320]{1,2,0:T(8,128)S(1)}, f32[16,1024,320]{1,2,0:T(8,128)}) fusion(bf16[16,1024,320]{1,2,0:T(8,128)(2,1)} %all-to-all-done), kind=kLoop, calls=%fused_computation.43 | loop fusion | flops 15728640 | bytes 52428800 | tf_op jit(solution)/shard_map/abs | solution.py:26
  971.3 10.0 copy.110
  981.3 8.1 reduce_max.90
  989.4 11.7 %copy.109 = f32[640,8,8,128]{3,2,1,0:T(8,128)S(1)} copy(f32[640,8,8,128]{3,1,2,0:T(8,128)} %bitcast.199) | data formatting | bytes 41943040
  1001.5 37.5 %fusion.4 = bf16[8,128,5120]{1,0,2:T(8,128)(2,1)S(1)} fusion(f32[640,8,8,128]{3,2,1,0:T(8,128)S(1)} %copy.109, f32[8,5120]{0,1:T(8,128)S(1)} %bitcast.213), kind=kLoop, calls=%fused_computation.57 | loop fusion | flops 256901120 | bytes 31621120 | tf_op jit(solution)/shard_map/convert_element_type | solution.py:28
  1044.4 112.4 %all-reduce.1 = bf16[3,16,5120]{2,1,0:T(8,128)(2,1)S(1)} all-reduce(f32[3,16,5120]{2,1,0:T(8,128)S(1)} %bitcast.221), channel_id=1, replica_groups=mesh['grp'=2,'wide'=16] {'wide'}, use_global_device_ids=true, to_apply=%region_21.22 | all-reduce | flops 245760 | bytes 1474560 | tf_op jit(solution)/shard_map/psum | solution.py:49
  (92 shorter events, 37.7 us)
Async XLA Ops:
  34.4 29.2 %copy-start.8 = (s32[16]{0:T(128)S(1)}, s32[16]{0:T(128)}, u32[]{:S(2)}) copy-start(s32[16]{0:T(128)} %param.19) | copy-start | bytes 196
  34.4 30.5 %copy-start.6 = (bf16[3,2,1,8,128]{4,3,2,1,0:T(8,128)(2,1)S(1)}, bf16[3,2,1,8,128]{4,3,2,1,0:T(8,128)(2,1)}, u32[]{:S(2)}) copy-start(bf16[3,2,1,8,128]{4,3,2,1,0:T(8,128)(2,1)} %param.18) | copy-start | bytes 36868
  34.4 30.5 %copy-start.4 = (bf16[3,1,8,8,128]{4,3,2,1,0:T(8,128)(2,1)S(1)}, bf16[3,1,8,8,128]{4,3,2,1,0:T(8,128)(2,1)}, u32[]{:S(2)}) copy-start(bf16[3,1,8,8,128]{4,3,2,1,0:T(8,128)(2,1)} %param.16) | copy-start | bytes 147460
  34.4 30.6 %copy-start.1 = (bf16[2,1,8,512,128]{4,3,2,1,0:T(8,128)(2,1)S(1)}, bf16[2,1,8,512,128]{4,3,2,1,0:T(8,128)(2,1)}, u32[]{:S(2)}) copy-start(bf16[2,1,8,512,128]{4,3,2,1,0:T(8,128)(2,1)} %param.17) | copy-start | bytes 6291460
  56.2 157.9 %all-to-all-start.2 = ((bf16[512,16,320]{0,2,1:T(8,128)(2,1)}), bf16[512,16,320]{0,2,1:T(8,128)(2,1)}, u32[]{:S(2)}, u32[]{:S(2)}) async-start(bf16[512,16,320]{0,2,1:T(8,128)(2,1)} %bitcast.212), calls=%async_computation.2 | async-start | bytes 10485760 | tf_op jit(solution)/shard_map/all_to_all | solution.py:111
  68.4 175.4 %copy-start.5 = (bf16[3,16,320]{2,1,0:T(8,128)(2,1)S(1)}, bf16[3,16,320]{2,1,0:T(8,128)(2,1)}, u32[]{:S(2)}) copy-start(bf16[3,16,320]{2,1,0:T(8,128)(2,1)} %param.10) | copy-start | bytes 92164
  244.5 13.5 %all-to-all-start.3 = ((bf16[3,16,320]{2,0,1:T(4,128)(2,1)}), bf16[3,16,320]{2,0,1:T(4,128)(2,1)S(1)}, u32[]{:S(2)}, u32[]{:S(2)}) async-start(bf16[3,16,320]{2,0,1:T(4,128)(2,1)} %copy.83), calls=%async_computation.3 | async-start | bytes 98304 | tf_op jit(solution)/shard_map/all_to_all | solution.py:128
  257.9 193.3 %all-to-all-start.1 = ((bf16[320,16,1024]{2,0,1:T(8,128)(2,1)}), bf16[320,16,1024]{2,0,1:T(8,128)(2,1)}, u32[]{:S(2)}, u32[]{:S(2)}) async-start(bf16[320,16,1024]{2,0,1:T(8,128)(2,1)} %bitcast.208), calls=%async_computation.1 | async-start | bytes 20971520 | tf_op jit(solution)/shard_map/all_to_all | solution.py:106
  264.1 232.2 %copy-start.7 = (bf16[5120]{0:T(1024)(128)(2,1)S(1)}, bf16[5120]{0:T(1024)(128)(2,1)}, u32[]{:S(2)}) copy-start(bf16[5120]{0:T(1024)(128)(2,1)} %param.11) | copy-start | bytes 30724
  451.3 283.2 %all-to-all-start.4 = ((bf16[320,16,1024]{2,0,1:T(8,128)(2,1)}), bf16[320,16,1024]{2,0,1:T(8,128)(2,1)}, u32[]{:S(2)}, u32[]{:S(2)}) async-start(bf16[320,16,1024]{2,0,1:T(8,128)(2,1)} %bitcast.207), calls=%async_computation.4 | async-start | bytes 20971520 | tf_op jit(solution)/shard_map/all_to_all | solution.py:107
  506.8 196.7 %copy-start.3 = (bf16[3,1,5120]{2,0,1:T(4,128)(2,1)}, bf16[3,1,5120]{2,0,1:T(4,128)(2,1)S(1)}, u32[]{:S(2)}) copy-start(bf16[3,1,5120]{2,0,1:T(4,128)(2,1)S(1)} %all_to_all.59) | copy-start | bytes 92164
  734.5 224.3 %all-to-all-start = ((bf16[16,1024,320]{1,2,0:T(8,128)(2,1)}), bf16[16,1024,320]{1,2,0:T(8,128)(2,1)}, u32[]{:S(2)}, u32[]{:S(2)}) async-start(bf16[16,1024,320]{1,2,0:T(8,128)(2,1)} %bitcast.206), calls=%async_computation | async-start | bytes 20971520 | tf_op jit(solution)/shard_map/all_to_all | solution.py:109
  831.7 13.0 %copy-start = (f32[320,16,1024]{2,0,1:T(8,128)S(1)}, f32[320,16,1024]{2,0,1:T(8,128)}, u32[]{:S(2)}) copy-start(f32[320,16,1024]{2,0,1:T(8,128)} %get-tuple-element.22) | copy-start | bytes 62914564
  989.4 11.8 %copy-start.2 = (f32[6,8,8,128]{3,2,1,0:T(8,128)S(1)}, f32[6,8,8,128]{3,2,1,0:T(8,128)}, u32[]{:S(2)}) copy-start(f32[6,8,8,128]{3,2,1,0:T(8,128)} %copy.104) | copy-start | bytes 589828
where the time goes:
time: 1170 us; the launch traced here: 1160 us
  blocking collectives  452 us (39%)
  waiting for transfers between devices  254 us (22%)
  other arithmetic  135 us (12%)
  local copies, waits for them, and re-layouts  119 us (10%)
  starting transfers between devices  99.3 us (8%)
  matrix products  95.6 us (8%)
    all_gather x1, blocking collectives, on_device(): piece = lax.all_gather(normed, 'wide', axis=1, tiled=True)  196 us
    all_to_all x1, waiting for transfers between devices, on_device(): lax.all_to_all(gate_weight, 'wide', split_axis=1, concat_axis=0, tiled=True)  177 us
    psum x1, blocking collectives, reduce_rows(): total = lax.psum(partial_value, 'wide')  112 us
    all_gather x1, blocking collectives, on_device(): piece = lax.all_gather(flat_heads, 'wide', axis=1, tiled=True)  104 us
    dot_general x4, matrix products, scaled_product(): jnp.einsum('rki,kic->rkc', left.reshape(count, inner, BLOCK), levels.resh...  92.2 us
    all_to_all x1, waiting for transfers between devices, on_device(): lax.all_to_all(down_weight, 'wide', split_axis=0, concat_axis=1, tiled=True)  76.9 us
    convert_element_type x2, other arithmetic, quantize(): return (levels.reshape(rows, cols).astype(jnp.bfloat16), largest / QMAX)  57.8 us
    unnamed x30, local copies, waits for them, and re-layouts  56.1 us
  transfers between devices with their start and end apart: 5, of which 2 were waited for; matrix products, arithmetic and copies ran while one was open for 15% of the time, Pallas kernels for 0%

commit v1 on v0

v1 whole, which is shorter than its diff:
```python
import functools
import math

import jax
import jax.numpy as jnp
from jax import lax
from jax.experimental import pallas as pl
from jax.experimental.pallas import tpu as pltpu
from jax.sharding import PartitionSpec as P

BLOCK = 128
QMAX = 448.0
EPS_NORM = 1e-06
EPS_SCALE = 1e-06
NEG = -1e30
LANES = 128
VMEM = 56 * 2**20

f32 = jnp.float32
bf16 = jnp.bfloat16
f8 = jnp.float8_e4m3fn


def params(**more):
    return pltpu.CompilerParams(vmem_limit_bytes=VMEM, **more)


def cost(flops, read):
    return pl.CostEstimate(flops=int(flops), bytes_accessed=int(read), transcendentals=0)


def row_chunk_max(weight, chunk, tile):
    rows, cols = weight.shape
    parts = rows // chunk

    def kernel(w_ref, o_ref):
        for j in range(parts):
            o_ref[pl.ds(j, 1), :] = jnp.max(
                jnp.abs(w_ref[pl.ds(j * chunk, chunk), :]), axis=0, keepdims=True
            ).astype(f32)
        for g in range(tile // LANES):
            at = pl.ds(g * LANES, LANES)
            top = jnp.max(o_ref[:, at], axis=1, keepdims=True)
            o_ref[:, at] = jnp.broadcast_to(top, (parts, LANES))

    return pl.pallas_call(
        kernel,
        grid=(cols // tile,),
        in_specs=[pl.BlockSpec((rows, tile), lambda i: (0, i))],
        out_specs=pl.BlockSpec((parts, tile), lambda i: (0, i)),
        out_shape=jax.ShapeDtypeStruct((parts, cols), f32),
        compiler_params=params(),
        cost_estimate=cost(2 * rows * cols, 2 * rows * cols),
        name="row_chunk_max",
    )(weight)


def col_chunk_max(weight, chunk, tile):
    rows, cols = weight.shape
    per = tile // BLOCK

    def kernel(w_ref, o_ref):
        for j in range(per):
            o_ref[pl.ds(j, 1), :] = jnp.max(
                jnp.abs(w_ref[pl.ds(j * BLOCK, BLOCK), :]), axis=0, keepdims=True
            ).astype(f32)
        tops = o_ref[...]
        column = lax.broadcasted_iota(jnp.int32, (per, cols), 1) // chunk
        spread = jnp.zeros((per, cols), f32)
        for q in range(cols // chunk):
            here = column == q
            top = jnp.max(jnp.where(here, tops, 0.0), axis=1, keepdims=True)
            spread = jnp.where(here, top, spread)
        o_ref[...] = spread

    return pl.pallas_call(
        kernel,
        grid=(rows // tile,),
        in_specs=[pl.BlockSpec((tile, cols), lambda i: (i, 0))],
        out_specs=pl.BlockSpec((per, cols), lambda i: (i, 0)),
        out_shape=jax.ShapeDtypeStruct((rows // BLOCK, cols), f32),
        compiler_params=params(),
        cost_estimate=cost(2 * rows * cols, 2 * rows * cols),
        name="col_chunk_max",
    )(weight)


def join_group(parts, size, dim):
    count = lax.axis_size("wide")
    me = lax.axis_index("wide")
    share = parts.shape[dim]
    shape = list(parts.shape)
    shape[dim] = share * size
    out = jnp.zeros(shape, parts.dtype)
    out = lax.dynamic_update_slice_in_dim(out, parts, (me % size) * share, dim)
    for step in range(1, size):
        perm = [(i // size * size + (i + step) % size, i) for i in range(count)]
        got = lax.ppermute(parts, "wide", perm)
        out = lax.dynamic_update_slice_in_dim(out, got, ((me + step) % size) * share, dim)
    return out


def row_scales(tops, chunk, rows):
    size = math.lcm(rows, BLOCK) // rows
    per = BLOCK // chunk
    own = tops.shape[0]
    if size > 1:
        joined = join_group(tops, size, 0)
    else:
        joined = tops
    blocks = joined.reshape(size * own // per, per, -1)
    joined = jnp.broadcast_to(jnp.max(blocks, axis=1, keepdims=True), blocks.shape)
    joined = joined.reshape(size * own, -1)
    if size > 1:
        joined = lax.dynamic_slice_in_dim(
            joined, (lax.axis_index("wide") % size) * own, own, 0
        )
    largest = joined + EPS_SCALE
    return QMAX / largest, largest / QMAX


def col_scales(tops, cols):
    size = math.lcm(cols, BLOCK) // cols
    joined = join_group(tops, size, 1) if size > 1 else tops
    blocks = joined.reshape(joined.shape[0], -1, BLOCK)
    joined = jnp.broadcast_to(jnp.max(blocks, axis=2, keepdims=True), blocks.shape)
    joined = joined.reshape(joined.shape[0], -1)
    if size > 1:
        joined = lax.dynamic_slice_in_dim(
            joined, (lax.axis_index("wide") % size) * cols, cols, 1
        )
    largest = joined + EPS_SCALE
    return QMAX / largest, largest / QMAX


def row_levels(weight, factor, chunk, tile):
    rows, cols = weight.shape
    parts = rows // chunk

    def kernel(w_ref, f_ref, o_ref):
        for j in range(parts):
            at = pl.ds(j * chunk, chunk)
            o_ref[at, :] = (w_ref[at, :].astype(f32) * f_ref[pl.ds(j, 1), :]).astype(f8)

    return pl.pallas_call(
        kernel,
        grid=(cols // tile,),
        in_specs=[
            pl.BlockSpec((rows, tile), lambda i: (0, i)),
            pl.BlockSpec((parts, tile), lambda i: (0, i)),
        ],
        out_specs=pl.BlockSpec((rows, tile), lambda i: (0, i)),
        out_shape=jax.ShapeDtypeStruct((rows, cols), f8),
        compiler_params=params(),
        cost_estimate=cost(4 * rows * cols, 3 * rows * cols),
        name="row_levels",
    )(weight, factor)


def col_levels(weight, factor, tile):
    rows, cols = weight.shape
    per = tile // BLOCK

    def kernel(w_ref, f_ref, o_ref):
        for j in range(per):
            at = pl.ds(j * BLOCK, BLOCK)
            o_ref[at, :] = (w_ref[at, :].astype(f32) * f_ref[pl.ds(j, 1), :]).astype(f8)

    return pl.pallas_call(
        kernel,
        grid=(rows // tile,),
        in_specs=[
            pl.BlockSpec((tile, cols), lambda i: (i, 0)),
            pl.BlockSpec((per, cols), lambda i: (i, 0)),
        ],
        out_specs=pl.BlockSpec((tile, cols), lambda i: (i, 0)),
        out_shape=jax.ShapeDtypeStruct((rows, cols), f8),
        compiler_params=params(),
        cost_estimate=cost(4 * rows * cols, 3 * rows * cols),
        name="col_levels",
    )(weight, factor)


def scaled_rows(x_ref, l_ref, s_ref, chunk, parts):
    total = None
    for j in range(parts):
        at = pl.ds(j * chunk, chunk)
        part = jnp.dot(x_ref[:, at], l_ref[at, :].astype(bf16), preferred_element_type=f32)
        part = part * s_ref[pl.ds(j, 1), :]
        total = part if total is None else total + part
    return total


def out_product(left, levels, scale, chunk, owners):
    count, rows = left.shape
    cols = levels.shape[1]
    parts = rows // chunk
    share = cols // owners
    tile = math.lcm(share, LANES)
    per = tile // share

    def kernel(x_ref, l_ref, s_ref, o_ref):
        total = scaled_rows(x_ref, l_ref, s_ref, chunk, parts).astype(bf16)
        for q in range(per):
            o_ref[q] = total[:, q * share : (q + 1) * share]

    return pl.pallas_call(
        kernel,
        grid=(cols // tile,),
        in_specs=[
            pl.BlockSpec((count, rows), lambda i: (0, 0)),
            pl.BlockSpec((rows, tile), lambda i: (0, i)),
            pl.BlockSpec((parts, tile), lambda i: (0, i)),
        ],
        out_specs=pl.BlockSpec((per, count, share), lambda i: (i, 0, 0)),
        out_shape=jax.ShapeDtypeStruct((owners, count, share), bf16),
        compiler_params=params(),
        cost_estimate=cost(2 * count * rows * cols, rows * cols),
        name="out_product",
    )(left, levels, scale)


def gate_up_product(core, left, gate, gate_scale, up, up_scale, power, chunk, owners):
    count, rows = left.shape
    parts = rows // chunk
    share = gate.shape[1] // owners
    chips = owners // 2

    def kernel(core_ref, x_ref, g_ref, gs_ref, u_ref, us_ref, p_ref, o_ref):
        o_ref[0, 0, :, pl.ds(0, share)] = scaled_rows(x_ref, g_ref, gs_ref, chunk, parts).astype(
            bf16
        )
        o_ref[0, 0, :, pl.ds(share, share)] = scaled_rows(
            x_ref, u_ref, us_ref, chunk, parts
        ).astype(bf16)
        o_ref[0, 0, :, pl.ds(2 * share, LANES)] = p_ref[...]

    def owner(i, core_ref):
        return (0, 2 * (i % chips) + (core_ref[0] + i // chips) % 2)

    fixed = lambda i, core_ref: (0, 0)
    return pl.pallas_call(
        kernel,
        grid_spec=pltpu.PrefetchScalarGridSpec(
            num_scalar_prefetch=1,
            grid=(owners,),
            in_specs=[
                pl.BlockSpec((count, rows), fixed),
                pl.BlockSpec((rows, share), owner),
                pl.BlockSpec((parts, share), owner),
                pl.BlockSpec((rows, share), owner),
                pl.BlockSpec((parts, share), owner),
                pl.BlockSpec((count, LANES), fixed),
            ],
            out_specs=pl.BlockSpec(
                (1, 1, count, 2 * share + LANES),
                lambda i, core_ref: (i // chips, i % chips, 0, 0),
            ),
        ),
        out_shape=jax.ShapeDtypeStruct((2, chips, count, 2 * share + LANES), bf16),
        compiler_params=params(),
        cost_estimate=cost(4 * count * rows * share * owners, 2 * rows * share * owners),
        name="gate_up_product",
    )(core, left, gate, gate_scale, up, up_scale, power)


def down_product(core, same, other, levels, scale):
    chips, count, share = same.shape
    rows, cols = levels.shape
    blocks = share // BLOCK
    group = max(1, 8 * BLOCK // (2 * share))

    def kernel(core_ref, a_ref, b_ref, l_ref, s_ref, o_ref, acc_ref):
        i = pl.program_id(0)

        @pl.when(i == 0)
        def _():
            acc_ref[...] = jnp.zeros_like(acc_ref)

        core_at = core_ref[0]
        total = acc_ref[...]
        for n in range(group):
            for side, ref in ((core_at, a_ref), (1 - core_at, b_ref)):
                for j in range(blocks):
                    block = (2 * n + side) * blocks + j
                    at = pl.ds(pl.multiple_of(block * BLOCK, BLOCK), BLOCK)
                    part = jnp.dot(
                        ref[n, :, pl.ds(j * BLOCK, BLOCK)],
                        l_ref[at, :].astype(bf16),
                        preferred_element_type=f32,
                    )
                    total = total + part * s_ref[pl.ds(block, 1), :]
        acc_ref[...] = total

        @pl.when(i == chips // group - 1)
        def _():
            o_ref[...] = acc_ref[...].astype(bf16)

    return pl.pallas_call(
        kernel,
        grid_spec=pltpu.PrefetchScalarGridSpec(
            num_scalar_prefetch=1,
            grid=(chips // group,),
            in_specs=[
                pl.BlockSpec((group, count, share), lambda i, c: (i, 0, 0)),
                pl.BlockSpec((group, count, share), lambda i, c: (i, 0, 0)),
                pl.BlockSpec((2 * group * share, cols), lambda i, c: (i, 0)),
                pl.BlockSpec((2 * group * blocks, cols), lambda i, c: (i, 0)),
            ],
            out_specs=pl.BlockSpec((count, cols), lambda i, c: (0, 0)),
            scratch_shapes=[pltpu.VMEM((count, cols), f32)],
        ),
        out_shape=jax.ShapeDtypeStruct((count, cols), bf16),
        compiler_params=params(),
        cost_estimate=cost(2 * count * rows * cols, rows * cols),
        name="down_product",
    )(core, same, other, levels, scale)


def attention(queries, kv_cache, new_kv, live):
    steps = queries.shape[0]
    factor = queries.shape[-1] ** (-0.5)
    keys = kv_cache[0]
    values = kv_cache[1]
    new_keys = new_kv[:, 0]
    new_values = new_kv[:, 1]
    position = jnp.arange(keys.shape[2], dtype=jnp.int32)
    valid = position[None, None, None, None, :] < live[None, :, None, None, None]
    cached = (
        jnp.einsum("nshqd,shcd->nshqc", queries, keys, preferred_element_type=f32) * factor
    )
    recent = (
        jnp.einsum("nshqd,tshd->nshqt", queries, new_keys, preferred_element_type=f32) * factor
    )
    order = jnp.arange(steps, dtype=jnp.int32)
    fresh = (order[None, :] <= order[:, None])[:, None, None, None, :]
    top = jnp.maximum(
        jnp.max(jnp.where(valid, cached, NEG), axis=-1),
        jnp.max(jnp.where(fresh, recent, NEG), axis=-1),
    )[..., None]
    e_cached = jnp.where(valid, jnp.exp(cached - top), 0.0)
    e_recent = jnp.where(fresh, jnp.exp(recent - top), 0.0)
    total = jnp.sum(e_cached, axis=-1, keepdims=True) + jnp.sum(e_recent, axis=-1, keepdims=True)
    p_cached = (e_cached / total).astype(bf16)
    p_recent = (e_recent / total).astype(bf16)
    mixed = jnp.einsum("nshqc,shcd->nshqd", p_cached, values, preferred_element_type=f32)
    mixed = mixed + jnp.einsum(
        "nshqt,tshd->nshqd", p_recent, new_values, preferred_element_type=f32
    )
    return mixed.astype(bf16)


def swap_cores(value):
    count = lax.axis_size("wide")
    return lax.ppermute(value, "wide", [(i, i ^ 1) for i in range(count)])


def exchange(value):
    return lax.all_to_all(value, "wide", split_axis=0, concat_axis=0, tiled=True)


def exchange_chips(value):
    count = lax.axis_size("wide")
    groups = [list(range(core, count, 2)) for core in range(2)]
    return lax.all_to_all(
        value, "wide", split_axis=0, concat_axis=0, tiled=True, axis_index_groups=groups
    )


def on_device(
    residual_in,
    norm_gain,
    gate_weight,
    up_weight,
    down_weight,
    out_weight,
    queries,
    kv_cache,
    new_kv,
    cache_len,
):
    owners = lax.axis_size("wide")
    me = lax.axis_index("wide")
    core = (me % 2).astype(jnp.int32).reshape(1)
    steps, seqs, width_dev = residual_in.shape
    seq_dev = seqs // owners
    tokens = steps * seqs
    mine = steps * seq_dev
    width = width_dev * owners

    live = lax.dynamic_slice_in_dim(cache_len, me * seq_dev, seq_dev, 0)
    attn_out = attention(queries, kv_cache, new_kv, live)
    heads = attn_out.reshape(steps, seq_dev, owners, -1)
    heads = exchange(jnp.transpose(heads, (2, 1, 0, 3)))
    heads = heads.reshape(tokens, -1)

    out_rows = out_weight.shape[0]
    out_chunk = math.gcd(out_rows, BLOCK)
    out_tops = row_chunk_max(out_weight, out_chunk, math.lcm(width_dev, LANES))
    out_factor, out_scale = row_scales(out_tops, out_chunk, out_rows)
    out_levels = row_levels(out_weight, out_factor, out_chunk, math.lcm(width_dev, LANES))

    projected = out_product(heads, out_levels, out_scale, out_chunk, owners)
    projected = jnp.sum(exchange(projected).astype(f32), axis=0)
    residual = jnp.transpose(residual_in, (1, 0, 2)).reshape(tokens, width_dev)
    hidden = (residual.astype(f32) + projected).astype(bf16)

    hidden_out = exchange(hidden.reshape(owners, mine, width_dev))
    hidden_out = jnp.transpose(
        hidden_out.reshape(owners, seq_dev, steps, width_dev), (2, 1, 0, 3)
    ).reshape(steps, seq_dev, width)

    rows = gate_weight.shape[0]
    chunk = math.gcd(rows, BLOCK)
    tile = 1024
    gate_factor, gate_scale = row_scales(row_chunk_max(gate_weight, chunk, tile), chunk, rows)
    up_factor, up_scale = row_scales(row_chunk_max(up_weight, chunk, tile), chunk, rows)
    gate_levels = row_levels(gate_weight, gate_factor, chunk, tile)
    up_levels = row_levels(up_weight, up_factor, chunk, tile)

    states = hidden.astype(f32)
    gain = lax.dynamic_slice_in_dim(norm_gain, me * width_dev, width_dev, 0).astype(f32)
    scaled = (states * gain).astype(bf16)
    squares = jnp.sum(states * states, axis=1, keepdims=True)
    high = squares.astype(bf16)
    low = (squares - high.astype(f32)).astype(bf16)
    lane = lax.broadcasted_iota(jnp.int32, (tokens, LANES), 1)
    power = jnp.where(lane == 0, high, jnp.where(lane == 1, low, jnp.zeros_like(low)))

    partial = gate_up_product(
        core, scaled, gate_levels, gate_scale, up_levels, up_scale, power, chunk, owners
    )
    other = swap_cores(partial[1])
    chip_sum = (partial[0].astype(f32) + other.astype(f32)).astype(bf16)
    summed = jnp.sum(exchange_chips(chip_sum).astype(f32), axis=0)
    share = gate_weight.shape[1] // owners
    total = summed[:, 2 * share : 2 * share + 1] + summed[:, 2 * share + 1 : 2 * share + 2]
    scale = lax.rsqrt(total / width + EPS_NORM)
    gate = summed[:, :share] * scale
    up = summed[:, share : 2 * share] * scale
    act = (jax.nn.silu(gate) * up).astype(bf16)

    down_rows, down_cols = down_weight.shape
    down_chunk = math.gcd(down_cols, BLOCK)
    down_factor, down_scale = col_scales(col_chunk_max(down_weight, down_chunk, 1024), down_cols)
    down_levels = col_levels(down_weight, down_factor, 1024)
    same = exchange_chips(jnp.broadcast_to(act[None], (owners // 2,) + act.shape))
    other = swap_cores(same)
    ffn = down_product(core, same, other, down_levels, down_scale)
    ffn = exchange(ffn.reshape(owners, mine, width_dev))
    ffn_out = jnp.transpose(
        ffn.reshape(owners, seq_dev, steps, width_dev), (2, 1, 0, 3)
    ).reshape(steps, seq_dev, width)
    return (ffn_out, attn_out, hidden_out)


def solution(mesh):
    placed = (
        P("grp", None, "wide"),
        P(),
        P("wide", None),
        P("wide", None),
        P(None, "wide"),
        P("wide", None),
        P("grp", "wide", None, None, None),
        P(None, ("grp", "wide"), None, None, None),
        P("grp", None, "wide", None, None),
        P("grp"),
    )
    return jax.shard_map(
        on_device,
        mesh=mesh,
        in_specs=placed,
        out_specs=(
            P("grp", "wide", None),
            P("grp", "wide", None, None, None),
            P("grp", "wide", None),
        ),
        check_vma=False,
    )
```

time: 1170 us -> 260 us (0.22)
  blocking collectives: 452 us -> 45.6 us
  waiting for transfers between devices: 254 us -> 8.6 us
  other arithmetic: 135 us -> 11.2 us
  Pallas kernels: 0 us -> 118 us
  matrix products: 95.6 us -> 2.6 us
  local copies, waits for them, and re-layouts: 119 us -> 38.6 us
  starting transfers between devices: 99.3 us -> 30.4 us
    all_gather x3 -> x0, blocking collectives: 340 us -> none  [the longest x1 196 us: on_device(): piece = lax.all_gather(normed, 'wide', axis=1, tiled=True)]
    all_to_all x5, waiting for transfers between devices: 254 us -> 5.41 us  [the longest x4 5.4 us: exchange(): lax.all_to_all(value, 'wide', split_axis=0, concat_axis=0, tiled=True)]
    pallas_call x0 -> x11, Pallas kernels: none -> 118 us  [the longest x3 31.8 us: row_levels(): pl.pallas_call(kernel, grid=(cols // tile,), in_specs=[pl.BlockSpec((rows...]
    psum x1 -> x0, blocking collectives: 112 us -> none  [reduce_rows(): total = lax.psum(partial_value, 'wide')]
    dot_general x16 -> x4, matrix products: 95.6 us -> 2.6 us  [the longest x1 1.69 us: attention(): jnp.einsum('nshqd,shcd->nshqc', queries, keys, preferred_element_type=f32)]
    all_to_all x5, starting transfers between devices: 99.3 us -> 28.9 us  [the longest x4 25.4 us: exchange(): lax.all_to_all(value, 'wide', split_axis=0, concat_axis=0, tiled=True)]
    convert_element_type x6, other arithmetic: 58 us -> 1.95 us  [the longest x1 0.76 us: on_device(): lax.dynamic_slice_in_dim(norm_gain, me * width_dev, width_dev, 0)]
    all_to_all x0 -> x1, blocking collectives: none -> 45.6 us  [exchange_chips(): lax.all_to_all(value, 'wide', split_axis=0, concat_axis=0, tiled=True, ax...]
  transfers between devices with their start and end apart: 5 -> 10, of which waited for: 2 -> 2; matrix products, arithmetic and copies ran while one was open for 15% -> 15% of each run, Pallas kernels for 0% -> 40%
where the time goes in v1:
time: 260 us; the launch traced here: 256 us
  Pallas kernels  118 us (45%)
  blocking collectives  45.6 us (18%)
  local copies, waits for them, and re-layouts  38.6 us (15%)
  starting transfers between devices  30.4 us (12%)
  other arithmetic  11.2 us (4%)
  waiting for transfers between devices  8.6 us (3%)
  matrix products  2.6 us (1%)
    all_to_all x1, blocking collectives, exchange_chips(): lax.all_to_all(value, 'wide', split_axis=0, concat_axis=0, tiled=True, ax...  45.6 us
    pallas_call x3, Pallas kernels, row_levels(): pl.pallas_call(kernel, grid=(cols // tile,), in_specs=[pl.BlockSpec((rows...  31.8 us
    pallas_call x3, Pallas kernels, row_chunk_max(): pl.pallas_call(kernel, grid=(cols // tile,), in_specs=[pl.BlockSpec((rows...  30.9 us
    all_to_all x4, starting transfers between devices, exchange(): lax.all_to_all(value, 'wide', split_axis=0, concat_axis=0, tiled=True)  25.4 us
    unnamed x21, local copies, waits for them, and re-layouts  16.7 us
    pallas_call x1, Pallas kernels, gate_up_product(): pl.pallas_call(kernel, grid_spec=pltpu.PrefetchScalarGridSpec(num_scalar_...  14.6 us
    pallas_call x1, Pallas kernels, col_levels(): pl.pallas_call(kernel, grid=(rows // tile,), in_specs=[pl.BlockSpec((tile...  13.2 us
    pallas_call x1, Pallas kernels, col_chunk_max(): pl.pallas_call(kernel, grid=(rows // tile,), in_specs=[pl.BlockSpec((tile...  12.6 us
  transfers between devices with their start and end apart: 10, of which 2 were waited for; matrix products, arithmetic and copies ran while one was open for 15% of the time, Pallas kernels for 40%

profile of v1, /device:TPU:0, one launch (start us, length us, event | category | flops | bytes accessed | tf_op | source)
XLA Modules:
  0.0 255.7 jit_solution(9824154441136580165)
XLA Ops:
  0.7 1.4 dynamic_slice.15
  3.4 1.7 select_reduce_fusion
  7.2 7.4 %all-to-all-start = ((bf16[16,1,3,512]{3,2,1,0:T(4,128)(2,1)}), bf16[16,1,3,512]{3,2,1,0:T(4,128)(2,1)S(1)}, u32[]{:S(2)}, u32[]{:S(2)}) async-start(bf16[16,1,3,512]{3,2,1,0:T(4,128)(2,1)} %copy.105), calls=%async_computation | async-start | bytes 131072 | tf_op jit(solution)/shard_map/all_to_all | solution.py:359
  14.6 12.2 %row_chunk_max.4 = f32[5,16384]{1,0:T(8,128)} custom-call(bf16[320,16384]{1,0:T(8,128)(2,1)} %w_ref.11), custom_call_target="tpu_custom_call" | custom-call | flops 10485760 | bytes 10485760 | tf_op jit(solution)/shard_map/row_chunk_max/pallas_call | solution.py:46
  27.1 12.1 %row_chunk_max.5 = f32[5,16384]{1,0:T(8,128)} custom-call(bf16[320,16384]{1,0:T(8,128)(2,1)} %w_ref.13), custom_call_target="tpu_custom_call" | custom-call | flops 10485760 | bytes 10485760 | tf_op jit(solution)/shard_map/row_chunk_max/pallas_call | solution.py:46
  39.4 6.6 %row_chunk_max.3 = f32[4,5120]{1,0:T(4,128)} custom-call(bf16[512,5120]{1,0:T(8,128)(2,1)} %w_ref.9), custom_call_target="tpu_custom_call" | custom-call | flops 5242880 | bytes 5242880 | tf_op jit(solution)/shard_map/row_chunk_max/pallas_call | solution.py:46
  46.0 1.7 add_multiply_fusion.1
  50.5 6.8 %row_levels.3.l_ref = f8e4m3fn[512,5120]{1,0:T(32,128)(4,1)} custom-call(bf16[512,5120]{1,0:T(8,128)(2,1)} %w_ref.9, f32[4,5120]{1,0:T(4,128)} %get-tuple-element.33.f_ref), custom_call_target="tpu_custom_call" | custom-call | flops 10485760 | bytes 7864320 | tf_op jit(solution)/shard_map/row_levels/pallas_call | solution.py:145
  58.0 6.6 %out_product.1 = bf16[16,48,320]{2,1,0:T(8,128)(2,1)} custom-call(bf16[48,512]{1,0:T(8,128)(2,1)} %reshape.185.x_ref, f8e4m3fn[512,5120]{1,0:T(32,128)(4,1)} %row_levels.3.l_ref, f32[4,5120]{1,0:T(4,128)} %get-tuple-element.32.s_ref), custom_call_target="tpu_custom_call" | custom-call | flops 251658240 | bytes 2621440 | tf_op jit(solution)/shard_map/out_product/pallas_call | solution.py:207
  64.6 5.9 %all-to-all-start.1 = ((bf16[16,48,320]{2,1,0:T(8,128)(2,1)}), bf16[16,48,320]{2,1,0:T(8,128)(2,1)S(1)}, u32[]{:S(2)}, u32[]{:S(2)}) async-start(bf16[16,48,320]{2,1,0:T(8,128)(2,1)} %out_product.1), calls=%async_computation.1 | async-start | bytes 1179648 | tf_op jit(solution)/shard_map/all_to_all | solution.py:359
  70.5 2.5 dynamic_update_slice.19
  73.4 1.5 fusion.2
  74.9 1.5 reshape.187
  76.5 2.5 dynamic_update_slice.21
  79.4 1.5 fusion.1
  80.9 1.5 reshape.189
  82.4 1.4 fusion.13
  83.8 12.5 %row_levels.4.g_ref = f8e4m3fn[320,16384]{1,0:T(32,128)(4,1)} custom-call(bf16[320,16384]{1,0:T(8,128)(2,1)} %w_ref.11, f32[5,16384]{1,0:T(8,128)} %get-tuple-element.29.f_ref), custom_call_target="tpu_custom_call" | custom-call | flops 20971520 | bytes 15728640 | tf_op jit(solution)/shard_map/row_levels/pallas_call | solution.py:145
  96.3 12.4 %row_levels.5.u_ref = f8e4m3fn[320,16384]{1,0:T(32,128)(4,1)} custom-call(bf16[320,16384]{1,0:T(8,128)(2,1)} %w_ref.13, f32[5,16384]{1,0:T(8,128)} %get-tuple-element.42.f_ref), custom_call_target="tpu_custom_call" | custom-call | flops 20971520 | bytes 15728640 | tf_op jit(solution)/shard_map/row_levels/pallas_call | solution.py:145
  110.5 14.6 %gate_up_product.1 = bf16[2,8,48,2176]{3,2,1,0:T(8,128)(2,1)} custom-call(s32[1]{0:T(128)} %bitcast.core_ref, bf16[48,320]{1,0:T(8,128)(2,1)} %multiply_convert_fusion.x_ref, f8e4m3fn[320,16384]{1,0:T(32,128)(4,1)} %row_levels.4.g_ref, f32[5,16384]{1,0:T(8,128)} %get-tuple-element.28.gs_ref, f8e4m3fn[320,16384]{1,0:T(32,128)(4,1)} %row_levels.5.u_ref, ...), custom_call_target="tpu_custom_call" | custom-call | flops 1006632960 | bytes 10485760 | tf_op jit(solution)/shard_map/gate_up_product/pallas_call | solution.py:242
  125.1 1.7 slice_bitcast_fusion
  127.2 3.2 %collective-permute-done.2 = bf16[8,48,2176]{2,1,0:T(8,128)(2,1)S(1)} collective-permute-done((bf16[8,48,2176]{2,1,0:T(8,128)(2,1)S(1)}, bf16[8,48,2176]{2,1,0:T(8,128)(2,1)S(1)}, u32[]{:S(2)}, u32[]{:S(2)}) %collective-permute-start.2) | collective-permute-done | bytes 1671200 | tf_op jit(solution)/shard_map/ppermute | solution.py:355
  130.8 45.6 %all_to_all.30 = bf16[8,48,2176]{2,1,0:T(8,128)(2,1)S(1)} all-to-all(bf16[8,48,2176]{2,1,0:T(8,128)(2,1)S(1)} %fusion.3), channel_id=1, replica_groups={{0,2,4,6,8,10,12,14},{1,3,5,7,9,11,13,15},{16,18,20,22,24,26,28,30},{17..., dimensions={0} | all-to-all | bytes 3342336 | tf_op jit(solution)/shard_map/all_to_all | solution.py:365
  177.9 3.5 %all-to-all-start.3 = ((bf16[8,48,1024]{2,1,0:T(8,128)(2,1)}), bf16[8,48,1024]{2,1,0:T(8,128)(2,1)S(1)}, u32[]{:S(2)}, u32[]{:S(2)}) async-start(bf16[8,48,1024]{2,1,0:T(8,128)(2,1)} %broadcast_in_dim.111), calls=%async_computation.3 | async-start | bytes 1572864 | tf_op jit(solution)/shard_map/all_to_all | solution.py:365
  181.5 15.0 %copy.112.w_ref = bf16[16384,320]{1,0:T(8,128)(2,1)} copy(bf16[16384,320]{0,1:T(8,128)(2,1)} %param.14) | data formatting | bytes 20971520 | tf_op args[4]
  196.5 12.6 %col_chunk_max.1 = f32[128,320]{1,0:T(8,128)} custom-call(bf16[16384,320]{1,0:T(8,128)(2,1)} %copy.112.w_ref), custom_call_target="tpu_custom_call" | custom-call | flops 10485760 | bytes 10485760 | tf_op jit(solution)/shard_map/col_chunk_max/pallas_call | solution.py:76
  211.9 6.0 %all-to-all-start.5 = ((bf16[16,3,320]{2,1,0:T(4,128)(2,1)}), bf16[16,3,320]{2,1,0:T(4,128)(2,1)S(1)}, u32[]{:S(2)}, u32[]{:S(2)}) async-start(bf16[16,3,320]{2,1,0:T(4,128)(2,1)} %copy.114), calls=%async_computation.5 | async-start | bytes 98304 | tf_op jit(solution)/shard_map/all_to_all | solution.py:359
  218.8 13.2 %col_levels.1.l_ref = f8e4m3fn[16384,320]{1,0:T(32,128)(4,1)} custom-call(bf16[16384,320]{1,0:T(8,128)(2,1)} %copy.112.w_ref, f32[128,320]{1,0:T(8,128)} %get-tuple-element.31.f_ref), custom_call_target="tpu_custom_call" | custom-call | flops 20971520 | bytes 15728640 | tf_op jit(solution)/shard_map/col_levels/pallas_call | solution.py:169
  232.8 7.9 %down_product.1 = bf16[48,320]{1,0:T(8,128)(2,1)} custom-call(s32[1]{0:T(128)} %bitcast.core_ref, bf16[8,48,1024]{2,1,0:T(8,128)(2,1)} %copy-done.3, bf16[8,48,1024]{2,1,0:T(8,128)(2,1)} %copy-done.6, f8e4m3fn[16384,320]{1,0:T(32,128)(4,1)} %col_levels.1.l_ref, f32[128,320]{1,0:T(8,128)} %get-tuple-element.30.s_ref), custom_call_target="tpu_custom_call" | custom-call | flops 503316480 | bytes 5242880 | tf_op jit(solution)/shard_map/down_product/pallas_call | solution.py:299
  240.7 1.4 reshape.192
  242.1 6.0 %all-to-all-start.4 = ((bf16[16,3,320]{2,1,0:T(4,128)(2,1)}), bf16[16,3,320]{2,1,0:T(4,128)(2,1)S(1)}, u32[]{:S(2)}, u32[]{:S(2)}) async-start(bf16[16,3,320]{2,1,0:T(4,128)(2,1)} %reshape.192), calls=%async_computation.4 | async-start | bytes 98304 | tf_op jit(solution)/shard_map/all_to_all | solution.py:359
  249.5 5.4 %all-to-all-done.4 = bf16[16,3,320]{2,1,0:T(4,128)(2,1)S(1)} async-done(((bf16[16,3,320]{2,1,0:T(4,128)(2,1)}), bf16[16,3,320]{2,1,0:T(4,128)(2,1)S(1)}, u32[]{:S(2)}, u32[]{:S(2)}) %all-to-all-start.4) | async-done | bytes 30752 | tf_op jit(solution)/shard_map/all_to_all | solution.py:359
  (84 shorter events, 18.7 us)
Async XLA Ops:
  0.6 2.8 %copy-start = (bf16[3,1,8,8,128]{4,3,2,1,0:T(8,128)(2,1)S(1)}, bf16[3,1,8,8,128]{4,3,2,1,0:T(8,128)(2,1)}, u32[]{:S(2)}) copy-start(bf16[3,1,8,8,128]{4,3,2,1,0:T(8,128)(2,1)} %param.16) | copy-start | bytes 147460
  0.6 5.2 %copy-start.8 = (bf16[2,1,8,512,128]{4,3,2,1,0:T(8,128)(2,1)S(1)}, bf16[2,1,8,512,128]{4,3,2,1,0:T(8,128)(2,1)}, u32[]{:S(2)}) copy-start(bf16[2,1,8,512,128]{4,3,2,1,0:T(8,128)(2,1)} %param.17) | copy-start | bytes 6291460
  7.2 50.1 %all-to-all-start = ((bf16[16,1,3,512]{3,2,1,0:T(4,128)(2,1)}), bf16[16,1,3,512]{3,2,1,0:T(4,128)(2,1)S(1)}, u32[]{:S(2)}, u32[]{:S(2)}) async-start(bf16[16,1,3,512]{3,2,1,0:T(4,128)(2,1)} %copy.105), calls=%async_computation | async-start | bytes 131072 | tf_op jit(solution)/shard_map/all_to_all | solution.py:359
  26.7 43.8 %collective-permute-start = (f32[5,16384]{1,0:T(8,128)}, f32[5,16384]{1,0:T(8,128)}, u32[]{:S(2)}, u32[]{:S(2)}) collective-permute-start(f32[5,16384]{1,0:T(8,128)} %row_chunk_max.4), channel_id=1, source_target_pairs={{1,0},{0,1},{3,2},{2,3},{5,4},{4,5},{7,6},{6,7},{9,8},{8,9},{11,10... | collective-permute-start | bytes 983048 | tf_op jit(solution)/shard_map/ppermute | solution.py:98
  39.3 9.1 %copy-start.7 = (bf16[3,16,320]{2,1,0:T(8,128)(2,1)S(1)}, bf16[3,16,320]{2,1,0:T(8,128)(2,1)}, u32[]{:S(2)}) copy-start(bf16[3,16,320]{2,1,0:T(8,128)(2,1)} %param.10) | copy-start | bytes 92164
  39.3 9.4 %copy-start.5 = (f32[5,16384]{1,0:T(8,128)S(1)}, f32[5,16384]{1,0:T(8,128)}, u32[]{:S(2)}) copy-start(f32[5,16384]{1,0:T(8,128)} %row_chunk_max.4) | copy-start | bytes 983044
  39.3 37.2 %collective-permute-start.1 = (f32[5,16384]{1,0:T(8,128)}, f32[5,16384]{1,0:T(8,128)}, u32[]{:S(2)}, u32[]{:S(2)}) collective-permute-start(f32[5,16384]{1,0:T(8,128)} %row_chunk_max.5), channel_id=1, source_target_pairs={{1,0},{0,1},{3,2},{2,3},{5,4},{4,5},{7,6},{6,7},{9,8},{8,9},{11,10... | collective-permute-start | bytes 983048 | tf_op jit(solution)/shard_map/ppermute | solution.py:98
  46.0 3.6 %copy-start.4 = (f32[5,16384]{1,0:T(8,128)S(1)}, f32[5,16384]{1,0:T(8,128)}, u32[]{:S(2)}) copy-start(f32[5,16384]{1,0:T(8,128)} %row_chunk_max.5) | copy-start | bytes 983044
  64.6 44.2 %all-to-all-start.1 = ((bf16[16,48,320]{2,1,0:T(8,128)(2,1)}), bf16[16,48,320]{2,1,0:T(8,128)(2,1)S(1)}, u32[]{:S(2)}, u32[]{:S(2)}) async-start(bf16[16,48,320]{2,1,0:T(8,128)(2,1)} %out_product.1), calls=%async_computation.1 | async-start | bytes 1179648 | tf_op jit(solution)/shard_map/all_to_all | solution.py:359
  125.1 5.3 %copy-start.2 = (bf16[2,8,48,2176]{3,2,1,0:T(8,128)(2,1)S(1)}, bf16[2,8,48,2176]{3,2,1,0:T(8,128)(2,1)}, u32[]{:S(2)}) copy-start(bf16[2,8,48,2176]{3,2,1,0:T(8,128)(2,1)} %gate_up_product.1) | copy-start | bytes 10027012
  126.8 3.6 %collective-permute-start.2 = (bf16[8,48,2176]{2,1,0:T(8,128)(2,1)S(1)}, bf16[8,48,2176]{2,1,0:T(8,128)(2,1)S(1)}, u32[]{:S(2)}, u32[]{:S(2)}) collective-permute-start(bf16[8,48,2176]{2,1,0:T(8,128)(2,1)S(1)} %slice_bitcast_fusion), channel_id=1, source_target_pairs={{0,1},{1,0},{2,3},{3,2},{4,5},{5,4},{6,7},{7,6},{8,9},{9,8},{10,11... | collective-permute-start | bytes 5013512 | tf_op jit(solution)/shard_map/ppermute | solution.py:355
  177.9 32.2 %all-to-all-start.3 = ((bf16[8,48,1024]{2,1,0:T(8,128)(2,1)}), bf16[8,48,1024]{2,1,0:T(8,128)(2,1)S(1)}, u32[]{:S(2)}, u32[]{:S(2)}) async-start(bf16[8,48,1024]{2,1,0:T(8,128)(2,1)} %broadcast_in_dim.111), calls=%async_computation.3 | async-start | bytes 1572864 | tf_op jit(solution)/shard_map/all_to_all | solution.py:365
  209.1 1.7 collective-permute-start.4
  210.2 21.8 %copy-start.3 = (bf16[8,48,1024]{2,1,0:T(8,128)(2,1)}, bf16[8,48,1024]{2,1,0:T(8,128)(2,1)S(1)}, u32[]{:S(2)}) copy-start(bf16[8,48,1024]{2,1,0:T(8,128)(2,1)S(1)} %all-to-all-done.3.a_ref) | copy-start | bytes 2359300
  210.2 21.8 %collective-permute-start.3 = (bf16[8,48,1024]{2,1,0:T(8,128)(2,1)S(1)}, bf16[8,48,1024]{2,1,0:T(8,128)(2,1)S(1)}, u32[]{:S(2)}, u32[]{:S(2)}) collective-permute-start(bf16[8,48,1024]{2,1,0:T(8,128)(2,1)S(1)} %all-to-all-done.3.a_ref), channel_id=1, source_target_pairs={{0,1},{1,0},{2,3},{3,2},{4,5},{5,4},{6,7},{7,6},{8,9},{9,8},{10,11... | collective-permute-start | bytes 2359304 | tf_op jit(solution)/shard_map/ppermute | solution.py:355
  211.9 30.2 %all-to-all-start.5 = ((bf16[16,3,320]{2,1,0:T(4,128)(2,1)}), bf16[16,3,320]{2,1,0:T(4,128)(2,1)S(1)}, u32[]{:S(2)}, u32[]{:S(2)}) async-start(bf16[16,3,320]{2,1,0:T(4,128)(2,1)} %copy.114), calls=%async_computation.5 | async-start | bytes 98304 | tf_op jit(solution)/shard_map/all_to_all | solution.py:359
  231.9 0.9 copy-start.6
  231.9 23.7 %copy-start.1 = (bf16[3,1,8,8,128]{4,3,2,1,0:T(8,128)(2,1)S(1)}, bf16[3,1,8,8,128]{4,3,2,1,0:T(8,128)(2,1)}, u32[]{:S(2)}) copy-start(bf16[3,1,8,8,128]{4,3,2,1,0:T(8,128)(2,1)} %param.16) | copy-start | bytes 147460
  242.1 12.8 %all-to-all-start.4 = ((bf16[16,3,320]{2,1,0:T(4,128)(2,1)}), bf16[16,3,320]{2,1,0:T(4,128)(2,1)S(1)}, u32[]{:S(2)}, u32[]{:S(2)}) async-start(bf16[16,3,320]{2,1,0:T(4,128)(2,1)} %reshape.192), calls=%async_computation.4 | async-start | bytes 98304 | tf_op jit(solution)/shard_map/all_to_all | solution.py:359

commit v2 on v1

v2 whole, which is shorter than its diff:
```python
import functools
import math

import jax
import jax.numpy as jnp
from jax import lax
from jax.experimental import pallas as pl
from jax.experimental.pallas import tpu as pltpu
from jax.sharding import PartitionSpec as P

BLOCK = 128
QMAX = 448.0
EPS_NORM = 1e-06
EPS_SCALE = 1e-06
NEG = -1e30
LANES = 128
VMEM = 56 * 2**20

f32 = jnp.float32
bf16 = jnp.bfloat16
f8 = jnp.float8_e4m3fn


def params(**more):
    return pltpu.CompilerParams(vmem_limit_bytes=VMEM, **more)


def cost(flops, read):
    return pl.CostEstimate(flops=int(flops), bytes_accessed=int(read), transcendentals=0)


def pick_tile(cols, most):
    tile = most
    while cols % tile:
        tile -= LANES
    return tile


def chunk_max(weights, chunk, tile):
    rows, cols = weights[0].shape
    parts = rows // chunk
    count = len(weights)

    def kernel(*refs):
        o_ref = refs[count]
        for a in range(count):
            tops = [
                jnp.max(
                    jnp.abs(refs[a][pl.ds(j * chunk, chunk), :]), axis=0, keepdims=True
                ).astype(f32)
                for j in range(parts)
            ]
            tops = jnp.concatenate(tops + [tops[0]] * (8 - parts), axis=0)
            for g in range(tile // LANES):
                at = slice(g * LANES, (g + 1) * LANES)
                top = jnp.max(tops[:, at], axis=1, keepdims=True)
                o_ref[a, :, at] = jnp.broadcast_to(top, (8, LANES))

    return pl.pallas_call(
        kernel,
        grid=(cols // tile,),
        in_specs=[pl.BlockSpec((rows, tile), lambda i: (0, i))] * count,
        out_specs=pl.BlockSpec((count, 8, tile), lambda i: (0, 0, i)),
        out_shape=jax.ShapeDtypeStruct((count, 8, cols), f32),
        compiler_params=params(),
        cost_estimate=cost(2 * count * rows * cols, 2 * count * rows * cols),
        name="chunk_max",
    )(*weights)


def levels_of(weights, own, got, odd, chunk, tile):
    rows, cols = weights[0].shape
    parts = rows // chunk
    count = len(weights)
    extra = 1 if got is None else 2

    def kernel(odd_ref, *refs):
        w_refs = refs[:count]
        top_refs = refs[count : count + extra]
        o_refs = refs[count + extra : 2 * count + extra]
        s_ref = refs[2 * count + extra]
        factor = refs[2 * count + extra + 1]
        is_odd = odd_ref[0] == 1
        for a in range(count):
            if got is None:
                tops = top_refs[0][a]
            else:
                mine, other = top_refs[0], top_refs[1]
                joined = []
                for j in range(parts):
                    even = mine[a, pl.ds(j ^ 1, 1)] if j ^ 1 < parts else other[a, pl.ds(0, 1)]
                    back = j - 1 if j % 2 == 0 else j + 1
                    near = other[a, pl.ds(parts - 1, 1)] if back < 0 else mine[a, pl.ds(back, 1)]
                    joined.append(
                        jnp.maximum(mine[a, pl.ds(j, 1)], jnp.where(is_odd, near, even))
                    )
                tops = jnp.concatenate(joined + [joined[0]] * (8 - parts), axis=0)
            largest = tops + EPS_SCALE
            factor[a] = QMAX / largest
            s_ref[a] = largest * (1.0 / QMAX)
        for a in range(count):
            for j in range(parts):
                rows_at = pl.ds(j * chunk, chunk)
                value = w_refs[a][rows_at, :].astype(f32) * factor[a, pl.ds(j, 1), :]
                o_refs[a][rows_at, :] = value.astype(f8)

    tops = [own] if got is None else [own, got]
    return pl.pallas_call(
        kernel,
        grid_spec=pltpu.PrefetchScalarGridSpec(
            num_scalar_prefetch=1,
            grid=(cols // tile,),
            in_specs=[pl.BlockSpec((rows, tile), lambda i, c: (0, i))] * count
            + [pl.BlockSpec((count, 8, tile), lambda i, c: (0, 0, i))] * extra,
            out_specs=[pl.BlockSpec((rows, tile), lambda i, c: (0, i))] * count
            + [pl.BlockSpec((count, 8, tile), lambda i, c: (0, 0, i))],
            scratch_shapes=[pltpu.VMEM((count, 8, tile), f32)],
        ),
        out_shape=[jax.ShapeDtypeStruct((rows, cols), f8)] * count
        + [jax.ShapeDtypeStruct((count, 8, cols), f32)],
        compiler_params=params(),
        cost_estimate=cost(4 * count * rows * cols, 3 * count * rows * cols),
        name="levels_of",
    )(odd, *weights, *tops)


def join_group(parts, size, dim):
    count = lax.axis_size("wide")
    me = lax.axis_index("wide")
    share = parts.shape[dim]
    shape = list(parts.shape)
    shape[dim] = share * size
    out = jnp.zeros(shape, parts.dtype)
    out = lax.dynamic_update_slice_in_dim(out, parts, (me % size) * share, dim)
    for step in range(1, size):
        perm = [(i // size * size + (i + step) % size, i) for i in range(count)]
        got = lax.ppermute(parts, "wide", perm)
        out = lax.dynamic_update_slice_in_dim(out, got, ((me + step) % size) * share, dim)
    return out


def quantize(weights, tops, chunk, odd, tile):
    rows = weights[0].shape[0]
    size = math.lcm(rows, BLOCK) // rows
    per = BLOCK // chunk
    parts = rows // chunk
    if size == 1 and per == 1:
        return levels_of(weights, tops, None, odd, chunk, tile)
    if size == 2 and per == 2:
        return levels_of(weights, tops, swap_cores(tops), odd, chunk, tile)
    joined = join_group(tops[:, :parts], size, 1)
    blocks = joined.reshape(joined.shape[0], -1, per, joined.shape[2])
    joined = jnp.broadcast_to(jnp.max(blocks, axis=2, keepdims=True), blocks.shape)
    joined = joined.reshape(joined.shape[0], size * parts, -1)
    own = lax.dynamic_slice_in_dim(joined, (lax.axis_index("wide") % size) * parts, parts, 1)
    own = jnp.pad(own, ((0, 0), (0, 8 - parts), (0, 0)))
    return levels_of(weights, own, None, odd, chunk, tile)


def scaled_rows(x_ref, l_ref, scale_of, chunk, parts):
    total = None
    for j in range(parts):
        at = pl.ds(j * chunk, chunk)
        part = jnp.dot(x_ref[:, at], l_ref[at, :].astype(bf16), preferred_element_type=f32)
        part = part * scale_of(j)
        total = part if total is None else total + part
    return total


def out_product(left, levels, scale, chunk, owners):
    count, rows = left.shape
    cols = levels.shape[1]
    parts = rows // chunk
    share = cols // owners
    tile = pick_tile(cols, 2 * math.lcm(share, LANES))
    per = tile // share

    def kernel(x_ref, l_ref, s_ref, o_ref):
        total = scaled_rows(x_ref, l_ref, lambda j: s_ref[0, pl.ds(j, 1), :], chunk, parts)
        total = total.astype(bf16)
        for q in range(per):
            o_ref[q] = total[:, q * share : (q + 1) * share]

    return pl.pallas_call(
        kernel,
        grid=(cols // tile,),
        in_specs=[
            pl.BlockSpec((count, rows), lambda i: (0, 0)),
            pl.BlockSpec((rows, tile), lambda i: (0, i)),
            pl.BlockSpec((1, 8, tile), lambda i: (0, 0, i)),
        ],
        out_specs=pl.BlockSpec((per, count, share), lambda i: (i, 0, 0)),
        out_shape=jax.ShapeDtypeStruct((owners, count, share), bf16),
        compiler_params=params(),
        cost_estimate=cost(2 * count * rows * cols, rows * cols),
        name="out_product",
    )(left, levels, scale)


def gate_up_product(side, left, gate, up, scale, power, chunk, owners, out_type):
    count, rows = left.shape
    parts = rows // chunk
    share = gate.shape[1] // owners
    chips = owners // 2
    width = 2 * share + LANES
    per = max(1, min(chips, 2048 // share))
    tile = per * share
    steps = chips // per

    def kernel(side_ref, x_ref, g_ref, u_ref, s_ref, p_ref, o_ref):
        for a, ref in enumerate((g_ref, u_ref)):
            total = scaled_rows(
                x_ref, ref, lambda j, a=a: s_ref[a, pl.ds(j, 1), :], chunk, parts
            ).astype(out_type)
            for q in range(per):
                o_ref[q, :, pl.ds(a * share, share)] = total[:, q * share : (q + 1) * share]
        for q in range(per):
            o_ref[q, :, pl.ds(2 * share, LANES)] = p_ref[...].astype(out_type)

    def columns(i, side_ref):
        return (0, side_ref[0] * steps + i)

    def fixed(i, side_ref):
        return (0, 0)

    return pl.pallas_call(
        kernel,
        grid_spec=pltpu.PrefetchScalarGridSpec(
            num_scalar_prefetch=1,
            grid=(steps,),
            in_specs=[
                pl.BlockSpec((count, rows), fixed),
                pl.BlockSpec((rows, tile), columns),
                pl.BlockSpec((rows, tile), columns),
                pl.BlockSpec((2, 8, tile), lambda i, side_ref: (0, 0, side_ref[0] * steps + i)),
                pl.BlockSpec((count, LANES), fixed),
            ],
            out_specs=pl.BlockSpec((per, count, width), lambda i, side_ref: (i, 0, 0)),
        ),
        out_shape=jax.ShapeDtypeStruct((chips, count, width), out_type),
        compiler_params=params(),
        cost_estimate=cost(4 * count * rows * share * chips, 2 * rows * share * chips),
        name="gate_up_product",
    )(side, left, gate, up, scale, power)


def down_product(side, act, levels, scale):
    chips, count, share = act.shape
    width, hidden = levels.shape
    blocks = share // BLOCK
    per = max(1, min(chips, 4096 // share))
    tile = per * share
    steps = chips // per

    def kernel(side_ref, a_ref, l_ref, s_ref, o_ref):
        total = jnp.zeros((count, width), f32)
        for q in range(per):
            for j in range(blocks):
                block = q * blocks + j
                part = lax.dot_general(
                    a_ref[q, :, pl.ds(j * BLOCK, BLOCK)],
                    l_ref[:, pl.ds(block * BLOCK, BLOCK)].astype(bf16),
                    (((1,), (1,)), ((), ())),
                    preferred_element_type=f32,
                )
                total = total + part * s_ref[pl.ds(block, 1), :]

        @pl.when(pl.program_id(0) == 0)
        def _():
            o_ref[...] = total

        @pl.when(pl.program_id(0) > 0)
        def _():
            o_ref[...] += total

    return pl.pallas_call(
        kernel,
        grid_spec=pltpu.PrefetchScalarGridSpec(
            num_scalar_prefetch=1,
            grid=(steps,),
            in_specs=[
                pl.BlockSpec((per, count, share), lambda i, c: (i, 0, 0)),
                pl.BlockSpec((width, tile), lambda i, c: (0, c[0] * steps + i)),
                pl.BlockSpec((per * blocks, width), lambda i, c: (c[0] * steps + i, 0)),
            ],
            out_specs=pl.BlockSpec((count, width), lambda i, c: (0, 0)),
        ),
        out_shape=jax.ShapeDtypeStruct((count, width), f32),
        compiler_params=params(),
        cost_estimate=cost(2 * count * width * hidden // 2, width * hidden // 2),
        name="down_product",
    )(side, act, levels, scale)


def attention(queries, kv_cache, new_kv, live):
    steps = queries.shape[0]
    factor = queries.shape[-1] ** (-0.5)
    keys = kv_cache[0]
    values = kv_cache[1]
    new_keys = new_kv[:, 0]
    new_values = new_kv[:, 1]
    position = jnp.arange(keys.shape[2], dtype=jnp.int32)
    valid = position[None, None, None, None, :] < live[None, :, None, None, None]
    cached = (
        jnp.einsum("nshqd,shcd->nshqc", queries, keys, preferred_element_type=f32) * factor
    )
    recent = (
        jnp.einsum("nshqd,tshd->nshqt", queries, new_keys, preferred_element_type=f32) * factor
    )
    order = jnp.arange(steps, dtype=jnp.int32)
    fresh = (order[None, :] <= order[:, None])[:, None, None, None, :]
    top = jnp.maximum(
        jnp.max(jnp.where(valid, cached, NEG), axis=-1),
        jnp.max(jnp.where(fresh, recent, NEG), axis=-1),
    )[..., None]
    e_cached = jnp.where(valid, jnp.exp(cached - top), 0.0)
    e_recent = jnp.where(fresh, jnp.exp(recent - top), 0.0)
    total = jnp.sum(e_cached, axis=-1, keepdims=True) + jnp.sum(e_recent, axis=-1, keepdims=True)
    p_cached = (e_cached / total).astype(bf16)
    p_recent = (e_recent / total).astype(bf16)
    mixed = jnp.einsum("nshqc,shcd->nshqd", p_cached, values, preferred_element_type=f32)
    mixed = mixed + jnp.einsum(
        "nshqt,tshd->nshqd", p_recent, new_values, preferred_element_type=f32
    )
    return mixed.astype(bf16)


def swap_cores(value):
    count = lax.axis_size("wide")
    return lax.ppermute(value, "wide", [(i, i ^ 1) for i in range(count)])


def exchange(value):
    return lax.all_to_all(value, "wide", split_axis=0, concat_axis=0, tiled=True)


def exchange_chips(value):
    count = lax.axis_size("wide")
    groups = [list(range(core, count, 2)) for core in range(2)]
    return lax.all_to_all(
        value, "wide", split_axis=0, concat_axis=0, tiled=True, axis_index_groups=groups
    )


def on_device(
    residual_in,
    norm_gain,
    gate_weight,
    up_weight,
    down_weight,
    out_weight,
    queries,
    kv_cache,
    new_kv,
    cache_len,
):
    owners = lax.axis_size("wide")
    me = lax.axis_index("wide")
    core = (me % 2).astype(jnp.int32).reshape(1)
    steps, seqs, width_dev = residual_in.shape
    seq_dev = seqs // owners
    tokens = steps * seqs
    mine = steps * seq_dev
    width = width_dev * owners

    odd = core

    live = lax.dynamic_slice_in_dim(cache_len, me * seq_dev, seq_dev, 0)
    attn_out = attention(queries, kv_cache, new_kv, live)
    heads = attn_out.reshape(steps, seq_dev, owners, -1)
    heads = exchange(jnp.transpose(heads, (2, 1, 0, 3)))

    out_chunk = math.gcd(out_weight.shape[0], BLOCK)
    out_tile = pick_tile(out_weight.shape[1], 2560)
    out_tops = chunk_max([out_weight], out_chunk, out_tile)
    out_levels, out_scale = quantize([out_weight], out_tops, out_chunk, odd, out_tile)
    chunk = math.gcd(gate_weight.shape[0], BLOCK)
    tile = pick_tile(gate_weight.shape[1], 2048)
    down_tile = pick_tile(gate_weight.shape[1], 4096)
    gate_up_tops = chunk_max([gate_weight, up_weight], chunk, tile)
    heads, out_levels, out_scale, gate_up_tops = lax.optimization_barrier(
        (heads, out_levels, out_scale, gate_up_tops)
    )

    heads = heads.reshape(tokens, -1)
    projected = exchange(out_product(heads, out_levels, out_scale, out_chunk, owners))

    gate_levels, up_levels, gate_up_scale = quantize(
        [gate_weight, up_weight], gate_up_tops, chunk, odd, tile
    )
    projected, gate_levels, up_levels, gate_up_scale = lax.optimization_barrier(
        (projected, gate_levels, up_levels, gate_up_scale)
    )

    projected = jnp.sum(projected.astype(f32), axis=0)
    residual = jnp.transpose(residual_in, (1, 0, 2)).reshape(tokens, width_dev)
    hidden = (residual.astype(f32) + projected).astype(bf16)

    states = hidden.astype(f32)
    gain = lax.dynamic_slice_in_dim(norm_gain, me * width_dev, width_dev, 0).astype(f32)
    scaled = (states * gain).astype(bf16)
    squares = jnp.sum(states * states, axis=1, keepdims=True)
    high = squares.astype(bf16)
    low = (squares - high.astype(f32)).astype(bf16)
    lane = lax.broadcasted_iota(jnp.int32, (tokens, LANES), 1)
    power = jnp.where(lane == 0, high, jnp.where(lane == 1, low, jnp.zeros_like(low)))

    product = functools.partial(
        gate_up_product,
        left=scaled,
        gate=gate_levels,
        up=up_levels,
        scale=gate_up_scale,
        power=power,
        chunk=chunk,
        owners=owners,
    )
    sent = product(1 - core, out_type=bf16)
    got = swap_cores(sent)
    kept = product(core, out_type=f32)
    chip_sum = exchange_chips((kept + got.astype(f32)).astype(bf16))

    down = down_weight.T
    down_chunk = math.gcd(down.shape[0], BLOCK)
    down_tops = chunk_max([down], down_chunk, down_tile)
    down_levels, down_scale = quantize([down], down_tops, down_chunk, odd, down_tile)
    down_parts = down.shape[0] // down_chunk
    down_scale = jnp.repeat(down_scale[0, :down_parts, ::LANES].T, down_chunk, axis=1)
    hidden_out = exchange(hidden.reshape(owners, mine, width_dev))
    hidden_out = jnp.transpose(
        hidden_out.reshape(owners, seq_dev, steps, width_dev), (2, 1, 0, 3)
    ).reshape(steps, seq_dev, width)
    chip_sum, down_levels, down_scale, hidden_out = lax.optimization_barrier(
        (chip_sum, down_levels, down_scale, hidden_out)
    )

    summed = jnp.sum(chip_sum.astype(f32), axis=0)
    share = gate_weight.shape[1] // owners
    total = summed[:, 2 * share : 2 * share + 1] + summed[:, 2 * share + 1 : 2 * share + 2]
    scale = lax.rsqrt(total / width + EPS_NORM)
    gate = summed[:, :share] * scale
    up = summed[:, share : 2 * share] * scale
    act = (jax.nn.silu(gate) * up).astype(bf16)

    same = exchange_chips(jnp.broadcast_to(act[None], (owners // 2,) + act.shape))
    other = swap_cores(same)
    ffn = down_product(core, same, down_levels, down_scale)
    ffn = ffn + down_product(1 - core, other, down_levels, down_scale)
    ffn = exchange(ffn.astype(bf16).reshape(owners, mine, width_dev))
    ffn_out = jnp.transpose(
        ffn.reshape(owners, seq_dev, steps, width_dev), (2, 1, 0, 3)
    ).reshape(steps, seq_dev, width)
    return (ffn_out, attn_out, hidden_out)


def solution(mesh):
    placed = (
        P("grp", None, "wide"),
        P(),
        P("wide", None),
        P("wide", None),
        P(None, "wide"),
        P("wide", None),
        P("grp", "wide", None, None, None),
        P(None, ("grp", "wide"), None, None, None),
        P("grp", None, "wide", None, None),
        P("grp"),
    )
    return jax.shard_map(
        on_device,
        mesh=mesh,
        in_specs=placed,
        out_specs=(
            P("grp", "wide", None),
            P("grp", "wide", None, None, None),
            P("grp", "wide", None),
        ),
        check_vma=False,
    )
```

time: 260 us -> 180 us (0.69)
  Pallas kernels: 118 us -> 73.3 us
  local copies, waits for them, and re-layouts: 38.6 us -> 12.2 us
  blocking collectives: 45.6 us -> 23.7 us
  waiting for transfers between devices: 8.6 us -> 27.9 us
  other arithmetic: 11.2 us -> 8.22 us
    pallas_call x8 -> x6, Pallas kernels: 88.4 us -> 49.1 us  [the longest x3 27.1 us: levels_of(): pl.pallas_call(kernel, grid_spec=pltpu.PrefetchScalarGridSpec(num_scalar_...]
    all_to_all x1, blocking collectives: 45.6 us -> 23.7 us  [exchange_chips(): lax.all_to_all(value, 'wide', split_axis=0, concat_axis=0, tiled=True, ax...]
    all_to_all x1, waiting for transfers between devices: 0.01 us -> 19.6 us  [exchange_chips(): lax.all_to_all(value, 'wide', split_axis=0, concat_axis=0, tiled=True, ax...]
    unnamed x21 -> x19, local copies, waits for them, and re-layouts: 16.7 us -> 3.37 us
    dynamic_update_slice x6 -> x0, local copies, waits for them, and re-layouts: 6.73 us -> none  [the longest x3 5.01 us: join_group(): lax.dynamic_update_slice_in_dim(out, got, (me + step) % size * share, dim)]
    reshape x5 -> x1, local copies, waits for them, and re-layouts: 5.27 us -> 0.64 us  [on_device(): ffn = exchange(ffn.astype(bf16).reshape(owners, mine, width_dev))]
    convert_element_type x1 -> x2, other arithmetic: 0.4 us -> 4.38 us  [the longest x1 3.48 us: on_device(): chip_sum = exchange_chips((kept + got.astype(f32)).astype(bf16))]
    div x3 -> x0, other arithmetic: 3.88 us -> none  [the longest x2 3.1 us: row_scales(): return (QMAX / largest, largest / QMAX)]
  transfers between devices with their start and end apart: 10 -> 9, of which waited for: 2 -> 3; matrix products, arithmetic and copies ran while one was open for 15% -> 5% of each run, Pallas kernels for 40% -> 36%
where the time goes in v2:
time: 180 us; the launch traced here: 178 us
  Pallas kernels  73.3 us (41%)
  starting transfers between devices  29.4 us (16%)
  waiting for transfers between devices  27.9 us (16%)
  blocking collectives  23.7 us (13%)
  local copies, waits for them, and re-layouts  12.2 us (7%)
  other arithmetic  8.22 us (5%)
  matrix products  2.6 us (1%)
    pallas_call x3, Pallas kernels, levels_of(): pl.pallas_call(kernel, grid_spec=pltpu.PrefetchScalarGridSpec(num_scalar_...  27.1 us
    all_to_all x1, blocking collectives, exchange_chips(): lax.all_to_all(value, 'wide', split_axis=0, concat_axis=0, tiled=True, ax...  23.7 us
    all_to_all x4, starting transfers between devices, exchange(): lax.all_to_all(value, 'wide', split_axis=0, concat_axis=0, tiled=True)  22.6 us
    pallas_call x3, Pallas kernels, chunk_max(): pl.pallas_call(kernel, grid=(cols // tile,), in_specs=[pl.BlockSpec((rows...  22 us
    all_to_all x1, waiting for transfers between devices, exchange_chips(): lax.all_to_all(value, 'wide', split_axis=0, concat_axis=0, tiled=True, ax...  19.6 us
    pallas_call x2, Pallas kernels, gate_up_product(): pl.pallas_call(kernel, grid_spec=pltpu.PrefetchScalarGridSpec(num_scalar_...  11.9 us
    pallas_call x2, Pallas kernels, down_product(): pl.pallas_call(kernel, grid_spec=pltpu.PrefetchScalarGridSpec(num_scalar_...  7.94 us
    all_to_all x4, waiting for transfers between devices, exchange(): lax.all_to_all(value, 'wide', split_axis=0, concat_axis=0, tiled=True)  6.14 us
  transfers between devices with their start and end apart: 9, of which 3 were waited for; matrix products, arithmetic and copies ran while one was open for 5% of the time, Pallas kernels for 36%

profile of v2, /device:TPU:0, one launch (start us, length us, event | category | flops | bytes accessed | tf_op | source)
XLA Modules:
  0.0 178.2 jit_solution(10910027423350695618)
XLA Ops:
  0.7 1.4 dynamic_slice.6
  3.4 1.7 select_reduce_fusion
  7.2 7.4 %all-to-all-start = ((bf16[16,1,3,512]{3,2,1,0:T(4,128)(2,1)}), bf16[16,1,3,512]{3,2,1,0:T(4,128)(2,1)S(1)}, u32[]{:S(2)}, u32[]{:S(2)}) async-start(bf16[16,1,3,512]{3,2,1,0:T(4,128)(2,1)} %copy.89), calls=%async_computation | async-start | bytes 131072 | tf_op jit(solution)/shard_map/all_to_all | solution.py:334
  14.6 3.7 %chunk_max.3.refs_1_ = f32[1,8,5120]{2,1,0:T(8,128)} custom-call(bf16[512,5120]{1,0:T(8,128)(2,1)} %refs_0_.5), custom_call_target="tpu_custom_call" | custom-call | flops 5242880 | bytes 5242880 | tf_op jit(solution)/shard_map/chunk_max/pallas_call | solution.py:59
  18.3 4.4 %levels_of.3 = (f8e4m3fn[512,5120]{1,0:T(32,128)(4,1)}, f32[1,8,5120]{2,1,0:T(8,128)}) custom-call(s32[1]{0:T(128)} %bitcast.odd_ref.side_ref, bf16[512,5120]{1,0:T(8,128)(2,1)} %refs_0_.5, f32[1,8,5120]{2,1,0:T(8,128)} %chunk_max.3.refs_1_), custom_call_target="tpu_custom_call" | custom-call | flops 10485760 | bytes 7864320 | tf_op jit(solution)/shard_map/levels_of/pallas_call | solution.py:108
  22.7 11.8 %chunk_max.4.refs_2_ = f32[2,8,16384]{2,1,0:T(8,128)} custom-call(bf16[320,16384]{1,0:T(8,128)(2,1)} %refs_0_.7, bf16[320,16384]{1,0:T(8,128)(2,1)} %refs_1_.3), custom_call_target="tpu_custom_call" | custom-call | flops 20971520 | bytes 20971520 | tf_op jit(solution)/shard_map/chunk_max/pallas_call | solution.py:59
  35.6 4.3 %out_product.1 = bf16[16,48,320]{2,1,0:T(8,128)(2,1)} custom-call(bf16[48,512]{1,0:T(8,128)(2,1)} %reshape.162.x_ref, f8e4m3fn[512,5120]{1,0:T(32,128)(4,1)} %get-tuple-element.25.l_ref, f32[1,8,5120]{2,1,0:T(8,128)} %get-tuple-element.26.s_ref), custom_call_target="tpu_custom_call" | custom-call | flops 251658240 | bytes 2621440 | tf_op jit(solution)/shard_map/out_product/pallas_call | solution.py:184
  39.9 5.8 %all-to-all-start.1 = ((bf16[16,48,320]{2,1,0:T(8,128)(2,1)}), bf16[16,48,320]{2,1,0:T(8,128)(2,1)S(1)}, u32[]{:S(2)}, u32[]{:S(2)}) async-start(bf16[16,48,320]{2,1,0:T(8,128)(2,1)} %out_product.1), calls=%async_computation.1 | async-start | bytes 1179648 | tf_op jit(solution)/shard_map/all_to_all | solution.py:334
  45.8 0.8 dynamic-slice_convert_fusion
  46.6 1.0 copy-done.3
  47.6 14.3 %levels_of.4 = (f8e4m3fn[320,16384]{1,0:T(32,128)(4,1)}, f8e4m3fn[320,16384]{1,0:T(32,128)(4,1)}, f32[2,8,16384]{2,1,0:T(8,128)}) custom-call(s32[1]{0:T(128)} %bitcast.odd_ref.side_ref, bf16[320,16384]{1,0:T(8,128)(2,1)} %refs_0_.7, bf16[320,16384]{1,0:T(8,128)(2,1)} %refs_1_.3, f32[2,8,16384]{2,1,0:T(8,128)} %chunk_max.4.refs_2_, f32[2,8,16384]{2,1,0:T(8,128)} %copy-done.3), custom_call_target="tpu_custom_call" | custom-call | flops 41943040 | bytes 31457280 | tf_op jit(solution)/shard_map/levels_of/pallas_call | solution.py:108
  63.6 5.8 %gate_up_product.3 = bf16[8,48,2176]{2,1,0:T(8,128)(2,1)} custom-call(s32[1]{0:T(128)S(6)} %sub.33.side_ref, bf16[48,320]{1,0:T(8,128)(2,1)} %multiply_convert_fusion.x_ref, f8e4m3fn[320,16384]{1,0:T(32,128)(4,1)} %get-tuple-element.32.g_ref, f8e4m3fn[320,16384]{1,0:T(32,128)(4,1)} %get-tuple-element.33.u_ref, f32[2,8,16384]{2,1,0:T(8,128)} %get-tuple-element.34.s_ref, ...), custom_call_target="tpu_custom_call" | custom-call | flops 503316480 | bytes 5242880 | tf_op jit(solution)/shard_map/gate_up_product/pallas_call | solution.py:226
  70.5 5.8 %all-to-all-start.3 = ((bf16[16,3,320]{2,1,0:T(4,128)(2,1)}), bf16[16,3,320]{2,1,0:T(4,128)(2,1)S(1)}, u32[]{:S(2)}, u32[]{:S(2)}) async-start(bf16[16,3,320]{2,1,0:T(4,128)(2,1)} %copy.92), calls=%async_computation.3 | async-start | bytes 98304 | tf_op jit(solution)/shard_map/all_to_all | solution.py:334
  76.2 6.1 %gate_up_product.2 = f32[8,48,2176]{2,1,0:T(8,128)} custom-call(s32[1]{0:T(128)} %bitcast.odd_ref.side_ref, bf16[48,320]{1,0:T(8,128)(2,1)} %multiply_convert_fusion.x_ref, f8e4m3fn[320,16384]{1,0:T(32,128)(4,1)} %get-tuple-element.32.g_ref, f8e4m3fn[320,16384]{1,0:T(32,128)(4,1)} %get-tuple-element.33.u_ref, f32[2,8,16384]{2,1,0:T(8,128)} %get-tuple-element.34.s_ref, ...), custom_call_target="tpu_custom_call" | custom-call | flops 503316480 | bytes 5242880 | tf_op jit(solution)/shard_map/gate_up_product/pallas_call | solution.py:226
  82.4 3.5 %add_convert_fusion = bf16[8,48,2176]{2,1,0:T(8,128)(2,1)} fusion(f32[8,48,2176]{2,1,0:T(8,128)} %gate_up_product.2, bf16[8,48,2176]{2,1,0:T(8,128)(2,1)S(1)} %collective-permute-done.1), kind=kLoop, calls=%fused_computation.1 | loop fusion | flops 2506752 | bytes 6684672 | tf_op jit(solution)/shard_map/convert_element_type | solution.py:421
  85.8 5.9 %all-to-all-start.2 = ((bf16[8,48,2176]{2,1,0:T(8,128)(2,1)}), bf16[8,48,2176]{2,1,0:T(8,128)(2,1)S(1)}, u32[]{:S(2)}, u32[]{:S(2)}) async-start(bf16[8,48,2176]{2,1,0:T(8,128)(2,1)} %add_convert_fusion), calls=%async_computation.2 | async-start | bytes 3342336 | tf_op jit(solution)/shard_map/all_to_all | solution.py:340
  91.7 6.5 %chunk_max.5.refs_1_ = f32[1,8,16384]{2,1,0:T(8,128)} custom-call(bf16[320,16384]{1,0:T(8,128)(2,1)} %bitcast.90), custom_call_target="tpu_custom_call" | custom-call | flops 10485760 | bytes 10485760 | tf_op jit(solution)/shard_map/chunk_max/pallas_call | solution.py:59
  98.3 2.1 %collective-permute-done.2.refs_2_ = f32[1,8,16384]{2,1,0:T(8,128)S(1)} collective-permute-done((f32[1,8,16384]{2,1,0:T(8,128)}, f32[1,8,16384]{2,1,0:T(8,128)S(1)}, u32[]{:S(2)}, u32[]{:S(2)}) %collective-permute-start.2) | collective-permute-done | bytes 524320 | tf_op jit(solution)/shard_map/ppermute | solution.py:330
  100.4 0.8 copy-done.5
  101.2 8.4 %levels_of.5 = (f8e4m3fn[320,16384]{1,0:T(32,128)(4,1)}, f32[1,8,16384]{2,1,0:T(8,128)}) custom-call(s32[1]{0:T(128)} %bitcast.odd_ref.side_ref, bf16[320,16384]{1,0:T(8,128)(2,1)} %bitcast.91, f32[1,8,16384]{2,1,0:T(8,128)} %chunk_max.5.refs_1_, f32[1,8,16384]{2,1,0:T(8,128)} %copy-done.5), custom_call_target="tpu_custom_call" | custom-call | flops 20971520 | bytes 15728640 | tf_op jit(solution)/shard_map/levels_of/pallas_call | solution.py:108
  109.5 1.2 slice.31
  110.8 0.7 reshape.165
  111.5 19.6 %all-to-all-done.2 = bf16[8,48,2176]{2,1,0:T(8,128)(2,1)S(1)} async-done(((bf16[8,48,2176]{2,1,0:T(8,128)(2,1)}), bf16[8,48,2176]{2,1,0:T(8,128)(2,1)S(1)}, u32[]{:S(2)}, u32[]{:S(2)}) %all-to-all-start.2) | async-done | bytes 1671200 | tf_op jit(solution)/shard_map/all_to_all | solution.py:340
  131.8 23.7 %all_to_all.30.a_ref = bf16[8,48,1024]{2,1,0:T(8,128)(2,1)S(1)} all-to-all(bf16[8,48,1024]{2,1,0:T(8,128)(2,1)S(1)} %broadcast_in_dim.92), channel_id=1, replica_groups={{0,2,4,6,8,10,12,14},{1,3,5,7,9,11,13,15},{16,18,20,22,24,26,28,30},{17..., dimensions={0} | all-to-all | bytes 1572864 | tf_op jit(solution)/shard_map/all_to_all | solution.py:340
  155.6 1.0 copy.94.s_ref
  156.6 4.0 %down_product.2 = f32[48,320]{1,0:T(8,128)} custom-call(s32[1]{0:T(128)} %bitcast.odd_ref.side_ref, bf16[8,48,1024]{2,1,0:T(8,128)(2,1)} %copy-done.2, f8e4m3fn[320,16384]{1,0:T(32,128)(4,1)} %get-tuple-element.38.l_ref, f32[128,320]{1,0:T(8,128)} %copy.94.s_ref), custom_call_target="tpu_custom_call" | custom-call | flops 251658240 | bytes 2621440 | tf_op jit(solution)/shard_map/down_product/pallas_call | solution.py:276
  160.5 0.9 copy-done.4
  161.5 4.0 %down_product.3 = f32[48,320]{1,0:T(8,128)} custom-call(s32[1]{0:T(128)S(6)} %sub.33.side_ref, bf16[8,48,1024]{2,1,0:T(8,128)(2,1)} %copy-done.4, f8e4m3fn[320,16384]{1,0:T(32,128)(4,1)} %get-tuple-element.38.l_ref, f32[128,320]{1,0:T(8,128)} %copy.94.s_ref), custom_call_target="tpu_custom_call" | custom-call | flops 251658240 | bytes 2621440 | tf_op jit(solution)/shard_map/down_product/pallas_call | solution.py:276
  165.4 0.9 add_convert_fusion.1
  167.0 3.7 %all-to-all-start.5 = ((bf16[16,3,320]{2,1,0:T(4,128)(2,1)}), bf16[16,3,320]{2,1,0:T(4,128)(2,1)S(1)}, u32[]{:S(2)}, u32[]{:S(2)}) async-start(bf16[16,3,320]{2,1,0:T(4,128)(2,1)} %reshape.166), calls=%async_computation.5 | async-start | bytes 98304 | tf_op jit(solution)/shard_map/all_to_all | solution.py:334
  171.3 6.1 %all-to-all-done.5 = bf16[16,3,320]{2,1,0:T(4,128)(2,1)S(1)} async-done(((bf16[16,3,320]{2,1,0:T(4,128)(2,1)}), bf16[16,3,320]{2,1,0:T(4,128)(2,1)S(1)}, u32[]{:S(2)}, u32[]{:S(2)}) %all-to-all-start.5) | async-done | bytes 30752 | tf_op jit(solution)/shard_map/all_to_all | solution.py:334
  177.5 0.7 reshape.168
  (61 shorter events, 9.3 us)
Async XLA Ops:
  0.6 2.8 %copy-start = (bf16[3,1,8,8,128]{4,3,2,1,0:T(8,128)(2,1)S(1)}, bf16[3,1,8,8,128]{4,3,2,1,0:T(8,128)(2,1)}, u32[]{:S(2)}) copy-start(bf16[3,1,8,8,128]{4,3,2,1,0:T(8,128)(2,1)} %param.16) | copy-start | bytes 147460
  0.6 5.2 %copy-start.8 = (bf16[2,1,8,512,128]{4,3,2,1,0:T(8,128)(2,1)S(1)}, bf16[2,1,8,512,128]{4,3,2,1,0:T(8,128)(2,1)}, u32[]{:S(2)}) copy-start(bf16[2,1,8,512,128]{4,3,2,1,0:T(8,128)(2,1)} %param.17) | copy-start | bytes 6291460
  7.2 27.3 %all-to-all-start = ((bf16[16,1,3,512]{3,2,1,0:T(4,128)(2,1)}), bf16[16,1,3,512]{3,2,1,0:T(4,128)(2,1)S(1)}, u32[]{:S(2)}, u32[]{:S(2)}) async-start(bf16[16,1,3,512]{3,2,1,0:T(4,128)(2,1)} %copy.89), calls=%async_computation | async-start | bytes 131072 | tf_op jit(solution)/shard_map/all_to_all | solution.py:334
  34.5 11.2 %copy-start.7 = (bf16[3,16,320]{2,1,0:T(8,128)(2,1)S(1)}, bf16[3,16,320]{2,1,0:T(8,128)(2,1)}, u32[]{:S(2)}) copy-start(bf16[3,16,320]{2,1,0:T(8,128)(2,1)} %param.10) | copy-start | bytes 92164
  34.5 12.1 %collective-permute-start = (f32[2,8,16384]{2,1,0:T(8,128)}, f32[2,8,16384]{2,1,0:T(8,128)S(1)}, u32[]{:S(2)}, u32[]{:S(2)}) collective-permute-start(f32[2,8,16384]{2,1,0:T(8,128)} %chunk_max.4.refs_2_), channel_id=1, source_target_pairs={{0,1},{1,0},{2,3},{3,2},{4,5},{5,4},{6,7},{7,6},{8,9},{9,8},{10,11... | collective-permute-start | bytes 3145736 | tf_op jit(solution)/shard_map/ppermute | solution.py:330
  39.9 22.0 %all-to-all-start.1 = ((bf16[16,48,320]{2,1,0:T(8,128)(2,1)}), bf16[16,48,320]{2,1,0:T(8,128)(2,1)S(1)}, u32[]{:S(2)}, u32[]{:S(2)}) async-start(bf16[16,48,320]{2,1,0:T(8,128)(2,1)} %out_product.1), calls=%async_computation.1 | async-start | bytes 1179648 | tf_op jit(solution)/shard_map/all_to_all | solution.py:334
  46.6 1.0 copy-start.3
  69.4 12.9 %collective-permute-start.1 = (bf16[8,48,2176]{2,1,0:T(8,128)(2,1)}, bf16[8,48,2176]{2,1,0:T(8,128)(2,1)S(1)}, u32[]{:S(2)}, u32[]{:S(2)}) collective-permute-start(bf16[8,48,2176]{2,1,0:T(8,128)(2,1)} %gate_up_product.3), channel_id=1, source_target_pairs={{0,1},{1,0},{2,3},{3,2},{4,5},{5,4},{6,7},{7,6},{8,9},{9,8},{10,11... | collective-permute-start | bytes 5013512 | tf_op jit(solution)/shard_map/ppermute | solution.py:330
  70.5 15.4 %all-to-all-start.3 = ((bf16[16,3,320]{2,1,0:T(4,128)(2,1)}), bf16[16,3,320]{2,1,0:T(4,128)(2,1)S(1)}, u32[]{:S(2)}, u32[]{:S(2)}) async-start(bf16[16,3,320]{2,1,0:T(4,128)(2,1)} %copy.92), calls=%async_computation.3 | async-start | bytes 98304 | tf_op jit(solution)/shard_map/all_to_all | solution.py:334
  85.8 45.3 %all-to-all-start.2 = ((bf16[8,48,2176]{2,1,0:T(8,128)(2,1)}), bf16[8,48,2176]{2,1,0:T(8,128)(2,1)S(1)}, u32[]{:S(2)}, u32[]{:S(2)}) async-start(bf16[8,48,2176]{2,1,0:T(8,128)(2,1)} %add_convert_fusion), calls=%async_computation.2 | async-start | bytes 3342336 | tf_op jit(solution)/shard_map/all_to_all | solution.py:340
  98.3 2.1 %collective-permute-start.2 = (f32[1,8,16384]{2,1,0:T(8,128)}, f32[1,8,16384]{2,1,0:T(8,128)S(1)}, u32[]{:S(2)}, u32[]{:S(2)}) collective-permute-start(f32[1,8,16384]{2,1,0:T(8,128)} %chunk_max.5.refs_1_), channel_id=1, source_target_pairs={{0,1},{1,0},{2,3},{3,2},{4,5},{5,4},{6,7},{7,6},{8,9},{9,8},{10,11... | collective-permute-start | bytes 1572872 | tf_op jit(solution)/shard_map/ppermute | solution.py:330
  100.4 0.8 copy-start.5
  155.6 1.0 copy-start.2
  155.6 5.0 %collective-permute-start.3 = (bf16[8,48,1024]{2,1,0:T(8,128)(2,1)S(1)}, bf16[8,48,1024]{2,1,0:T(8,128)(2,1)S(1)}, u32[]{:S(2)}, u32[]{:S(2)}) collective-permute-start(bf16[8,48,1024]{2,1,0:T(8,128)(2,1)S(1)} %all_to_all.30.a_ref), channel_id=1, source_target_pairs={{0,1},{1,0},{2,3},{3,2},{4,5},{5,4},{6,7},{7,6},{8,9},{9,8},{10,11... | collective-permute-start | bytes 2359304 | tf_op jit(solution)/shard_map/ppermute | solution.py:330
  156.6 21.7 %copy-start.1 = (bf16[3,1,8,8,128]{4,3,2,1,0:T(8,128)(2,1)S(1)}, bf16[3,1,8,8,128]{4,3,2,1,0:T(8,128)(2,1)}, u32[]{:S(2)}) copy-start(bf16[3,1,8,8,128]{4,3,2,1,0:T(8,128)(2,1)} %param.16) | copy-start | bytes 147460
  160.5 4.9 %copy-start.6 = (f32[48,320]{1,0:T(8,128)S(1)}, f32[48,320]{1,0:T(8,128)}, u32[]{:S(2)}) copy-start(f32[48,320]{1,0:T(8,128)} %down_product.2) | copy-start | bytes 184324
  160.5 0.9 copy-start.4
  167.0 10.5 %all-to-all-start.5 = ((bf16[16,3,320]{2,1,0:T(4,128)(2,1)}), bf16[16,3,320]{2,1,0:T(4,128)(2,1)S(1)}, u32[]{:S(2)}, u32[]{:S(2)}) async-start(bf16[16,3,320]{2,1,0:T(4,128)(2,1)} %reshape.166), calls=%async_computation.5 | async-start | bytes 98304 | tf_op jit(solution)/shard_map/all_to_all | solution.py:334

commit v3 on v2

v3 whole, which is shorter than its diff:
```python
import functools
import math

import jax
import jax.numpy as jnp
from jax import lax
from jax.experimental import pallas as pl
from jax.experimental.pallas import tpu as pltpu
from jax.sharding import PartitionSpec as P

BLOCK = 128
QMAX = 448.0
EPS_NORM = 1e-06
EPS_SCALE = 1e-06
NEG = -1e30
LANES = 128
VMEM = 56 * 2**20

f32 = jnp.float32
bf16 = jnp.bfloat16
f8 = jnp.float8_e4m3fn


def params(**more):
    return pltpu.CompilerParams(vmem_limit_bytes=VMEM, **more)


def cost(flops, read):
    return pl.CostEstimate(flops=int(flops), bytes_accessed=int(read), transcendentals=0)


def pick_tile(cols, most):
    tile = most
    while cols % tile:
        tile -= LANES
    return tile


def spread_lanes(tops):
    out = []
    for g in range(tops.shape[1] // LANES):
        top = jnp.max(tops[:, g * LANES : (g + 1) * LANES], axis=1, keepdims=True)
        out.append(jnp.broadcast_to(top, (tops.shape[0], LANES)))
    return jnp.concatenate(out, axis=1)


def rows_max(ref, start, size):
    return jnp.max(jnp.abs(ref[pl.ds(start, size), :]), axis=0, keepdims=True).astype(f32)


def fill_rows(rows):
    return jnp.concatenate(rows + [rows[0]] * (8 - len(rows)), axis=0)


def chunk_max(place, weights, cols, chunk, tile):
    rows = weights[0].shape[0]
    parts = rows // chunk
    count = len(weights)
    steps = cols // tile

    def kernel(place_ref, *refs):
        for a in range(count):
            tops = [rows_max(refs[a], j * chunk, chunk) for j in range(parts)]
            refs[count][a] = spread_lanes(fill_rows(tops))

    return pl.pallas_call(
        kernel,
        grid_spec=pltpu.PrefetchScalarGridSpec(
            num_scalar_prefetch=1,
            grid=(steps,),
            in_specs=[pl.BlockSpec((rows, tile), lambda i, p: (0, p[1] * steps + i))] * count,
            out_specs=pl.BlockSpec((count, 8, tile), lambda i, p: (0, 0, i)),
        ),
        out_shape=jax.ShapeDtypeStruct((count, 8, cols), f32),
        compiler_params=params(),
        cost_estimate=cost(2 * count * rows * cols, 2 * count * rows * cols),
        name="chunk_max",
    )(place, *weights)


def edge_max(place, weights, cols, chunk, tile):
    parts = weights[0].shape[0] // chunk
    count = len(weights)
    steps = cols // tile

    def kernel(place_ref, *refs):
        refs[count][...] = spread_lanes(
            fill_rows([rows_max(refs[a], 0, chunk) for a in range(count)])
        )

    return pl.pallas_call(
        kernel,
        grid_spec=pltpu.PrefetchScalarGridSpec(
            num_scalar_prefetch=1,
            grid=(steps,),
            in_specs=[
                pl.BlockSpec(
                    (chunk, tile), lambda i, p: ((1 - p[0]) * (parts - 1), p[1] * steps + i)
                )
            ]
            * count,
            out_specs=pl.BlockSpec((8, tile), lambda i, p: (0, i)),
        ),
        out_shape=jax.ShapeDtypeStruct((8, cols), f32),
        compiler_params=params(),
        cost_estimate=cost(2 * count * chunk * cols, 2 * count * chunk * cols),
        name="edge_max",
    )(place, *weights)


def levels_of(place, weights, edge, first, tops, cols, chunk, tile):
    rows = weights[0].shape[0]
    parts = rows // chunk
    count = len(weights)
    steps = cols // tile

    def kernel(place_ref, *refs):
        w_refs = refs[:count]
        top_ref = refs[count]
        o_refs = refs[count + 1 : 2 * count + 1]
        s_ref = refs[2 * count + 1]
        factor = refs[2 * count + 2]
        odd = place_ref[0] == 1
        for a in range(count):
            if edge is None:
                joined = top_ref[a]
            else:
                other = top_ref[pl.ds(first + a, 1), :]
                mine = [rows_max(w_refs[a], j * chunk, chunk) for j in range(parts)]
                joined = []
                for j in range(parts):
                    even = mine[j ^ 1] if j ^ 1 < parts else other
                    back = j - 1 if j % 2 == 0 else j + 1
                    near = other if back < 0 else mine[back]
                    joined.append(jnp.maximum(mine[j], jnp.where(odd, near, even)))
                joined = spread_lanes(fill_rows(joined))
            largest = joined + EPS_SCALE
            factor[a] = QMAX / largest
            s_ref[a] = largest * (1.0 / QMAX)
        for a in range(count):
            for j in range(parts):
                rows_at = pl.ds(j * chunk, chunk)
                value = w_refs[a][rows_at, :].astype(f32) * factor[a, pl.ds(j, 1), :]
                o_refs[a][rows_at, :] = value.astype(f8)

    if edge is None:
        top_spec = pl.BlockSpec((count, 8, tile), lambda i, p: (0, 0, i))
    else:
        top_spec = pl.BlockSpec((8, tile), lambda i, p: (0, i))
    return pl.pallas_call(
        kernel,
        grid_spec=pltpu.PrefetchScalarGridSpec(
            num_scalar_prefetch=1,
            grid=(steps,),
            in_specs=[pl.BlockSpec((rows, tile), lambda i, p: (0, p[1] * steps + i))] * count
            + [top_spec],
            out_specs=[pl.BlockSpec((rows, tile), lambda i, p: (0, i))] * count
            + [pl.BlockSpec((count, 8, tile), lambda i, p: (0, 0, i))],
            scratch_shapes=[pltpu.VMEM((count, 8, tile), f32)],
        ),
        out_shape=[jax.ShapeDtypeStruct((rows, cols), f8)] * count
        + [jax.ShapeDtypeStruct((count, 8, cols), f32)],
        compiler_params=params(),
        cost_estimate=cost(4 * count * rows * cols, 3 * count * rows * cols),
        name="levels_of",
    )(place, *weights, tops if edge is None else edge)


def join_group(parts, size, dim):
    count = lax.axis_size("wide")
    me = lax.axis_index("wide")
    share = parts.shape[dim]
    shape = list(parts.shape)
    shape[dim] = share * size
    out = jnp.zeros(shape, parts.dtype)
    out = lax.dynamic_update_slice_in_dim(out, parts, (me % size) * share, dim)
    for step in range(1, size):
        perm = [(i // size * size + (i + step) % size, i) for i in range(count)]
        got = lax.ppermute(parts, "wide", perm)
        out = lax.dynamic_update_slice_in_dim(out, got, ((me + step) % size) * share, dim)
    return out


def pair_shares_blocks(rows):
    return math.lcm(rows, BLOCK) == 2 * rows and math.gcd(rows, BLOCK) == BLOCK // 2


def joined_max(place, weights, cols, chunk, tile):
    rows = weights[0].shape[0]
    size = math.lcm(rows, BLOCK) // rows
    per = BLOCK // chunk
    parts = rows // chunk
    tops = chunk_max(place, weights, cols, chunk, tile)
    if size == 1:
        return tops
    joined = join_group(tops[:, :parts], size, 1)
    blocks = joined.reshape(joined.shape[0], -1, per, joined.shape[2])
    joined = jnp.broadcast_to(jnp.max(blocks, axis=2, keepdims=True), blocks.shape)
    joined = joined.reshape(joined.shape[0], size * parts, -1)
    own = lax.dynamic_slice_in_dim(joined, (lax.axis_index("wide") % size) * parts, parts, 1)
    return jnp.pad(own, ((0, 0), (0, 8 - parts), (0, 0)))


def out_product(left, weight, owners):
    count, rows = left.shape
    cols = weight.shape[1]
    parts = rows // BLOCK
    share = cols // owners
    tile = pick_tile(cols, 2 * math.lcm(share, LANES))
    per = tile // share

    def kernel(x_ref, w_ref, o_ref):
        tops = spread_lanes(
            jnp.concatenate([rows_max(w_ref, j * BLOCK, BLOCK) for j in range(parts)], axis=0)
        )
        largest = tops + EPS_SCALE
        factor = QMAX / largest
        scale = largest * (1.0 / QMAX)
        total = None
        for j in range(parts):
            at = pl.ds(j * BLOCK, BLOCK)
            levels = (w_ref[at, :].astype(f32) * factor[j : j + 1]).astype(f8).astype(bf16)
            part = jnp.dot(x_ref[:, at], levels, preferred_element_type=f32)
            part = part * scale[j : j + 1]
            total = part if total is None else total + part
        total = total.astype(bf16)
        for q in range(per):
            o_ref[q] = total[:, q * share : (q + 1) * share]

    return pl.pallas_call(
        kernel,
        grid=(cols // tile,),
        in_specs=[
            pl.BlockSpec((count, rows), lambda i: (0, 0)),
            pl.BlockSpec((rows, tile), lambda i: (0, i)),
        ],
        out_specs=pl.BlockSpec((per, count, share), lambda i: (i, 0, 0)),
        out_shape=jax.ShapeDtypeStruct((owners, count, share), bf16),
        compiler_params=params(),
        cost_estimate=cost(8 * count * rows * cols, 2 * rows * cols),
        name="out_product",
    )(left, weight)


def gate_up_product(at, left, gate, up, scale, power, added, share, chips, chunk, staged):
    count, rows = left.shape
    parts = rows // chunk
    extra = 0 if power is None else power.shape[1]
    width = 2 * share + extra
    split = 2 if chips % 2 == 0 else 1
    tile, chips_at = chips * share // split, chips // split

    def kernel(at_ref, x_ref, g_ref, u_ref, s_ref, *refs):
        refs = list(refs)
        o_refs = [refs.pop()]
        if staged:
            o_refs = [refs.pop(), o_refs[0]]
        p_ref = None if power is None else refs.pop(0)
        add_ref = None if added is None else refs.pop(0)
        blocks = []
        for a, ref in enumerate((g_ref, u_ref)):
            total = None
            for j in range(parts):
                rows_at = pl.ds(j * chunk, chunk)
                part = jnp.dot(
                    x_ref[:, rows_at], ref[rows_at, :].astype(bf16), preferred_element_type=f32
                )
                part = part * s_ref[a, pl.ds(j, 1), :]
                total = part if total is None else total + part
            blocks.append(total)
        for q in range(chips_at):
            here = slice(q * share, (q + 1) * share)
            values = [total[:, here] for total in blocks]
            if power is not None:
                values.append(p_ref[...])
            starts = [0, share, 2 * share][: len(values)]

            def write(o_ref, position):
                for start, value in zip(starts, values):
                    lanes = pl.ds(start, value.shape[1])
                    if added is not None:
                        value = value + add_ref[q, :, lanes].astype(f32)
                    o_ref[position, :, lanes] = value.astype(bf16)

            if not staged:
                write(o_refs[0], q)
                continue
            away = (pl.program_id(0) * chips_at + q) ^ at_ref[1]
            position, rest = 0, away // 2
            for _ in range(chips.bit_length() - 2):
                position, rest = position * 2 + rest % 2, rest // 2
            for side in range(2):
                pl.when(away % 2 == side)(functools.partial(write, o_refs[side], position))

    def fixed(i, p):
        return (0, 0)

    owner_spec = pl.BlockSpec((chips_at, count, width), lambda i, p: (i, 0, 0))
    in_specs = [
        pl.BlockSpec((count, rows), fixed),
        pl.BlockSpec((rows, tile), lambda i, p: (0, p[0] * split + i)),
        pl.BlockSpec((rows, tile), lambda i, p: (0, p[0] * split + i)),
        pl.BlockSpec((2, 8, tile), lambda i, p: (0, 0, p[0] * split + i)),
    ]
    operands = [left, gate, up, scale]
    if power is not None:
        in_specs.append(pl.BlockSpec((count, extra), fixed))
        operands.append(power)
    if added is not None:
        in_specs.append(owner_spec)
        operands.append(added)
    out_spec, out_shape = owner_spec, jax.ShapeDtypeStruct((chips, count, width), bf16)
    if staged:
        out_spec = [pl.BlockSpec((chips // 2, count, width), lambda i, p: (0, 0, 0))] * 2
        out_shape = [jax.ShapeDtypeStruct((chips // 2, count, width), bf16)] * 2
    return pl.pallas_call(
        kernel,
        grid_spec=pltpu.PrefetchScalarGridSpec(
            num_scalar_prefetch=1, grid=(split,), in_specs=in_specs, out_specs=out_spec
        ),
        out_shape=out_shape,
        compiler_params=params(),
        cost_estimate=cost(4 * count * rows * share * chips, 2 * rows * share * chips),
        name="gate_up_product",
    )(at, *operands)


def down_product(at, act, levels, scale, added, staged):
    chips, count, share = act.shape
    width, hidden = levels.shape
    blocks = share // BLOCK
    tile = chips * share

    def kernel(at_ref, a_ref, l_ref, s_ref, *refs):
        total = refs[0][...] if added is not None else jnp.zeros((count, width), f32)
        for q in range(chips):
            chip = q
            if staged:
                chip, rest = 0, q
                for _ in range(chips.bit_length() - 1):
                    chip, rest = chip * 2 + rest % 2, rest // 2
                chip = chip ^ at_ref[1]
            for j in range(blocks):
                block = chip * blocks + j
                start = block * BLOCK
                if staged:
                    start = pl.multiple_of(start, BLOCK)
                part = lax.dot_general(
                    a_ref[q, :, pl.ds(j * BLOCK, BLOCK)],
                    l_ref[:, pl.ds(start, BLOCK)].astype(bf16),
                    (((1,), (1,)), ((), ())),
                    preferred_element_type=f32,
                )
                total = total + part * s_ref[pl.ds(block, 1), :]
        refs[-1][...] = total

    fixed = pl.BlockSpec((count, width), lambda i, p: (0, 0))
    return pl.pallas_call(
        kernel,
        grid_spec=pltpu.PrefetchScalarGridSpec(
            num_scalar_prefetch=1,
            grid=(1,),
            in_specs=[
                pl.BlockSpec((chips, count, share), lambda i, p: (0, 0, 0)),
                pl.BlockSpec((width, tile), lambda i, p: (0, p[0])),
                pl.BlockSpec((chips * blocks, width), lambda i, p: (p[0], 0)),
            ]
            + ([] if added is None else [fixed]),
            out_specs=fixed,
        ),
        out_shape=jax.ShapeDtypeStruct((count, width), f32),
        compiler_params=params(),
        cost_estimate=cost(2 * count * width * tile, width * tile),
        name="down_product",
    )(at, act, levels, scale, *([] if added is None else [added]))


def attention(queries, kv_cache, new_kv, live):
    steps = queries.shape[0]
    factor = queries.shape[-1] ** (-0.5)
    keys = kv_cache[0]
    values = kv_cache[1]
    new_keys = new_kv[:, 0]
    new_values = new_kv[:, 1]
    position = jnp.arange(keys.shape[2], dtype=jnp.int32)
    valid = position[None, None, None, None, :] < live[None, :, None, None, None]
    cached = (
        jnp.einsum("nshqd,shcd->nshqc", queries, keys, preferred_element_type=f32) * factor
    )
    recent = (
        jnp.einsum("nshqd,tshd->nshqt", queries, new_keys, preferred_element_type=f32) * factor
    )
    order = jnp.arange(steps, dtype=jnp.int32)
    fresh = (order[None, :] <= order[:, None])[:, None, None, None, :]
    top = jnp.maximum(
        jnp.max(jnp.where(valid, cached, NEG), axis=-1),
        jnp.max(jnp.where(fresh, recent, NEG), axis=-1),
    )[..., None]
    e_cached = jnp.where(valid, jnp.exp(cached - top), 0.0)
    e_recent = jnp.where(fresh, jnp.exp(recent - top), 0.0)
    total = jnp.sum(e_cached, axis=-1, keepdims=True) + jnp.sum(e_recent, axis=-1, keepdims=True)
    p_cached = (e_cached / total).astype(bf16)
    p_recent = (e_recent / total).astype(bf16)
    mixed = jnp.einsum("nshqc,shcd->nshqd", p_cached, values, preferred_element_type=f32)
    mixed = mixed + jnp.einsum(
        "nshqt,tshd->nshqd", p_recent, new_values, preferred_element_type=f32
    )
    return mixed.astype(bf16)


def swap_cores(value):
    count = lax.axis_size("wide")
    return lax.ppermute(value, "wide", [(i, i ^ 1) for i in range(count)])


def exchange(value):
    return lax.all_to_all(value, "wide", split_axis=0, concat_axis=0, tiled=True)


def exchange_chips(value):
    count = lax.axis_size("wide")
    groups = [list(range(core, count, 2)) for core in range(2)]
    return lax.all_to_all(
        value, "wide", split_axis=0, concat_axis=0, tiled=True, axis_index_groups=groups
    )


def exchange_halves(keep, send):
    count = lax.axis_size("wide")
    bit = 2
    while True:
        got = lax.ppermute(send, "wide", [(i, i ^ bit) for i in range(count)])
        total = keep.astype(f32) + got.astype(f32)
        bit *= 2
        if bit == count:
            return total[0]
        total = total.astype(bf16)
        half = total.shape[0] // 2
        keep, send = total[:half], total[half:]


def gather_halves(value):
    count = lax.axis_size("wide")
    value = value[None]
    bit = count // 2
    while bit > 1:
        got = lax.ppermute(value, "wide", [(i, i ^ bit) for i in range(count)])
        value = jnp.concatenate([value, got], axis=0)
        bit //= 2
    return value


def on_device(
    residual_in,
    norm_gain,
    gate_weight,
    up_weight,
    down_weight,
    out_weight,
    queries,
    kv_cache,
    new_kv,
    cache_len,
):
    owners = lax.axis_size("wide")
    groups = lax.axis_size("grp")
    me = lax.axis_index("wide")
    steps, seqs, width_dev = residual_in.shape
    seq_dev = seqs // owners
    tokens = steps * seqs
    mine = steps * seq_dev
    width = width_dev * owners
    chips = owners // 2
    hidden_units = gate_weight.shape[1]

    halves = 2
    parts = groups if hidden_units % (groups * owners * halves * BLOCK) == 0 else 1
    units = hidden_units // parts
    share = units // (owners * halves)
    part = lax.axis_index("grp") if parts > 1 else jnp.zeros((), jnp.int32)
    odd = me % 2
    place = jnp.stack([odd, part]).astype(jnp.int32)

    live = lax.dynamic_slice_in_dim(cache_len, me * seq_dev, seq_dev, 0)
    attn_out = attention(queries, kv_cache, new_kv, live)
    heads = attn_out.reshape(steps, seq_dev, owners, -1)
    heads = exchange(jnp.transpose(heads, (2, 1, 0, 3)))

    down = down_weight.T
    rows = gate_weight.shape[0]
    chunk = math.gcd(rows, BLOCK)
    tile = pick_tile(units, 2048)
    paired = pair_shares_blocks(rows) and down.shape[0] == rows
    if paired:
        edge = edge_max(place, [gate_weight, up_weight, down], units, chunk, pick_tile(units, 4096))
        heads, edge = lax.optimization_barrier((heads, edge))
        edge = swap_cores(edge)

    heads = heads.reshape(tokens, -1)
    projected = exchange(out_product(heads, out_weight, owners))

    if paired:
        gate_levels, up_levels, gate_up_scale = levels_of(
            place, [gate_weight, up_weight], edge, 0, None, units, chunk, tile
        )
    else:
        tops = joined_max(place, [gate_weight, up_weight], units, chunk, tile)
        gate_levels, up_levels, gate_up_scale = levels_of(
            place, [gate_weight, up_weight], None, 0, tops, units, chunk, tile
        )
    projected, gate_levels, up_levels, gate_up_scale = lax.optimization_barrier(
        (projected, gate_levels, up_levels, gate_up_scale)
    )

    projected = jnp.sum(projected.astype(f32), axis=0)
    residual = jnp.transpose(residual_in, (1, 0, 2)).reshape(tokens, width_dev)
    hidden = (residual.astype(f32) + projected).astype(bf16)

    states = hidden
    if parts > 1:
        if groups == 2:
            got = lax.ppermute(hidden, "grp", [(0, 1), (1, 0)])
            first = part == 0
            states = jnp.concatenate(
                [jnp.where(first, hidden, got), jnp.where(first, got, hidden)], axis=0
            )
        else:
            states = lax.all_gather(hidden, "grp", axis=0, tiled=True)
    states = states.astype(f32)
    gain = lax.dynamic_slice_in_dim(norm_gain, me * width_dev, width_dev, 0).astype(f32)
    scaled = (states * gain).astype(bf16)
    squares = jnp.sum(states * states, axis=1, keepdims=True)
    spread = -(-2 * owners // LANES) * LANES
    lane = lax.broadcasted_iota(jnp.int32, (states.shape[0], spread), 1)
    high = squares.astype(bf16).astype(f32)
    power = jnp.where(lane == 2 * me, high, jnp.where(lane == 2 * me + 1, squares - high, 0.0))

    def run_at(half, side):
        return jnp.stack([half * 2 + side, me // 2]).astype(jnp.int32)

    def product(half, side, added, staged):
        return gate_up_product(
            run_at(half, side),
            scaled,
            gate_levels,
            up_levels,
            gate_up_scale,
            power if half == 0 else None,
            added,
            share,
            chips,
            chunk,
            staged,
        )

    sent = [swap_cores(product(half, 1 - odd, None, False)) for half in range(halves)]
    keep, send = product(0, odd, sent[0], True)
    kept = product(1, odd, sent[1], False)
    kept, place = lax.optimization_barrier((kept, place))
    sums = [exchange_halves(keep, send), exchange_chips(kept)]

    down_chunk = math.gcd(down.shape[0], BLOCK)
    down_tile = pick_tile(units, 4096)
    if paired:
        down_levels, down_scale = levels_of(
            place, [down], edge, 2, None, units, down_chunk, down_tile
        )
    else:
        tops = joined_max(place, [down], units, down_chunk, down_tile)
        down_levels, down_scale = levels_of(
            place, [down], None, 0, tops, units, down_chunk, down_tile
        )
    down_scale = down_scale[0, : down.shape[0] // down_chunk, ::LANES].T
    down_scale = jnp.repeat(down_scale, down_chunk, axis=1)
    sums[0], down_levels, down_scale = lax.optimization_barrier((sums[0], down_levels, down_scale))

    squares = jnp.sum(sums[0][:, 2 * share :], axis=1, keepdims=True)
    scale = lax.rsqrt(squares / width + EPS_NORM)

    def act_of(summed):
        gate = summed[:, :share] * scale
        up = summed[:, share : 2 * share] * scale
        return (jax.nn.silu(gate) * up).astype(bf16)

    same = gather_halves(act_of(sums[0]))
    act = act_of(jnp.sum(sums[1].astype(f32), axis=0))
    last = exchange_chips(jnp.broadcast_to(act[None], (chips,) + act.shape))
    other = swap_cores(same)
    ffn = down_product(run_at(0, odd), same, down_levels, down_scale, None, True)
    ffn = down_product(run_at(0, 1 - odd), other, down_levels, down_scale, ffn, True)
    last, ffn = lax.optimization_barrier((last, ffn))
    other = swap_cores(last)
    ffn = down_product(run_at(1, odd), last, down_levels, down_scale, ffn, False)
    ffn = down_product(run_at(1, 1 - odd), other, down_levels, down_scale, ffn, False)

    axes = ("grp", "wide") if parts > 1 else "wide"
    blocks = (parts * owners, mine, width_dev)
    both = jnp.concatenate(
        [ffn.astype(bf16).reshape(blocks), states.astype(bf16).reshape(blocks)], axis=1
    )
    both = lax.all_to_all(both, axes, split_axis=0, concat_axis=0, tiled=True)
    both = both.reshape(parts, owners, 2, seq_dev, steps, width_dev)
    ffn = both[0, :, 0]
    if parts > 1:
        ffn = jnp.sum(both[:, :, 0].astype(f32), axis=0).astype(bf16)
    ffn_out = jnp.transpose(ffn, (2, 1, 0, 3)).reshape(steps, seq_dev, width)
    hidden_out = jnp.transpose(both[0, :, 1], (2, 1, 0, 3)).reshape(steps, seq_dev, width)
    return (ffn_out, attn_out, hidden_out)


def solution(mesh):
    placed = (
        P("grp", None, "wide"),
        P(),
        P("wide", None),
        P("wide", None),
        P(None, "wide"),
        P("wide", None),
        P("grp", "wide", None, None, None),
        P(None, ("grp", "wide"), None, None, None),
        P("grp", None, "wide", None, None),
        P("grp"),
    )
    return jax.shard_map(
        on_device,
        mesh=mesh,
        in_specs=placed,
        out_specs=(
            P("grp", "wide", None),
            P("grp", "wide", None, None, None),
            P("grp", "wide", None),
        ),
        check_vma=False,
    )
```

time: 180 us -> 161 us (0.89)
  blocking collectives: 23.7 us -> 0 us
  Pallas kernels: 73.3 us -> 55 us
  waiting for transfers between devices: 27.9 us -> 41.1 us
  starting transfers between devices: 29.4 us -> 38.9 us
    ppermute x0 -> x7, waiting for transfers between devices: none -> 26 us  [the longest x3 13.4 us: exchange_halves(): got = lax.ppermute(send, 'wide', [(i, i ^ bit) for i in range(count)])]
    all_to_all x1 -> x0, blocking collectives: 23.7 us -> none  [exchange_chips(): lax.all_to_all(value, 'wide', split_axis=0, concat_axis=0, tiled=True, ax...]
    all_to_all x1 -> x2, waiting for transfers between devices: 19.6 us -> 0.01 us  [exchange_chips(): lax.all_to_all(value, 'wide', split_axis=0, concat_axis=0, tiled=True, ax...]
    pallas_call x3 -> x1, Pallas kernels: 22 us -> 3.57 us  [edge_max(): pl.pallas_call(kernel, grid_spec=pltpu.PrefetchScalarGridSpec(num_scalar_...]
    ppermute x0 -> x7, starting transfers between devices: none -> 13.5 us  [the longest x3 9.87 us: exchange_halves(): got = lax.ppermute(send, 'wide', [(i, i ^ bit) for i in range(count)])]
    all_to_all x4 -> x2, starting transfers between devices: 22.6 us -> 11 us  [exchange(): lax.all_to_all(value, 'wide', split_axis=0, concat_axis=0, tiled=True)]
    pallas_call x3 -> x2, Pallas kernels: 27.1 us -> 15.8 us  [levels_of(): pl.pallas_call(kernel, grid_spec=pltpu.PrefetchScalarGridSpec(num_scalar_...]
    all_to_all x0 -> x1, waiting for transfers between devices: none -> 8.25 us  [on_device(): both = lax.all_to_all(both, axes, split_axis=0, concat_axis=0, tiled=True)]
  transfers between devices with their start and end apart: 9 -> 17, of which waited for: 3 -> 10; matrix products, arithmetic and copies ran while one was open for 5% -> 4% of each run, Pallas kernels for 36% -> 26%
where the time goes in v3:
time: 161 us; the launch traced here: 160 us
  Pallas kernels  55 us (34%)
  waiting for transfers between devices  41.1 us (26%)
  starting transfers between devices  38.9 us (24%)
  local copies, waits for them, and re-layouts  12.7 us (8%)
  other arithmetic  8.19 us (5%)
  matrix products  2.6 us (2%)
    pallas_call x4, Pallas kernels, gate_up_product(): pl.pallas_call(kernel, grid_spec=pltpu.PrefetchScalarGridSpec(num_scalar_...  17.1 us
    pallas_call x2, Pallas kernels, levels_of(): pl.pallas_call(kernel, grid_spec=pltpu.PrefetchScalarGridSpec(num_scalar_...  15.8 us
    ppermute x3, waiting for transfers between devices, exchange_halves(): got = lax.ppermute(send, 'wide', [(i, i ^ bit) for i in range(count)])  13.4 us
    pallas_call x4, Pallas kernels, down_product(): pl.pallas_call(kernel, grid_spec=pltpu.PrefetchScalarGridSpec(num_scalar_...  12.6 us
    all_to_all x2, starting transfers between devices, exchange(): lax.all_to_all(value, 'wide', split_axis=0, concat_axis=0, tiled=True)  11 us
    ppermute x3, waiting for transfers between devices, gather_halves(): got = lax.ppermute(value, 'wide', [(i, i ^ bit) for i in range(count)])  10.8 us
    ppermute x3, starting transfers between devices, exchange_halves(): got = lax.ppermute(send, 'wide', [(i, i ^ bit) for i in range(count)])  9.87 us
    all_to_all x1, waiting for transfers between devices, on_device(): both = lax.all_to_all(both, axes, split_axis=0, concat_axis=0, tiled=True)  8.25 us
  transfers between devices with their start and end apart: 17, of which 10 were waited for; matrix products, arithmetic and copies ran while one was open for 4% of the time, Pallas kernels for 26%

profile of v3, /device:TPU:0, one launch (start us, length us, event | category | flops | bytes accessed | tf_op | source)
XLA Modules:
  0.0 159.5 jit_solution(14632004225215073155)
XLA Ops:
  0.7 1.4 dynamic_slice.6
  3.4 1.7 %select_reduce_fusion = (f32[3,8,8]{2,0,1:T(4,128)S(1)}, f32[3,1,8,8,512]{4,3,0,2,1:T(8,128)S(1)}) fusion(pred[512]{0:T(512)(128)(4,1)S(1)} %iota_compare_fusion.1, bf16[2,1,8,512,128]{4,3,2,1,0:T(8,128)(2,1)} %param.17, bf16[3,1,8,8,128]{4,3,2,1,0:T(8,128)(2,1)S(1)} %copy-done), kind=kOutput, calls=%fused_computation.19 | convolution fusion | flops 25460544 | bytes 1492224 | tf_op jit(solution)/shard_map/nshqd,shcd->nshqc/dot_general | solution.py:388
  7.2 7.4 %all-to-all-start = ((bf16[16,1,3,512]{3,2,1,0:T(4,128)(2,1)}), bf16[16,1,3,512]{3,2,1,0:T(4,128)(2,1)S(1)}, u32[]{:S(2)}, u32[]{:S(2)}) async-start(bf16[16,1,3,512]{3,2,1,0:T(4,128)(2,1)} %copy.40), calls=%async_computation | async-start | bytes 131072 | tf_op jit(solution)/shard_map/all_to_all | solution.py:417
  15.2 3.6 %edge_max.1 = f32[8,8192]{1,0:T(8,128)} custom-call(s32[2]{0:T(128)} %pad_add_fusion.2.place_ref, bf16[320,16384]{1,0:T(8,128)(2,1)} %refs_0_.3, bf16[320,16384]{1,0:T(8,128)(2,1)} %refs_1_.3, bf16[320,16384]{1,0:T(8,128)(2,1)} %bitcast.98), custom_call_target="tpu_custom_call" | custom-call | flops 3145728 | bytes 3145728 | tf_op jit(solution)/shard_map/edge_max/pallas_call | solution.py:91
  18.7 2.7 %all-to-all-done = bf16[16,1,3,512]{3,2,1,0:T(4,128)(2,1)S(1)} async-done(((bf16[16,1,3,512]{3,2,1,0:T(4,128)(2,1)}), bf16[16,1,3,512]{3,2,1,0:T(4,128)(2,1)S(1)}, u32[]{:S(2)}, u32[]{:S(2)}) %all-to-all-start) | async-done | bytes 49184 | tf_op jit(solution)/shard_map/all_to_all | solution.py:417
  22.1 6.0 %out_product.1 = bf16[16,48,320]{2,1,0:T(8,128)(2,1)} custom-call(bf16[48,512]{1,0:T(8,128)(2,1)} %reshape.153.x_ref, bf16[512,5120]{1,0:T(8,128)(2,1)} %w_ref.1), custom_call_target="tpu_custom_call" | custom-call | flops 1006632960 | bytes 5242880 | tf_op jit(solution)/shard_map/out_product/pallas_call | solution.py:230
  28.1 3.6 %all-to-all-start.1 = ((bf16[16,48,320]{2,1,0:T(8,128)(2,1)}), bf16[16,48,320]{2,1,0:T(8,128)(2,1)S(1)}, u32[]{:S(2)}, u32[]{:S(2)}) async-start(bf16[16,48,320]{2,1,0:T(8,128)(2,1)} %out_product.1), calls=%async_computation.1 | async-start | bytes 1179648 | tf_op jit(solution)/shard_map/all_to_all | solution.py:417
  34.0 9.4 %levels_of.2 = (f8e4m3fn[320,8192]{1,0:T(32,128)(4,1)}, f8e4m3fn[320,8192]{1,0:T(32,128)(4,1)}, f32[2,8,8192]{2,1,0:T(8,128)}) custom-call(s32[2]{0:T(128)} %pad_add_fusion.2.place_ref, bf16[320,16384]{1,0:T(8,128)(2,1)} %refs_0_.3, bf16[320,16384]{1,0:T(8,128)(2,1)} %refs_1_.3, f32[8,8192]{1,0:T(8,128)} %copy-done.3), custom_call_target="tpu_custom_call" | custom-call | flops 20971520 | bytes 15728640 | tf_op jit(solution)/shard_map/levels_of/pallas_call | solution.py:150
  43.5 3.8 %all-to-all-done.1 = bf16[16,48,320]{2,1,0:T(8,128)(2,1)S(1)} async-done(((bf16[16,48,320]{2,1,0:T(8,128)(2,1)}), bf16[16,48,320]{2,1,0:T(8,128)(2,1)S(1)}, u32[]{:S(2)}, u32[]{:S(2)}) %all-to-all-start.1) | async-done | bytes 491552 | tf_op jit(solution)/shard_map/all_to_all | solution.py:417
  47.3 1.6 collective-permute-start.1
  49.5 1.8 %collective-permute-done.1 = bf16[48,320]{1,0:T(8,128)(2,1)S(1)} collective-permute-done((bf16[48,320]{1,0:T(8,128)(2,1)S(1)}, bf16[48,320]{1,0:T(8,128)(2,1)S(1)}, u32[]{:S(2)}, u32[]{:S(2)}) %collective-permute-start.1) | collective-permute-done | bytes 30752 | tf_op jit(solution)/shard_map/ppermute | solution.py:522
  52.9 4.1 %gate_up_product.6 = bf16[8,96,640]{2,1,0:T(8,128)(2,1)} custom-call(s32[2]{0:T(128)} %pad_add_fusion.3.at_ref, bf16[96,320]{1,0:T(8,128)(2,1)} %get-tuple-element.53.x_ref, f8e4m3fn[320,8192]{1,0:T(32,128)(4,1)} %get-tuple-element.29.g_ref, f8e4m3fn[320,8192]{1,0:T(32,128)(4,1)} %get-tuple-element.30.u_ref, f32[2,8,8192]{2,1,0:T(8,128)} %get-tuple-element.31.s_ref, ...), custom_call_target="tpu_custom_call" | custom-call | flops 251658240 | bytes 1310720 | tf_op jit(solution)/shard_map/gate_up_product/pallas_call | solution.py:316
  57.5 4.0 %gate_up_product.4 = bf16[8,96,512]{2,1,0:T(8,128)(2,1)} custom-call(s32[2]{0:T(128)} %get-tuple-element.66.at_ref, bf16[96,320]{1,0:T(8,128)(2,1)} %get-tuple-element.53.x_ref, f8e4m3fn[320,8192]{1,0:T(32,128)(4,1)} %get-tuple-element.29.g_ref, f8e4m3fn[320,8192]{1,0:T(32,128)(4,1)} %get-tuple-element.30.u_ref, f32[2,8,8192]{2,1,0:T(8,128)} %get-tuple-element.31.s_ref), custom_call_target="tpu_custom_call" | custom-call | flops 251658240 | bytes 1310720 | tf_op jit(solution)/shard_map/gate_up_product/pallas_call | solution.py:316
  63.0 4.8 %gate_up_product.7 = (bf16[4,96,640]{2,1,0:T(8,128)(2,1)}, bf16[4,96,640]{2,1,0:T(8,128)(2,1)}) custom-call(s32[2]{0:T(128)} %get-tuple-element.67.at_ref, bf16[96,320]{1,0:T(8,128)(2,1)} %get-tuple-element.53.x_ref, f8e4m3fn[320,8192]{1,0:T(32,128)(4,1)} %get-tuple-element.29.g_ref, f8e4m3fn[320,8192]{1,0:T(32,128)(4,1)} %get-tuple-element.30.u_ref, ...), custom_call_target="tpu_custom_call" | custom-call | flops 251658240 | bytes 1310720 | tf_op jit(solution)/shard_map/gate_up_product/pallas_call | solution.py:316
  70.0 4.2 %gate_up_product.5 = bf16[8,96,512]{2,1,0:T(8,128)(2,1)} custom-call(s32[2]{0:T(128)} %pad_add_fusion.1.at_ref, bf16[96,320]{1,0:T(8,128)(2,1)} %get-tuple-element.53.x_ref, f8e4m3fn[320,8192]{1,0:T(32,128)(4,1)} %get-tuple-element.29.g_ref, f8e4m3fn[320,8192]{1,0:T(32,128)(4,1)} %get-tuple-element.30.u_ref, f32[2,8,8192]{2,1,0:T(8,128)} %get-tuple-element.31.s_ref, ...), custom_call_target="tpu_custom_call" | custom-call | flops 251658240 | bytes 1310720 | tf_op jit(solution)/shard_map/gate_up_product/pallas_call | solution.py:316
  74.2 4.5 %all-to-all-start.2 = ((bf16[8,96,512]{2,1,0:T(8,128)(2,1)}), bf16[8,96,512]{2,1,0:T(8,128)(2,1)S(1)}, u32[]{:S(2)}, u32[]{:S(2)}) async-start(bf16[8,96,512]{2,1,0:T(8,128)(2,1)} %gate_up_product.5), calls=%async_computation.2 | async-start | bytes 1572864 | tf_op jit(solution)/shard_map/all_to_all | solution.py:423
  78.8 2.5 %collective-permute-done.4 = bf16[4,96,640]{2,1,0:T(8,128)(2,1)S(1)} collective-permute-done((bf16[4,96,640]{2,1,0:T(8,128)(2,1)}, bf16[4,96,640]{2,1,0:T(8,128)(2,1)S(1)}, u32[]{:S(2)}, u32[]{:S(2)}) %collective-permute-start.4) | collective-permute-done | bytes 491552 | tf_op jit(solution)/shard_map/ppermute | solution.py:432
  81.5 4.8 %collective-permute-start.5 = (bf16[2,96,640]{2,1,0:T(8,128)(2,1)S(1)}, bf16[2,96,640]{2,1,0:T(8,128)(2,1)S(1)}, u32[]{:S(2)}, u32[]{:S(2)}) collective-permute-start(bf16[2,96,640]{2,1,0:T(8,128)(2,1)S(1)} %slice.66), channel_id=1, source_target_pairs={{0,4},{1,5},{2,6},{3,7},{4,0},{5,1},{6,2},{7,3},{8,12},{9,13},{10,... | collective-permute-start | bytes 737288 | tf_op jit(solution)/shard_map/ppermute | solution.py:432
  86.2 10.9 %collective-permute-done.5 = bf16[2,96,640]{2,1,0:T(8,128)(2,1)S(1)} collective-permute-done((bf16[2,96,640]{2,1,0:T(8,128)(2,1)S(1)}, bf16[2,96,640]{2,1,0:T(8,128)(2,1)S(1)}, u32[]{:S(2)}, u32[]{:S(2)}) %collective-permute-start.5) | collective-permute-done | bytes 245792 | tf_op jit(solution)/shard_map/ppermute | solution.py:432
  97.2 4.4 %collective-permute-start.6 = (bf16[1,96,640]{2,1,0:T(8,128)(2,1)S(1)}, bf16[1,96,640]{2,1,0:T(8,128)(2,1)S(1)}, u32[]{:S(2)}, u32[]{:S(2)}) collective-permute-start(bf16[1,96,640]{2,1,0:T(8,128)(2,1)S(1)} %slice.68), channel_id=1, source_target_pairs={{0,8},{1,9},{2,10},{3,11},{4,12},{5,13},{6,14},{7,15},{8,0},{9,1},... | collective-permute-start | bytes 368648 | tf_op jit(solution)/shard_map/ppermute | solution.py:432
  101.6 6.4 %levels_of.3 = (f8e4m3fn[320,8192]{1,0:T(32,128)(4,1)}, f32[1,8,8192]{2,1,0:T(8,128)}) custom-call(s32[2]{0:T(128)} %pad_add_fusion.2.place_ref, bf16[320,16384]{1,0:T(8,128)(2,1)} %bitcast.99, f32[8,8192]{1,0:T(8,128)} %copy-done.3), custom_call_target="tpu_custom_call" | custom-call | flops 10485760 | bytes 7864320 | tf_op jit(solution)/shard_map/levels_of/pallas_call | solution.py:150
  107.9 1.1 slice.57
  109.6 5.1 %collective-permute-done.7 = bf16[1,96,256]{2,1,0:T(8,128)(2,1)S(1)} collective-permute-done((bf16[1,96,256]{2,1,0:T(8,128)(2,1)S(1)}, bf16[1,96,256]{2,1,0:T(8,128)(2,1)S(1)}, u32[]{:S(2)}, u32[]{:S(2)}) %collective-permute-start.7) | collective-permute-done | bytes 49184 | tf_op jit(solution)/shard_map/ppermute | solution.py:447
  114.8 4.6 %collective-permute-done.8 = bf16[2,96,256]{2,1,0:T(8,128)(2,1)S(1)} collective-permute-done((bf16[2,96,256]{2,1,0:T(8,128)(2,1)S(1)}, bf16[2,96,256]{2,1,0:T(8,128)(2,1)S(1)}, u32[]{:S(2)}, u32[]{:S(2)}) %collective-permute-start.8) | collective-permute-done | bytes 98336 | tf_op jit(solution)/shard_map/ppermute | solution.py:447
  119.4 1.9 %collective-permute-start.9 = (bf16[4,96,256]{2,1,0:T(8,128)(2,1)S(1)}, bf16[4,96,256]{2,1,0:T(8,128)(2,1)S(1)}, u32[]{:S(2)}, u32[]{:S(2)}) collective-permute-start(bf16[4,96,256]{2,1,0:T(8,128)(2,1)S(1)} %pad_maximum_fusion.1), channel_id=1, source_target_pairs={{0,2},{1,3},{2,0},{3,1},{4,6},{5,7},{6,4},{7,5},{8,10},{9,11},{10,... | collective-permute-start | bytes 589832 | tf_op jit(solution)/shard_map/ppermute | solution.py:447
  122.1 3.6 %all-to-all-start.3 = ((bf16[8,96,256]{2,1,0:T(8,128)(2,1)}), bf16[8,96,256]{2,1,0:T(8,128)(2,1)S(1)}, u32[]{:S(2)}, u32[]{:S(2)}) async-start(bf16[8,96,256]{2,1,0:T(8,128)(2,1)} %broadcast_in_dim.91), calls=%async_computation.3 | async-start | bytes 786432 | tf_op jit(solution)/shard_map/all_to_all | solution.py:423
  127.6 3.1 %down_product.4.refs_0_ = f32[96,320]{1,0:T(8,128)} custom-call(s32[2]{0:T(128)} %get-tuple-element.67.at_ref, bf16[8,96,256]{2,1,0:T(8,128)(2,1)} %copy-done.2, f8e4m3fn[320,8192]{1,0:T(32,128)(4,1)} %get-tuple-element.39.l_ref, f32[64,320]{1,0:T(8,128)} %copy.42.s_ref), custom_call_target="tpu_custom_call" | custom-call | flops 125829120 | bytes 655360 | tf_op jit(solution)/shard_map/down_product/pallas_call | solution.py:358
  131.5 3.2 %down_product.5.refs_0_ = f32[96,320]{1,0:T(8,128)} custom-call(s32[2]{0:T(128)} %pad_add_fusion.3.at_ref, bf16[8,96,256]{2,1,0:T(8,128)(2,1)} %copy-done.8, f8e4m3fn[320,8192]{1,0:T(32,128)(4,1)} %get-tuple-element.39.l_ref, f32[64,320]{1,0:T(8,128)} %copy.42.s_ref, f32[96,320]{1,0:T(8,128)} %down_product.4.refs_0_), custom_call_target="tpu_custom_call" | custom-call | flops 125829120 | bytes 655360 | tf_op jit(solution)/shard_map/down_product/pallas_call | solution.py:358
  135.5 3.2 %down_product.6.refs_0_ = f32[96,320]{1,0:T(8,128)} custom-call(s32[2]{0:T(128)} %pad_add_fusion.1.at_ref, bf16[8,96,256]{2,1,0:T(8,128)(2,1)} %copy-done.1, f8e4m3fn[320,8192]{1,0:T(32,128)(4,1)} %get-tuple-element.39.l_ref, f32[64,320]{1,0:T(8,128)} %copy.42.s_ref, f32[96,320]{1,0:T(8,128)} %down_product.5.refs_0_), custom_call_target="tpu_custom_call" | custom-call | flops 125829120 | bytes 655360 | tf_op jit(solution)/shard_map/down_product/pallas_call | solution.py:358
  139.4 3.2 %down_product.7 = f32[96,320]{1,0:T(8,128)} custom-call(s32[2]{0:T(128)} %get-tuple-element.66.at_ref, bf16[8,96,256]{2,1,0:T(8,128)(2,1)} %copy-done.7, f8e4m3fn[320,8192]{1,0:T(32,128)(4,1)} %get-tuple-element.39.l_ref, f32[64,320]{1,0:T(8,128)} %copy.42.s_ref, f32[96,320]{1,0:T(8,128)} %down_product.6.refs_0_), custom_call_target="tpu_custom_call" | custom-call | flops 125829120 | bytes 655360 | tf_op jit(solution)/shard_map/down_product/pallas_call | solution.py:358
  144.3 4.8 %all-to-all-start.4 = ((bf16[32,6,320]{2,1,0:T(8,128)(2,1)}), bf16[32,6,320]{2,1,0:T(8,128)(2,1)S(1)}, u32[]{:S(2)}, u32[]{:S(2)}) async-start(bf16[32,6,320]{2,1,0:T(8,128)(2,1)} %pad_maximum_fusion.2), calls=%async_computation.4 | async-start | bytes 393216 | tf_op jit(solution)/shard_map/all_to_all | solution.py:601
  149.8 8.3 %all-to-all-done.4 = bf16[32,6,320]{2,1,0:T(8,128)(2,1)S(1)} async-done(((bf16[32,6,320]{2,1,0:T(8,128)(2,1)}), bf16[32,6,320]{2,1,0:T(8,128)(2,1)S(1)}, u32[]{:S(2)}, u32[]{:S(2)}) %all-to-all-start.4) | async-done | bytes 122912 | tf_op jit(solution)/shard_map/all_to_all | solution.py:601
  (96 shorter events, 23.1 us)
Async XLA Ops:
  0.6 2.8 %copy-start = (bf16[3,1,8,8,128]{4,3,2,1,0:T(8,128)(2,1)S(1)}, bf16[3,1,8,8,128]{4,3,2,1,0:T(8,128)(2,1)}, u32[]{:S(2)}) copy-start(bf16[3,1,8,8,128]{4,3,2,1,0:T(8,128)(2,1)} %param.16) | copy-start | bytes 147460
  0.6 5.2 %copy-start.11 = (bf16[2,1,8,512,128]{4,3,2,1,0:T(8,128)(2,1)S(1)}, bf16[2,1,8,512,128]{4,3,2,1,0:T(8,128)(2,1)}, u32[]{:S(2)}) copy-start(bf16[2,1,8,512,128]{4,3,2,1,0:T(8,128)(2,1)} %param.17) | copy-start | bytes 6291460
  7.2 14.3 %all-to-all-start = ((bf16[16,1,3,512]{3,2,1,0:T(4,128)(2,1)}), bf16[16,1,3,512]{3,2,1,0:T(4,128)(2,1)S(1)}, u32[]{:S(2)}, u32[]{:S(2)}) async-start(bf16[16,1,3,512]{3,2,1,0:T(4,128)(2,1)} %copy.40), calls=%async_computation | async-start | bytes 131072 | tf_op jit(solution)/shard_map/all_to_all | solution.py:417
  22.1 9.6 %copy-start.9 = (f32[8,8192]{1,0:T(8,128)S(1)}, f32[8,8192]{1,0:T(8,128)}, u32[]{:S(2)}) copy-start(f32[8,8192]{1,0:T(8,128)} %edge_max.1) | copy-start | bytes 786436
  22.1 10.0 %copy-start.10 = (bf16[3,16,320]{2,1,0:T(8,128)(2,1)S(1)}, bf16[3,16,320]{2,1,0:T(8,128)(2,1)}, u32[]{:S(2)}) copy-start(bf16[3,16,320]{2,1,0:T(8,128)(2,1)} %param.10) | copy-start | bytes 92164
  28.1 19.1 %all-to-all-start.1 = ((bf16[16,48,320]{2,1,0:T(8,128)(2,1)}), bf16[16,48,320]{2,1,0:T(8,128)(2,1)S(1)}, u32[]{:S(2)}, u32[]{:S(2)}) async-start(bf16[16,48,320]{2,1,0:T(8,128)(2,1)} %out_product.1), calls=%async_computation.1 | async-start | bytes 1179648 | tf_op jit(solution)/shard_map/all_to_all | solution.py:417
  31.7 1.6 %collective-permute-start = (f32[8,8192]{1,0:T(8,128)S(1)}, f32[8,8192]{1,0:T(8,128)S(1)}, u32[]{:S(2)}, u32[]{:S(2)}) collective-permute-start(f32[8,8192]{1,0:T(8,128)S(1)} %copy-done.9), channel_id=1, source_target_pairs={{0,1},{1,0},{2,3},{3,2},{4,5},{5,4},{6,7},{7,6},{8,9},{9,8},{10,11... | collective-permute-start | bytes 786440 | tf_op jit(solution)/shard_map/ppermute | solution.py:413
  33.3 0.7 copy-start.3
  47.3 4.0 %collective-permute-start.1 = (bf16[48,320]{1,0:T(8,128)(2,1)S(1)}, bf16[48,320]{1,0:T(8,128)(2,1)S(1)}, u32[]{:S(2)}, u32[]{:S(2)}) collective-permute-start(bf16[48,320]{1,0:T(8,128)(2,1)S(1)} %add_convert_fusion.2), channel_id=1, source_target_pairs={{0,16},{16,0},{1,17},{17,1},{2,18},{18,2},{3,19},{19,3},{4,20},{20... | collective-permute-start | bytes 92168 | tf_op jit(solution)/shard_map/ppermute | solution.py:522
  56.9 5.1 %collective-permute-start.3 = (bf16[8,96,640]{2,1,0:T(8,128)(2,1)}, bf16[8,96,640]{2,1,0:T(8,128)(2,1)S(1)}, u32[]{:S(2)}, u32[]{:S(2)}) collective-permute-start(bf16[8,96,640]{2,1,0:T(8,128)(2,1)} %gate_up_product.6), channel_id=1, source_target_pairs={{0,1},{1,0},{2,3},{3,2},{4,5},{5,4},{6,7},{7,6},{8,9},{9,8},{10,11... | collective-permute-start | bytes 2949128 | tf_op jit(solution)/shard_map/ppermute | solution.py:413
  61.6 7.6 %collective-permute-start.2 = (bf16[8,96,512]{2,1,0:T(8,128)(2,1)}, bf16[8,96,512]{2,1,0:T(8,128)(2,1)S(1)}, u32[]{:S(2)}, u32[]{:S(2)}) collective-permute-start(bf16[8,96,512]{2,1,0:T(8,128)(2,1)} %gate_up_product.4), channel_id=1, source_target_pairs={{0,1},{1,0},{2,3},{3,2},{4,5},{5,4},{6,7},{7,6},{8,9},{9,8},{10,11... | collective-permute-start | bytes 2359304 | tf_op jit(solution)/shard_map/ppermute | solution.py:413
  62.1 1.0 copy-start.4
  67.8 13.5 %collective-permute-start.4 = (bf16[4,96,640]{2,1,0:T(8,128)(2,1)}, bf16[4,96,640]{2,1,0:T(8,128)(2,1)S(1)}, u32[]{:S(2)}, u32[]{:S(2)}) collective-permute-start(bf16[4,96,640]{2,1,0:T(8,128)(2,1)} %get-tuple-element.34), channel_id=1, source_target_pairs={{0,2},{1,3},{2,0},{3,1},{4,6},{5,7},{6,4},{7,5},{8,10},{9,11},{10,... | collective-permute-start | bytes 1474568 | tf_op jit(solution)/shard_map/ppermute | solution.py:432
  69.2 12.1 %copy-start.6 = (bf16[4,96,640]{2,1,0:T(8,128)(2,1)S(1)}, bf16[4,96,640]{2,1,0:T(8,128)(2,1)}, u32[]{:S(2)}) copy-start(bf16[4,96,640]{2,1,0:T(8,128)(2,1)} %get-tuple-element.33) | copy-start | bytes 1474564
  69.2 0.9 copy-start.5
  74.2 35.0 %all-to-all-start.2 = ((bf16[8,96,512]{2,1,0:T(8,128)(2,1)}), bf16[8,96,512]{2,1,0:T(8,128)(2,1)S(1)}, u32[]{:S(2)}, u32[]{:S(2)}) async-start(bf16[8,96,512]{2,1,0:T(8,128)(2,1)} %gate_up_product.5), calls=%async_computation.2 | async-start | bytes 1572864 | tf_op jit(solution)/shard_map/all_to_all | solution.py:423
  81.5 15.6 %collective-permute-start.5 = (bf16[2,96,640]{2,1,0:T(8,128)(2,1)S(1)}, bf16[2,96,640]{2,1,0:T(8,128)(2,1)S(1)}, u32[]{:S(2)}, u32[]{:S(2)}) collective-permute-start(bf16[2,96,640]{2,1,0:T(8,128)(2,1)S(1)} %slice.66), channel_id=1, source_target_pairs={{0,4},{1,5},{2,6},{3,7},{4,0},{5,1},{6,2},{7,3},{8,12},{9,13},{10,... | collective-permute-start | bytes 737288 | tf_op jit(solution)/shard_map/ppermute | solution.py:432
  97.2 11.8 %collective-permute-start.6 = (bf16[1,96,640]{2,1,0:T(8,128)(2,1)S(1)}, bf16[1,96,640]{2,1,0:T(8,128)(2,1)S(1)}, u32[]{:S(2)}, u32[]{:S(2)}) collective-permute-start(bf16[1,96,640]{2,1,0:T(8,128)(2,1)S(1)} %slice.68), channel_id=1, source_target_pairs={{0,8},{1,9},{2,10},{3,11},{4,12},{5,13},{6,14},{7,15},{8,0},{9,1},... | collective-permute-start | bytes 368648 | tf_op jit(solution)/shard_map/ppermute | solution.py:432
  109.5 5.2 %collective-permute-start.7 = (bf16[1,96,256]{2,1,0:T(8,128)(2,1)S(1)}, bf16[1,96,256]{2,1,0:T(8,128)(2,1)S(1)}, u32[]{:S(2)}, u32[]{:S(2)}) collective-permute-start(bf16[1,96,256]{2,1,0:T(8,128)(2,1)S(1)} %get-tuple-element.58), channel_id=1, source_target_pairs={{0,8},{1,9},{2,10},{3,11},{4,12},{5,13},{6,14},{7,15},{8,0},{9,1},... | collective-permute-start | bytes 147464 | tf_op jit(solution)/shard_map/ppermute | solution.py:447
  114.7 4.7 %collective-permute-start.8 = (bf16[2,96,256]{2,1,0:T(8,128)(2,1)S(1)}, bf16[2,96,256]{2,1,0:T(8,128)(2,1)S(1)}, u32[]{:S(2)}, u32[]{:S(2)}) collective-permute-start(bf16[2,96,256]{2,1,0:T(8,128)(2,1)S(1)} %pad_maximum_fusion.3), channel_id=1, source_target_pairs={{0,4},{1,5},{2,6},{3,7},{4,0},{5,1},{6,2},{7,3},{8,12},{9,13},{10,... | collective-permute-start | bytes 294920 | tf_op jit(solution)/shard_map/ppermute | solution.py:447
  119.4 7.3 %collective-permute-start.9 = (bf16[4,96,256]{2,1,0:T(8,128)(2,1)S(1)}, bf16[4,96,256]{2,1,0:T(8,128)(2,1)S(1)}, u32[]{:S(2)}, u32[]{:S(2)}) collective-permute-start(bf16[4,96,256]{2,1,0:T(8,128)(2,1)S(1)} %pad_maximum_fusion.1), channel_id=1, source_target_pairs={{0,2},{1,3},{2,0},{3,1},{4,6},{5,7},{6,4},{7,5},{8,10},{9,11},{10,... | collective-permute-start | bytes 589832 | tf_op jit(solution)/shard_map/ppermute | solution.py:447
  122.1 12.6 %all-to-all-start.3 = ((bf16[8,96,256]{2,1,0:T(8,128)(2,1)}), bf16[8,96,256]{2,1,0:T(8,128)(2,1)S(1)}, u32[]{:S(2)}, u32[]{:S(2)}) async-start(bf16[8,96,256]{2,1,0:T(8,128)(2,1)} %broadcast_in_dim.91), calls=%async_computation.3 | async-start | bytes 786432 | tf_op jit(solution)/shard_map/all_to_all | solution.py:423
  126.8 0.8 copy-start.2
  126.8 4.0 %collective-permute-start.10 = (bf16[8,96,256]{2,1,0:T(8,128)(2,1)S(1)}, bf16[8,96,256]{2,1,0:T(8,128)(2,1)S(1)}, u32[]{:S(2)}, u32[]{:S(2)}) collective-permute-start(bf16[8,96,256]{2,1,0:T(8,128)(2,1)S(1)} %pad_maximum_fusion.a_ref), channel_id=1, source_target_pairs={{0,1},{1,0},{2,3},{3,2},{4,5},{5,4},{6,7},{7,6},{8,9},{9,8},{10,11... | collective-permute-start | bytes 1179656 | tf_op jit(solution)/shard_map/ppermute | solution.py:413
  130.8 0.7 copy-start.8
  134.7 0.8 copy-start.1
  134.7 3.9 %collective-permute-start.11 = (bf16[8,96,256]{2,1,0:T(8,128)(2,1)S(1)}, bf16[8,96,256]{2,1,0:T(8,128)(2,1)S(1)}, u32[]{:S(2)}, u32[]{:S(2)}) collective-permute-start(bf16[8,96,256]{2,1,0:T(8,128)(2,1)S(1)} %all-to-all-done.3.a_ref), channel_id=1, source_target_pairs={{0,1},{1,0},{2,3},{3,2},{4,5},{5,4},{6,7},{7,6},{8,9},{9,8},{10,11... | collective-permute-start | bytes 1179656 | tf_op jit(solution)/shard_map/ppermute | solution.py:413
  138.6 0.8 copy-start.7
  144.3 13.7 %all-to-all-start.4 = ((bf16[32,6,320]{2,1,0:T(8,128)(2,1)}), bf16[32,6,320]{2,1,0:T(8,128)(2,1)S(1)}, u32[]{:S(2)}, u32[]{:S(2)}) async-start(bf16[32,6,320]{2,1,0:T(8,128)(2,1)} %pad_maximum_fusion.2), calls=%async_computation.4 | async-start | bytes 393216 | tf_op jit(solution)/shard_map/all_to_all | solution.py:601

commit v4 on v3

v4 whole, which is shorter than its diff:
```python
import functools
import math

import jax
import jax.numpy as jnp
from jax import lax
from jax.experimental import pallas as pl
from jax.experimental.pallas import tpu as pltpu
from jax.sharding import PartitionSpec as P

BLOCK = 128
QMAX = 448.0
EPS_NORM = 1e-06
EPS_SCALE = 1e-06
NEG = -1e30
LANES = 128
VMEM = 56 * 2**20

f32 = jnp.float32
bf16 = jnp.bfloat16
f8 = jnp.float8_e4m3fn


def params(**more):
    return pltpu.CompilerParams(vmem_limit_bytes=VMEM, **more)


def in_hbm(*arrays):
    return [pltpu.with_memory_space_constraint(x, pltpu.HBM) for x in arrays]


def cost(flops, read):
    return pl.CostEstimate(flops=int(flops), bytes_accessed=int(read), transcendentals=0)


def pick_tile(cols, most):
    tile = most
    while cols % tile:
        tile -= LANES
    return tile


def spread_lanes(tops):
    out = []
    for g in range(tops.shape[1] // LANES):
        top = jnp.max(tops[:, g * LANES : (g + 1) * LANES], axis=1, keepdims=True)
        out.append(jnp.broadcast_to(top, (tops.shape[0], LANES)))
    return jnp.concatenate(out, axis=1)


def rows_max(ref, start, size):
    return jnp.max(jnp.abs(ref[pl.ds(start, size), :]), axis=0, keepdims=True).astype(f32)


def fill_rows(rows):
    return jnp.concatenate(rows + [rows[0]] * (8 - len(rows)), axis=0)


def chunk_max(place, weights, cols, chunk, tile):
    rows = weights[0].shape[0]
    parts = rows // chunk
    count = len(weights)
    steps = cols // tile

    def kernel(place_ref, *refs):
        for a in range(count):
            tops = [rows_max(refs[a], j * chunk, chunk) for j in range(parts)]
            refs[count][a] = spread_lanes(fill_rows(tops))

    return pl.pallas_call(
        kernel,
        grid_spec=pltpu.PrefetchScalarGridSpec(
            num_scalar_prefetch=1,
            grid=(steps,),
            in_specs=[pl.BlockSpec((rows, tile), lambda i, p: (0, p[1] * steps + i))] * count,
            out_specs=pl.BlockSpec((count, 8, tile), lambda i, p: (0, 0, i)),
        ),
        out_shape=jax.ShapeDtypeStruct((count, 8, cols), f32),
        compiler_params=params(),
        cost_estimate=cost(2 * count * rows * cols, 2 * count * rows * cols),
        name="chunk_max",
    )(place, *in_hbm(*weights))


def edge_max(place, weights, cols, chunk, tile):
    parts = weights[0].shape[0] // chunk
    count = len(weights)
    steps = cols // tile

    def kernel(place_ref, *refs):
        refs[count][...] = spread_lanes(
            fill_rows([rows_max(refs[a], 0, chunk) for a in range(count)])
        )

    return pl.pallas_call(
        kernel,
        grid_spec=pltpu.PrefetchScalarGridSpec(
            num_scalar_prefetch=1,
            grid=(steps,),
            in_specs=[
                pl.BlockSpec(
                    (chunk, tile), lambda i, p: ((1 - p[0]) * (parts - 1), p[1] * steps + i)
                )
            ]
            * count,
            out_specs=pl.BlockSpec((8, tile), lambda i, p: (0, i)),
        ),
        out_shape=jax.ShapeDtypeStruct((8, cols), f32),
        compiler_params=params(),
        cost_estimate=cost(2 * count * chunk * cols, 2 * count * chunk * cols),
        name="edge_max",
    )(place, *in_hbm(*weights))


def join_pair(w_ref, other, odd, chunk, parts):
    mine = [rows_max(w_ref, j * chunk, chunk) for j in range(parts)]
    joined = []
    for j in range(parts):
        even = mine[j ^ 1] if j ^ 1 < parts else other
        back = j - 1 if j % 2 == 0 else j + 1
        near = other if back < 0 else mine[back]
        joined.append(jnp.maximum(mine[j], jnp.where(odd, near, even)))
    return fill_rows(joined)


def levels_of(place, weights, edge, tops, flip, cols, chunk, tile):
    rows = weights[0].shape[0]
    parts = rows // chunk
    count = len(weights)
    steps = cols // (2 * tile)

    def columns(i, p):
        return 2 * i + (p[0] ^ flip)

    def kernel(place_ref, *refs):
        w_refs = refs[:count]
        top_ref = refs[count]
        o_refs = refs[count + 1 : 2 * count + 1]
        s_ref = refs[2 * count + 1]
        factor = refs[2 * count + 2]
        odd = place_ref[0] == 1
        for a in range(count):
            if edge is None:
                joined = top_ref[a]
            else:
                other = top_ref[pl.ds(a, 1), :]
                joined = spread_lanes(join_pair(w_refs[a], other, odd, chunk, parts))
            largest = joined + EPS_SCALE
            factor[a] = QMAX / largest
            s_ref[a] = largest * (1.0 / QMAX)
        for a in range(count):
            for j in range(parts):
                rows_at = pl.ds(j * chunk, chunk)
                value = w_refs[a][rows_at, :].astype(f32) * factor[a, pl.ds(j, 1), :]
                o_refs[a][rows_at, :] = value.astype(f8)

    if edge is None:
        top_spec = pl.BlockSpec((count, 8, tile), lambda i, p: (0, 0, columns(i, p)))
    else:
        top_spec = pl.BlockSpec((8, tile), lambda i, p: (0, columns(i, p)))
    return pl.pallas_call(
        kernel,
        grid_spec=pltpu.PrefetchScalarGridSpec(
            num_scalar_prefetch=1,
            grid=(steps,),
            in_specs=[
                pl.BlockSpec((rows, tile), lambda i, p: (0, 2 * p[1] * steps + columns(i, p)))
            ]
            * count
            + [top_spec],
            out_specs=[pl.BlockSpec((rows, tile), lambda i, p: (0, i))] * count
            + [pl.BlockSpec((count, 8, tile), lambda i, p: (0, 0, i))],
            scratch_shapes=[pltpu.VMEM((count, 8, tile), f32)],
        ),
        out_shape=[jax.ShapeDtypeStruct((rows, cols // 2), f8)] * count
        + [jax.ShapeDtypeStruct((count, 8, cols // 2), f32)],
        compiler_params=params(),
        cost_estimate=cost(2 * count * rows * cols, 2 * count * rows * cols),
        name="levels_of",
    )(place, *in_hbm(*weights), tops if edge is None else edge)


def down_levels_of(place, weight, edge, row, tops, cols, chunk, tile):
    rows = weight.shape[0]
    parts = rows // chunk
    steps = cols // tile

    def kernel(place_ref, w_ref, top_ref, o_ref, s_ref):
        odd = place_ref[0] == 1
        if edge is None:
            joined = top_ref[0]
        else:
            other = top_ref[pl.ds(row, 1), :]
            joined = spread_lanes(join_pair(w_ref, other, odd, chunk, parts))
        largest = joined + EPS_SCALE
        factor = QMAX / largest
        scale = largest * (1.0 / QMAX)
        for g in range(tile // LANES):
            at = slice(g * LANES, (g + 1) * LANES)
            value = jnp.concatenate(
                [
                    w_ref[pl.ds(j * chunk, chunk), pl.ds(g * LANES, LANES)].astype(f32)
                    * factor[j : j + 1, at]
                    for j in range(parts)
                ],
                axis=0,
            )
            o_ref[pl.ds(g * LANES, LANES), :] = value.T.astype(f8)
            s_ref[pl.ds(g, 1), :] = jnp.concatenate(
                [scale[j : j + 1, at][:, :chunk] for j in range(parts)], axis=1
            )

    if edge is None:
        top_spec = pl.BlockSpec((1, 8, tile), lambda i, p: (0, 0, i))
    else:
        top_spec = pl.BlockSpec((8, tile), lambda i, p: (0, i))
    return pl.pallas_call(
        kernel,
        grid_spec=pltpu.PrefetchScalarGridSpec(
            num_scalar_prefetch=1,
            grid=(steps,),
            in_specs=[
                pl.BlockSpec((rows, tile), lambda i, p: (0, p[1] * steps + i)),
                top_spec,
            ],
            out_specs=[
                pl.BlockSpec((tile, rows), lambda i, p: (i, 0)),
                pl.BlockSpec((tile // LANES, rows), lambda i, p: (i, 0)),
            ],
        ),
        out_shape=[
            jax.ShapeDtypeStruct((cols, rows), f8),
            jax.ShapeDtypeStruct((cols // LANES, rows), f32),
        ],
        compiler_params=params(),
        cost_estimate=cost(8 * rows * cols, 3 * rows * cols),
        name="down_levels_of",
    )(place, *in_hbm(weight), tops if edge is None else edge)


def join_group(parts, size, dim):
    count = lax.axis_size("wide")
    me = lax.axis_index("wide")
    share = parts.shape[dim]
    shape = list(parts.shape)
    shape[dim] = share * size
    out = jnp.zeros(shape, parts.dtype)
    out = lax.dynamic_update_slice_in_dim(out, parts, (me % size) * share, dim)
    for step in range(1, size):
        perm = [(i // size * size + (i + step) % size, i) for i in range(count)]
        got = lax.ppermute(parts, "wide", perm)
        out = lax.dynamic_update_slice_in_dim(out, got, ((me + step) % size) * share, dim)
    return out


def pair_shares_blocks(rows):
    return math.lcm(rows, BLOCK) == 2 * rows and math.gcd(rows, BLOCK) == BLOCK // 2


def joined_max(place, weights, cols, chunk, tile):
    rows = weights[0].shape[0]
    size = math.lcm(rows, BLOCK) // rows
    per = BLOCK // chunk
    parts = rows // chunk
    tops = chunk_max(place, weights, cols, chunk, tile)
    if size == 1:
        return tops
    joined = join_group(tops[:, :parts], size, 1)
    blocks = joined.reshape(joined.shape[0], -1, per, joined.shape[2])
    joined = jnp.broadcast_to(jnp.max(blocks, axis=2, keepdims=True), blocks.shape)
    joined = joined.reshape(joined.shape[0], size * parts, -1)
    own = lax.dynamic_slice_in_dim(joined, (lax.axis_index("wide") % size) * parts, parts, 1)
    return jnp.pad(own, ((0, 0), (0, 8 - parts), (0, 0)))


def out_levels_of(weight, tile):
    rows, cols = weight.shape
    parts = rows // BLOCK

    def kernel(w_ref, o_ref, s_ref):
        tops = spread_lanes(fill_rows([rows_max(w_ref, j * BLOCK, BLOCK) for j in range(parts)]))
        largest = tops + EPS_SCALE
        factor = QMAX / largest
        s_ref[...] = largest * (1.0 / QMAX)
        for j in range(parts):
            at = pl.ds(j * BLOCK, BLOCK)
            o_ref[at, :] = (w_ref[at, :].astype(f32) * factor[j : j + 1]).astype(f8)

    columns = lambda i: (0, i)
    return pl.pallas_call(
        kernel,
        grid=(cols // tile,),
        in_specs=[pl.BlockSpec((rows, tile), columns)],
        out_specs=[pl.BlockSpec((rows, tile), columns), pl.BlockSpec((8, tile), columns)],
        out_shape=[
            jax.ShapeDtypeStruct((rows, cols), f8),
            jax.ShapeDtypeStruct((8, cols), f32),
        ],
        compiler_params=params(),
        cost_estimate=cost(8 * rows * cols, 3 * rows * cols),
        name="out_levels_of",
    )(*in_hbm(weight))


def out_product(left, levels, scale, owners):
    count, rows = left.shape
    cols = levels.shape[1]
    parts = rows // BLOCK
    share = cols // owners
    tile = pick_tile(cols, 4 * math.lcm(share, LANES))
    per = tile // share

    def kernel(x_ref, l_ref, s_ref, o_ref):
        total = None
        for j in range(parts):
            at = pl.ds(j * BLOCK, BLOCK)
            part = jnp.dot(x_ref[:, at], l_ref[at, :].astype(bf16), preferred_element_type=f32)
            part = part * s_ref[pl.ds(j, 1), :]
            total = part if total is None else total + part
        total = total.astype(bf16)
        for q in range(per):
            o_ref[q] = total[:, q * share : (q + 1) * share]

    return pl.pallas_call(
        kernel,
        grid=(cols // tile,),
        in_specs=[
            pl.BlockSpec((count, rows), lambda i: (0, 0)),
            pl.BlockSpec((rows, tile), lambda i: (0, i)),
            pl.BlockSpec((8, tile), lambda i: (0, i)),
        ],
        out_specs=pl.BlockSpec((per, count, share), lambda i: (i, 0, 0)),
        out_shape=jax.ShapeDtypeStruct((owners, count, share), bf16),
        compiler_params=params(),
        cost_estimate=cost(2 * count * rows * cols, rows * cols),
        name="out_product",
    )(left, levels, scale)


def gate_up_product(place, hidden, gain, gate, up, scale, added, runs, chips, paired):
    groups = len(hidden)
    rows = gate.shape[0]
    count = groups * hidden[0].shape[0]
    chunk = math.gcd(rows, BLOCK)
    extra = -(-4 * chips // LANES) * LANES
    units = [run * BLOCK for run in runs]
    widths = (2 * units[0], 2 * units[1] + extra)
    tile = chips * BLOCK
    staged = added is not None

    def kernel(place_ref, *refs):
        refs = list(refs)
        h_refs, refs = refs[:groups], refs[groups:]
        gain_ref, g_ref, u_ref, s_ref = refs[:4]
        a_refs = refs[4:6] if staged else (None, None)
        o_refs = refs[6:-2] if staged else refs[4:-2]
        x_ref, p_ref = refs[-2:]
        step = pl.program_id(0)
        odd = place_ref[0]

        @pl.when(step == 0)
        def _():
            values = [ref[...].astype(f32) for ref in h_refs]
            if groups == 2:
                first = place_ref[1] == 0
                values = [
                    jnp.where(first, values[0], values[1]),
                    jnp.where(first, values[1], values[0]),
                ]
            states = jnp.concatenate(values, axis=0)
            left = (states * gain_ref[...]).astype(bf16)
            if paired:
                turned = jnp.concatenate([left[:, chunk:], left[:, :chunk]], axis=1)
                left = jnp.where(odd == 1, turned, left)
            x_ref[...] = left
            squares = jnp.sum(states * states, axis=1, keepdims=True)
            high = squares.astype(bf16).astype(f32)
            lane = lax.broadcasted_iota(jnp.int32, (count, extra), 1)
            at = 2 * place_ref[3]
            p_ref[...] = jnp.where(
                lane == at, high, jnp.where(lane == at + 1, squares - high, 0.0)
            )

        if paired:
            whole = rows // BLOCK
            blocks = [
                (odd * chunk + j * BLOCK, j * BLOCK, BLOCK, odd + 2 * j) for j in range(whole)
            ]
            blocks.append(
                ((1 - odd) * whole * BLOCK, whole * BLOCK, chunk, (1 - odd) * 2 * whole)
            )
        else:
            blocks = [(j * chunk, j * chunk, chunk, j) for j in range(rows // chunk)]
        totals = []
        for a, ref in enumerate((g_ref, u_ref)):
            total = None
            for start, x_at, size, s_at in blocks:
                if paired:
                    start = pl.multiple_of(start, chunk)
                part = jnp.dot(
                    x_ref[:, pl.ds(x_at, size)],
                    ref[pl.ds(start, size), :].astype(bf16),
                    preferred_element_type=f32,
                )
                part = part * s_ref[a, pl.ds(s_at, 1), :]
                total = part if total is None else total + part
            totals.append(total)

        def write(run, block, ref, position, q):
            values = [
                (a * units[run] + block * BLOCK, total[:, q * BLOCK : (q + 1) * BLOCK])
                for a, total in enumerate(totals)
            ]
            if run == 1 and block == 0:
                values.append((2 * units[1], p_ref[...]))
            for start, value in values:
                lanes = pl.ds(start, value.shape[1])
                if staged:
                    value = value + a_refs[run][q, :, lanes].astype(f32)
                ref[position, :, lanes] = value.astype(bf16)

        def write_first(block):
            for q in range(chips):
                if not staged:
                    write(0, block, o_refs[0], q, q)
                    continue
                away = q ^ place_ref[2]
                position, rest = 0, away // 2
                for _ in range(chips.bit_length() - 2):
                    position, rest = position * 2 + rest % 2, rest // 2
                for side in range(2):
                    pl.when(away % 2 == side)(
                        functools.partial(write, 0, block, o_refs[side], position, q)
                    )

        def write_second(block):
            for q in range(chips):
                write(1, block, o_refs[-1], q, q)

        for block in range(runs[0]):
            pl.when(step == block)(functools.partial(write_first, block))
        for block in range(runs[1]):
            pl.when(step == runs[0] + block)(functools.partial(write_second, block))

    fixed = lambda i, p: (0, 0)
    whole_of = lambda shape: pl.BlockSpec(shape, lambda i, p: (0, 0, 0))
    run_shapes = [(chips, count, width) for width in widths]
    out_shapes = list(run_shapes)
    if staged:
        out_shapes[:1] = [(chips // 2, count, widths[0])] * 2
    return pl.pallas_call(
        kernel,
        grid_spec=pltpu.PrefetchScalarGridSpec(
            num_scalar_prefetch=1,
            grid=(sum(runs),),
            in_specs=[pl.BlockSpec(x.shape, fixed) for x in hidden]
            + [
                pl.BlockSpec((1, rows), fixed),
                pl.BlockSpec((rows, tile), lambda i, p: (0, i)),
                pl.BlockSpec((rows, tile), lambda i, p: (0, i)),
                pl.BlockSpec((2, 8, tile), lambda i, p: (0, 0, i)),
            ]
            + ([whole_of(shape) for shape in run_shapes] if staged else []),
            out_specs=[whole_of(shape) for shape in out_shapes],
            scratch_shapes=[pltpu.VMEM((count, rows), bf16), pltpu.VMEM((count, extra), f32)],
        ),
        out_shape=[jax.ShapeDtypeStruct(shape, bf16) for shape in out_shapes],
        compiler_params=params(),
        cost_estimate=cost(4 * count * rows * gate.shape[1], 2 * rows * gate.shape[1]),
        name="gate_up_product",
    )(place, *hidden, gain, gate, up, scale, *(added if staged else []))


def down_product(place, act, levels, scale, added, flip, states, mine):
    chips, count, units = act.shape
    hidden, width = levels.shape
    tile = chips * BLOCK
    blocks = units // BLOCK
    last = added is not None

    def kernel(place_ref, a_ref, l_ref, s_ref, *refs):
        step = pl.program_id(0)
        o_ref, total_ref = refs[-2:]
        total = jnp.zeros((count, width), f32)
        for q in range(chips):
            part = jnp.dot(
                a_ref[q],
                l_ref[pl.ds(q * BLOCK, BLOCK), :].astype(bf16),
                preferred_element_type=f32,
            )
            total = total + part * s_ref[pl.ds(q, 1), :]

        @pl.when(step == 0)
        def _():
            total_ref[...] = refs[0][...] + total if last else total

        @pl.when(step > 0)
        def _():
            total_ref[...] += total

        @pl.when(step == blocks - 1)
        def _():
            if not last:
                o_ref[...] = total_ref[...]
                return
            values = [ref[...].astype(f32) for ref in refs[1 : 1 + len(states)]]
            if len(states) == 2:
                first = place_ref[1] == 0
                values = [
                    jnp.where(first, values[0], values[1]),
                    jnp.where(first, values[1], values[0]),
                ]
            sums, values = total_ref[...], jnp.concatenate(values, axis=0)
            for b in range(count // mine):
                at = slice(b * mine, (b + 1) * mine)
                o_ref[b] = jnp.concatenate([sums[at], values[at]], axis=0).astype(bf16)

    def at(i, p):
        return 2 * i + (p[0] ^ flip)

    fixed = lambda shape: pl.BlockSpec(shape, lambda i, p: (0,) * len(shape))
    more = [added, *states] if last else []
    shape = (count // mine, 2 * mine, width) if last else (count, width)
    return pl.pallas_call(
        kernel,
        grid_spec=pltpu.PrefetchScalarGridSpec(
            num_scalar_prefetch=1,
            grid=(blocks,),
            in_specs=[
                pl.BlockSpec((chips, count, BLOCK), lambda i, p: (0, 0, i)),
                pl.BlockSpec((tile, width), lambda i, p: (at(i, p), 0)),
                pl.BlockSpec((chips, width), lambda i, p: (at(i, p), 0)),
            ]
            + [fixed(x.shape) for x in more],
            out_specs=fixed(shape),
            scratch_shapes=[pltpu.VMEM((count, width), f32)],
        ),
        out_shape=jax.ShapeDtypeStruct(shape, bf16 if last else f32),
        compiler_params=params(),
        cost_estimate=cost(2 * count * width * tile * blocks, width * tile * blocks),
        name="down_product",
    )(place, act, levels, scale, *more)


def attention(queries, kv_cache, new_kv, live):
    steps = queries.shape[0]
    factor = queries.shape[-1] ** (-0.5)
    keys = kv_cache[0]
    values = kv_cache[1]
    new_keys = new_kv[:, 0]
    new_values = new_kv[:, 1]
    position = jnp.arange(keys.shape[2], dtype=jnp.int32)
    valid = position[None, None, None, None, :] < live[None, :, None, None, None]
    cached = (
        jnp.einsum("nshqd,shcd->nshqc", queries, keys, preferred_element_type=f32) * factor
    )
    recent = (
        jnp.einsum("nshqd,tshd->nshqt", queries, new_keys, preferred_element_type=f32) * factor
    )
    order = jnp.arange(steps, dtype=jnp.int32)
    fresh = (order[None, :] <= order[:, None])[:, None, None, None, :]
    top = jnp.maximum(
        jnp.max(jnp.where(valid, cached, NEG), axis=-1),
        jnp.max(jnp.where(fresh, recent, NEG), axis=-1),
    )[..., None]
    e_cached = jnp.where(valid, jnp.exp(cached - top), 0.0)
    e_recent = jnp.where(fresh, jnp.exp(recent - top), 0.0)
    total = jnp.sum(e_cached, axis=-1, keepdims=True) + jnp.sum(e_recent, axis=-1, keepdims=True)
    p_cached = (e_cached / total).astype(bf16)
    p_recent = (e_recent / total).astype(bf16)
    mixed = jnp.einsum("nshqc,shcd->nshqd", p_cached, values, preferred_element_type=f32)
    mixed = mixed + jnp.einsum(
        "nshqt,tshd->nshqd", p_recent, new_values, preferred_element_type=f32
    )
    return mixed.astype(bf16)


def swap_cores(value):
    count = lax.axis_size("wide")
    return lax.ppermute(value, "wide", [(i, i ^ 1) for i in range(count)])


def exchange(value):
    return lax.all_to_all(value, "wide", split_axis=0, concat_axis=0, tiled=True)


def exchange_chips(value):
    count = lax.axis_size("wide")
    groups = [list(range(core, count, 2)) for core in range(2)]
    return lax.all_to_all(
        value, "wide", split_axis=0, concat_axis=0, tiled=True, axis_index_groups=groups
    )


def exchange_halves(keep, send, beside):
    count = lax.axis_size("wide")
    bit = 2
    while True:
        got = lax.ppermute(send, "wide", [(i, i ^ bit) for i in range(count)])
        if bit == 2:
            got, beside = lax.optimization_barrier((got, beside))
        total = keep.astype(f32) + got.astype(f32)
        bit *= 2
        if bit == count:
            return total[0], beside
        total = total.astype(bf16)
        half = total.shape[0] // 2
        keep, send = total[:half], total[half:]


def on_device(
    residual_in,
    norm_gain,
    gate_weight,
    up_weight,
    down_weight,
    out_weight,
    queries,
    kv_cache,
    new_kv,
    cache_len,
):
    owners = lax.axis_size("wide")
    groups = lax.axis_size("grp")
    me = lax.axis_index("wide")
    steps, seqs, width_dev = residual_in.shape
    seq_dev = seqs // owners
    tokens = steps * seqs
    mine = steps * seq_dev
    width = width_dev * owners
    chips = owners // 2
    hidden_units = gate_weight.shape[1]

    parts = groups if hidden_units % (groups * owners * 2 * BLOCK) == 0 else 1
    units = hidden_units // parts
    per_owner = units // (owners * BLOCK)
    runs = (per_owner - max(1, per_owner // 4), max(1, per_owner // 4))
    part = lax.axis_index("grp") if parts > 1 else jnp.zeros((), jnp.int32)
    place = jnp.stack([me % 2, part, me // 2, me]).astype(jnp.int32)

    live = lax.dynamic_slice_in_dim(cache_len, me * seq_dev, seq_dev, 0)
    attn_out = attention(queries, kv_cache, new_kv, live)
    heads = attn_out.reshape(steps, seq_dev, owners, -1)
    heads = exchange(jnp.transpose(heads, (2, 1, 0, 3)))

    out_levels, out_scale = out_levels_of(out_weight, pick_tile(out_weight.shape[1], 2560))
    heads, out_levels, out_scale = lax.optimization_barrier((heads, out_levels, out_scale))
    heads = heads.reshape(tokens, -1)
    projected = exchange(out_product(heads, out_levels, out_scale, owners))

    down = down_weight.T
    rows = gate_weight.shape[0]
    chunk = math.gcd(rows, BLOCK)
    tile = pick_tile(units, 2048)
    paired = pair_shares_blocks(rows) and down.shape[0] == rows
    if paired:
        edge = edge_max(place, [gate_weight, up_weight, down], units, chunk, pick_tile(units, 4096))
        edge, tops = swap_cores(edge), None
    else:
        edge, tops = None, joined_max(place, [gate_weight, up_weight], units, chunk, tile)

    def levels(flip, place):
        weights = [gate_weight, up_weight]
        return levels_of(place, weights, edge, tops, flip, units, chunk, chips * BLOCK)

    away_levels = levels(1, place)
    gain = lax.dynamic_slice_in_dim(norm_gain, me * width_dev, width_dev, 0).astype(f32)[None]
    residual = jnp.transpose(residual_in, (1, 0, 2)).reshape(tokens, width_dev).astype(f32)
    projected, away_levels, gain, residual = lax.optimization_barrier(
        (projected, away_levels, gain, residual)
    )
    hidden = (residual + jnp.sum(projected.astype(f32), axis=0)).astype(bf16)

    states = [hidden]
    if parts == 2:
        states.append(lax.ppermute(hidden, "grp", [(0, 1), (1, 0)]))
    elif parts > 1:
        states = [lax.all_gather(hidden, "grp", axis=0, tiled=True)]

    def product(levels, added):
        return gate_up_product(place, states, gain, *levels, added, runs, chips, paired)

    sent = product(away_levels, None)
    *sent, place = lax.optimization_barrier((*sent, place))
    sent = [swap_cores(value) for value in sent]
    sent[0], home_levels = lax.optimization_barrier((sent[0], levels(0, place)))
    keep, send, kept = product(home_levels, sent)
    kept, place = lax.optimization_barrier((kept, place))

    down_chunk = math.gcd(down.shape[0], BLOCK)
    down_tile = pick_tile(units, 4096)
    tops = None if paired else joined_max(place, [down], units, down_chunk, down_tile)
    down_levels, down_scale = down_levels_of(
        place, down, edge if paired else None, 2, tops, units, down_chunk, down_tile
    )
    last = exchange_chips(kept)
    first, (down_levels, down_scale) = exchange_halves(keep, send, (down_levels, down_scale))

    last = jnp.sum(last.astype(f32), axis=0)
    squares = jnp.sum(last[:, 2 * runs[1] * BLOCK :], axis=1, keepdims=True)
    scale = lax.rsqrt(squares / width + EPS_NORM)

    def act_of(summed, run):
        size = run * BLOCK
        gate = summed[:, :size] * scale
        up = summed[:, size : 2 * size] * scale
        return (jax.nn.silu(gate) * up).astype(bf16)

    act = jnp.concatenate([act_of(first, runs[0]), act_of(last, runs[1])], axis=1)
    act = exchange_chips(jnp.broadcast_to(act[None], (chips,) + act.shape))
    other = swap_cores(act)
    ffn = down_product(place, act, down_levels, down_scale, None, 0, states, mine)
    both = down_product(place, other, down_levels, down_scale, ffn, 1, states, mine)

    axes = ("grp", "wide") if parts > 1 else "wide"
    both = lax.all_to_all(both, axes, split_axis=0, concat_axis=0, tiled=True)
    both = both.reshape(parts, owners, 2, seq_dev, steps, width_dev)
    ffn = both[0, :, 0]
    if parts > 1:
        ffn = jnp.sum(both[:, :, 0].astype(f32), axis=0).astype(bf16)
    ffn_out = jnp.transpose(ffn, (2, 1, 0, 3)).reshape(steps, seq_dev, width)
    hidden_out = jnp.transpose(both[0, :, 1], (2, 1, 0, 3)).reshape(steps, seq_dev, width)
    return (ffn_out, attn_out, hidden_out)


def solution(mesh):
    placed = (
        P("grp", None, "wide"),
        P(),
        P("wide", None),
        P("wide", None),
        P(None, "wide"),
        P("wide", None),
        P("grp", "wide", None, None, None),
        P(None, ("grp", "wide"), None, None, None),
        P("grp", None, "wide", None, None),
        P("grp"),
    )
    return jax.shard_map(
        on_device,
        mesh=mesh,
        in_specs=placed,
        out_specs=(
            P("grp", "wide", None),
            P("grp", "wide", None, None, None),
            P("grp", "wide", None),
        ),
        check_vma=False,
    )
```

time: 161 us -> 155 us (0.963)
  blocking collectives: 0 us -> 20.1 us
  starting transfers between devices: 38.9 us -> 28.4 us
  waiting for transfers between devices: 41.1 us -> 31.6 us
  other arithmetic: 8.19 us -> 3.15 us
    all_to_all x0 -> x1, blocking collectives: none -> 20.1 us  [exchange_chips(): lax.all_to_all(value, 'wide', split_axis=0, concat_axis=0, tiled=True, ax...]
    pallas_call x0 -> x2, Pallas kernels: none -> 14.1 us  [the longest x1 8.63 us: down_levels_of(): pl.pallas_call(kernel, grid_spec=pltpu.PrefetchScalarGridSpec(num_scalar_...]
    ppermute x4 -> x1, waiting for transfers between devices: 12.6 us -> 2.47 us  [on_device(): states.append(lax.ppermute(hidden, 'grp', [(0, 1), (1, 0)]))]
    ppermute x3, starting transfers between devices: 9.87 us -> 5.89 us  [exchange_halves(): got = lax.ppermute(send, 'wide', [(i, i ^ bit) for i in range(count)])]
    pallas_call x4 -> x2, Pallas kernels: 17.1 us -> 13.1 us  [gate_up_product(): pl.pallas_call(kernel, grid_spec=pltpu.PrefetchScalarGridSpec(num_scalar_...]
    all_to_all x2 -> x1, starting transfers between devices: 8.17 us -> 4.55 us  [exchange_chips(): lax.all_to_all(value, 'wide', split_axis=0, concat_axis=0, tiled=True, ax...]
    ppermute x3, waiting for transfers between devices: 13.4 us -> 17 us  [exchange_halves(): got = lax.ppermute(send, 'wide', [(i, i ^ bit) for i in range(count)])]
    pallas_call x2, Pallas kernels: 15.8 us -> 12.4 us  [levels_of(): pl.pallas_call(kernel, grid_spec=pltpu.PrefetchScalarGridSpec(num_scalar_...]
  transfers between devices with their start and end apart: 17 -> 12, of which waited for: 10 -> 7; matrix products, arithmetic and copies ran while one was open for 4% -> 2% of each run, Pallas kernels for 26% -> 23%
where the time goes in v4:
time: 155 us; the launch traced here: 154 us
  Pallas kernels  55.9 us (36%)
  waiting for transfers between devices  31.6 us (20%)
  starting transfers between devices  28.4 us (18%)
  blocking collectives  20.1 us (13%)
  local copies, waits for them, and re-layouts  11.3 us (7%)
  other arithmetic  3.15 us (2%)
  matrix products  2.6 us (2%)
    all_to_all x1, blocking collectives, exchange_chips(): lax.all_to_all(value, 'wide', split_axis=0, concat_axis=0, tiled=True, ax...  20.1 us
    ppermute x3, waiting for transfers between devices, exchange_halves(): got = lax.ppermute(send, 'wide', [(i, i ^ bit) for i in range(count)])  17 us
    pallas_call x2, Pallas kernels, gate_up_product(): pl.pallas_call(kernel, grid_spec=pltpu.PrefetchScalarGridSpec(num_scalar_...  13.1 us
    pallas_call x2, Pallas kernels, levels_of(): pl.pallas_call(kernel, grid_spec=pltpu.PrefetchScalarGridSpec(num_scalar_...  12.4 us
    all_to_all x2, starting transfers between devices, exchange(): lax.all_to_all(value, 'wide', split_axis=0, concat_axis=0, tiled=True)  11.9 us
    pallas_call x2, Pallas kernels, down_product(): pl.pallas_call(kernel, grid_spec=pltpu.PrefetchScalarGridSpec(num_scalar_...  9.41 us
    pallas_call x1, Pallas kernels, down_levels_of(): pl.pallas_call(kernel, grid_spec=pltpu.PrefetchScalarGridSpec(num_scalar_...  8.63 us
    all_to_all x1, waiting for transfers between devices, on_device(): both = lax.all_to_all(both, axes, split_axis=0, concat_axis=0, tiled=True)  8.25 us
  transfers between devices with their start and end apart: 12, of which 7 were waited for; matrix products, arithmetic and copies ran while one was open for 2% of the time, Pallas kernels for 23%

profile of v4, /device:TPU:0, one launch (start us, length us, event | category | flops | bytes accessed | tf_op | source)
XLA Modules:
  0.0 154.0 jit_solution(16333344785164984966)
XLA Ops:
  0.7 1.4 dynamic_slice.6
  3.7 1.7 %select_reduce_fusion = (f32[3,8,8]{2,0,1:T(4,128)S(1)}, f32[3,1,8,8,512]{4,3,0,2,1:T(8,128)S(1)}) fusion(pred[512]{0:T(512)(128)(4,1)S(1)} %iota_compare_fusion.1, bf16[2,1,8,512,128]{4,3,2,1,0:T(8,128)(2,1)} %param.17, bf16[3,1,8,8,128]{4,3,2,1,0:T(8,128)(2,1)S(1)} %copy-done), kind=kOutput, calls=%fused_computation.18 | convolution fusion | flops 25460544 | bytes 1492224 | tf_op jit(solution)/shard_map/nshqd,shcd->nshqc/dot_general | solution.py:555
  7.2 7.4 %all-to-all-start = ((bf16[16,1,3,512]{3,2,1,0:T(4,128)(2,1)}), bf16[16,1,3,512]{3,2,1,0:T(4,128)(2,1)S(1)}, u32[]{:S(2)}, u32[]{:S(2)}) async-start(bf16[16,1,3,512]{3,2,1,0:T(4,128)(2,1)} %copy.34), calls=%async_computation | async-start | bytes 131072 | tf_op jit(solution)/shard_map/all_to_all | solution.py:584
  14.5 5.4 %out_levels_of.1 = (f8e4m3fn[512,5120]{1,0:T(32,128)(4,1)}, f32[8,5120]{1,0:T(8,128)}) custom-call(bf16[512,5120]{1,0:T(8,128)(2,1)} %w_ref.1), custom_call_target="tpu_custom_call" | custom-call | flops 20971520 | bytes 7864320 | tf_op jit(solution)/shard_map/out_levels_of/pallas_call | solution.py:290
  20.0 1.5 all-to-all-done
  22.1 3.2 %out_product.1 = bf16[16,48,320]{2,1,0:T(8,128)(2,1)} custom-call(bf16[48,512]{1,0:T(8,128)(2,1)} %reshape.133.x_ref, f8e4m3fn[512,5120]{1,0:T(32,128)(4,1)} %get-tuple-element.42.l_ref, f32[8,5120]{1,0:T(8,128)} %get-tuple-element.43.s_ref), custom_call_target="tpu_custom_call" | custom-call | flops 251658240 | bytes 2621440 | tf_op jit(solution)/shard_map/out_product/pallas_call | solution.py:324
  25.3 4.6 %all-to-all-start.1 = ((bf16[16,48,320]{2,1,0:T(8,128)(2,1)}), bf16[16,48,320]{2,1,0:T(8,128)(2,1)S(1)}, u32[]{:S(2)}, u32[]{:S(2)}) async-start(bf16[16,48,320]{2,1,0:T(8,128)(2,1)} %out_product.1), calls=%async_computation.1 | async-start | bytes 1179648 | tf_op jit(solution)/shard_map/all_to_all | solution.py:584
  30.5 3.7 %edge_max.1 = f32[8,8192]{1,0:T(8,128)} custom-call(s32[4]{0:T(128)} %pad_add_fusion.place_ref, bf16[320,16384]{1,0:T(8,128)(2,1)} %refs_0_.5, bf16[320,16384]{1,0:T(8,128)(2,1)} %refs_1_.5, bf16[320,16384]{1,0:T(8,128)(2,1)} %bitcast.90), custom_call_target="tpu_custom_call" | custom-call | flops 3145728 | bytes 3145728 | tf_op jit(solution)/shard_map/edge_max/pallas_call | solution.py:95
  36.7 6.2 %levels_of.2 = (f8e4m3fn[320,4096]{1,0:T(32,128)(4,1)}, f8e4m3fn[320,4096]{1,0:T(32,128)(4,1)}, f32[2,8,4096]{2,1,0:T(8,128)}) custom-call(s32[4]{0:T(128)} %pad_add_fusion.place_ref, bf16[320,16384]{1,0:T(8,128)(2,1)} %refs_0_.5, bf16[320,16384]{1,0:T(8,128)(2,1)} %refs_1_.5, f32[8,8192]{1,0:T(8,128)} %copy-done.2), custom_call_target="tpu_custom_call" | custom-call | flops 10485760 | bytes 10485760 | tf_op jit(solution)/shard_map/levels_of/pallas_call | solution.py:161
  43.0 2.5 %all-to-all-done.1 = bf16[16,48,320]{2,1,0:T(8,128)(2,1)S(1)} async-done(((bf16[16,48,320]{2,1,0:T(8,128)(2,1)}), bf16[16,48,320]{2,1,0:T(8,128)(2,1)S(1)}, u32[]{:S(2)}, u32[]{:S(2)}) %all-to-all-start.1) | async-done | bytes 491552 | tf_op jit(solution)/shard_map/all_to_all | solution.py:584
  45.6 1.6 %collective-permute-start.1 = (bf16[48,320]{1,0:T(8,128)(2,1)S(1)}, bf16[48,320]{1,0:T(8,128)(2,1)S(1)}, u32[]{:S(2)}, u32[]{:S(2)}) collective-permute-start(bf16[48,320]{1,0:T(8,128)(2,1)S(1)} %add_convert_fusion.2.refs_0_.refs_1_), channel_id=1, source_target_pairs={{0,16},{16,0},{1,17},{17,1},{2,18},{18,2},{3,19},{19,3},{4,20},{20... | collective-permute-start | bytes 92168 | tf_op jit(solution)/shard_map/ppermute | solution.py:676
  47.1 2.5 %collective-permute-done.1.refs_1_.refs_2_ = bf16[48,320]{1,0:T(8,128)(2,1)S(1)} collective-permute-done((bf16[48,320]{1,0:T(8,128)(2,1)S(1)}, bf16[48,320]{1,0:T(8,128)(2,1)S(1)}, u32[]{:S(2)}, u32[]{:S(2)}) %collective-permute-start.1) | collective-permute-done | bytes 30752 | tf_op jit(solution)/shard_map/ppermute | solution.py:676
  50.2 5.9 %gate_up_product.2 = (bf16[8,96,768]{2,1,0:T(8,128)(2,1)}, bf16[8,96,384]{2,1,0:T(8,128)(2,1)}) custom-call(s32[4]{0:T(128)} %pad_add_fusion.place_ref, bf16[48,320]{1,0:T(8,128)(2,1)} %copy-done.7, bf16[48,320]{1,0:T(8,128)(2,1)} %copy-done.8, f32[1,320]{1,0:T(1,128)} %reshape.137.refs_2_, f8e4m3fn[320,4096]{1,0:T(32,128)(4,1)} %get-tuple-element.50.refs_3_, ...), custom_call_target="tpu_custom_call" | custom-call | flops 503316480 | bytes 2621440 | tf_op jit(solution)/shard_map/gate_up_product/pallas_call | solution.py:451
  56.7 6.2 %levels_of.3 = (f8e4m3fn[320,4096]{1,0:T(32,128)(4,1)}, f8e4m3fn[320,4096]{1,0:T(32,128)(4,1)}, f32[2,8,4096]{2,1,0:T(8,128)}) custom-call(s32[4]{0:T(128)} %pad_add_fusion.place_ref, bf16[320,16384]{1,0:T(8,128)(2,1)} %refs_0_.5, bf16[320,16384]{1,0:T(8,128)(2,1)} %refs_1_.5, f32[8,8192]{1,0:T(8,128)} %copy-done.2), custom_call_target="tpu_custom_call" | custom-call | flops 10485760 | bytes 10485760 | tf_op jit(solution)/shard_map/levels_of/pallas_call | solution.py:161
  62.9 1.0 copy-done.3
  63.9 0.8 copy-done.6
  64.7 7.1 %gate_up_product.3 = (bf16[4,96,768]{2,1,0:T(8,128)(2,1)}, bf16[4,96,768]{2,1,0:T(8,128)(2,1)}, bf16[8,96,384]{2,1,0:T(8,128)(2,1)}) custom-call(s32[4]{0:T(128)} %pad_add_fusion.place_ref, bf16[48,320]{1,0:T(8,128)(2,1)} %copy-done.7, bf16[48,320]{1,0:T(8,128)(2,1)} %copy-done.8, f32[1,320]{1,0:T(1,128)} %reshape.137.refs_2_, ...), custom_call_target="tpu_custom_call" | custom-call | flops 503316480 | bytes 2621440 | tf_op jit(solution)/shard_map/gate_up_product/pallas_call | solution.py:451
  71.9 0.8 collective-permute-start.4
  72.6 4.5 %all-to-all-start.2 = ((bf16[8,96,384]{2,1,0:T(8,128)(2,1)}), bf16[8,96,384]{2,1,0:T(8,128)(2,1)S(1)}, u32[]{:S(2)}, u32[]{:S(2)}) async-start(bf16[8,96,384]{2,1,0:T(8,128)(2,1)} %get-tuple-element.72), calls=%async_computation.2 | async-start | bytes 1179648 | tf_op jit(solution)/shard_map/all_to_all | solution.py:590
  77.2 8.6 %down_levels_of.1 = (f8e4m3fn[8192,320]{1,0:T(32,128)(4,1)}, f32[64,320]{1,0:T(8,128)}) custom-call(s32[4]{0:T(128)} %pad_add_fusion.place_ref, bf16[320,16384]{1,0:T(8,128)(2,1)} %bitcast.91, f32[8,8192]{1,0:T(8,128)} %copy-done.2), custom_call_target="tpu_custom_call" | custom-call | flops 20971520 | bytes 7864320 | tf_op jit(solution)/shard_map/down_levels_of/pallas_call | solution.py:217
  85.8 7.0 %collective-permute-done.4 = bf16[4,96,768]{2,1,0:T(8,128)(2,1)S(1)} collective-permute-done((bf16[4,96,768]{2,1,0:T(8,128)(2,1)}, bf16[4,96,768]{2,1,0:T(8,128)(2,1)S(1)}, u32[]{:S(2)}, u32[]{:S(2)}) %collective-permute-start.4) | collective-permute-done | bytes 589856 | tf_op jit(solution)/shard_map/ppermute | solution.py:599
  93.0 1.6 %collective-permute-start.5 = (bf16[2,96,768]{2,1,0:T(8,128)(2,1)S(1)}, bf16[2,96,768]{2,1,0:T(8,128)(2,1)S(1)}, u32[]{:S(2)}, u32[]{:S(2)}) collective-permute-start(bf16[2,96,768]{2,1,0:T(8,128)(2,1)S(1)} %slice.61), channel_id=1, source_target_pairs={{0,4},{1,5},{2,6},{3,7},{4,0},{5,1},{6,2},{7,3},{8,12},{9,13},{10,... | collective-permute-start | bytes 884744 | tf_op jit(solution)/shard_map/ppermute | solution.py:599
  94.6 5.8 %collective-permute-done.5 = bf16[2,96,768]{2,1,0:T(8,128)(2,1)S(1)} collective-permute-done((bf16[2,96,768]{2,1,0:T(8,128)(2,1)S(1)}, bf16[2,96,768]{2,1,0:T(8,128)(2,1)S(1)}, u32[]{:S(2)}, u32[]{:S(2)}) %collective-permute-start.5) | collective-permute-done | bytes 294944 | tf_op jit(solution)/shard_map/ppermute | solution.py:599
  100.4 3.6 %collective-permute-start.6 = (bf16[1,96,768]{2,1,0:T(8,128)(2,1)S(1)}, bf16[1,96,768]{2,1,0:T(8,128)(2,1)S(1)}, u32[]{:S(2)}, u32[]{:S(2)}) collective-permute-start(bf16[1,96,768]{2,1,0:T(8,128)(2,1)S(1)} %slice.63), channel_id=1, source_target_pairs={{0,8},{1,9},{2,10},{3,11},{4,12},{5,13},{6,14},{7,15},{8,0},{9,1},... | collective-permute-start | bytes 442376 | tf_op jit(solution)/shard_map/ppermute | solution.py:599
  104.3 4.2 %collective-permute-done.6 = bf16[1,96,768]{2,1,0:T(8,128)(2,1)S(1)} collective-permute-done((bf16[1,96,768]{2,1,0:T(8,128)(2,1)S(1)}, bf16[1,96,768]{2,1,0:T(8,128)(2,1)S(1)}, u32[]{:S(2)}, u32[]{:S(2)}) %collective-permute-start.6) | collective-permute-done | bytes 147488 | tf_op jit(solution)/shard_map/ppermute | solution.py:599
  108.7 20.1 %all_to_all.25.a_ref = bf16[8,96,512]{2,1,0:T(8,128)(2,1)S(1)} all-to-all(bf16[8,96,512]{2,1,0:T(8,128)(2,1)S(1)} %broadcast_in_dim.67), channel_id=1, replica_groups={{0,2,4,6,8,10,12,14},{1,3,5,7,9,11,13,15},{16,18,20,22,24,26,28,30},{17..., dimensions={0} | all-to-all | bytes 1572864 | tf_op jit(solution)/shard_map/all_to_all | solution.py:590
  128.8 0.9 copy-done.1
  129.7 4.5 %down_product.2.refs_0_ = f32[96,320]{1,0:T(8,128)} custom-call(s32[4]{0:T(128)} %pad_add_fusion.place_ref, bf16[8,96,512]{2,1,0:T(8,128)(2,1)} %copy-done.1, f8e4m3fn[8192,320]{1,0:T(32,128)(4,1)} %get-tuple-element.73.l_ref, f32[64,320]{1,0:T(8,128)} %get-tuple-element.74.s_ref), custom_call_target="tpu_custom_call" | custom-call | flops 251658240 | bytes 1310720 | tf_op jit(solution)/shard_map/down_product/pallas_call | solution.py:524
  134.3 0.9 copy-done.4
  135.2 4.9 %down_product.3 = bf16[32,6,320]{2,1,0:T(8,128)(2,1)} custom-call(s32[4]{0:T(128)} %pad_add_fusion.place_ref, bf16[8,96,512]{2,1,0:T(8,128)(2,1)} %copy-done.4, f8e4m3fn[8192,320]{1,0:T(32,128)(4,1)} %get-tuple-element.73.l_ref, f32[64,320]{1,0:T(8,128)} %get-tuple-element.74.s_ref, f32[96,320]{1,0:T(8,128)} %down_product.2.refs_0_, ...), custom_call_target="tpu_custom_call" | custom-call | flops 251658240 | bytes 1310720 | tf_op jit(solution)/shard_map/down_product/pallas_call | solution.py:524
  140.0 3.5 %all-to-all-start.4 = ((bf16[32,6,320]{2,1,0:T(8,128)(2,1)}), bf16[32,6,320]{2,1,0:T(8,128)(2,1)S(1)}, u32[]{:S(2)}, u32[]{:S(2)}) async-start(bf16[32,6,320]{2,1,0:T(8,128)(2,1)} %down_product.3), calls=%async_computation.4 | async-start | bytes 393216 | tf_op jit(solution)/shard_map/all_to_all | solution.py:716
  144.2 8.3 %all-to-all-done.4 = bf16[32,6,320]{2,1,0:T(8,128)(2,1)S(1)} async-done(((bf16[32,6,320]{2,1,0:T(8,128)(2,1)}), bf16[32,6,320]{2,1,0:T(8,128)(2,1)S(1)}, u32[]{:S(2)}, u32[]{:S(2)}) %all-to-all-start.4) | async-done | bytes 122912 | tf_op jit(solution)/shard_map/all_to_all | solution.py:716
  (67 shorter events, 11.3 us)
Async XLA Ops:
  0.6 2.8 %copy-start = (bf16[3,1,8,8,128]{4,3,2,1,0:T(8,128)(2,1)S(1)}, bf16[3,1,8,8,128]{4,3,2,1,0:T(8,128)(2,1)}, u32[]{:S(2)}) copy-start(bf16[3,1,8,8,128]{4,3,2,1,0:T(8,128)(2,1)} %param.16) | copy-start | bytes 147460
  0.6 5.1 %copy-start.10 = (bf16[2,1,8,512,128]{4,3,2,1,0:T(8,128)(2,1)S(1)}, bf16[2,1,8,512,128]{4,3,2,1,0:T(8,128)(2,1)}, u32[]{:S(2)}) copy-start(bf16[2,1,8,512,128]{4,3,2,1,0:T(8,128)(2,1)} %param.17) | copy-start | bytes 6291460
  7.2 14.3 %all-to-all-start = ((bf16[16,1,3,512]{3,2,1,0:T(4,128)(2,1)}), bf16[16,1,3,512]{3,2,1,0:T(4,128)(2,1)S(1)}, u32[]{:S(2)}, u32[]{:S(2)}) async-start(bf16[16,1,3,512]{3,2,1,0:T(4,128)(2,1)} %copy.34), calls=%async_computation | async-start | bytes 131072 | tf_op jit(solution)/shard_map/all_to_all | solution.py:584
  25.3 20.1 %all-to-all-start.1 = ((bf16[16,48,320]{2,1,0:T(8,128)(2,1)}), bf16[16,48,320]{2,1,0:T(8,128)(2,1)S(1)}, u32[]{:S(2)}, u32[]{:S(2)}) async-start(bf16[16,48,320]{2,1,0:T(8,128)(2,1)} %out_product.1), calls=%async_computation.1 | async-start | bytes 1179648 | tf_op jit(solution)/shard_map/all_to_all | solution.py:584
  30.5 5.4 %copy-start.9 = (bf16[3,16,320]{2,1,0:T(8,128)(2,1)S(1)}, bf16[3,16,320]{2,1,0:T(8,128)(2,1)}, u32[]{:S(2)}) copy-start(bf16[3,16,320]{2,1,0:T(8,128)(2,1)} %param.10) | copy-start | bytes 92164
  34.2 1.8 %collective-permute-start = (f32[8,8192]{1,0:T(8,128)}, f32[8,8192]{1,0:T(8,128)S(1)}, u32[]{:S(2)}, u32[]{:S(2)}) collective-permute-start(f32[8,8192]{1,0:T(8,128)} %edge_max.1), channel_id=1, source_target_pairs={{0,1},{1,0},{2,3},{3,2},{4,5},{5,4},{6,7},{7,6},{8,9},{9,8},{10,11... | collective-permute-start | bytes 786440 | tf_op jit(solution)/shard_map/ppermute | solution.py:580
  36.0 0.7 copy-start.2
  45.5 4.0 %copy-start.7 = (bf16[48,320]{1,0:T(8,128)(2,1)}, bf16[48,320]{1,0:T(8,128)(2,1)S(1)}, u32[]{:S(2)}) copy-start(bf16[48,320]{1,0:T(8,128)(2,1)S(1)} %add_convert_fusion.2.refs_0_.refs_1_) | copy-start | bytes 92164
  45.6 4.0 %collective-permute-start.1 = (bf16[48,320]{1,0:T(8,128)(2,1)S(1)}, bf16[48,320]{1,0:T(8,128)(2,1)S(1)}, u32[]{:S(2)}, u32[]{:S(2)}) collective-permute-start(bf16[48,320]{1,0:T(8,128)(2,1)S(1)} %add_convert_fusion.2.refs_0_.refs_1_), channel_id=1, source_target_pairs={{0,16},{16,0},{1,17},{17,1},{2,18},{18,2},{3,19},{19,3},{4,20},{20... | collective-permute-start | bytes 92168 | tf_op jit(solution)/shard_map/ppermute | solution.py:676
  49.6 0.6 copy-start.8
  56.1 6.7 %collective-permute-start.2 = (bf16[8,96,768]{2,1,0:T(8,128)(2,1)}, bf16[8,96,768]{2,1,0:T(8,128)(2,1)S(1)}, u32[]{:S(2)}, u32[]{:S(2)}) collective-permute-start(bf16[8,96,768]{2,1,0:T(8,128)(2,1)} %get-tuple-element.56), channel_id=1, source_target_pairs={{0,1},{1,0},{2,3},{3,2},{4,5},{5,4},{6,7},{7,6},{8,9},{9,8},{10,11... | collective-permute-start | bytes 3538952 | tf_op jit(solution)/shard_map/ppermute | solution.py:580
  56.1 6.7 %collective-permute-start.3 = (bf16[8,96,384]{2,1,0:T(8,128)(2,1)}, bf16[8,96,384]{2,1,0:T(8,128)(2,1)S(1)}, u32[]{:S(2)}, u32[]{:S(2)}) collective-permute-start(bf16[8,96,384]{2,1,0:T(8,128)(2,1)} %get-tuple-element.64), channel_id=1, source_target_pairs={{0,1},{1,0},{2,3},{3,2},{4,5},{5,4},{6,7},{7,6},{8,9},{9,8},{10,11... | collective-permute-start | bytes 1769480 | tf_op jit(solution)/shard_map/ppermute | solution.py:580
  62.9 1.0 copy-start.3
  63.9 0.8 copy-start.6
  71.9 21.0 %collective-permute-start.4 = (bf16[4,96,768]{2,1,0:T(8,128)(2,1)}, bf16[4,96,768]{2,1,0:T(8,128)(2,1)S(1)}, u32[]{:S(2)}, u32[]{:S(2)}) collective-permute-start(bf16[4,96,768]{2,1,0:T(8,128)(2,1)} %get-tuple-element.68), channel_id=1, source_target_pairs={{0,2},{1,3},{2,0},{3,1},{4,6},{5,7},{6,4},{7,5},{8,10},{9,11},{10,... | collective-permute-start | bytes 1769480 | tf_op jit(solution)/shard_map/ppermute | solution.py:599
  72.6 31.4 %all-to-all-start.2 = ((bf16[8,96,384]{2,1,0:T(8,128)(2,1)}), bf16[8,96,384]{2,1,0:T(8,128)(2,1)S(1)}, u32[]{:S(2)}, u32[]{:S(2)}) async-start(bf16[8,96,384]{2,1,0:T(8,128)(2,1)} %get-tuple-element.72), calls=%async_computation.2 | async-start | bytes 1179648 | tf_op jit(solution)/shard_map/all_to_all | solution.py:590
  77.2 15.7 %copy-start.5 = (bf16[4,96,768]{2,1,0:T(8,128)(2,1)S(1)}, bf16[4,96,768]{2,1,0:T(8,128)(2,1)}, u32[]{:S(2)}) copy-start(bf16[4,96,768]{2,1,0:T(8,128)(2,1)} %get-tuple-element.67) | copy-start | bytes 1769476
  93.0 7.3 %collective-permute-start.5 = (bf16[2,96,768]{2,1,0:T(8,128)(2,1)S(1)}, bf16[2,96,768]{2,1,0:T(8,128)(2,1)S(1)}, u32[]{:S(2)}, u32[]{:S(2)}) collective-permute-start(bf16[2,96,768]{2,1,0:T(8,128)(2,1)S(1)} %slice.61), channel_id=1, source_target_pairs={{0,4},{1,5},{2,6},{3,7},{4,0},{5,1},{6,2},{7,3},{8,12},{9,13},{10,... | collective-permute-start | bytes 884744 | tf_op jit(solution)/shard_map/ppermute | solution.py:599
  100.4 8.1 %collective-permute-start.6 = (bf16[1,96,768]{2,1,0:T(8,128)(2,1)S(1)}, bf16[1,96,768]{2,1,0:T(8,128)(2,1)S(1)}, u32[]{:S(2)}, u32[]{:S(2)}) collective-permute-start(bf16[1,96,768]{2,1,0:T(8,128)(2,1)S(1)} %slice.63), channel_id=1, source_target_pairs={{0,8},{1,9},{2,10},{3,11},{4,12},{5,13},{6,14},{7,15},{8,0},{9,1},... | collective-permute-start | bytes 442376 | tf_op jit(solution)/shard_map/ppermute | solution.py:599
  128.8 0.9 copy-start.1
  128.8 5.4 %collective-permute-start.7 = (bf16[8,96,512]{2,1,0:T(8,128)(2,1)S(1)}, bf16[8,96,512]{2,1,0:T(8,128)(2,1)S(1)}, u32[]{:S(2)}, u32[]{:S(2)}) collective-permute-start(bf16[8,96,512]{2,1,0:T(8,128)(2,1)S(1)} %all_to_all.25.a_ref), channel_id=1, source_target_pairs={{0,1},{1,0},{2,3},{3,2},{4,5},{5,4},{6,7},{7,6},{8,9},{9,8},{10,11... | collective-permute-start | bytes 2359304 | tf_op jit(solution)/shard_map/ppermute | solution.py:580
  134.3 0.9 copy-start.4
  140.0 12.4 %all-to-all-start.4 = ((bf16[32,6,320]{2,1,0:T(8,128)(2,1)}), bf16[32,6,320]{2,1,0:T(8,128)(2,1)S(1)}, u32[]{:S(2)}, u32[]{:S(2)}) async-start(bf16[32,6,320]{2,1,0:T(8,128)(2,1)} %down_product.3), calls=%async_computation.4 | async-start | bytes 393216 | tf_op jit(solution)/shard_map/all_to_all | solution.py:716

commit v5 on v4

--- a/solution.py
+++ b/solution.py
@@ -21,8 +21,8 @@
 f8 = jnp.float8_e4m3fn
 
 
-def params(**more):
-    return pltpu.CompilerParams(vmem_limit_bytes=VMEM, **more)
+def params(limit=VMEM):
+    return pltpu.CompilerParams(vmem_limit_bytes=limit)
 
 
 def in_hbm(*arrays):
@@ -123,119 +123,66 @@
     return fill_rows(joined)
 
 
-def levels_of(place, weights, edge, tops, flip, cols, chunk, tile):
+def block_scales(w_ref, top_ref, place_ref, a, paired, chunk, parts):
+    if paired:
+        other = top_ref[pl.ds(a, 1), :]
+        tops = spread_lanes(join_pair(w_ref, other, place_ref[0] == 1, chunk, parts))
+    else:
+        tops = top_ref[a]
+    largest = tops + EPS_SCALE
+    return QMAX / largest, largest * (1.0 / QMAX)
+
+
+def rounded_chunk(w_ref, j, chunk, factor, scale):
+    value = w_ref[pl.ds(j * chunk, chunk), :].astype(f32) * factor[j : j + 1]
+    return (value.astype(f8).astype(f32) * scale[j : j + 1]).astype(bf16)
+
+
+def top_spec_of(tops, paired, tile, at):
+    if paired:
+        return pl.BlockSpec((tops.shape[0], tile), lambda i, p: (0, at(i, p)))
+    return pl.BlockSpec((tops.shape[0], 8, tile), lambda i, p: (0, 0, at(i, p)))
+
+
+def rounded_weights(place, weights, tops, paired, first, flip, cols, chunk, tile):
     rows = weights[0].shape[0]
     parts = rows // chunk
     count = len(weights)
-    steps = cols // (2 * tile)
+    taken = 1 if flip is None else 2
+    steps = cols // (taken * tile)
 
     def columns(i, p):
-        return 2 * i + (p[0] ^ flip)
+        return i if flip is None else (p[0] ^ flip) * steps + i
 
     def kernel(place_ref, *refs):
-        w_refs = refs[:count]
-        top_ref = refs[count]
-        o_refs = refs[count + 1 : 2 * count + 1]
-        s_ref = refs[2 * count + 1]
-        factor = refs[2 * count + 2]
-        odd = place_ref[0] == 1
         for a in range(count):
-            if edge is None:
-                joined = top_ref[a]
-            else:
-                other = top_ref[pl.ds(a, 1), :]
-                joined = spread_lanes(join_pair(w_refs[a], other, odd, chunk, parts))
-            largest = joined + EPS_SCALE
-            factor[a] = QMAX / largest
-            s_ref[a] = largest * (1.0 / QMAX)
-        for a in range(count):
+            factor, scale = block_scales(
+                refs[a], refs[count], place_ref, first + a, paired, chunk, parts
+            )
             for j in range(parts):
-                rows_at = pl.ds(j * chunk, chunk)
-                value = w_refs[a][rows_at, :].astype(f32) * factor[a, pl.ds(j, 1), :]
-                o_refs[a][rows_at, :] = value.astype(f8)
-
-    if edge is None:
-        top_spec = pl.BlockSpec((count, 8, tile), lambda i, p: (0, 0, columns(i, p)))
-    else:
-        top_spec = pl.BlockSpec((8, tile), lambda i, p: (0, columns(i, p)))
+                refs[count + 1 + a][pl.ds(j * chunk, chunk), :] = rounded_chunk(
+                    refs[a], j, chunk, factor, scale
+                )
+
     return pl.pallas_call(
         kernel,
         grid_spec=pltpu.PrefetchScalarGridSpec(
             num_scalar_prefetch=1,
             grid=(steps,),
             in_specs=[
-                pl.BlockSpec((rows, tile), lambda i, p: (0, 2 * p[1] * steps + columns(i, p)))
+                pl.BlockSpec((rows, tile), lambda i, p: (0, taken * p[1] * steps + columns(i, p)))
             ]
             * count
-            + [top_spec],
-            out_specs=[pl.BlockSpec((rows, tile), lambda i, p: (0, i))] * count
-            + [pl.BlockSpec((count, 8, tile), lambda i, p: (0, 0, i))],
-            scratch_shapes=[pltpu.VMEM((count, 8, tile), f32)],
+            + [top_spec_of(tops, paired, tile, columns)],
+            out_specs=[pl.BlockSpec((rows, tile), lambda i, p: (0, i))] * count,
         ),
-        out_shape=[jax.ShapeDtypeStruct((rows, cols // 2), f8)] * count
-        + [jax.ShapeDtypeStruct((count, 8, cols // 2), f32)],
+        out_shape=[jax.ShapeDtypeStruct((rows, cols // taken), bf16)] * count,
         compiler_params=params(),
-        cost_estimate=cost(2 * count * rows * cols, 2 * count * rows * cols),
-        name="levels_of",
-    )(place, *in_hbm(*weights), tops if edge is None else edge)
-
-
-def down_levels_of(place, weight, edge, row, tops, cols, chunk, tile):
-    rows = weight.shape[0]
-    parts = rows // chunk
-    steps = cols // tile
-
-    def kernel(place_ref, w_ref, top_ref, o_ref, s_ref):
-        odd = place_ref[0] == 1
-        if edge is None:
-            joined = top_ref[0]
-        else:
-            other = top_ref[pl.ds(row, 1), :]
-            joined = spread_lanes(join_pair(w_ref, other, odd, chunk, parts))
-        largest = joined + EPS_SCALE
-        factor = QMAX / largest
-        scale = largest * (1.0 / QMAX)
-        for g in range(tile // LANES):
-            at = slice(g * LANES, (g + 1) * LANES)
-            value = jnp.concatenate(
-                [
-                    w_ref[pl.ds(j * chunk, chunk), pl.ds(g * LANES, LANES)].astype(f32)
-                    * factor[j : j + 1, at]
-                    for j in range(parts)
-                ],
-                axis=0,
-            )
-            o_ref[pl.ds(g * LANES, LANES), :] = value.T.astype(f8)
-            s_ref[pl.ds(g, 1), :] = jnp.concatenate(
-                [scale[j : j + 1, at][:, :chunk] for j in range(parts)], axis=1
-            )
-
-    if edge is None:
-        top_spec = pl.BlockSpec((1, 8, tile), lambda i, p: (0, 0, i))
-    else:
-        top_spec = pl.BlockSpec((8, tile), lambda i, p: (0, i))
-    return pl.pallas_call(
-        kernel,
-        grid_spec=pltpu.PrefetchScalarGridSpec(
-            num_scalar_prefetch=1,
-            grid=(steps,),
-            in_specs=[
-                pl.BlockSpec((rows, tile), lambda i, p: (0, p[1] * steps + i)),
-                top_spec,
-            ],
-            out_specs=[
-                pl.BlockSpec((tile, rows), lambda i, p: (i, 0)),
-                pl.BlockSpec((tile // LANES, rows), lambda i, p: (i, 0)),
-            ],
+        cost_estimate=cost(
+            6 * count * rows * cols // taken, 4 * count * rows * cols // taken
         ),
-        out_shape=[
-            jax.ShapeDtypeStruct((cols, rows), f8),
-            jax.ShapeDtypeStruct((cols // LANES, rows), f32),
-        ],
-        compiler_params=params(),
-        cost_estimate=cost(8 * rows * cols, 3 * rows * cols),
-        name="down_levels_of",
-    )(place, *in_hbm(weight), tops if edge is None else edge)
+        name="rounded_weights",
+    )(place, *in_hbm(*weights), tops)
 
 
 def join_group(parts, size, dim):
@@ -337,26 +284,23 @@
     )(left, levels, scale)
 
 
-def gate_up_product(place, hidden, gain, gate, up, scale, added, runs, chips, paired):
+def gate_up_product(place, hidden, gain, gate, up, tops, runs, chips, paired, cols):
     groups = len(hidden)
     rows = gate.shape[0]
     count = groups * hidden[0].shape[0]
     chunk = math.gcd(rows, BLOCK)
+    parts = rows // chunk
     extra = -(-4 * chips // LANES) * LANES
     units = [run * BLOCK for run in runs]
     widths = (2 * units[0], 2 * units[1] + extra)
-    tile = chips * BLOCK
-    staged = added is not None
+    together = 2 if sum(runs) % 2 == 0 else 1
+    tile = together * chips * BLOCK
 
     def kernel(place_ref, *refs):
-        refs = list(refs)
-        h_refs, refs = refs[:groups], refs[groups:]
-        gain_ref, g_ref, u_ref, s_ref = refs[:4]
-        a_refs = refs[4:6] if staged else (None, None)
-        o_refs = refs[6:-2] if staged else refs[4:-2]
-        x_ref, p_ref = refs[-2:]
+        h_refs = refs[:groups]
+        gain_ref, g_ref, u_ref = refs[groups : groups + 3]
+        o_refs, x_ref, p_ref = refs[-4:-2], refs[-2], refs[-1]
         step = pl.program_id(0)
-        odd = place_ref[0]
 
         @pl.when(step == 0)
         def _():
@@ -368,11 +312,7 @@
                     jnp.where(first, values[1], values[0]),
                 ]
             states = jnp.concatenate(values, axis=0)
-            left = (states * gain_ref[...]).astype(bf16)
-            if paired:
-                turned = jnp.concatenate([left[:, chunk:], left[:, :chunk]], axis=1)
-                left = jnp.where(odd == 1, turned, left)
-            x_ref[...] = left
+            x_ref[...] = (states * gain_ref[...]).astype(bf16)
             squares = jnp.sum(states * states, axis=1, keepdims=True)
             high = squares.astype(bf16).astype(f32)
             lane = lax.broadcasted_iota(jnp.int32, (count, extra), 1)
@@ -381,114 +321,98 @@
                 lane == at, high, jnp.where(lane == at + 1, squares - high, 0.0)
             )
 
-        if paired:
-            whole = rows // BLOCK
-            blocks = [
-                (odd * chunk + j * BLOCK, j * BLOCK, BLOCK, odd + 2 * j) for j in range(whole)
-            ]
-            blocks.append(
-                ((1 - odd) * whole * BLOCK, whole * BLOCK, chunk, (1 - odd) * 2 * whole)
-            )
-        else:
-            blocks = [(j * chunk, j * chunk, chunk, j) for j in range(rows // chunk)]
         totals = []
         for a, ref in enumerate((g_ref, u_ref)):
-            total = None
-            for start, x_at, size, s_at in blocks:
-                if paired:
-                    start = pl.multiple_of(start, chunk)
-                part = jnp.dot(
-                    x_ref[:, pl.ds(x_at, size)],
-                    ref[pl.ds(start, size), :].astype(bf16),
-                    preferred_element_type=f32,
+            if tops is None:
+                weight = ref[...]
+            else:
+                factor, scale = block_scales(
+                    ref, refs[groups + 3], place_ref, a, paired, chunk, parts
                 )
-                part = part * s_ref[a, pl.ds(s_at, 1), :]
-                total = part if total is None else total + part
-            totals.append(total)
-
-        def write(run, block, ref, position, q):
-            values = [
-                (a * units[run] + block * BLOCK, total[:, q * BLOCK : (q + 1) * BLOCK])
-                for a, total in enumerate(totals)
-            ]
+                weight = jnp.concatenate(
+                    [rounded_chunk(ref, j, chunk, factor, scale) for j in range(parts)], axis=0
+                )
+            totals.append(jnp.dot(x_ref[...], weight, preferred_element_type=f32))
+
+        def write(run, block, position, q):
+            ref = o_refs[run]
+            at = ((runs[0] * run + block) % together * chips + q) * BLOCK
+            for a, total in enumerate(totals):
+                lanes = pl.ds(a * units[run] + block * BLOCK, BLOCK)
+                ref[position, :, lanes] = total[:, at : at + BLOCK].astype(bf16)
             if run == 1 and block == 0:
-                values.append((2 * units[1], p_ref[...]))
-            for start, value in values:
-                lanes = pl.ds(start, value.shape[1])
-                if staged:
-                    value = value + a_refs[run][q, :, lanes].astype(f32)
-                ref[position, :, lanes] = value.astype(bf16)
+                ref[position, :, pl.ds(2 * units[1], extra)] = p_ref[...].astype(bf16)
 
         def write_first(block):
             for q in range(chips):
-                if not staged:
-                    write(0, block, o_refs[0], q, q)
-                    continue
-                away = q ^ place_ref[2]
-                position, rest = 0, away // 2
-                for _ in range(chips.bit_length() - 2):
+                position, rest = 0, q ^ place_ref[2]
+                for _ in range(chips.bit_length() - 1):
                     position, rest = position * 2 + rest % 2, rest // 2
-                for side in range(2):
-                    pl.when(away % 2 == side)(
-                        functools.partial(write, 0, block, o_refs[side], position, q)
-                    )
+                write(0, block, position, q)
 
         def write_second(block):
             for q in range(chips):
-                write(1, block, o_refs[-1], q, q)
+                write(1, block, q, q)
 
         for block in range(runs[0]):
-            pl.when(step == block)(functools.partial(write_first, block))
+            pl.when(step == block // together)(functools.partial(write_first, block))
         for block in range(runs[1]):
-            pl.when(step == runs[0] + block)(functools.partial(write_second, block))
-
+            pl.when(step == (runs[0] + block) // together)(
+                functools.partial(write_second, block)
+            )
+
+    steps = sum(runs) // together
+    home = lambda i, p: p[0] * steps + i
     fixed = lambda i, p: (0, 0)
-    whole_of = lambda shape: pl.BlockSpec(shape, lambda i, p: (0, 0, 0))
-    run_shapes = [(chips, count, width) for width in widths]
-    out_shapes = list(run_shapes)
-    if staged:
-        out_shapes[:1] = [(chips // 2, count, widths[0])] * 2
+    out_shapes = [(chips, count, width) for width in widths]
+    if tops is None:
+        weight_spec = pl.BlockSpec((rows, tile), lambda i, p: (0, i))
+    else:
+        weight_spec = pl.BlockSpec((rows, tile), lambda i, p: (0, 2 * p[1] * steps + home(i, p)))
+    in_specs = [pl.BlockSpec(x.shape, fixed) for x in hidden]
+    in_specs += [pl.BlockSpec((1, rows), fixed), weight_spec, weight_spec]
+    if tops is not None:
+        in_specs.append(top_spec_of(tops, paired, tile, home))
     return pl.pallas_call(
         kernel,
         grid_spec=pltpu.PrefetchScalarGridSpec(
             num_scalar_prefetch=1,
-            grid=(sum(runs),),
-            in_specs=[pl.BlockSpec(x.shape, fixed) for x in hidden]
-            + [
-                pl.BlockSpec((1, rows), fixed),
-                pl.BlockSpec((rows, tile), lambda i, p: (0, i)),
-                pl.BlockSpec((rows, tile), lambda i, p: (0, i)),
-                pl.BlockSpec((2, 8, tile), lambda i, p: (0, 0, i)),
-            ]
-            + ([whole_of(shape) for shape in run_shapes] if staged else []),
-            out_specs=[whole_of(shape) for shape in out_shapes],
+            grid=(steps,),
+            in_specs=in_specs,
+            out_specs=[pl.BlockSpec(shape, lambda i, p: (0, 0, 0)) for shape in out_shapes],
             scratch_shapes=[pltpu.VMEM((count, rows), bf16), pltpu.VMEM((count, extra), f32)],
         ),
         out_shape=[jax.ShapeDtypeStruct(shape, bf16) for shape in out_shapes],
         compiler_params=params(),
-        cost_estimate=cost(4 * count * rows * gate.shape[1], 2 * rows * gate.shape[1]),
+        cost_estimate=cost(4 * count * rows * cols // 2, 2 * rows * cols),
         name="gate_up_product",
-    )(place, *hidden, gain, gate, up, scale, *(added if staged else []))
-
-
-def down_product(place, act, levels, scale, added, flip, states, mine):
+    )(place, *hidden, gain, *in_hbm(gate, up), *([] if tops is None else [tops]))
+
+
+def down_product(place, act, weight, added, states, mine):
     chips, count, units = act.shape
-    hidden, width = levels.shape
-    tile = chips * BLOCK
-    blocks = units // BLOCK
+    width = weight.shape[0]
+    together = 2 if units % (2 * BLOCK) == 0 else 1
+    tile = together * chips * BLOCK
+    steps = units // (together * BLOCK)
     last = added is not None
 
-    def kernel(place_ref, a_ref, l_ref, s_ref, *refs):
+    def kernel(place_ref, a_ref, w_ref, *refs):
         step = pl.program_id(0)
         o_ref, total_ref = refs[-2:]
-        total = jnp.zeros((count, width), f32)
-        for q in range(chips):
-            part = jnp.dot(
-                a_ref[q],
-                l_ref[pl.ds(q * BLOCK, BLOCK), :].astype(bf16),
-                preferred_element_type=f32,
-            )
-            total = total + part * s_ref[pl.ds(q, 1), :]
+        total = lax.dot_general(
+            jnp.concatenate(
+                [
+                    a_ref[q, :, pl.ds(t * BLOCK, BLOCK)]
+                    for t in range(together)
+                    for q in range(chips)
+                ],
+                axis=1,
+            ),
+            w_ref[...],
+            (((1,), (1,)), ((), ())),
+            preferred_element_type=f32,
+        )
 
         @pl.when(step == 0)
         def _():
@@ -498,7 +422,7 @@
         def _():
             total_ref[...] += total
 
-        @pl.when(step == blocks - 1)
+        @pl.when(step == steps - 1)
         def _():
             if not last:
                 o_ref[...] = total_ref[...]
@@ -515,9 +439,6 @@
                 at = slice(b * mine, (b + 1) * mine)
                 o_ref[b] = jnp.concatenate([sums[at], values[at]], axis=0).astype(bf16)
 
-    def at(i, p):
-        return 2 * i + (p[0] ^ flip)
-
     fixed = lambda shape: pl.BlockSpec(shape, lambda i, p: (0,) * len(shape))
     more = [added, *states] if last else []
     shape = (count // mine, 2 * mine, width) if last else (count, width)
@@ -525,21 +446,20 @@
         kernel,
         grid_spec=pltpu.PrefetchScalarGridSpec(
             num_scalar_prefetch=1,
-            grid=(blocks,),
+            grid=(steps,),
             in_specs=[
-                pl.BlockSpec((chips, count, BLOCK), lambda i, p: (0, 0, i)),
-                pl.BlockSpec((tile, width), lambda i, p: (at(i, p), 0)),
-                pl.BlockSpec((chips, width), lambda i, p: (at(i, p), 0)),
+                pl.BlockSpec((chips, count, together * BLOCK), lambda i, p: (0, 0, i)),
+                pl.BlockSpec((width, tile), lambda i, p: (0, i)),
             ]
             + [fixed(x.shape) for x in more],
             out_specs=fixed(shape),
             scratch_shapes=[pltpu.VMEM((count, width), f32)],
         ),
         out_shape=jax.ShapeDtypeStruct(shape, bf16 if last else f32),
-        compiler_params=params(),
-        cost_estimate=cost(2 * count * width * tile * blocks, width * tile * blocks),
+        compiler_params=params(16 * 2**20),
+        cost_estimate=cost(2 * count * width * tile * steps, 2 * width * tile * steps),
         name="down_product",
-    )(place, act, levels, scale, *more)
+    )(place, act, weight, *more)
 
 
 def attention(queries, kv_cache, new_kv, live):
@@ -592,20 +512,23 @@
     )
 
 
-def exchange_halves(keep, send, beside):
+def exchange_halves(kept, got, send, beside):
     count = lax.axis_size("wide")
     bit = 2
     while True:
-        got = lax.ppermute(send, "wide", [(i, i ^ bit) for i in range(count)])
+        half = kept.shape[0] // 2
+        received = lax.ppermute(send, "wide", [(i, i ^ bit) for i in range(count)])
         if bit == 2:
-            got, beside = lax.optimization_barrier((got, beside))
-        total = keep.astype(f32) + got.astype(f32)
+            received, beside = lax.optimization_barrier((received, beside))
+        total = kept[:half].astype(f32) + received.astype(f32)
+        if got is not None:
+            total = total + got[:half].astype(f32)
+        got = None
         bit *= 2
         if bit == count:
             return total[0], beside
-        total = total.astype(bf16)
-        half = total.shape[0] // 2
-        keep, send = total[:half], total[half:]
+        kept = total.astype(bf16)
+        send = kept[half // 2 :]
 
 
 def on_device(
@@ -653,21 +576,19 @@
     chunk = math.gcd(rows, BLOCK)
     tile = pick_tile(units, 2048)
     paired = pair_shares_blocks(rows) and down.shape[0] == rows
+    weights = [gate_weight, up_weight]
     if paired:
-        edge = edge_max(place, [gate_weight, up_weight, down], units, chunk, pick_tile(units, 4096))
-        edge, tops = swap_cores(edge), None
+        tops = edge_max(place, [*weights, down], units, chunk, pick_tile(units, 4096))
+        tops = swap_cores(tops)
     else:
-        edge, tops = None, joined_max(place, [gate_weight, up_weight], units, chunk, tile)
-
-    def levels(flip, place):
-        weights = [gate_weight, up_weight]
-        return levels_of(place, weights, edge, tops, flip, units, chunk, chips * BLOCK)
-
-    away_levels = levels(1, place)
+        tops = joined_max(place, weights, units, chunk, tile)
+    away = rounded_weights(
+        place, weights, tops, paired, 0, 1, units, chunk, pick_tile(units // 2, 2048)
+    )
     gain = lax.dynamic_slice_in_dim(norm_gain, me * width_dev, width_dev, 0).astype(f32)[None]
     residual = jnp.transpose(residual_in, (1, 0, 2)).reshape(tokens, width_dev).astype(f32)
-    projected, away_levels, gain, residual = lax.optimization_barrier(
-        (projected, away_levels, gain, residual)
+    projected, away, gain, residual = lax.optimization_barrier(
+        (projected, away, gain, residual)
     )
     hidden = (residual + jnp.sum(projected.astype(f32), axis=0)).astype(bf16)
 
@@ -677,24 +598,29 @@
     elif parts > 1:
         states = [lax.all_gather(hidden, "grp", axis=0, tiled=True)]
 
-    def product(levels, added):
-        return gate_up_product(place, states, gain, *levels, added, runs, chips, paired)
-
-    sent = product(away_levels, None)
-    *sent, place = lax.optimization_barrier((*sent, place))
-    sent = [swap_cores(value) for value in sent]
-    sent[0], home_levels = lax.optimization_barrier((sent[0], levels(0, place)))
-    keep, send, kept = product(home_levels, sent)
-    kept, place = lax.optimization_barrier((kept, place))
+    def product(weights, tops):
+        return gate_up_product(place, states, gain, *weights, tops, runs, chips, paired, units)
+
+    got = [swap_cores(value) for value in product(away, None)]
+    kept = list(product(weights, tops))
+    half = chips // 2
+    send = (kept[0][half:].astype(f32) + got[0][half:].astype(f32)).astype(bf16)
+    send, kept[1], got[1] = lax.optimization_barrier((send, kept[1], got[1]))
+    second = (kept[1].astype(f32) + got[1].astype(f32)).astype(bf16)
+    second, place = lax.optimization_barrier((second, place))
 
     down_chunk = math.gcd(down.shape[0], BLOCK)
-    down_tile = pick_tile(units, 4096)
-    tops = None if paired else joined_max(place, [down], units, down_chunk, down_tile)
-    down_levels, down_scale = down_levels_of(
-        place, down, edge if paired else None, 2, tops, units, down_chunk, down_tile
-    )
-    last = exchange_chips(kept)
-    first, (down_levels, down_scale) = exchange_halves(keep, send, (down_levels, down_scale))
+    row = 2
+    if not paired:
+        tops, row = joined_max(place, [down], units, down_chunk, pick_tile(units, 4096)), 0
+    home, away = [
+        rounded_weights(
+            place, [down], tops, paired, row, flip, units, down_chunk, pick_tile(units // 2, 4096)
+        )[0]
+        for flip in range(2)
+    ]
+    last = exchange_chips(second)
+    first, (home, away) = exchange_halves(kept[0], got[0], send, (home, away))
 
     last = jnp.sum(last.astype(f32), axis=0)
     squares = jnp.sum(last[:, 2 * runs[1] * BLOCK :], axis=1, keepdims=True)
@@ -709,8 +635,8 @@
     act = jnp.concatenate([act_of(first, runs[0]), act_of(last, runs[1])], axis=1)
     act = exchange_chips(jnp.broadcast_to(act[None], (chips,) + act.shape))
     other = swap_cores(act)
-    ffn = down_product(place, act, down_levels, down_scale, None, 0, states, mine)
-    both = down_product(place, other, down_levels, down_scale, ffn, 1, states, mine)
+    ffn = down_product(place, act, home, None, states, mine)
+    both = down_product(place, other, away, ffn, states, mine)
 
     axes = ("grp", "wide") if parts > 1 else "wide"
     both = lax.all_to_all(both, axes, split_axis=0, concat_axis=0, tiled=True)

time: 155 us -> 145 us (0.935)
  waiting for transfers between devices: 31.6 us -> 27.1 us
  Pallas kernels: 55.9 us -> 51.6 us
  local copies, waits for them, and re-layouts: 11.3 us -> 7.58 us
  other arithmetic: 3.15 us -> 5.46 us
  starting transfers between devices: 28.4 us -> 26.3 us
    pallas_call x2, Pallas kernels: 9.41 us -> 4.74 us  [down_product(): pl.pallas_call(kernel, grid_spec=pltpu.PrefetchScalarGridSpec(num_scalar_...]
    unnamed x23 -> x29, local copies, waits for them, and re-layouts: 5.59 us -> 2.02 us
    ppermute x3, waiting for transfers between devices: 17 us -> 14 us  [exchange_halves(): received = lax.ppermute(send, 'wide', [(i, i ^ bit) for i in range(count)])]
    convert_element_type x2 -> x4, other arithmetic: 0.21 us -> 2.52 us  [the longest x1 1.26 us: on_device(): send = (kept[0][half:].astype(f32) + got[0][half:].astype(f32)).astype(bf16)]
    ppermute x3, starting transfers between devices: 5.89 us -> 3.81 us  [exchange_halves(): received = lax.ppermute(send, 'wide', [(i, i ^ bit) for i in range(count)])]
    all_to_all x2, waiting for transfers between devices: 3.92 us -> 2.16 us  [exchange(): lax.all_to_all(value, 'wide', split_axis=0, concat_axis=0, tiled=True)]
    all_to_all x1, blocking collectives: 20.1 us -> 21.6 us  [exchange_chips(): lax.all_to_all(value, 'wide', split_axis=0, concat_axis=0, tiled=True, ax...]
  transfers between devices with their start and end apart: 12 -> 12, of which waited for: 7 -> 8; matrix products, arithmetic and copies ran while one was open for 2% -> 4% of each run, Pallas kernels for 23% -> 28%
where the time goes in v5:
time: 145 us; the launch traced here: 143 us
  Pallas kernels  51.6 us (36%)
  waiting for transfers between devices  27.1 us (19%)
  starting transfers between devices  26.3 us (18%)
  blocking collectives  21.6 us (15%)
  local copies, waits for them, and re-layouts  7.58 us (5%)
  other arithmetic  5.46 us (4%)
  matrix products  2.74 us (2%)
    all_to_all x1, blocking collectives, exchange_chips(): lax.all_to_all(value, 'wide', split_axis=0, concat_axis=0, tiled=True, ax...  21.6 us
    pallas_call x3, Pallas kernels, rounded_weights(): pl.pallas_call(kernel, grid_spec=pltpu.PrefetchScalarGridSpec(num_scalar_...  20.6 us
    ppermute x3, waiting for transfers between devices, exchange_halves(): received = lax.ppermute(send, 'wide', [(i, i ^ bit) for i in range(count)])  14 us
    pallas_call x2, Pallas kernels, gate_up_product(): pl.pallas_call(kernel, grid_spec=pltpu.PrefetchScalarGridSpec(num_scalar_...  13.9 us
    all_to_all x2, starting transfers between devices, exchange(): lax.all_to_all(value, 'wide', split_axis=0, concat_axis=0, tiled=True)  11.9 us
    all_to_all x1, waiting for transfers between devices, on_device(): both = lax.all_to_all(both, axes, split_axis=0, concat_axis=0, tiled=True)  8.25 us
    pallas_call x1, Pallas kernels, out_levels_of(): pl.pallas_call(kernel, grid=(cols // tile,), in_specs=[pl.BlockSpec((rows...  5.44 us
    pallas_call x2, Pallas kernels, down_product(): pl.pallas_call(kernel, grid_spec=pltpu.PrefetchScalarGridSpec(num_scalar_...  4.74 us
  transfers between devices with their start and end apart: 12, of which 8 were waited for; matrix products, arithmetic and copies ran while one was open for 4% of the time, Pallas kernels for 28%

profile of v5, /device:TPU:0, one launch (start us, length us, event | category | flops | bytes accessed | tf_op | source)
XLA Modules:
  0.0 143.5 jit_solution(5076983634049957100)
XLA Ops:
  0.7 1.2 dynamic_slice.6
  3.6 1.8 %select_reduce_fusion = (f32[3,8,8]{2,0,1:T(4,128)S(1)}, f32[3,1,8,8,512]{4,3,0,2,1:T(8,128)S(1)}) fusion(pred[512]{0:T(512)(128)(4,1)S(1)} %iota_compare_fusion.1, bf16[2,1,8,512,128]{4,3,2,1,0:T(8,128)(2,1)} %param.17, bf16[3,1,8,8,128]{4,3,2,1,0:T(8,128)(2,1)S(1)} %copy-done), kind=kOutput, calls=%fused_computation.20 | convolution fusion | flops 25460544 | bytes 1492224 | tf_op jit(solution)/shard_map/nshqd,shcd->nshqc/dot_general | solution.py:475
  7.2 7.4 %all-to-all-start = ((bf16[16,1,3,512]{3,2,1,0:T(4,128)(2,1)}), bf16[16,1,3,512]{3,2,1,0:T(4,128)(2,1)S(1)}, u32[]{:S(2)}, u32[]{:S(2)}) async-start(bf16[16,1,3,512]{3,2,1,0:T(4,128)(2,1)} %copy.34), calls=%async_computation | async-start | bytes 131072 | tf_op jit(solution)/shard_map/all_to_all | solution.py:504
  14.5 5.4 %out_levels_of.1 = (f8e4m3fn[512,5120]{1,0:T(32,128)(4,1)}, f32[8,5120]{1,0:T(8,128)}) custom-call(bf16[512,5120]{1,0:T(8,128)(2,1)} %w_ref.1), custom_call_target="tpu_custom_call" | custom-call | flops 20971520 | bytes 7864320 | tf_op jit(solution)/shard_map/out_levels_of/pallas_call | solution.py:237
  20.0 1.5 %all-to-all-done = bf16[16,1,3,512]{3,2,1,0:T(4,128)(2,1)S(1)} async-done(((bf16[16,1,3,512]{3,2,1,0:T(4,128)(2,1)}), bf16[16,1,3,512]{3,2,1,0:T(4,128)(2,1)S(1)}, u32[]{:S(2)}, u32[]{:S(2)}) %all-to-all-start) | async-done | bytes 49184 | tf_op jit(solution)/shard_map/all_to_all | solution.py:504
  22.1 3.2 %out_product.1 = bf16[16,48,320]{2,1,0:T(8,128)(2,1)} custom-call(bf16[48,512]{1,0:T(8,128)(2,1)} %reshape.133.x_ref, f8e4m3fn[512,5120]{1,0:T(32,128)(4,1)} %get-tuple-element.30.l_ref, f32[8,5120]{1,0:T(8,128)} %get-tuple-element.31.s_ref), custom_call_target="tpu_custom_call" | custom-call | flops 251658240 | bytes 2621440 | tf_op jit(solution)/shard_map/out_product/pallas_call | solution.py:271
  25.3 4.5 %all-to-all-start.1 = ((bf16[16,48,320]{2,1,0:T(8,128)(2,1)}), bf16[16,48,320]{2,1,0:T(8,128)(2,1)S(1)}, u32[]{:S(2)}, u32[]{:S(2)}) async-start(bf16[16,48,320]{2,1,0:T(8,128)(2,1)} %out_product.1), calls=%async_computation.1 | async-start | bytes 1179648 | tf_op jit(solution)/shard_map/all_to_all | solution.py:504
  30.5 3.7 %edge_max.1 = f32[8,8192]{1,0:T(8,128)} custom-call(s32[4]{0:T(128)} %pad_add_fusion.place_ref, bf16[320,16384]{1,0:T(8,128)(2,1)} %refs_3_.1, bf16[320,16384]{1,0:T(8,128)(2,1)} %refs_4_.1, bf16[320,16384]{1,0:T(8,128)(2,1)} %bitcast.90), custom_call_target="tpu_custom_call" | custom-call | flops 3145728 | bytes 3145728 | tf_op jit(solution)/shard_map/edge_max/pallas_call | solution.py:95
  34.6 0.8 dynamic-slice_convert_fusion
  36.7 8.0 %rounded_weights.3 = (bf16[320,4096]{1,0:T(8,128)(2,1)}, bf16[320,4096]{1,0:T(8,128)(2,1)}) custom-call(s32[4]{0:T(128)} %pad_add_fusion.place_ref, bf16[320,16384]{1,0:T(8,128)(2,1)} %refs_3_.1, bf16[320,16384]{1,0:T(8,128)(2,1)} %refs_4_.1, f32[8,8192]{1,0:T(8,128)} %copy-done.9), custom_call_target="tpu_custom_call" | custom-call | flops 15728640 | bytes 10485760 | tf_op jit(solution)/shard_map/rounded_weights/pallas_call | solution.py:167
  45.5 1.6 %collective-permute-start.1 = (bf16[48,320]{1,0:T(8,128)(2,1)S(1)}, bf16[48,320]{1,0:T(8,128)(2,1)S(1)}, u32[]{:S(2)}, u32[]{:S(2)}) collective-permute-start(bf16[48,320]{1,0:T(8,128)(2,1)S(1)} %add_convert_fusion.4.refs_0_.refs_1_), channel_id=1, source_target_pairs={{0,16},{16,0},{1,17},{17,1},{2,18},{18,2},{3,19},{19,3},{4,20},{20... | collective-permute-start | bytes 92168 | tf_op jit(solution)/shard_map/ppermute | solution.py:597
  47.1 2.5 %collective-permute-done.1.refs_1_.refs_2_ = bf16[48,320]{1,0:T(8,128)(2,1)S(1)} collective-permute-done((bf16[48,320]{1,0:T(8,128)(2,1)S(1)}, bf16[48,320]{1,0:T(8,128)(2,1)S(1)}, u32[]{:S(2)}, u32[]{:S(2)}) %collective-permute-start.1) | collective-permute-done | bytes 30752 | tf_op jit(solution)/shard_map/ppermute | solution.py:597
  50.2 5.6 %gate_up_product.3 = (bf16[8,96,768]{2,1,0:T(8,128)(2,1)}, bf16[8,96,384]{2,1,0:T(8,128)(2,1)}) custom-call(s32[4]{0:T(128)} %pad_add_fusion.place_ref, bf16[48,320]{1,0:T(8,128)(2,1)} %copy-done.4, bf16[48,320]{1,0:T(8,128)(2,1)} %copy-done.6, f32[1,320]{1,0:T(1,128)} %reshape.137.refs_2_, bf16[320,4096]{1,0:T(8,128)(2,1)} %get-tuple-element.38.refs_3_, ...), custom_call_target="tpu_custom_call" | custom-call | flops 503316480 | bytes 5242880 | tf_op jit(solution)/shard_map/gate_up_product/pallas_call | solution.py:376
  56.3 8.3 %gate_up_product.2 = (bf16[8,96,768]{2,1,0:T(8,128)(2,1)}, bf16[8,96,384]{2,1,0:T(8,128)(2,1)}) custom-call(s32[4]{0:T(128)} %pad_add_fusion.place_ref, bf16[48,320]{1,0:T(8,128)(2,1)} %copy-done.4, bf16[48,320]{1,0:T(8,128)(2,1)} %copy-done.6, f32[1,320]{1,0:T(1,128)} %reshape.137.refs_2_, bf16[320,16384]{1,0:T(8,128)(2,1)} %refs_3_.1, ...), custom_call_target="tpu_custom_call" | custom-call | flops 503316480 | bytes 5242880 | tf_op jit(solution)/shard_map/gate_up_product/pallas_call | solution.py:376
  64.6 1.3 add_convert_fusion.2
  65.9 1.2 collective-permute-start.4
  67.1 1.0 add_convert_fusion.1
  68.1 4.5 %all-to-all-start.2 = ((bf16[8,96,384]{2,1,0:T(8,128)(2,1)}), bf16[8,96,384]{2,1,0:T(8,128)(2,1)S(1)}, u32[]{:S(2)}, u32[]{:S(2)}) async-start(bf16[8,96,384]{2,1,0:T(8,128)(2,1)} %add_convert_fusion.1), calls=%async_computation.2 | async-start | bytes 1179648 | tf_op jit(solution)/shard_map/all_to_all | solution.py:510
  72.6 6.2 %rounded_weights.5.w_ref = bf16[320,4096]{1,0:T(8,128)(2,1)} custom-call(s32[4]{0:T(128)} %pad_add_fusion.place_ref, bf16[320,16384]{1,0:T(8,128)(2,1)} %bitcast.91, f32[8,8192]{1,0:T(8,128)} %copy-done.9), custom_call_target="tpu_custom_call" | custom-call | flops 7864320 | bytes 5242880 | tf_op jit(solution)/shard_map/rounded_weights/pallas_call | solution.py:167
  78.8 6.4 %rounded_weights.4.w_ref = bf16[320,4096]{1,0:T(8,128)(2,1)} custom-call(s32[4]{0:T(128)} %pad_add_fusion.place_ref, bf16[320,16384]{1,0:T(8,128)(2,1)} %bitcast.92, f32[8,8192]{1,0:T(8,128)} %copy-done.9), custom_call_target="tpu_custom_call" | custom-call | flops 7864320 | bytes 5242880 | tf_op jit(solution)/shard_map/rounded_weights/pallas_call | solution.py:167
  85.2 1.5 %collective-permute-done.4 = bf16[4,96,768]{2,1,0:T(8,128)(2,1)S(1)} collective-permute-done((bf16[4,96,768]{2,1,0:T(8,128)(2,1)S(1)}, bf16[4,96,768]{2,1,0:T(8,128)(2,1)S(1)}, u32[]{:S(2)}, u32[]{:S(2)}) %collective-permute-start.4) | collective-permute-done | bytes 589856 | tf_op jit(solution)/shard_map/ppermute | solution.py:520
  87.0 0.7 collective-permute-start.5
  87.7 7.0 %collective-permute-done.5 = bf16[2,96,768]{2,1,0:T(8,128)(2,1)S(1)} collective-permute-done((bf16[2,96,768]{2,1,0:T(8,128)(2,1)S(1)}, bf16[2,96,768]{2,1,0:T(8,128)(2,1)S(1)}, u32[]{:S(2)}, u32[]{:S(2)}) %collective-permute-start.5) | collective-permute-done | bytes 294944 | tf_op jit(solution)/shard_map/ppermute | solution.py:520
  94.8 1.9 %collective-permute-start.6 = (bf16[1,96,768]{2,1,0:T(8,128)(2,1)S(1)}, bf16[1,96,768]{2,1,0:T(8,128)(2,1)S(1)}, u32[]{:S(2)}, u32[]{:S(2)}) collective-permute-start(bf16[1,96,768]{2,1,0:T(8,128)(2,1)S(1)} %slice.81), channel_id=1, source_target_pairs={{0,8},{1,9},{2,10},{3,11},{4,12},{5,13},{6,14},{7,15},{8,0},{9,1},... | collective-permute-start | bytes 442376 | tf_op jit(solution)/shard_map/ppermute | solution.py:520
  97.0 5.5 %collective-permute-done.6 = bf16[1,96,768]{2,1,0:T(8,128)(2,1)S(1)} collective-permute-done((bf16[1,96,768]{2,1,0:T(8,128)(2,1)S(1)}, bf16[1,96,768]{2,1,0:T(8,128)(2,1)S(1)}, u32[]{:S(2)}, u32[]{:S(2)}) %collective-permute-start.6) | collective-permute-done | bytes 147488 | tf_op jit(solution)/shard_map/ppermute | solution.py:520
  102.8 21.6 %all_to_all.25.a_ref = bf16[8,96,512]{2,1,0:T(8,128)(2,1)S(1)} all-to-all(bf16[8,96,512]{2,1,0:T(8,128)(2,1)S(1)} %broadcast_in_dim.67), channel_id=1, replica_groups={{0,2,4,6,8,10,12,14},{1,3,5,7,9,11,13,15},{16,18,20,22,24,26,28,30},{17..., dimensions={0} | all-to-all | bytes 1572864 | tf_op jit(solution)/shard_map/all_to_all | solution.py:510
  124.4 2.0 %down_product.2.refs_0_ = f32[96,320]{1,0:T(8,128)S(1)} custom-call(s32[4]{0:T(128)S(1)} %copy-done.8, bf16[8,96,512]{2,1,0:T(8,128)(2,1)S(1)} %all_to_all.25.a_ref, bf16[320,4096]{1,0:T(8,128)(2,1)S(1)} %copy-done.3), custom_call_target="tpu_custom_call" | custom-call | flops 251658240 | bytes 2621440 | tf_op jit(solution)/shard_map/down_product/pallas_call | solution.py:445
  126.7 2.7 %down_product.3 = bf16[32,6,320]{2,1,0:T(8,128)(2,1)} custom-call(s32[4]{0:T(128)S(1)} %copy-done.8, bf16[8,96,512]{2,1,0:T(8,128)(2,1)S(1)} %collective-permute-done.7.a_ref, bf16[320,4096]{1,0:T(8,128)(2,1)S(1)} %copy-done.2, f32[96,320]{1,0:T(8,128)S(1)} %down_product.2.refs_0_, bf16[48,320]{1,0:T(8,128)(2,1)S(1)} %copy-done.5, bf16[48,320]{1,0:T(8,128)(2,1)S(1)} %copy-done.7), custom_call_target="tpu_custom_call" | custom-call | flops 251658240 | bytes 2621440 | tf_op jit(solution)/shard_map/down_product/pallas_call | solution.py:445
  129.4 3.6 %all-to-all-start.4 = ((bf16[32,6,320]{2,1,0:T(8,128)(2,1)}), bf16[32,6,320]{2,1,0:T(8,128)(2,1)S(1)}, u32[]{:S(2)}, u32[]{:S(2)}) async-start(bf16[32,6,320]{2,1,0:T(8,128)(2,1)} %down_product.3), calls=%async_computation.4 | async-start | bytes 393216 | tf_op jit(solution)/shard_map/all_to_all | solution.py:642
  133.7 8.3 %all-to-all-done.4 = bf16[32,6,320]{2,1,0:T(8,128)(2,1)S(1)} async-done(((bf16[32,6,320]{2,1,0:T(8,128)(2,1)}), bf16[32,6,320]{2,1,0:T(8,128)(2,1)S(1)}, u32[]{:S(2)}, u32[]{:S(2)}) %all-to-all-start.4) | async-done | bytes 122912 | tf_op jit(solution)/shard_map/all_to_all | solution.py:642
  142.0 0.7 reshape.135
  142.7 0.7 reshape.136
  (75 shorter events, 10.1 us)
Async XLA Ops:
  0.6 2.7 %copy-start = (bf16[3,1,8,8,128]{4,3,2,1,0:T(8,128)(2,1)S(1)}, bf16[3,1,8,8,128]{4,3,2,1,0:T(8,128)(2,1)}, u32[]{:S(2)}) copy-start(bf16[3,1,8,8,128]{4,3,2,1,0:T(8,128)(2,1)} %param.16) | copy-start | bytes 147460
  3.6 2.2 %copy-start.13 = (bf16[2,1,8,512,128]{4,3,2,1,0:T(8,128)(2,1)S(1)}, bf16[2,1,8,512,128]{4,3,2,1,0:T(8,128)(2,1)}, u32[]{:S(2)}) copy-start(bf16[2,1,8,512,128]{4,3,2,1,0:T(8,128)(2,1)} %param.17) | copy-start | bytes 6291460
  7.2 14.3 %all-to-all-start = ((bf16[16,1,3,512]{3,2,1,0:T(4,128)(2,1)}), bf16[16,1,3,512]{3,2,1,0:T(4,128)(2,1)S(1)}, u32[]{:S(2)}, u32[]{:S(2)}) async-start(bf16[16,1,3,512]{3,2,1,0:T(4,128)(2,1)} %copy.34), calls=%async_computation | async-start | bytes 131072 | tf_op jit(solution)/shard_map/all_to_all | solution.py:504
  25.3 20.1 %all-to-all-start.1 = ((bf16[16,48,320]{2,1,0:T(8,128)(2,1)}), bf16[16,48,320]{2,1,0:T(8,128)(2,1)S(1)}, u32[]{:S(2)}, u32[]{:S(2)}) async-start(bf16[16,48,320]{2,1,0:T(8,128)(2,1)} %out_product.1), calls=%async_computation.1 | async-start | bytes 1179648 | tf_op jit(solution)/shard_map/all_to_all | solution.py:504
  30.5 5.4 %copy-start.12 = (bf16[3,16,320]{2,1,0:T(8,128)(2,1)S(1)}, bf16[3,16,320]{2,1,0:T(8,128)(2,1)}, u32[]{:S(2)}) copy-start(bf16[3,16,320]{2,1,0:T(8,128)(2,1)} %param.10) | copy-start | bytes 92164
  34.2 1.8 %collective-permute-start = (f32[8,8192]{1,0:T(8,128)}, f32[8,8192]{1,0:T(8,128)S(1)}, u32[]{:S(2)}, u32[]{:S(2)}) collective-permute-start(f32[8,8192]{1,0:T(8,128)} %edge_max.1), channel_id=1, source_target_pairs={{0,1},{1,0},{2,3},{3,2},{4,5},{5,4},{6,7},{7,6},{8,9},{9,8},{10,11... | collective-permute-start | bytes 786440 | tf_op jit(solution)/shard_map/ppermute | solution.py:500
  36.0 0.7 copy-start.9
  45.5 4.0 %copy-start.4 = (bf16[48,320]{1,0:T(8,128)(2,1)}, bf16[48,320]{1,0:T(8,128)(2,1)S(1)}, u32[]{:S(2)}) copy-start(bf16[48,320]{1,0:T(8,128)(2,1)S(1)} %add_convert_fusion.4.refs_0_.refs_1_) | copy-start | bytes 92164
  45.5 4.0 %collective-permute-start.1 = (bf16[48,320]{1,0:T(8,128)(2,1)S(1)}, bf16[48,320]{1,0:T(8,128)(2,1)S(1)}, u32[]{:S(2)}, u32[]{:S(2)}) collective-permute-start(bf16[48,320]{1,0:T(8,128)(2,1)S(1)} %add_convert_fusion.4.refs_0_.refs_1_), channel_id=1, source_target_pairs={{0,16},{16,0},{1,17},{17,1},{2,18},{18,2},{3,19},{19,3},{4,20},{20... | collective-permute-start | bytes 92168 | tf_op jit(solution)/shard_map/ppermute | solution.py:597
  49.6 0.6 copy-start.6
  55.8 8.8 %collective-permute-start.2 = (bf16[8,96,768]{2,1,0:T(8,128)(2,1)}, bf16[8,96,768]{2,1,0:T(8,128)(2,1)S(1)}, u32[]{:S(2)}, u32[]{:S(2)}) collective-permute-start(bf16[8,96,768]{2,1,0:T(8,128)(2,1)} %get-tuple-element.40), channel_id=1, source_target_pairs={{0,1},{1,0},{2,3},{3,2},{4,5},{5,4},{6,7},{7,6},{8,9},{9,8},{10,11... | collective-permute-start | bytes 3538952 | tf_op jit(solution)/shard_map/ppermute | solution.py:500
  55.8 10.1 %collective-permute-start.3 = (bf16[8,96,384]{2,1,0:T(8,128)(2,1)}, bf16[8,96,384]{2,1,0:T(8,128)(2,1)S(1)}, u32[]{:S(2)}, u32[]{:S(2)}) collective-permute-start(bf16[8,96,384]{2,1,0:T(8,128)(2,1)} %get-tuple-element.42), channel_id=1, source_target_pairs={{0,1},{1,0},{2,3},{3,2},{4,5},{5,4},{6,7},{7,6},{8,9},{9,8},{10,11... | collective-permute-start | bytes 1769480 | tf_op jit(solution)/shard_map/ppermute | solution.py:500
  64.6 2.5 %copy-start.11 = (bf16[8,96,384]{2,1,0:T(8,128)(2,1)S(1)}, bf16[8,96,384]{2,1,0:T(8,128)(2,1)}, u32[]{:S(2)}) copy-start(bf16[8,96,384]{2,1,0:T(8,128)(2,1)} %get-tuple-element.43) | copy-start | bytes 1769476
  65.9 20.8 %collective-permute-start.4 = (bf16[4,96,768]{2,1,0:T(8,128)(2,1)S(1)}, bf16[4,96,768]{2,1,0:T(8,128)(2,1)S(1)}, u32[]{:S(2)}, u32[]{:S(2)}) collective-permute-start(bf16[4,96,768]{2,1,0:T(8,128)(2,1)S(1)} %add_convert_fusion.2), channel_id=1, source_target_pairs={{0,2},{1,3},{2,0},{3,1},{4,6},{5,7},{6,4},{7,5},{8,10},{9,11},{10,... | collective-permute-start | bytes 1769480 | tf_op jit(solution)/shard_map/ppermute | solution.py:520
  68.1 28.6 %all-to-all-start.2 = ((bf16[8,96,384]{2,1,0:T(8,128)(2,1)}), bf16[8,96,384]{2,1,0:T(8,128)(2,1)S(1)}, u32[]{:S(2)}, u32[]{:S(2)}) async-start(bf16[8,96,384]{2,1,0:T(8,128)(2,1)} %add_convert_fusion.1), calls=%async_computation.2 | async-start | bytes 1179648 | tf_op jit(solution)/shard_map/all_to_all | solution.py:510
  78.8 7.9 %copy-start.10 = (bf16[8,96,768]{2,1,0:T(8,128)(2,1)S(1)}, bf16[8,96,768]{2,1,0:T(8,128)(2,1)}, u32[]{:S(2)}) copy-start(bf16[8,96,768]{2,1,0:T(8,128)(2,1)} %get-tuple-element.37) | copy-start | bytes 3538948
  87.0 7.7 %collective-permute-start.5 = (bf16[2,96,768]{2,1,0:T(8,128)(2,1)S(1)}, bf16[2,96,768]{2,1,0:T(8,128)(2,1)S(1)}, u32[]{:S(2)}, u32[]{:S(2)}) collective-permute-start(bf16[2,96,768]{2,1,0:T(8,128)(2,1)S(1)} %slice.79), channel_id=1, source_target_pairs={{0,4},{1,5},{2,6},{3,7},{4,0},{5,1},{6,2},{7,3},{8,12},{9,13},{10,... | collective-permute-start | bytes 884744 | tf_op jit(solution)/shard_map/ppermute | solution.py:520
  94.8 7.7 %collective-permute-start.6 = (bf16[1,96,768]{2,1,0:T(8,128)(2,1)S(1)}, bf16[1,96,768]{2,1,0:T(8,128)(2,1)S(1)}, u32[]{:S(2)}, u32[]{:S(2)}) collective-permute-start(bf16[1,96,768]{2,1,0:T(8,128)(2,1)S(1)} %slice.81), channel_id=1, source_target_pairs={{0,8},{1,9},{2,10},{3,11},{4,12},{5,13},{6,14},{7,15},{8,0},{9,1},... | collective-permute-start | bytes 442376 | tf_op jit(solution)/shard_map/ppermute | solution.py:520
  102.7 21.8 %copy-start.3 = (bf16[320,4096]{1,0:T(8,128)(2,1)S(1)}, bf16[320,4096]{1,0:T(8,128)(2,1)}, u32[]{:S(2)}) copy-start(bf16[320,4096]{1,0:T(8,128)(2,1)} %rounded_weights.4.w_ref) | copy-start | bytes 7864324
  102.7 21.7 %copy-start.8 = (s32[4]{0:T(128)S(1)}, s32[4]{0:T(128)}, u32[]{:S(2)}) copy-start(s32[4]{0:T(128)} %pad_add_fusion.place_ref) | copy-start | bytes 52
  124.4 2.3 %copy-start.2 = (bf16[320,4096]{1,0:T(8,128)(2,1)S(1)}, bf16[320,4096]{1,0:T(8,128)(2,1)}, u32[]{:S(2)}) copy-start(bf16[320,4096]{1,0:T(8,128)(2,1)} %rounded_weights.5.w_ref) | copy-start | bytes 7864324
  124.4 2.3 %copy-start.5 = (bf16[48,320]{1,0:T(8,128)(2,1)S(1)}, bf16[48,320]{1,0:T(8,128)(2,1)}, u32[]{:S(2)}) copy-start(bf16[48,320]{1,0:T(8,128)(2,1)} %copy-done.4) | copy-start | bytes 92164
  124.4 2.3 %copy-start.7 = (bf16[48,320]{1,0:T(8,128)(2,1)S(1)}, bf16[48,320]{1,0:T(8,128)(2,1)}, u32[]{:S(2)}) copy-start(bf16[48,320]{1,0:T(8,128)(2,1)} %copy-done.6) | copy-start | bytes 92164
  124.4 2.3 %collective-permute-start.7 = (bf16[8,96,512]{2,1,0:T(8,128)(2,1)S(1)}, bf16[8,96,512]{2,1,0:T(8,128)(2,1)S(1)}, u32[]{:S(2)}, u32[]{:S(2)}) collective-permute-start(bf16[8,96,512]{2,1,0:T(8,128)(2,1)S(1)} %all_to_all.25.a_ref), channel_id=1, source_target_pairs={{0,1},{1,0},{2,3},{3,2},{4,5},{5,4},{6,7},{7,6},{8,9},{9,8},{10,11... | collective-permute-start | bytes 2359304 | tf_op jit(solution)/shard_map/ppermute | solution.py:500
  126.7 16.8 %copy-start.1 = (bf16[3,1,8,8,128]{4,3,2,1,0:T(8,128)(2,1)S(1)}, bf16[3,1,8,8,128]{4,3,2,1,0:T(8,128)(2,1)}, u32[]{:S(2)}) copy-start(bf16[3,1,8,8,128]{4,3,2,1,0:T(8,128)(2,1)} %param.16) | copy-start | bytes 147460
  129.4 12.5 %all-to-all-start.4 = ((bf16[32,6,320]{2,1,0:T(8,128)(2,1)}), bf16[32,6,320]{2,1,0:T(8,128)(2,1)S(1)}, u32[]{:S(2)}, u32[]{:S(2)}) async-start(bf16[32,6,320]{2,1,0:T(8,128)(2,1)} %down_product.3), calls=%async_computation.4 | async-start | bytes 393216 | tf_op jit(solution)/shard_map/all_to_all | solution.py:642

commit v6 on v5

--- a/solution.py
+++ b/solution.py
@@ -27,6 +27,10 @@
 
 def in_hbm(*arrays):
     return [pltpu.with_memory_space_constraint(x, pltpu.HBM) for x in arrays]
+
+
+def in_vmem(*arrays):
+    return [pltpu.with_memory_space_constraint(x, pltpu.VMEM) for x in arrays]
 
 
 def cost(flops, read):
@@ -182,7 +186,7 @@
             6 * count * rows * cols // taken, 4 * count * rows * cols // taken
         ),
         name="rounded_weights",
-    )(place, *in_hbm(*weights), tops)
+    )(place, *in_hbm(*weights), *in_vmem(tops))
 
 
 def join_group(parts, size, dim):
@@ -386,7 +390,7 @@
         compiler_params=params(),
         cost_estimate=cost(4 * count * rows * cols // 2, 2 * rows * cols),
         name="gate_up_product",
-    )(place, *hidden, gain, *in_hbm(gate, up), *([] if tops is None else [tops]))
+    )(place, *in_vmem(*hidden), gain, *in_hbm(gate, up), *([] if tops is None else in_vmem(tops)))
 
 
 def down_product(place, act, weight, added, states, mine):
@@ -462,37 +466,104 @@
     )(place, act, weight, *more)
 
 
-def attention(queries, kv_cache, new_kv, live):
-    steps = queries.shape[0]
-    factor = queries.shape[-1] ** (-0.5)
-    keys = kv_cache[0]
-    values = kv_cache[1]
-    new_keys = new_kv[:, 0]
-    new_values = new_kv[:, 1]
-    position = jnp.arange(keys.shape[2], dtype=jnp.int32)
-    valid = position[None, None, None, None, :] < live[None, :, None, None, None]
-    cached = (
-        jnp.einsum("nshqd,shcd->nshqc", queries, keys, preferred_element_type=f32) * factor
-    )
-    recent = (
-        jnp.einsum("nshqd,tshd->nshqt", queries, new_keys, preferred_element_type=f32) * factor
-    )
-    order = jnp.arange(steps, dtype=jnp.int32)
-    fresh = (order[None, :] <= order[:, None])[:, None, None, None, :]
-    top = jnp.maximum(
-        jnp.max(jnp.where(valid, cached, NEG), axis=-1),
-        jnp.max(jnp.where(fresh, recent, NEG), axis=-1),
-    )[..., None]
-    e_cached = jnp.where(valid, jnp.exp(cached - top), 0.0)
-    e_recent = jnp.where(fresh, jnp.exp(recent - top), 0.0)
-    total = jnp.sum(e_cached, axis=-1, keepdims=True) + jnp.sum(e_recent, axis=-1, keepdims=True)
-    p_cached = (e_cached / total).astype(bf16)
-    p_recent = (e_recent / total).astype(bf16)
-    mixed = jnp.einsum("nshqc,shcd->nshqd", p_cached, values, preferred_element_type=f32)
-    mixed = mixed + jnp.einsum(
-        "nshqt,tshd->nshqd", p_recent, new_values, preferred_element_type=f32
-    )
-    return mixed.astype(bf16)
+def attention(cache_len, queries, kv_cache, new_kv, owners):
+    steps, seqs, heads, per, size = queries.shape
+    slots = kv_cache.shape[3]
+    factor = size ** (-0.5)
+    share = heads * per // owners
+    splits = 2 if heads % 2 == 0 and owners % 2 == 0 else 1
+    mine = heads // splits
+    rows = steps * per
+    pad = 8 - steps
+
+    def kernel(len_ref, q_ref, kv_ref, new_ref, o_ref, h_ref):
+        live = len_ref[lax.axis_index("wide") * seqs + pl.program_id(0)]
+        valid = lax.broadcasted_iota(jnp.int32, (rows, slots), 1) < live
+        step_of = lax.broadcasted_iota(jnp.int32, (rows, 8), 0) // per
+        fresh = lax.broadcasted_iota(jnp.int32, (rows, 8), 1) <= step_of
+
+        def product(left, right, dim):
+            return lax.dot_general(
+                left, right, (((1,), (dim,)), ((), ())), preferred_element_type=f32
+            )
+
+        new = []
+        for n in range(2):
+            value = new_ref[:, n, 0].astype(f32)
+            if splits == 2:
+                value = jnp.where(pl.program_id(1) == 0, value[:, :mine], value[:, mine:])
+            new.append(value)
+        at = range(mine)
+        queries_of = [
+            q_ref[:, 0, h].astype(f32).reshape(rows, size).astype(bf16) for h in at
+        ]
+        new_keys, new_values = [
+            [
+                jnp.concatenate([value[:, h], jnp.zeros((pad, size), f32)], axis=0).astype(bf16)
+                for h in at
+            ]
+            for value in new
+        ]
+        cached = [product(queries_of[h], kv_ref[0, 0, h], 1) for h in at]
+        recent = [product(queries_of[h], new_keys[h], 1) for h in at]
+        cached = [jnp.where(valid, value * factor, NEG) for value in cached]
+        recent = [jnp.where(fresh, value * factor, NEG) for value in recent]
+        top = [
+            jnp.maximum(
+                jnp.max(cached[h], axis=1, keepdims=True), jnp.max(recent[h], axis=1, keepdims=True)
+            )
+            for h in at
+        ]
+        cached = [jnp.exp(cached[h] - top[h]) for h in at]
+        recent = [jnp.exp(recent[h] - top[h]) for h in at]
+        share_of = [
+            1.0
+            / (
+                jnp.sum(cached[h], axis=1, keepdims=True)
+                + jnp.sum(recent[h], axis=1, keepdims=True)
+            )
+            for h in at
+        ]
+        cached = [(cached[h] * share_of[h]).astype(bf16) for h in at]
+        recent = [(recent[h] * share_of[h]).astype(bf16) for h in at]
+        mixed = [
+            product(cached[h], kv_ref[1, 0, h], 0) + product(recent[h], new_values[h], 0)
+            for h in at
+        ]
+        for h in at:
+            value = mixed[h].reshape(steps, per, size)
+            o_ref[:, 0, h] = value.astype(bf16)
+            for j in range(per):
+                head = h * per + j
+                h_ref[head // share, 0, :, pl.ds(head % share * size, size)] = value[:, j].astype(
+                    bf16
+                )
+
+    return pl.pallas_call(
+        kernel,
+        grid_spec=pltpu.PrefetchScalarGridSpec(
+            num_scalar_prefetch=1,
+            grid=(seqs, splits),
+            in_specs=[
+                pl.BlockSpec((steps, 1, mine, per, size), lambda s, i, n: (0, s, i, 0, 0)),
+                pl.BlockSpec((2, 1, mine, slots, size), lambda s, i, n: (0, s, i, 0, 0)),
+                pl.BlockSpec((steps, 2, 1, heads, size), lambda s, i, n: (0, 0, s, 0, 0)),
+            ],
+            out_specs=[
+                pl.BlockSpec((steps, 1, mine, per, size), lambda s, i, n: (0, s, i, 0, 0)),
+                pl.BlockSpec(
+                    (owners // splits, 1, steps, share * size), lambda s, i, n: (i, s, 0, 0)
+                ),
+            ],
+        ),
+        out_shape=[
+            jax.ShapeDtypeStruct(queries.shape, bf16),
+            jax.ShapeDtypeStruct((owners, seqs, steps, share * size), bf16),
+        ],
+        compiler_params=params(),
+        cost_estimate=cost(4 * rows * heads * slots * size * seqs, 4 * heads * slots * size * seqs),
+        name="attention",
+    )(cache_len, queries, *in_hbm(kv_cache), new_kv)
 
 
 def swap_cores(value):
@@ -561,10 +632,8 @@
     part = lax.axis_index("grp") if parts > 1 else jnp.zeros((), jnp.int32)
     place = jnp.stack([me % 2, part, me // 2, me]).astype(jnp.int32)
 
-    live = lax.dynamic_slice_in_dim(cache_len, me * seq_dev, seq_dev, 0)
-    attn_out = attention(queries, kv_cache, new_kv, live)
-    heads = attn_out.reshape(steps, seq_dev, owners, -1)
-    heads = exchange(jnp.transpose(heads, (2, 1, 0, 3)))
+    attn_out, heads = attention(cache_len, queries, kv_cache, new_kv, owners)
+    heads = exchange(heads)
 
     out_levels, out_scale = out_levels_of(out_weight, pick_tile(out_weight.shape[1], 2560))
     heads, out_levels, out_scale = lax.optimization_barrier((heads, out_levels, out_scale))

time: 145 us -> 141 us (0.972)
  blocking collectives: 21.6 us -> 34.6 us
  waiting for transfers between devices: 27.1 us -> 18.3 us
  local copies, waits for them, and re-layouts: 7.58 us -> 2.9 us
  starting transfers between devices: 26.3 us -> 23.2 us
  Pallas kernels: 51.6 us -> 54.6 us
  matrix products: 2.74 us -> 0 us
    all_to_all x0 -> x1, blocking collectives: none -> 12.3 us  [on_device(): both = lax.all_to_all(both, axes, split_axis=0, concat_axis=0, tiled=True)]
    all_to_all x1 -> x0, waiting for transfers between devices: 8.25 us -> none  [on_device(): both = lax.all_to_all(both, axes, split_axis=0, concat_axis=0, tiled=True)]
    pallas_call x0 -> x1, Pallas kernels: none -> 4.03 us  [attention(): pl.pallas_call(kernel, grid_spec=pltpu.PrefetchScalarGridSpec(num_scalar_...]
    all_to_all x1 -> x0, starting transfers between devices: 3.6 us -> none  [on_device(): both = lax.all_to_all(both, axes, split_axis=0, concat_axis=0, tiled=True)]
    dot_general x4 -> x0, matrix products: 2.74 us -> none  [the longest x1 1.84 us: attention(): jnp.einsum('nshqd,shcd->nshqc', queries, keys, preferred_element_type=f32)]
    unnamed x29 -> x12, local copies, waits for them, and re-layouts: 2.02 us -> 0.02 us
  transfers between devices with their start and end apart: 12 -> 11, of which waited for: 8 -> 7; matrix products, arithmetic and copies ran while one was open for 4% -> 4% of each run, Pallas kernels for 28% -> 28%
where the time goes in v6:
time: 141 us; the launch traced here: 140 us
  Pallas kernels  54.6 us (39%)
  blocking collectives  34.6 us (25%)
  starting transfers between devices  23.2 us (16%)
  waiting for transfers between devices  18.3 us (13%)
  other arithmetic  5.51 us (4%)
  local copies, waits for them, and re-layouts  2.9 us (2%)
    all_to_all x1, blocking collectives, exchange_chips(): lax.all_to_all(value, 'wide', split_axis=0, concat_axis=0, tiled=True, ax...  22.3 us
    pallas_call x3, Pallas kernels, rounded_weights(): pl.pallas_call(kernel, grid_spec=pltpu.PrefetchScalarGridSpec(num_scalar_...  20.6 us
    pallas_call x2, Pallas kernels, gate_up_product(): pl.pallas_call(kernel, grid_spec=pltpu.PrefetchScalarGridSpec(num_scalar_...  13.6 us
    ppermute x3, waiting for transfers between devices, exchange_halves(): received = lax.ppermute(send, 'wide', [(i, i ^ bit) for i in range(count)])  12.7 us
    all_to_all x1, blocking collectives, on_device(): both = lax.all_to_all(both, axes, split_axis=0, concat_axis=0, tiled=True)  12.3 us
    all_to_all x2, starting transfers between devices, exchange(): lax.all_to_all(value, 'wide', split_axis=0, concat_axis=0, tiled=True)  11.9 us
    pallas_call x1, Pallas kernels, out_levels_of(): pl.pallas_call(kernel, grid=(cols // tile,), in_specs=[pl.BlockSpec((rows...  5.44 us
    all_to_all x1, starting transfers between devices, exchange_chips(): lax.all_to_all(value, 'wide', split_axis=0, concat_axis=0, tiled=True, ax...  4.55 us
  transfers between devices with their start and end apart: 11, of which 7 were waited for; matrix products, arithmetic and copies ran while one was open for 4% of the time, Pallas kernels for 28%

profile of v6, /device:TPU:0, one launch (start us, length us, event | category | flops | bytes accessed | tf_op | source)
XLA Modules:
  0.0 140.0 jit_solution(14728959243866215871)
XLA Ops:
  0.6 4.0 %attention.1 = (bf16[3,1,8,8,128]{4,3,2,1,0:T(8,128)(2,1)}, bf16[16,1,3,512]{3,2,1,0:T(4,128)(2,1)}) custom-call(s32[16]{0:T(128)} %len_ref.1, bf16[3,1,8,8,128]{4,3,2,1,0:T(8,128)(2,1)} %q_ref.1, bf16[2,1,8,512,128]{4,3,2,1,0:T(8,128)(2,1)} %kv_ref.1, bf16[3,2,1,8,128]{4,3,2,1,0:T(8,128)(2,1)} %new_ref.1), custom_call_target="tpu_custom_call" | custom-call | flops 50331648 | bytes 2097152 | tf_op jit(solution)/shard_map/attention/pallas_call | solution.py:542
  4.7 7.4 %all-to-all-start = ((bf16[16,1,3,512]{3,2,1,0:T(4,128)(2,1)}), bf16[16,1,3,512]{3,2,1,0:T(4,128)(2,1)S(1)}, u32[]{:S(2)}, u32[]{:S(2)}) async-start(bf16[16,1,3,512]{3,2,1,0:T(4,128)(2,1)} %get-tuple-element.29), calls=%async_computation | async-start | bytes 131072 | tf_op jit(solution)/shard_map/all_to_all | solution.py:575
  12.1 5.4 %out_levels_of.1 = (f8e4m3fn[512,5120]{1,0:T(32,128)(4,1)}, f32[8,5120]{1,0:T(8,128)}) custom-call(bf16[512,5120]{1,0:T(8,128)(2,1)} %w_ref.1), custom_call_target="tpu_custom_call" | custom-call | flops 20971520 | bytes 7864320 | tf_op jit(solution)/shard_map/out_levels_of/pallas_call | solution.py:241
  17.5 1.5 %all-to-all-done = bf16[16,1,3,512]{3,2,1,0:T(4,128)(2,1)S(1)} async-done(((bf16[16,1,3,512]{3,2,1,0:T(4,128)(2,1)}), bf16[16,1,3,512]{3,2,1,0:T(4,128)(2,1)S(1)}, u32[]{:S(2)}, u32[]{:S(2)}) %all-to-all-start) | async-done | bytes 49184 | tf_op jit(solution)/shard_map/all_to_all | solution.py:575
  19.6 3.2 %out_product.1 = bf16[16,48,320]{2,1,0:T(8,128)(2,1)} custom-call(bf16[48,512]{1,0:T(8,128)(2,1)} %reshape.31.x_ref, f8e4m3fn[512,5120]{1,0:T(32,128)(4,1)} %get-tuple-element.33.l_ref, f32[8,5120]{1,0:T(8,128)} %get-tuple-element.34.s_ref), custom_call_target="tpu_custom_call" | custom-call | flops 251658240 | bytes 2621440 | tf_op jit(solution)/shard_map/out_product/pallas_call | solution.py:275
  22.8 4.5 %all-to-all-start.1 = ((bf16[16,48,320]{2,1,0:T(8,128)(2,1)}), bf16[16,48,320]{2,1,0:T(8,128)(2,1)S(1)}, u32[]{:S(2)}, u32[]{:S(2)}) async-start(bf16[16,48,320]{2,1,0:T(8,128)(2,1)} %out_product.1), calls=%async_computation.1 | async-start | bytes 1179648 | tf_op jit(solution)/shard_map/all_to_all | solution.py:575
  28.0 3.7 %edge_max.1 = f32[8,8192]{1,0:T(8,128)} custom-call(s32[4]{0:T(128)} %pad_add_fusion.place_ref, bf16[320,16384]{1,0:T(8,128)(2,1)} %refs_3_.1, bf16[320,16384]{1,0:T(8,128)(2,1)} %refs_4_.1, bf16[320,16384]{1,0:T(8,128)(2,1)} %bitcast.25), custom_call_target="tpu_custom_call" | custom-call | flops 3145728 | bytes 3145728 | tf_op jit(solution)/shard_map/edge_max/pallas_call | solution.py:99
  32.1 0.8 dynamic-slice_convert_fusion
  33.5 8.0 %rounded_weights.3 = (bf16[320,4096]{1,0:T(8,128)(2,1)}, bf16[320,4096]{1,0:T(8,128)(2,1)}) custom-call(s32[4]{0:T(128)} %pad_add_fusion.place_ref, bf16[320,16384]{1,0:T(8,128)(2,1)} %refs_3_.1, bf16[320,16384]{1,0:T(8,128)(2,1)} %refs_4_.1, f32[8,8192]{1,0:T(8,128)S(1)} %collective-permute-done.refs_2_.refs_5_.refs_1_), custom_call_target="tpu_custom_call" | custom-call | flops 15728640 | bytes 10485760 | tf_op jit(solution)/shard_map/rounded_weights/pallas_call | solution.py:171
  41.5 1.4 %all-to-all-done.1 = bf16[16,48,320]{2,1,0:T(8,128)(2,1)S(1)} async-done(((bf16[16,48,320]{2,1,0:T(8,128)(2,1)}), bf16[16,48,320]{2,1,0:T(8,128)(2,1)S(1)}, u32[]{:S(2)}, u32[]{:S(2)}) %all-to-all-start.1) | async-done | bytes 491552 | tf_op jit(solution)/shard_map/all_to_all | solution.py:575
  43.0 1.6 %collective-permute-start.1 = (bf16[48,320]{1,0:T(8,128)(2,1)S(1)}, bf16[48,320]{1,0:T(8,128)(2,1)S(1)}, u32[]{:S(2)}, u32[]{:S(2)}) collective-permute-start(bf16[48,320]{1,0:T(8,128)(2,1)S(1)} %add_convert_fusion.4.refs_0_.refs_1_), channel_id=1, source_target_pairs={{0,16},{16,0},{1,17},{17,1},{2,18},{18,2},{3,19},{19,3},{4,20},{20... | collective-permute-start | bytes 92168 | tf_op jit(solution)/shard_map/ppermute | solution.py:666
  44.6 2.5 %collective-permute-done.1.refs_1_.refs_2_ = bf16[48,320]{1,0:T(8,128)(2,1)S(1)} collective-permute-done((bf16[48,320]{1,0:T(8,128)(2,1)S(1)}, bf16[48,320]{1,0:T(8,128)(2,1)S(1)}, u32[]{:S(2)}, u32[]{:S(2)}) %collective-permute-start.1) | collective-permute-done | bytes 30752 | tf_op jit(solution)/shard_map/ppermute | solution.py:666
  47.0 5.6 %gate_up_product.3 = (bf16[8,96,768]{2,1,0:T(8,128)(2,1)}, bf16[8,96,384]{2,1,0:T(8,128)(2,1)}) custom-call(s32[4]{0:T(128)} %pad_add_fusion.place_ref, bf16[48,320]{1,0:T(8,128)(2,1)S(1)} %add_convert_fusion.4.refs_0_.refs_1_, bf16[48,320]{1,0:T(8,128)(2,1)S(1)} %collective-permute-done.1.refs_1_.refs_2_, f32[1,320]{1,0:T(1,128)} %reshape.35.refs_2_, ...), custom_call_target="tpu_custom_call" | custom-call | flops 503316480 | bytes 5242880 | tf_op jit(solution)/shard_map/gate_up_product/pallas_call | solution.py:380
  53.2 8.0 %gate_up_product.2 = (bf16[8,96,768]{2,1,0:T(8,128)(2,1)}, bf16[8,96,384]{2,1,0:T(8,128)(2,1)}) custom-call(s32[4]{0:T(128)} %pad_add_fusion.place_ref, bf16[48,320]{1,0:T(8,128)(2,1)S(1)} %add_convert_fusion.4.refs_0_.refs_1_, bf16[48,320]{1,0:T(8,128)(2,1)S(1)} %collective-permute-done.1.refs_1_.refs_2_, f32[1,320]{1,0:T(1,128)} %reshape.35.refs_2_, ...), custom_call_target="tpu_custom_call" | custom-call | flops 503316480 | bytes 5242880 | tf_op jit(solution)/shard_map/gate_up_product/pallas_call | solution.py:380
  61.2 1.3 add_convert_fusion.2
  62.5 0.8 collective-permute-start.4
  63.3 1.0 add_convert_fusion.1
  64.3 4.5 %all-to-all-start.2 = ((bf16[8,96,384]{2,1,0:T(8,128)(2,1)}), bf16[8,96,384]{2,1,0:T(8,128)(2,1)S(1)}, u32[]{:S(2)}, u32[]{:S(2)}) async-start(bf16[8,96,384]{2,1,0:T(8,128)(2,1)} %add_convert_fusion.1), calls=%async_computation.2 | async-start | bytes 1179648 | tf_op jit(solution)/shard_map/all_to_all | solution.py:581
  68.8 6.2 %rounded_weights.5.w_ref = bf16[320,4096]{1,0:T(8,128)(2,1)} custom-call(s32[4]{0:T(128)} %pad_add_fusion.place_ref, bf16[320,16384]{1,0:T(8,128)(2,1)} %bitcast.26, f32[8,8192]{1,0:T(8,128)S(1)} %collective-permute-done.refs_2_.refs_5_.refs_1_), custom_call_target="tpu_custom_call" | custom-call | flops 7864320 | bytes 5242880 | tf_op jit(solution)/shard_map/rounded_weights/pallas_call | solution.py:171
  75.1 6.4 %rounded_weights.4.w_ref = bf16[320,4096]{1,0:T(8,128)(2,1)} custom-call(s32[4]{0:T(128)} %pad_add_fusion.place_ref, bf16[320,16384]{1,0:T(8,128)(2,1)} %bitcast.27, f32[8,8192]{1,0:T(8,128)S(1)} %collective-permute-done.refs_2_.refs_5_.refs_1_), custom_call_target="tpu_custom_call" | custom-call | flops 7864320 | bytes 5242880 | tf_op jit(solution)/shard_map/rounded_weights/pallas_call | solution.py:171
  81.4 2.0 %collective-permute-done.4 = bf16[4,96,768]{2,1,0:T(8,128)(2,1)} collective-permute-done((bf16[4,96,768]{2,1,0:T(8,128)(2,1)S(1)}, bf16[4,96,768]{2,1,0:T(8,128)(2,1)}, u32[]{:S(2)}, u32[]{:S(2)}) %collective-permute-start.4) | collective-permute-done | bytes 589856 | tf_op jit(solution)/shard_map/ppermute | solution.py:591
  83.4 1.3 add_convert_fusion
  84.7 0.8 collective-permute-start.5
  85.5 6.0 %collective-permute-done.5 = bf16[2,96,768]{2,1,0:T(8,128)(2,1)S(1)} collective-permute-done((bf16[2,96,768]{2,1,0:T(8,128)(2,1)S(1)}, bf16[2,96,768]{2,1,0:T(8,128)(2,1)S(1)}, u32[]{:S(2)}, u32[]{:S(2)}) %collective-permute-start.5) | collective-permute-done | bytes 294944 | tf_op jit(solution)/shard_map/ppermute | solution.py:591
  91.6 2.6 %collective-permute-start.6 = (bf16[1,96,768]{2,1,0:T(8,128)(2,1)S(1)}, bf16[1,96,768]{2,1,0:T(8,128)(2,1)S(1)}, u32[]{:S(2)}, u32[]{:S(2)}) collective-permute-start(bf16[1,96,768]{2,1,0:T(8,128)(2,1)S(1)} %slice.65), channel_id=1, source_target_pairs={{0,8},{1,9},{2,10},{3,11},{4,12},{5,13},{6,14},{7,15},{8,0},{9,1},... | collective-permute-start | bytes 442376 | tf_op jit(solution)/shard_map/ppermute | solution.py:591
  94.6 4.7 %collective-permute-done.6 = bf16[1,96,768]{2,1,0:T(8,128)(2,1)S(1)} collective-permute-done((bf16[1,96,768]{2,1,0:T(8,128)(2,1)S(1)}, bf16[1,96,768]{2,1,0:T(8,128)(2,1)S(1)}, u32[]{:S(2)}, u32[]{:S(2)}) %collective-permute-start.6) | collective-permute-done | bytes 147488 | tf_op jit(solution)/shard_map/ppermute | solution.py:591
  99.6 22.3 %all_to_all.25.a_ref = bf16[8,96,512]{2,1,0:T(8,128)(2,1)S(1)} all-to-all(bf16[8,96,512]{2,1,0:T(8,128)(2,1)S(1)} %broadcast_in_dim.15), channel_id=1, replica_groups={{0,2,4,6,8,10,12,14},{1,3,5,7,9,11,13,15},{16,18,20,22,24,26,28,30},{17..., dimensions={0} | all-to-all | bytes 1572864 | tf_op jit(solution)/shard_map/all_to_all | solution.py:581
  121.8 2.0 %down_product.2.refs_0_ = f32[96,320]{1,0:T(8,128)S(1)} custom-call(s32[4]{0:T(128)S(1)} %copy-done.2, bf16[8,96,512]{2,1,0:T(8,128)(2,1)S(1)} %all_to_all.25.a_ref, bf16[320,4096]{1,0:T(8,128)(2,1)S(1)} %copy-done.1), custom_call_target="tpu_custom_call" | custom-call | flops 251658240 | bytes 2621440 | tf_op jit(solution)/shard_map/down_product/pallas_call | solution.py:449
  124.1 2.1 %down_product.3 = bf16[32,6,320]{2,1,0:T(8,128)(2,1)S(1)} custom-call(s32[4]{0:T(128)S(1)} %copy-done.2, bf16[8,96,512]{2,1,0:T(8,128)(2,1)S(1)} %collective-permute-done.7.a_ref, bf16[320,4096]{1,0:T(8,128)(2,1)S(1)} %copy-done, f32[96,320]{1,0:T(8,128)S(1)} %down_product.2.refs_0_, bf16[48,320]{1,0:T(8,128)(2,1)S(1)} %add_convert_fusion.4.refs_0_.refs_1_, ...), custom_call_target="tpu_custom_call" | custom-call | flops 251658240 | bytes 2621440 | tf_op jit(solution)/shard_map/down_product/pallas_call | solution.py:449
  126.2 12.3 %all_to_all.26 = bf16[32,6,320]{2,1,0:T(8,128)(2,1)S(1)} all-to-all(bf16[32,6,320]{2,1,0:T(8,128)(2,1)S(1)} %down_product.3), channel_id=1, replica_groups=mesh['grp'=2,'wide'=16] {'grp','wide'}, dimensions={0} | all-to-all | bytes 245760 | tf_op jit(solution)/shard_map/all_to_all | solution.py:711
  138.5 0.7 reshape.33
  139.3 0.7 reshape.34
  (43 shorter events, 3.9 us)
Async XLA Ops:
  4.7 14.3 %all-to-all-start = ((bf16[16,1,3,512]{3,2,1,0:T(4,128)(2,1)}), bf16[16,1,3,512]{3,2,1,0:T(4,128)(2,1)S(1)}, u32[]{:S(2)}, u32[]{:S(2)}) async-start(bf16[16,1,3,512]{3,2,1,0:T(4,128)(2,1)} %get-tuple-element.29), calls=%async_computation | async-start | bytes 131072 | tf_op jit(solution)/shard_map/all_to_all | solution.py:575
  22.8 20.1 %all-to-all-start.1 = ((bf16[16,48,320]{2,1,0:T(8,128)(2,1)}), bf16[16,48,320]{2,1,0:T(8,128)(2,1)S(1)}, u32[]{:S(2)}, u32[]{:S(2)}) async-start(bf16[16,48,320]{2,1,0:T(8,128)(2,1)} %out_product.1), calls=%async_computation.1 | async-start | bytes 1179648 | tf_op jit(solution)/shard_map/all_to_all | solution.py:575
  28.0 5.4 %copy-start.5 = (bf16[3,16,320]{2,1,0:T(8,128)(2,1)S(1)}, bf16[3,16,320]{2,1,0:T(8,128)(2,1)}, u32[]{:S(2)}) copy-start(bf16[3,16,320]{2,1,0:T(8,128)(2,1)} %param.10) | copy-start | bytes 92164
  31.7 1.8 %collective-permute-start = (f32[8,8192]{1,0:T(8,128)}, f32[8,8192]{1,0:T(8,128)S(1)}, u32[]{:S(2)}, u32[]{:S(2)}) collective-permute-start(f32[8,8192]{1,0:T(8,128)} %edge_max.1), channel_id=1, source_target_pairs={{0,1},{1,0},{2,3},{3,2},{4,5},{5,4},{6,7},{7,6},{8,9},{9,8},{10,11... | collective-permute-start | bytes 786440 | tf_op jit(solution)/shard_map/ppermute | solution.py:571
  43.0 4.0 %collective-permute-start.1 = (bf16[48,320]{1,0:T(8,128)(2,1)S(1)}, bf16[48,320]{1,0:T(8,128)(2,1)S(1)}, u32[]{:S(2)}, u32[]{:S(2)}) collective-permute-start(bf16[48,320]{1,0:T(8,128)(2,1)S(1)} %add_convert_fusion.4.refs_0_.refs_1_), channel_id=1, source_target_pairs={{0,16},{16,0},{1,17},{17,1},{2,18},{18,2},{3,19},{19,3},{4,20},{20... | collective-permute-start | bytes 92168 | tf_op jit(solution)/shard_map/ppermute | solution.py:666
  52.6 8.5 %collective-permute-start.2 = (bf16[8,96,768]{2,1,0:T(8,128)(2,1)}, bf16[8,96,768]{2,1,0:T(8,128)(2,1)S(1)}, u32[]{:S(2)}, u32[]{:S(2)}) collective-permute-start(bf16[8,96,768]{2,1,0:T(8,128)(2,1)} %get-tuple-element.43), channel_id=1, source_target_pairs={{0,1},{1,0},{2,3},{3,2},{4,5},{5,4},{6,7},{7,6},{8,9},{9,8},{10,11... | collective-permute-start | bytes 3538952 | tf_op jit(solution)/shard_map/ppermute | solution.py:571
  52.6 9.8 %collective-permute-start.3 = (bf16[8,96,384]{2,1,0:T(8,128)(2,1)}, bf16[8,96,384]{2,1,0:T(8,128)(2,1)S(1)}, u32[]{:S(2)}, u32[]{:S(2)}) collective-permute-start(bf16[8,96,384]{2,1,0:T(8,128)(2,1)} %get-tuple-element.45), channel_id=1, source_target_pairs={{0,1},{1,0},{2,3},{3,2},{4,5},{5,4},{6,7},{7,6},{8,9},{9,8},{10,11... | collective-permute-start | bytes 1769480 | tf_op jit(solution)/shard_map/ppermute | solution.py:571
  61.2 2.1 %copy-start.4 = (bf16[8,96,384]{2,1,0:T(8,128)(2,1)S(1)}, bf16[8,96,384]{2,1,0:T(8,128)(2,1)}, u32[]{:S(2)}) copy-start(bf16[8,96,384]{2,1,0:T(8,128)(2,1)} %get-tuple-element.46) | copy-start | bytes 1769476
  62.5 20.9 %collective-permute-start.4 = (bf16[4,96,768]{2,1,0:T(8,128)(2,1)S(1)}, bf16[4,96,768]{2,1,0:T(8,128)(2,1)}, u32[]{:S(2)}, u32[]{:S(2)}) collective-permute-start(bf16[4,96,768]{2,1,0:T(8,128)(2,1)S(1)} %add_convert_fusion.2), channel_id=1, source_target_pairs={{0,2},{1,3},{2,0},{3,1},{4,6},{5,7},{6,4},{7,5},{8,10},{9,11},{10,... | collective-permute-start | bytes 1769480 | tf_op jit(solution)/shard_map/ppermute | solution.py:591
  64.3 30.0 %all-to-all-start.2 = ((bf16[8,96,384]{2,1,0:T(8,128)(2,1)}), bf16[8,96,384]{2,1,0:T(8,128)(2,1)S(1)}, u32[]{:S(2)}, u32[]{:S(2)}) async-start(bf16[8,96,384]{2,1,0:T(8,128)(2,1)} %add_convert_fusion.1), calls=%async_computation.2 | async-start | bytes 1179648 | tf_op jit(solution)/shard_map/all_to_all | solution.py:581
  75.0 8.4 %copy-start.3 = (bf16[8,96,768]{2,1,0:T(8,128)(2,1)S(1)}, bf16[8,96,768]{2,1,0:T(8,128)(2,1)}, u32[]{:S(2)}) copy-start(bf16[8,96,768]{2,1,0:T(8,128)(2,1)} %get-tuple-element.40) | copy-start | bytes 3538948
  84.7 6.8 %collective-permute-start.5 = (bf16[2,96,768]{2,1,0:T(8,128)(2,1)S(1)}, bf16[2,96,768]{2,1,0:T(8,128)(2,1)S(1)}, u32[]{:S(2)}, u32[]{:S(2)}) collective-permute-start(bf16[2,96,768]{2,1,0:T(8,128)(2,1)S(1)} %slice.63), channel_id=1, source_target_pairs={{0,4},{1,5},{2,6},{3,7},{4,0},{5,1},{6,2},{7,3},{8,12},{9,13},{10,... | collective-permute-start | bytes 884744 | tf_op jit(solution)/shard_map/ppermute | solution.py:591
  91.6 7.7 %collective-permute-start.6 = (bf16[1,96,768]{2,1,0:T(8,128)(2,1)S(1)}, bf16[1,96,768]{2,1,0:T(8,128)(2,1)S(1)}, u32[]{:S(2)}, u32[]{:S(2)}) collective-permute-start(bf16[1,96,768]{2,1,0:T(8,128)(2,1)S(1)} %slice.65), channel_id=1, source_target_pairs={{0,8},{1,9},{2,10},{3,11},{4,12},{5,13},{6,14},{7,15},{8,0},{9,1},... | collective-permute-start | bytes 442376 | tf_op jit(solution)/shard_map/ppermute | solution.py:591
  99.4 22.4 %copy-start.1 = (bf16[320,4096]{1,0:T(8,128)(2,1)S(1)}, bf16[320,4096]{1,0:T(8,128)(2,1)}, u32[]{:S(2)}) copy-start(bf16[320,4096]{1,0:T(8,128)(2,1)} %rounded_weights.4.w_ref) | copy-start | bytes 7864324
  99.5 22.4 %copy-start.2 = (s32[4]{0:T(128)S(1)}, s32[4]{0:T(128)}, u32[]{:S(2)}) copy-start(s32[4]{0:T(128)} %pad_add_fusion.place_ref) | copy-start | bytes 52
  121.8 2.3 %copy-start = (bf16[320,4096]{1,0:T(8,128)(2,1)S(1)}, bf16[320,4096]{1,0:T(8,128)(2,1)}, u32[]{:S(2)}) copy-start(bf16[320,4096]{1,0:T(8,128)(2,1)} %rounded_weights.5.w_ref) | copy-start | bytes 7864324
  121.8 2.3 %collective-permute-start.7 = (bf16[8,96,512]{2,1,0:T(8,128)(2,1)S(1)}, bf16[8,96,512]{2,1,0:T(8,128)(2,1)S(1)}, u32[]{:S(2)}, u32[]{:S(2)}) collective-permute-start(bf16[8,96,512]{2,1,0:T(8,128)(2,1)S(1)} %all_to_all.25.a_ref), channel_id=1, source_target_pairs={{0,1},{1,0},{2,3},{3,2},{4,5},{5,4},{6,7},{7,6},{8,9},{9,8},{10,11... | collective-permute-start | bytes 2359304 | tf_op jit(solution)/shard_map/ppermute | solution.py:571

commit v7 on v6

--- a/solution.py
+++ b/solution.py
@@ -356,7 +356,7 @@
 
         def write_second(block):
             for q in range(chips):
-                write(1, block, q, q)
+                write(1, block, q ^ (place_ref[2] % 2), q)
 
         for block in range(runs[0]):
             pl.when(step == block // together)(functools.partial(write_first, block))
@@ -602,6 +602,18 @@
         send = kept[half // 2 :]
 
 
+def exchange_pairs(value):
+    count = lax.axis_size("wide")
+    groups = [[rest + 4 * k for k in range(count // 4)] for rest in range(4)]
+    value = value.reshape(count // 4, 2, *value.shape[1:])
+    value = lax.all_to_all(
+        value, "wide", split_axis=0, concat_axis=0, tiled=True, axis_index_groups=groups
+    )
+    value = jnp.sum(value.astype(f32), axis=0)
+    received = lax.ppermute(value[1].astype(bf16), "wide", [(i, i ^ 2) for i in range(count)])
+    return value[0] + received.astype(f32)
+
+
 def on_device(
     residual_in,
     norm_gain,
@@ -688,10 +700,9 @@
         )[0]
         for flip in range(2)
     ]
-    last = exchange_chips(second)
+    last = exchange_pairs(second)
     first, (home, away) = exchange_halves(kept[0], got[0], send, (home, away))
 
-    last = jnp.sum(last.astype(f32), axis=0)
     squares = jnp.sum(last[:, 2 * runs[1] * BLOCK :], axis=1, keepdims=True)
     scale = lax.rsqrt(squares / width + EPS_NORM)
 

time: 141 us -> 139 us (0.986)
  transfers between devices with their start and end apart: 11 -> 12, of which waited for: 7 -> 7; matrix products, arithmetic and copies ran while one was open for 4% -> 3% of each run, Pallas kernels for 28% -> 29%
where the time goes in v7:
time: 139 us; the launch traced here: 138 us
  Pallas kernels  54.7 us (39%)
  blocking collectives  33.4 us (24%)
  starting transfers between devices  24.4 us (18%)
  waiting for transfers between devices  17.5 us (13%)
  other arithmetic  4.49 us (3%)
  local copies, waits for them, and re-layouts  2.92 us (2%)
    all_to_all x1, blocking collectives, exchange_chips(): lax.all_to_all(value, 'wide', split_axis=0, concat_axis=0, tiled=True, ax...  21.1 us
    pallas_call x3, Pallas kernels, rounded_weights(): pl.pallas_call(kernel, grid_spec=pltpu.PrefetchScalarGridSpec(num_scalar_...  20.6 us
    pallas_call x2, Pallas kernels, gate_up_product(): pl.pallas_call(kernel, grid_spec=pltpu.PrefetchScalarGridSpec(num_scalar_...  13.6 us
    all_to_all x1, blocking collectives, on_device(): both = lax.all_to_all(both, axes, split_axis=0, concat_axis=0, tiled=True)  12.3 us
    all_to_all x2, starting transfers between devices, exchange(): lax.all_to_all(value, 'wide', split_axis=0, concat_axis=0, tiled=True)  11.9 us
    ppermute x3, waiting for transfers between devices, exchange_halves(): received = lax.ppermute(send, 'wide', [(i, i ^ bit) for i in range(count)])  11.9 us
    pallas_call x1, Pallas kernels, out_levels_of(): pl.pallas_call(kernel, grid=(cols // tile,), in_specs=[pl.BlockSpec((rows...  5.44 us
    ppermute x3, starting transfers between devices, exchange_halves(): received = lax.ppermute(send, 'wide', [(i, i ^ bit) for i in range(count)])  4.99 us
  transfers between devices with their start and end apart: 12, of which 7 were waited for; matrix products, arithmetic and copies ran while one was open for 3% of the time, Pallas kernels for 29%

profile of v7, /device:TPU:0, one launch (start us, length us, event | category | flops | bytes accessed | tf_op | source)
XLA Modules:
  0.0 138.3 jit_solution(11541250628395168415)
XLA Ops:
  0.6 4.0 %attention.1 = (bf16[3,1,8,8,128]{4,3,2,1,0:T(8,128)(2,1)}, bf16[16,1,3,512]{3,2,1,0:T(4,128)(2,1)}) custom-call(s32[16]{0:T(128)} %len_ref.1, bf16[3,1,8,8,128]{4,3,2,1,0:T(8,128)(2,1)} %q_ref.1, bf16[2,1,8,512,128]{4,3,2,1,0:T(8,128)(2,1)} %kv_ref.1, bf16[3,2,1,8,128]{4,3,2,1,0:T(8,128)(2,1)} %new_ref.1), custom_call_target="tpu_custom_call" | custom-call | flops 50331648 | bytes 2097152 | tf_op jit(solution)/shard_map/attention/pallas_call | solution.py:542
  4.7 7.4 %all-to-all-start = ((bf16[16,1,3,512]{3,2,1,0:T(4,128)(2,1)}), bf16[16,1,3,512]{3,2,1,0:T(4,128)(2,1)S(1)}, u32[]{:S(2)}, u32[]{:S(2)}) async-start(bf16[16,1,3,512]{3,2,1,0:T(4,128)(2,1)} %get-tuple-element.29), calls=%async_computation | async-start | bytes 131072 | tf_op jit(solution)/shard_map/all_to_all | solution.py:575
  12.1 5.4 %out_levels_of.1 = (f8e4m3fn[512,5120]{1,0:T(32,128)(4,1)}, f32[8,5120]{1,0:T(8,128)}) custom-call(bf16[512,5120]{1,0:T(8,128)(2,1)} %w_ref.1), custom_call_target="tpu_custom_call" | custom-call | flops 20971520 | bytes 7864320 | tf_op jit(solution)/shard_map/out_levels_of/pallas_call | solution.py:241
  17.5 1.5 %all-to-all-done = bf16[16,1,3,512]{3,2,1,0:T(4,128)(2,1)S(1)} async-done(((bf16[16,1,3,512]{3,2,1,0:T(4,128)(2,1)}), bf16[16,1,3,512]{3,2,1,0:T(4,128)(2,1)S(1)}, u32[]{:S(2)}, u32[]{:S(2)}) %all-to-all-start) | async-done | bytes 49184 | tf_op jit(solution)/shard_map/all_to_all | solution.py:575
  19.6 3.2 %out_product.1 = bf16[16,48,320]{2,1,0:T(8,128)(2,1)} custom-call(bf16[48,512]{1,0:T(8,128)(2,1)} %reshape.35.x_ref, f8e4m3fn[512,5120]{1,0:T(32,128)(4,1)} %get-tuple-element.33.l_ref, f32[8,5120]{1,0:T(8,128)} %get-tuple-element.34.s_ref), custom_call_target="tpu_custom_call" | custom-call | flops 251658240 | bytes 2621440 | tf_op jit(solution)/shard_map/out_product/pallas_call | solution.py:275
  22.8 4.6 %all-to-all-start.1 = ((bf16[16,48,320]{2,1,0:T(8,128)(2,1)}), bf16[16,48,320]{2,1,0:T(8,128)(2,1)S(1)}, u32[]{:S(2)}, u32[]{:S(2)}) async-start(bf16[16,48,320]{2,1,0:T(8,128)(2,1)} %out_product.1), calls=%async_computation.1 | async-start | bytes 1179648 | tf_op jit(solution)/shard_map/all_to_all | solution.py:575
  28.0 3.7 %edge_max.1 = f32[8,8192]{1,0:T(8,128)} custom-call(s32[4]{0:T(128)} %pad_add_fusion.place_ref, bf16[320,16384]{1,0:T(8,128)(2,1)} %refs_3_.1, bf16[320,16384]{1,0:T(8,128)(2,1)} %refs_4_.1, bf16[320,16384]{1,0:T(8,128)(2,1)} %bitcast.32), custom_call_target="tpu_custom_call" | custom-call | flops 3145728 | bytes 3145728 | tf_op jit(solution)/shard_map/edge_max/pallas_call | solution.py:99
  32.1 0.8 dynamic-slice_convert_fusion
  33.5 8.0 %rounded_weights.3 = (bf16[320,4096]{1,0:T(8,128)(2,1)}, bf16[320,4096]{1,0:T(8,128)(2,1)}) custom-call(s32[4]{0:T(128)} %pad_add_fusion.place_ref, bf16[320,16384]{1,0:T(8,128)(2,1)} %refs_3_.1, bf16[320,16384]{1,0:T(8,128)(2,1)} %refs_4_.1, f32[8,8192]{1,0:T(8,128)S(1)} %collective-permute-done.refs_2_.refs_5_.refs_1_), custom_call_target="tpu_custom_call" | custom-call | flops 15728640 | bytes 10485760 | tf_op jit(solution)/shard_map/rounded_weights/pallas_call | solution.py:171
  41.5 1.4 %all-to-all-done.1 = bf16[16,48,320]{2,1,0:T(8,128)(2,1)S(1)} async-done(((bf16[16,48,320]{2,1,0:T(8,128)(2,1)}), bf16[16,48,320]{2,1,0:T(8,128)(2,1)S(1)}, u32[]{:S(2)}, u32[]{:S(2)}) %all-to-all-start.1) | async-done | bytes 491552 | tf_op jit(solution)/shard_map/all_to_all | solution.py:575
  43.0 1.6 %collective-permute-start.1 = (bf16[48,320]{1,0:T(8,128)(2,1)S(1)}, bf16[48,320]{1,0:T(8,128)(2,1)S(1)}, u32[]{:S(2)}, u32[]{:S(2)}) collective-permute-start(bf16[48,320]{1,0:T(8,128)(2,1)S(1)} %add_convert_fusion.4.refs_0_.refs_1_), channel_id=1, source_target_pairs={{0,16},{16,0},{1,17},{17,1},{2,18},{18,2},{3,19},{19,3},{4,20},{20... | collective-permute-start | bytes 92168 | tf_op jit(solution)/shard_map/ppermute | solution.py:678
  44.6 2.5 %collective-permute-done.1.refs_1_.refs_2_ = bf16[48,320]{1,0:T(8,128)(2,1)S(1)} collective-permute-done((bf16[48,320]{1,0:T(8,128)(2,1)S(1)}, bf16[48,320]{1,0:T(8,128)(2,1)S(1)}, u32[]{:S(2)}, u32[]{:S(2)}) %collective-permute-start.1) | collective-permute-done | bytes 30752 | tf_op jit(solution)/shard_map/ppermute | solution.py:678
  47.1 5.6 %gate_up_product.3 = (bf16[8,96,768]{2,1,0:T(8,128)(2,1)}, bf16[8,96,384]{2,1,0:T(8,128)(2,1)}) custom-call(s32[4]{0:T(128)} %pad_add_fusion.place_ref, bf16[48,320]{1,0:T(8,128)(2,1)S(1)} %add_convert_fusion.4.refs_0_.refs_1_, bf16[48,320]{1,0:T(8,128)(2,1)S(1)} %collective-permute-done.1.refs_1_.refs_2_, f32[1,320]{1,0:T(1,128)} %reshape.40.refs_2_, ...), custom_call_target="tpu_custom_call" | custom-call | flops 503316480 | bytes 5242880 | tf_op jit(solution)/shard_map/gate_up_product/pallas_call | solution.py:380
  53.2 8.0 %gate_up_product.2 = (bf16[8,96,768]{2,1,0:T(8,128)(2,1)}, bf16[8,96,384]{2,1,0:T(8,128)(2,1)}) custom-call(s32[4]{0:T(128)} %pad_add_fusion.place_ref, bf16[48,320]{1,0:T(8,128)(2,1)S(1)} %add_convert_fusion.4.refs_0_.refs_1_, bf16[48,320]{1,0:T(8,128)(2,1)S(1)} %collective-permute-done.1.refs_1_.refs_2_, f32[1,320]{1,0:T(1,128)} %reshape.40.refs_2_, ...), custom_call_target="tpu_custom_call" | custom-call | flops 503316480 | bytes 5242880 | tf_op jit(solution)/shard_map/gate_up_product/pallas_call | solution.py:380
  61.2 1.3 add_convert_fusion.2
  62.5 1.0 add_convert_fusion.1
  63.5 3.9 %all-to-all-start.2 = ((bf16[4,2,96,384]{3,2,1,0:T(8,128)(2,1)}), bf16[4,2,96,384]{3,2,1,0:T(8,128)(2,1)S(1)}, u32[]{:S(2)}, u32[]{:S(2)}) async-start(bf16[4,2,96,384]{3,2,1,0:T(8,128)(2,1)} %bitcast.7), calls=%async_computation.2 | async-start | bytes 1179648 | tf_op jit(solution)/shard_map/all_to_all | solution.py:609
  67.3 1.1 collective-permute-start.4
  68.4 6.2 %rounded_weights.5.w_ref = bf16[320,4096]{1,0:T(8,128)(2,1)} custom-call(s32[4]{0:T(128)} %pad_add_fusion.place_ref, bf16[320,16384]{1,0:T(8,128)(2,1)} %bitcast.33, f32[8,8192]{1,0:T(8,128)S(1)} %collective-permute-done.refs_2_.refs_5_.refs_1_), custom_call_target="tpu_custom_call" | custom-call | flops 7864320 | bytes 5242880 | tf_op jit(solution)/shard_map/rounded_weights/pallas_call | solution.py:171
  74.6 6.4 %rounded_weights.4.w_ref = bf16[320,4096]{1,0:T(8,128)(2,1)} custom-call(s32[4]{0:T(128)} %pad_add_fusion.place_ref, bf16[320,16384]{1,0:T(8,128)(2,1)} %bitcast.34, f32[8,8192]{1,0:T(8,128)S(1)} %collective-permute-done.refs_2_.refs_5_.refs_1_), custom_call_target="tpu_custom_call" | custom-call | flops 7864320 | bytes 5242880 | tf_op jit(solution)/shard_map/rounded_weights/pallas_call | solution.py:171
  81.0 1.4 %collective-permute-done.4 = bf16[4,96,768]{2,1,0:T(8,128)(2,1)S(1)} collective-permute-done((bf16[4,96,768]{2,1,0:T(8,128)(2,1)S(1)}, bf16[4,96,768]{2,1,0:T(8,128)(2,1)S(1)}, u32[]{:S(2)}, u32[]{:S(2)}) %collective-permute-start.4) | collective-permute-done | bytes 589856 | tf_op jit(solution)/shard_map/ppermute | solution.py:591
  82.7 1.7 %collective-permute-start.5 = (bf16[2,96,768]{2,1,0:T(8,128)(2,1)S(1)}, bf16[2,96,768]{2,1,0:T(8,128)(2,1)S(1)}, u32[]{:S(2)}, u32[]{:S(2)}) collective-permute-start(bf16[2,96,768]{2,1,0:T(8,128)(2,1)S(1)} %slice.72), channel_id=1, source_target_pairs={{0,4},{1,5},{2,6},{3,7},{4,0},{5,1},{6,2},{7,3},{8,12},{9,13},{10,... | collective-permute-start | bytes 884744 | tf_op jit(solution)/shard_map/ppermute | solution.py:591
  84.4 1.2 collective-permute-start.7
  85.6 5.1 %collective-permute-done.5 = bf16[2,96,768]{2,1,0:T(8,128)(2,1)S(1)} collective-permute-done((bf16[2,96,768]{2,1,0:T(8,128)(2,1)S(1)}, bf16[2,96,768]{2,1,0:T(8,128)(2,1)S(1)}, u32[]{:S(2)}, u32[]{:S(2)}) %collective-permute-start.5) | collective-permute-done | bytes 294944 | tf_op jit(solution)/shard_map/ppermute | solution.py:591
  90.8 2.3 %collective-permute-start.6 = (bf16[1,96,768]{2,1,0:T(8,128)(2,1)S(1)}, bf16[1,96,768]{2,1,0:T(8,128)(2,1)S(1)}, u32[]{:S(2)}, u32[]{:S(2)}) collective-permute-start(bf16[1,96,768]{2,1,0:T(8,128)(2,1)S(1)} %slice.74), channel_id=1, source_target_pairs={{0,8},{1,9},{2,10},{3,11},{4,12},{5,13},{6,14},{7,15},{8,0},{9,1},... | collective-permute-start | bytes 442376 | tf_op jit(solution)/shard_map/ppermute | solution.py:591
  93.3 5.5 %collective-permute-done.6 = bf16[1,96,768]{2,1,0:T(8,128)(2,1)S(1)} collective-permute-done((bf16[1,96,768]{2,1,0:T(8,128)(2,1)S(1)}, bf16[1,96,768]{2,1,0:T(8,128)(2,1)S(1)}, u32[]{:S(2)}, u32[]{:S(2)}) %collective-permute-start.6) | collective-permute-done | bytes 147488 | tf_op jit(solution)/shard_map/ppermute | solution.py:591
  99.0 21.1 %all_to_all.25.a_ref = bf16[8,96,512]{2,1,0:T(8,128)(2,1)S(1)} all-to-all(bf16[8,96,512]{2,1,0:T(8,128)(2,1)S(1)} %broadcast_in_dim.15), channel_id=1, replica_groups={{0,2,4,6,8,10,12,14},{1,3,5,7,9,11,13,15},{16,18,20,22,24,26,28,30},{17..., dimensions={0} | all-to-all | bytes 1572864 | tf_op jit(solution)/shard_map/all_to_all | solution.py:581
  120.1 2.0 %down_product.2.refs_0_ = f32[96,320]{1,0:T(8,128)S(1)} custom-call(s32[4]{0:T(128)S(1)} %copy-done.2, bf16[8,96,512]{2,1,0:T(8,128)(2,1)S(1)} %all_to_all.25.a_ref, bf16[320,4096]{1,0:T(8,128)(2,1)S(1)} %copy-done.1), custom_call_target="tpu_custom_call" | custom-call | flops 251658240 | bytes 2621440 | tf_op jit(solution)/shard_map/down_product/pallas_call | solution.py:449
  122.4 2.1 %down_product.3 = bf16[32,6,320]{2,1,0:T(8,128)(2,1)S(1)} custom-call(s32[4]{0:T(128)S(1)} %copy-done.2, bf16[8,96,512]{2,1,0:T(8,128)(2,1)S(1)} %collective-permute-done.8.a_ref, bf16[320,4096]{1,0:T(8,128)(2,1)S(1)} %copy-done, f32[96,320]{1,0:T(8,128)S(1)} %down_product.2.refs_0_, bf16[48,320]{1,0:T(8,128)(2,1)S(1)} %add_convert_fusion.4.refs_0_.refs_1_, ...), custom_call_target="tpu_custom_call" | custom-call | flops 251658240 | bytes 2621440 | tf_op jit(solution)/shard_map/down_product/pallas_call | solution.py:449
  124.5 12.3 %all_to_all.26 = bf16[32,6,320]{2,1,0:T(8,128)(2,1)S(1)} all-to-all(bf16[32,6,320]{2,1,0:T(8,128)(2,1)S(1)} %down_product.3), channel_id=1, replica_groups=mesh['grp'=2,'wide'=16] {'grp','wide'}, dimensions={0} | all-to-all | bytes 245760 | tf_op jit(solution)/shard_map/all_to_all | solution.py:722
  136.8 0.7 reshape.38
  137.6 0.7 reshape.39
  (47 shorter events, 4.1 us)
Async XLA Ops:
  4.7 14.3 %all-to-all-start = ((bf16[16,1,3,512]{3,2,1,0:T(4,128)(2,1)}), bf16[16,1,3,512]{3,2,1,0:T(4,128)(2,1)S(1)}, u32[]{:S(2)}, u32[]{:S(2)}) async-start(bf16[16,1,3,512]{3,2,1,0:T(4,128)(2,1)} %get-tuple-element.29), calls=%async_computation | async-start | bytes 131072 | tf_op jit(solution)/shard_map/all_to_all | solution.py:575
  22.8 20.1 %all-to-all-start.1 = ((bf16[16,48,320]{2,1,0:T(8,128)(2,1)}), bf16[16,48,320]{2,1,0:T(8,128)(2,1)S(1)}, u32[]{:S(2)}, u32[]{:S(2)}) async-start(bf16[16,48,320]{2,1,0:T(8,128)(2,1)} %out_product.1), calls=%async_computation.1 | async-start | bytes 1179648 | tf_op jit(solution)/shard_map/all_to_all | solution.py:575
  28.0 5.4 %copy-start.5 = (bf16[3,16,320]{2,1,0:T(8,128)(2,1)S(1)}, bf16[3,16,320]{2,1,0:T(8,128)(2,1)}, u32[]{:S(2)}) copy-start(bf16[3,16,320]{2,1,0:T(8,128)(2,1)} %param.10) | copy-start | bytes 92164
  31.7 1.8 %collective-permute-start = (f32[8,8192]{1,0:T(8,128)}, f32[8,8192]{1,0:T(8,128)S(1)}, u32[]{:S(2)}, u32[]{:S(2)}) collective-permute-start(f32[8,8192]{1,0:T(8,128)} %edge_max.1), channel_id=1, source_target_pairs={{0,1},{1,0},{2,3},{3,2},{4,5},{5,4},{6,7},{7,6},{8,9},{9,8},{10,11... | collective-permute-start | bytes 786440 | tf_op jit(solution)/shard_map/ppermute | solution.py:571
  43.0 4.0 %collective-permute-start.1 = (bf16[48,320]{1,0:T(8,128)(2,1)S(1)}, bf16[48,320]{1,0:T(8,128)(2,1)S(1)}, u32[]{:S(2)}, u32[]{:S(2)}) collective-permute-start(bf16[48,320]{1,0:T(8,128)(2,1)S(1)} %add_convert_fusion.4.refs_0_.refs_1_), channel_id=1, source_target_pairs={{0,16},{16,0},{1,17},{17,1},{2,18},{18,2},{3,19},{19,3},{4,20},{20... | collective-permute-start | bytes 92168 | tf_op jit(solution)/shard_map/ppermute | solution.py:678
  52.7 8.5 %collective-permute-start.2 = (bf16[8,96,768]{2,1,0:T(8,128)(2,1)}, bf16[8,96,768]{2,1,0:T(8,128)(2,1)S(1)}, u32[]{:S(2)}, u32[]{:S(2)}) collective-permute-start(bf16[8,96,768]{2,1,0:T(8,128)(2,1)} %get-tuple-element.43), channel_id=1, source_target_pairs={{0,1},{1,0},{2,3},{3,2},{4,5},{5,4},{6,7},{7,6},{8,9},{9,8},{10,11... | collective-permute-start | bytes 3538952 | tf_op jit(solution)/shard_map/ppermute | solution.py:571
  52.7 9.8 %collective-permute-start.3 = (bf16[8,96,384]{2,1,0:T(8,128)(2,1)}, bf16[8,96,384]{2,1,0:T(8,128)(2,1)S(1)}, u32[]{:S(2)}, u32[]{:S(2)}) collective-permute-start(bf16[8,96,384]{2,1,0:T(8,128)(2,1)} %get-tuple-element.45), channel_id=1, source_target_pairs={{0,1},{1,0},{2,3},{3,2},{4,5},{5,4},{6,7},{7,6},{8,9},{9,8},{10,11... | collective-permute-start | bytes 1769480 | tf_op jit(solution)/shard_map/ppermute | solution.py:571
  61.2 1.3 copy-start.4
  63.5 20.9 %all-to-all-start.2 = ((bf16[4,2,96,384]{3,2,1,0:T(8,128)(2,1)}), bf16[4,2,96,384]{3,2,1,0:T(8,128)(2,1)S(1)}, u32[]{:S(2)}, u32[]{:S(2)}) async-start(bf16[4,2,96,384]{3,2,1,0:T(8,128)(2,1)} %bitcast.7), calls=%async_computation.2 | async-start | bytes 1179648 | tf_op jit(solution)/shard_map/all_to_all | solution.py:609
  67.3 15.1 %collective-permute-start.4 = (bf16[4,96,768]{2,1,0:T(8,128)(2,1)S(1)}, bf16[4,96,768]{2,1,0:T(8,128)(2,1)S(1)}, u32[]{:S(2)}, u32[]{:S(2)}) collective-permute-start(bf16[4,96,768]{2,1,0:T(8,128)(2,1)S(1)} %add_convert_fusion.2), channel_id=1, source_target_pairs={{0,2},{1,3},{2,0},{3,1},{4,6},{5,7},{6,4},{7,5},{8,10},{9,11},{10,... | collective-permute-start | bytes 1769480 | tf_op jit(solution)/shard_map/ppermute | solution.py:591
  74.6 7.8 %copy-start.3 = (bf16[8,96,768]{2,1,0:T(8,128)(2,1)S(1)}, bf16[8,96,768]{2,1,0:T(8,128)(2,1)}, u32[]{:S(2)}) copy-start(bf16[8,96,768]{2,1,0:T(8,128)(2,1)} %get-tuple-element.40) | copy-start | bytes 3538948
  82.7 8.0 %collective-permute-start.5 = (bf16[2,96,768]{2,1,0:T(8,128)(2,1)S(1)}, bf16[2,96,768]{2,1,0:T(8,128)(2,1)S(1)}, u32[]{:S(2)}, u32[]{:S(2)}) collective-permute-start(bf16[2,96,768]{2,1,0:T(8,128)(2,1)S(1)} %slice.72), channel_id=1, source_target_pairs={{0,4},{1,5},{2,6},{3,7},{4,0},{5,1},{6,2},{7,3},{8,12},{9,13},{10,... | collective-permute-start | bytes 884744 | tf_op jit(solution)/shard_map/ppermute | solution.py:591
  84.4 8.6 %collective-permute-start.7 = (bf16[96,384]{1,0:T(8,128)(2,1)S(1)}, bf16[96,384]{1,0:T(8,128)(2,1)S(1)}, u32[]{:S(2)}, u32[]{:S(2)}) collective-permute-start(bf16[96,384]{1,0:T(8,128)(2,1)S(1)} %fusion.3), channel_id=1, source_target_pairs={{0,2},{1,3},{2,0},{3,1},{4,6},{5,7},{6,4},{7,5},{8,10},{9,11},{10,... | collective-permute-start | bytes 221192 | tf_op jit(solution)/shard_map/ppermute | solution.py:613
  90.8 8.0 %collective-permute-start.6 = (bf16[1,96,768]{2,1,0:T(8,128)(2,1)S(1)}, bf16[1,96,768]{2,1,0:T(8,128)(2,1)S(1)}, u32[]{:S(2)}, u32[]{:S(2)}) collective-permute-start(bf16[1,96,768]{2,1,0:T(8,128)(2,1)S(1)} %slice.74), channel_id=1, source_target_pairs={{0,8},{1,9},{2,10},{3,11},{4,12},{5,13},{6,14},{7,15},{8,0},{9,1},... | collective-permute-start | bytes 442376 | tf_op jit(solution)/shard_map/ppermute | solution.py:591
  98.9 21.2 %copy-start.1 = (bf16[320,4096]{1,0:T(8,128)(2,1)S(1)}, bf16[320,4096]{1,0:T(8,128)(2,1)}, u32[]{:S(2)}) copy-start(bf16[320,4096]{1,0:T(8,128)(2,1)} %rounded_weights.4.w_ref) | copy-start | bytes 7864324
  98.9 21.2 %copy-start.2 = (s32[4]{0:T(128)S(1)}, s32[4]{0:T(128)}, u32[]{:S(2)}) copy-start(s32[4]{0:T(128)} %pad_add_fusion.place_ref) | copy-start | bytes 52
  120.1 2.3 %copy-start = (bf16[320,4096]{1,0:T(8,128)(2,1)S(1)}, bf16[320,4096]{1,0:T(8,128)(2,1)}, u32[]{:S(2)}) copy-start(bf16[320,4096]{1,0:T(8,128)(2,1)} %rounded_weights.5.w_ref) | copy-start | bytes 7864324
  120.1 2.3 %collective-permute-start.8 = (bf16[8,96,512]{2,1,0:T(8,128)(2,1)S(1)}, bf16[8,96,512]{2,1,0:T(8,128)(2,1)S(1)}, u32[]{:S(2)}, u32[]{:S(2)}) collective-permute-start(bf16[8,96,512]{2,1,0:T(8,128)(2,1)S(1)} %all_to_all.25.a_ref), channel_id=1, source_target_pairs={{0,1},{1,0},{2,3},{3,2},{4,5},{5,4},{6,7},{7,6},{8,9},{9,8},{10,11... | collective-permute-start | bytes 2359304 | tf_op jit(solution)/shard_map/ppermute | solution.py:571

commit v8 on v7

--- a/solution.py
+++ b/solution.py
@@ -393,6 +393,32 @@
     )(place, *in_vmem(*hidden), gain, *in_hbm(gate, up), *([] if tops is None else in_vmem(tops)))
 
 
+def packed(width):
+    return (2 * (width // LANES) + 1, LANES) if width % LANES == LANES // 2 else (2, width)
+
+
+def pack(pair):
+    width = pair[0].shape[1]
+    if packed(width)[1] == width:
+        return pair
+    whole = width // LANES * LANES
+    pieces = [x[:, at : at + LANES] for x in pair for at in range(0, whole, LANES)]
+    return [*pieces, jnp.concatenate([x[:, whole:] for x in pair], axis=1)]
+
+
+def unpack(pieces, width):
+    if packed(width)[1] == width:
+        return pieces
+    each, rest = width // LANES, width % LANES
+    last = pieces[-1]
+    return [
+        jnp.concatenate(
+            [*pieces[n * each : (n + 1) * each], last[..., n * rest : (n + 1) * rest]], axis=-1
+        )
+        for n in range(2)
+    ]
+
+
 def down_product(place, act, weight, added, states, mine):
     chips, count, units = act.shape
     width = weight.shape[0]
@@ -438,14 +464,15 @@
                     jnp.where(first, values[0], values[1]),
                     jnp.where(first, values[1], values[0]),
                 ]
-            sums, values = total_ref[...], jnp.concatenate(values, axis=0)
+            pieces = pack([total_ref[...], jnp.concatenate(values, axis=0)])
             for b in range(count // mine):
                 at = slice(b * mine, (b + 1) * mine)
-                o_ref[b] = jnp.concatenate([sums[at], values[at]], axis=0).astype(bf16)
+                o_ref[b] = jnp.concatenate([piece[at] for piece in pieces], axis=0).astype(bf16)
 
     fixed = lambda shape: pl.BlockSpec(shape, lambda i, p: (0,) * len(shape))
     more = [added, *states] if last else []
-    shape = (count // mine, 2 * mine, width) if last else (count, width)
+    pieces, lanes = packed(width)
+    shape = (count // mine, pieces * mine, lanes) if last else (count, width)
     return pl.pallas_call(
         kernel,
         grid_spec=pltpu.PrefetchScalarGridSpec(
@@ -720,12 +747,13 @@
 
     axes = ("grp", "wide") if parts > 1 else "wide"
     both = lax.all_to_all(both, axes, split_axis=0, concat_axis=0, tiled=True)
-    both = both.reshape(parts, owners, 2, seq_dev, steps, width_dev)
-    ffn = both[0, :, 0]
+    pieces, lanes = packed(width_dev)
+    both = both.reshape(parts, owners, pieces, seq_dev, steps, lanes)
+    ffn, hidden_out = unpack([both[:, :, n] for n in range(pieces)], width_dev)
     if parts > 1:
-        ffn = jnp.sum(both[:, :, 0].astype(f32), axis=0).astype(bf16)
-    ffn_out = jnp.transpose(ffn, (2, 1, 0, 3)).reshape(steps, seq_dev, width)
-    hidden_out = jnp.transpose(both[0, :, 1], (2, 1, 0, 3)).reshape(steps, seq_dev, width)
+        ffn = jnp.sum(ffn.astype(f32), axis=0, keepdims=True).astype(bf16)
+    ffn_out = jnp.transpose(ffn[0], (2, 1, 0, 3)).reshape(steps, seq_dev, width)
+    hidden_out = jnp.transpose(hidden_out[0], (2, 1, 0, 3)).reshape(steps, seq_dev, width)
     return (ffn_out, attn_out, hidden_out)
 
 

time: 139 us -> 139 us (level)
  no operation moved by 1% of the time
where the time goes in v8:
time: 139 us; the launch traced here: 138 us
  Pallas kernels  54.6 us (39%)
  blocking collectives  32.8 us (24%)
  starting transfers between devices  24.5 us (18%)
  waiting for transfers between devices  17.4 us (13%)
  other arithmetic  4.55 us (3%)
  local copies, waits for them, and re-layouts  3.01 us (2%)
    all_to_all x1, blocking collectives, exchange_chips(): lax.all_to_all(value, 'wide', split_axis=0, concat_axis=0, tiled=True, ax...  21.2 us
    pallas_call x3, Pallas kernels, rounded_weights(): pl.pallas_call(kernel, grid_spec=pltpu.PrefetchScalarGridSpec(num_scalar_...  20.6 us
    pallas_call x2, Pallas kernels, gate_up_product(): pl.pallas_call(kernel, grid_spec=pltpu.PrefetchScalarGridSpec(num_scalar_...  13.6 us
    all_to_all x2, starting transfers between devices, exchange(): lax.all_to_all(value, 'wide', split_axis=0, concat_axis=0, tiled=True)  12 us
    ppermute x3, waiting for transfers between devices, exchange_halves(): received = lax.ppermute(send, 'wide', [(i, i ^ bit) for i in range(count)])  11.9 us
    all_to_all x1, blocking collectives, on_device(): both = lax.all_to_all(both, axes, split_axis=0, concat_axis=0, tiled=True)  11.6 us
    pallas_call x1, Pallas kernels, out_levels_of(): pl.pallas_call(kernel, grid=(cols // tile,), in_specs=[pl.BlockSpec((rows...  5.48 us
    ppermute x3, starting transfers between devices, exchange_halves(): received = lax.ppermute(send, 'wide', [(i, i ^ bit) for i in range(count)])  5.03 us
  transfers between devices with their start and end apart: 12, of which 7 were waited for; matrix products, arithmetic and copies ran while one was open for 3% of the time, Pallas kernels for 29%

profile of v8, /device:TPU:0, one launch (start us, length us, event | category | flops | bytes accessed | tf_op | source)
XLA Modules:
  0.0 137.8 jit_solution(16936937437876009349)
XLA Ops:
  0.6 4.0 %attention.1 = (bf16[3,1,8,8,128]{4,3,2,1,0:T(8,128)(2,1)}, bf16[16,1,3,512]{3,2,1,0:T(4,128)(2,1)}) custom-call(s32[16]{0:T(128)} %len_ref.1, bf16[3,1,8,8,128]{4,3,2,1,0:T(8,128)(2,1)} %q_ref.1, bf16[2,1,8,512,128]{4,3,2,1,0:T(8,128)(2,1)} %kv_ref.1, bf16[3,2,1,8,128]{4,3,2,1,0:T(8,128)(2,1)} %new_ref.1), custom_call_target="tpu_custom_call" | custom-call | flops 50331648 | bytes 2097152 | tf_op jit(solution)/shard_map/attention/pallas_call | solution.py:569
  4.6 7.4 %all-to-all-start = ((bf16[16,1,3,512]{3,2,1,0:T(4,128)(2,1)}), bf16[16,1,3,512]{3,2,1,0:T(4,128)(2,1)S(1)}, u32[]{:S(2)}, u32[]{:S(2)}) async-start(bf16[16,1,3,512]{3,2,1,0:T(4,128)(2,1)} %get-tuple-element.29), calls=%async_computation | async-start | bytes 131072 | tf_op jit(solution)/shard_map/all_to_all | solution.py:602
  12.0 5.5 %out_levels_of.1 = (f8e4m3fn[512,5120]{1,0:T(32,128)(4,1)}, f32[8,5120]{1,0:T(8,128)}) custom-call(bf16[512,5120]{1,0:T(8,128)(2,1)} %w_ref.1), custom_call_target="tpu_custom_call" | custom-call | flops 20971520 | bytes 7864320 | tf_op jit(solution)/shard_map/out_levels_of/pallas_call | solution.py:241
  17.5 1.4 %all-to-all-done = bf16[16,1,3,512]{3,2,1,0:T(4,128)(2,1)S(1)} async-done(((bf16[16,1,3,512]{3,2,1,0:T(4,128)(2,1)}), bf16[16,1,3,512]{3,2,1,0:T(4,128)(2,1)S(1)}, u32[]{:S(2)}, u32[]{:S(2)}) %all-to-all-start) | async-done | bytes 49184 | tf_op jit(solution)/shard_map/all_to_all | solution.py:602
  19.6 3.2 %out_product.1 = bf16[16,48,320]{2,1,0:T(8,128)(2,1)} custom-call(bf16[48,512]{1,0:T(8,128)(2,1)} %reshape.50.x_ref, f8e4m3fn[512,5120]{1,0:T(32,128)(4,1)} %get-tuple-element.33.l_ref, f32[8,5120]{1,0:T(8,128)} %get-tuple-element.34.s_ref), custom_call_target="tpu_custom_call" | custom-call | flops 251658240 | bytes 2621440 | tf_op jit(solution)/shard_map/out_product/pallas_call | solution.py:275
  22.8 4.6 %all-to-all-start.1 = ((bf16[16,48,320]{2,1,0:T(8,128)(2,1)}), bf16[16,48,320]{2,1,0:T(8,128)(2,1)S(1)}, u32[]{:S(2)}, u32[]{:S(2)}) async-start(bf16[16,48,320]{2,1,0:T(8,128)(2,1)} %out_product.1), calls=%async_computation.1 | async-start | bytes 1179648 | tf_op jit(solution)/shard_map/all_to_all | solution.py:602
  28.0 3.7 %edge_max.1 = f32[8,8192]{1,0:T(8,128)} custom-call(s32[4]{0:T(128)} %pad_add_fusion.place_ref, bf16[320,16384]{1,0:T(8,128)(2,1)} %refs_3_.1, bf16[320,16384]{1,0:T(8,128)(2,1)} %refs_4_.1, bf16[320,16384]{1,0:T(8,128)(2,1)} %bitcast.44), custom_call_target="tpu_custom_call" | custom-call | flops 3145728 | bytes 3145728 | tf_op jit(solution)/shard_map/edge_max/pallas_call | solution.py:99
  32.1 0.8 dynamic-slice_convert_fusion
  33.6 8.0 %rounded_weights.3 = (bf16[320,4096]{1,0:T(8,128)(2,1)}, bf16[320,4096]{1,0:T(8,128)(2,1)}) custom-call(s32[4]{0:T(128)} %pad_add_fusion.place_ref, bf16[320,16384]{1,0:T(8,128)(2,1)} %refs_3_.1, bf16[320,16384]{1,0:T(8,128)(2,1)} %refs_4_.1, f32[8,8192]{1,0:T(8,128)S(1)} %collective-permute-done.refs_2_.refs_5_.refs_1_), custom_call_target="tpu_custom_call" | custom-call | flops 15728640 | bytes 10485760 | tf_op jit(solution)/shard_map/rounded_weights/pallas_call | solution.py:171
  41.5 1.4 %all-to-all-done.1 = bf16[16,48,320]{2,1,0:T(8,128)(2,1)S(1)} async-done(((bf16[16,48,320]{2,1,0:T(8,128)(2,1)}), bf16[16,48,320]{2,1,0:T(8,128)(2,1)S(1)}, u32[]{:S(2)}, u32[]{:S(2)}) %all-to-all-start.1) | async-done | bytes 491552 | tf_op jit(solution)/shard_map/all_to_all | solution.py:602
  43.0 1.6 %collective-permute-start.1 = (bf16[48,320]{1,0:T(8,128)(2,1)S(1)}, bf16[48,320]{1,0:T(8,128)(2,1)S(1)}, u32[]{:S(2)}, u32[]{:S(2)}) collective-permute-start(bf16[48,320]{1,0:T(8,128)(2,1)S(1)} %add_convert_fusion.4.refs_0_.refs_1_), channel_id=1, source_target_pairs={{0,16},{16,0},{1,17},{17,1},{2,18},{18,2},{3,19},{19,3},{4,20},{20... | collective-permute-start | bytes 92168 | tf_op jit(solution)/shard_map/ppermute | solution.py:705
  44.6 2.5 %collective-permute-done.1.refs_1_.refs_2_ = bf16[48,320]{1,0:T(8,128)(2,1)S(1)} collective-permute-done((bf16[48,320]{1,0:T(8,128)(2,1)S(1)}, bf16[48,320]{1,0:T(8,128)(2,1)S(1)}, u32[]{:S(2)}, u32[]{:S(2)}) %collective-permute-start.1) | collective-permute-done | bytes 30752 | tf_op jit(solution)/shard_map/ppermute | solution.py:705
  47.1 5.6 %gate_up_product.3 = (bf16[8,96,768]{2,1,0:T(8,128)(2,1)}, bf16[8,96,384]{2,1,0:T(8,128)(2,1)}) custom-call(s32[4]{0:T(128)} %pad_add_fusion.place_ref, bf16[48,320]{1,0:T(8,128)(2,1)S(1)} %add_convert_fusion.4.refs_0_.refs_1_, bf16[48,320]{1,0:T(8,128)(2,1)S(1)} %collective-permute-done.1.refs_1_.refs_2_, f32[1,320]{1,0:T(1,128)} %reshape.55.refs_2_, ...), custom_call_target="tpu_custom_call" | custom-call | flops 503316480 | bytes 5242880 | tf_op jit(solution)/shard_map/gate_up_product/pallas_call | solution.py:380
  53.2 8.0 %gate_up_product.2 = (bf16[8,96,768]{2,1,0:T(8,128)(2,1)}, bf16[8,96,384]{2,1,0:T(8,128)(2,1)}) custom-call(s32[4]{0:T(128)} %pad_add_fusion.place_ref, bf16[48,320]{1,0:T(8,128)(2,1)S(1)} %add_convert_fusion.4.refs_0_.refs_1_, bf16[48,320]{1,0:T(8,128)(2,1)S(1)} %collective-permute-done.1.refs_1_.refs_2_, f32[1,320]{1,0:T(1,128)} %reshape.55.refs_2_, ...), custom_call_target="tpu_custom_call" | custom-call | flops 503316480 | bytes 5242880 | tf_op jit(solution)/shard_map/gate_up_product/pallas_call | solution.py:380
  61.2 1.3 add_convert_fusion.2
  62.5 1.0 add_convert_fusion.1
  63.4 3.9 %all-to-all-start.2 = ((bf16[4,2,96,384]{3,2,1,0:T(8,128)(2,1)}), bf16[4,2,96,384]{3,2,1,0:T(8,128)(2,1)S(1)}, u32[]{:S(2)}, u32[]{:S(2)}) async-start(bf16[4,2,96,384]{3,2,1,0:T(8,128)(2,1)} %bitcast.7), calls=%async_computation.2 | async-start | bytes 1179648 | tf_op jit(solution)/shard_map/all_to_all | solution.py:636
  67.3 1.1 collective-permute-start.4
  68.4 6.2 %rounded_weights.5.w_ref = bf16[320,4096]{1,0:T(8,128)(2,1)} custom-call(s32[4]{0:T(128)} %pad_add_fusion.place_ref, bf16[320,16384]{1,0:T(8,128)(2,1)} %bitcast.45, f32[8,8192]{1,0:T(8,128)S(1)} %collective-permute-done.refs_2_.refs_5_.refs_1_), custom_call_target="tpu_custom_call" | custom-call | flops 7864320 | bytes 5242880 | tf_op jit(solution)/shard_map/rounded_weights/pallas_call | solution.py:171
  74.6 6.4 %rounded_weights.4.w_ref = bf16[320,4096]{1,0:T(8,128)(2,1)} custom-call(s32[4]{0:T(128)} %pad_add_fusion.place_ref, bf16[320,16384]{1,0:T(8,128)(2,1)} %bitcast.46, f32[8,8192]{1,0:T(8,128)S(1)} %collective-permute-done.refs_2_.refs_5_.refs_1_), custom_call_target="tpu_custom_call" | custom-call | flops 7864320 | bytes 5242880 | tf_op jit(solution)/shard_map/rounded_weights/pallas_call | solution.py:171
  81.0 1.4 %collective-permute-done.4 = bf16[4,96,768]{2,1,0:T(8,128)(2,1)S(1)} collective-permute-done((bf16[4,96,768]{2,1,0:T(8,128)(2,1)S(1)}, bf16[4,96,768]{2,1,0:T(8,128)(2,1)S(1)}, u32[]{:S(2)}, u32[]{:S(2)}) %collective-permute-start.4) | collective-permute-done | bytes 589856 | tf_op jit(solution)/shard_map/ppermute | solution.py:618
  82.7 1.7 %collective-permute-start.5 = (bf16[2,96,768]{2,1,0:T(8,128)(2,1)S(1)}, bf16[2,96,768]{2,1,0:T(8,128)(2,1)S(1)}, u32[]{:S(2)}, u32[]{:S(2)}) collective-permute-start(bf16[2,96,768]{2,1,0:T(8,128)(2,1)S(1)} %slice.96), channel_id=1, source_target_pairs={{0,4},{1,5},{2,6},{3,7},{4,0},{5,1},{6,2},{7,3},{8,12},{9,13},{10,... | collective-permute-start | bytes 884744 | tf_op jit(solution)/shard_map/ppermute | solution.py:618
  84.4 1.2 collective-permute-start.7
  85.6 5.0 %collective-permute-done.5 = bf16[2,96,768]{2,1,0:T(8,128)(2,1)S(1)} collective-permute-done((bf16[2,96,768]{2,1,0:T(8,128)(2,1)S(1)}, bf16[2,96,768]{2,1,0:T(8,128)(2,1)S(1)}, u32[]{:S(2)}, u32[]{:S(2)}) %collective-permute-start.5) | collective-permute-done | bytes 294944 | tf_op jit(solution)/shard_map/ppermute | solution.py:618
  90.7 2.3 %collective-permute-start.6 = (bf16[1,96,768]{2,1,0:T(8,128)(2,1)S(1)}, bf16[1,96,768]{2,1,0:T(8,128)(2,1)S(1)}, u32[]{:S(2)}, u32[]{:S(2)}) collective-permute-start(bf16[1,96,768]{2,1,0:T(8,128)(2,1)S(1)} %slice.98), channel_id=1, source_target_pairs={{0,8},{1,9},{2,10},{3,11},{4,12},{5,13},{6,14},{7,15},{8,0},{9,1},... | collective-permute-start | bytes 442376 | tf_op jit(solution)/shard_map/ppermute | solution.py:618
  93.3 5.4 %collective-permute-done.6 = bf16[1,96,768]{2,1,0:T(8,128)(2,1)S(1)} collective-permute-done((bf16[1,96,768]{2,1,0:T(8,128)(2,1)S(1)}, bf16[1,96,768]{2,1,0:T(8,128)(2,1)S(1)}, u32[]{:S(2)}, u32[]{:S(2)}) %collective-permute-start.6) | collective-permute-done | bytes 147488 | tf_op jit(solution)/shard_map/ppermute | solution.py:618
  99.0 21.2 %all_to_all.25.a_ref = bf16[8,96,512]{2,1,0:T(8,128)(2,1)S(1)} all-to-all(bf16[8,96,512]{2,1,0:T(8,128)(2,1)S(1)} %broadcast_in_dim.16), channel_id=1, replica_groups={{0,2,4,6,8,10,12,14},{1,3,5,7,9,11,13,15},{16,18,20,22,24,26,28,30},{17..., dimensions={0} | all-to-all | bytes 1572864 | tf_op jit(solution)/shard_map/all_to_all | solution.py:608
  120.1 2.0 %down_product.2.refs_0_ = f32[96,320]{1,0:T(8,128)S(1)} custom-call(s32[4]{0:T(128)S(1)} %copy-done.2, bf16[8,96,512]{2,1,0:T(8,128)(2,1)S(1)} %all_to_all.25.a_ref, bf16[320,4096]{1,0:T(8,128)(2,1)S(1)} %copy-done.1), custom_call_target="tpu_custom_call" | custom-call | flops 251658240 | bytes 2621440 | tf_op jit(solution)/shard_map/down_product/pallas_call | solution.py:476
  122.4 2.1 %down_product.3 = bf16[32,15,128]{2,1,0:T(8,128)(2,1)S(1)} custom-call(s32[4]{0:T(128)S(1)} %copy-done.2, bf16[8,96,512]{2,1,0:T(8,128)(2,1)S(1)} %collective-permute-done.8.a_ref, bf16[320,4096]{1,0:T(8,128)(2,1)S(1)} %copy-done, f32[96,320]{1,0:T(8,128)S(1)} %down_product.2.refs_0_, bf16[48,320]{1,0:T(8,128)(2,1)S(1)} %add_convert_fusion.4.refs_0_.refs_1_, ...), custom_call_target="tpu_custom_call" | custom-call | flops 251658240 | bytes 2621440 | tf_op jit(solution)/shard_map/down_product/pallas_call | solution.py:476
  124.5 11.6 %all_to_all.26 = bf16[32,15,128]{2,1,0:T(8,128)(2,1)S(1)} all-to-all(bf16[32,15,128]{2,1,0:T(8,128)(2,1)S(1)} %down_product.3), channel_id=1, replica_groups=mesh['grp'=2,'wide'=16] {'grp','wide'}, dimensions={0} | all-to-all | bytes 245760 | tf_op jit(solution)/shard_map/all_to_all | solution.py:749
  136.3 0.7 reshape.53
  137.1 0.7 reshape.54
  (50 shorter events, 4.3 us)
Async XLA Ops:
  4.6 14.3 %all-to-all-start = ((bf16[16,1,3,512]{3,2,1,0:T(4,128)(2,1)}), bf16[16,1,3,512]{3,2,1,0:T(4,128)(2,1)S(1)}, u32[]{:S(2)}, u32[]{:S(2)}) async-start(bf16[16,1,3,512]{3,2,1,0:T(4,128)(2,1)} %get-tuple-element.29), calls=%async_computation | async-start | bytes 131072 | tf_op jit(solution)/shard_map/all_to_all | solution.py:602
  22.8 20.2 %all-to-all-start.1 = ((bf16[16,48,320]{2,1,0:T(8,128)(2,1)}), bf16[16,48,320]{2,1,0:T(8,128)(2,1)S(1)}, u32[]{:S(2)}, u32[]{:S(2)}) async-start(bf16[16,48,320]{2,1,0:T(8,128)(2,1)} %out_product.1), calls=%async_computation.1 | async-start | bytes 1179648 | tf_op jit(solution)/shard_map/all_to_all | solution.py:602
  28.0 5.4 %copy-start.5 = (bf16[3,16,320]{2,1,0:T(8,128)(2,1)S(1)}, bf16[3,16,320]{2,1,0:T(8,128)(2,1)}, u32[]{:S(2)}) copy-start(bf16[3,16,320]{2,1,0:T(8,128)(2,1)} %param.10) | copy-start | bytes 92164
  31.7 1.8 %collective-permute-start = (f32[8,8192]{1,0:T(8,128)}, f32[8,8192]{1,0:T(8,128)S(1)}, u32[]{:S(2)}, u32[]{:S(2)}) collective-permute-start(f32[8,8192]{1,0:T(8,128)} %edge_max.1), channel_id=1, source_target_pairs={{0,1},{1,0},{2,3},{3,2},{4,5},{5,4},{6,7},{7,6},{8,9},{9,8},{10,11... | collective-permute-start | bytes 786440 | tf_op jit(solution)/shard_map/ppermute | solution.py:598
  43.0 4.0 %collective-permute-start.1 = (bf16[48,320]{1,0:T(8,128)(2,1)S(1)}, bf16[48,320]{1,0:T(8,128)(2,1)S(1)}, u32[]{:S(2)}, u32[]{:S(2)}) collective-permute-start(bf16[48,320]{1,0:T(8,128)(2,1)S(1)} %add_convert_fusion.4.refs_0_.refs_1_), channel_id=1, source_target_pairs={{0,16},{16,0},{1,17},{17,1},{2,18},{18,2},{3,19},{19,3},{4,20},{20... | collective-permute-start | bytes 92168 | tf_op jit(solution)/shard_map/ppermute | solution.py:705
  52.6 8.5 %collective-permute-start.2 = (bf16[8,96,768]{2,1,0:T(8,128)(2,1)}, bf16[8,96,768]{2,1,0:T(8,128)(2,1)S(1)}, u32[]{:S(2)}, u32[]{:S(2)}) collective-permute-start(bf16[8,96,768]{2,1,0:T(8,128)(2,1)} %get-tuple-element.43), channel_id=1, source_target_pairs={{0,1},{1,0},{2,3},{3,2},{4,5},{5,4},{6,7},{7,6},{8,9},{9,8},{10,11... | collective-permute-start | bytes 3538952 | tf_op jit(solution)/shard_map/ppermute | solution.py:598
  52.6 9.8 %collective-permute-start.3 = (bf16[8,96,384]{2,1,0:T(8,128)(2,1)}, bf16[8,96,384]{2,1,0:T(8,128)(2,1)S(1)}, u32[]{:S(2)}, u32[]{:S(2)}) collective-permute-start(bf16[8,96,384]{2,1,0:T(8,128)(2,1)} %get-tuple-element.45), channel_id=1, source_target_pairs={{0,1},{1,0},{2,3},{3,2},{4,5},{5,4},{6,7},{7,6},{8,9},{9,8},{10,11... | collective-permute-start | bytes 1769480 | tf_op jit(solution)/shard_map/ppermute | solution.py:598
  61.2 1.3 copy-start.4
  63.4 20.9 %all-to-all-start.2 = ((bf16[4,2,96,384]{3,2,1,0:T(8,128)(2,1)}), bf16[4,2,96,384]{3,2,1,0:T(8,128)(2,1)S(1)}, u32[]{:S(2)}, u32[]{:S(2)}) async-start(bf16[4,2,96,384]{3,2,1,0:T(8,128)(2,1)} %bitcast.7), calls=%async_computation.2 | async-start | bytes 1179648 | tf_op jit(solution)/shard_map/all_to_all | solution.py:636
  67.3 15.1 %collective-permute-start.4 = (bf16[4,96,768]{2,1,0:T(8,128)(2,1)S(1)}, bf16[4,96,768]{2,1,0:T(8,128)(2,1)S(1)}, u32[]{:S(2)}, u32[]{:S(2)}) collective-permute-start(bf16[4,96,768]{2,1,0:T(8,128)(2,1)S(1)} %add_convert_fusion.2), channel_id=1, source_target_pairs={{0,2},{1,3},{2,0},{3,1},{4,6},{5,7},{6,4},{7,5},{8,10},{9,11},{10,... | collective-permute-start | bytes 1769480 | tf_op jit(solution)/shard_map/ppermute | solution.py:618
  74.6 7.8 %copy-start.3 = (bf16[8,96,768]{2,1,0:T(8,128)(2,1)S(1)}, bf16[8,96,768]{2,1,0:T(8,128)(2,1)}, u32[]{:S(2)}) copy-start(bf16[8,96,768]{2,1,0:T(8,128)(2,1)} %get-tuple-element.40) | copy-start | bytes 3538948
  82.7 8.0 %collective-permute-start.5 = (bf16[2,96,768]{2,1,0:T(8,128)(2,1)S(1)}, bf16[2,96,768]{2,1,0:T(8,128)(2,1)S(1)}, u32[]{:S(2)}, u32[]{:S(2)}) collective-permute-start(bf16[2,96,768]{2,1,0:T(8,128)(2,1)S(1)} %slice.96), channel_id=1, source_target_pairs={{0,4},{1,5},{2,6},{3,7},{4,0},{5,1},{6,2},{7,3},{8,12},{9,13},{10,... | collective-permute-start | bytes 884744 | tf_op jit(solution)/shard_map/ppermute | solution.py:618
  84.4 8.6 %collective-permute-start.7 = (bf16[96,384]{1,0:T(8,128)(2,1)S(1)}, bf16[96,384]{1,0:T(8,128)(2,1)S(1)}, u32[]{:S(2)}, u32[]{:S(2)}) collective-permute-start(bf16[96,384]{1,0:T(8,128)(2,1)S(1)} %fusion.3), channel_id=1, source_target_pairs={{0,2},{1,3},{2,0},{3,1},{4,6},{5,7},{6,4},{7,5},{8,10},{9,11},{10,... | collective-permute-start | bytes 221192 | tf_op jit(solution)/shard_map/ppermute | solution.py:640
  90.7 8.0 %collective-permute-start.6 = (bf16[1,96,768]{2,1,0:T(8,128)(2,1)S(1)}, bf16[1,96,768]{2,1,0:T(8,128)(2,1)S(1)}, u32[]{:S(2)}, u32[]{:S(2)}) collective-permute-start(bf16[1,96,768]{2,1,0:T(8,128)(2,1)S(1)} %slice.98), channel_id=1, source_target_pairs={{0,8},{1,9},{2,10},{3,11},{4,12},{5,13},{6,14},{7,15},{8,0},{9,1},... | collective-permute-start | bytes 442376 | tf_op jit(solution)/shard_map/ppermute | solution.py:618
  98.9 21.3 %copy-start.1 = (bf16[320,4096]{1,0:T(8,128)(2,1)S(1)}, bf16[320,4096]{1,0:T(8,128)(2,1)}, u32[]{:S(2)}) copy-start(bf16[320,4096]{1,0:T(8,128)(2,1)} %rounded_weights.4.w_ref) | copy-start | bytes 7864324
  98.9 21.2 %copy-start.2 = (s32[4]{0:T(128)S(1)}, s32[4]{0:T(128)}, u32[]{:S(2)}) copy-start(s32[4]{0:T(128)} %pad_add_fusion.place_ref) | copy-start | bytes 52
  120.1 2.3 %copy-start = (bf16[320,4096]{1,0:T(8,128)(2,1)S(1)}, bf16[320,4096]{1,0:T(8,128)(2,1)}, u32[]{:S(2)}) copy-start(bf16[320,4096]{1,0:T(8,128)(2,1)} %rounded_weights.5.w_ref) | copy-start | bytes 7864324
  120.1 2.3 %collective-permute-start.8 = (bf16[8,96,512]{2,1,0:T(8,128)(2,1)S(1)}, bf16[8,96,512]{2,1,0:T(8,128)(2,1)S(1)}, u32[]{:S(2)}, u32[]{:S(2)}) collective-permute-start(bf16[8,96,512]{2,1,0:T(8,128)(2,1)S(1)} %all_to_all.25.a_ref), channel_id=1, source_target_pairs={{0,1},{1,0},{2,3},{3,2},{4,5},{5,4},{6,7},{7,6},{8,9},{9,8},{10,11... | collective-permute-start | bytes 2359304 | tf_op jit(solution)/shard_map/ppermute | solution.py:598

commit v9 on v8

--- a/solution.py
+++ b/solution.py
@@ -253,6 +253,32 @@
     )(*in_hbm(weight))
 
 
+def folded(count, width):
+    if width % LANES != LANES // 2 or count % 16:
+        return count, width
+    return count * width // LANES, LANES
+
+
+def fold(value):
+    count, width = value.shape
+    if folded(count, width) == (count, width):
+        return value
+    whole, half = width // LANES * LANES, count // 2
+    pieces = [value[:, at : at + LANES] for at in range(0, whole, LANES)]
+    rest = jnp.concatenate([value[:half, whole:], value[half:, whole:]], axis=1)
+    return jnp.concatenate([*pieces, rest], axis=0)
+
+
+def unfold(value, count, width):
+    if value.shape == (count, width):
+        return value
+    whole = width // LANES
+    rest = value[whole * count :]
+    rest = jnp.concatenate([rest[:, : LANES // 2], rest[:, LANES // 2 :]], axis=0)
+    pieces = [value[n * count : (n + 1) * count] for n in range(whole)]
+    return jnp.concatenate([*pieces, rest], axis=1)
+
+
 def out_product(left, levels, scale, owners):
     count, rows = left.shape
     cols = levels.shape[1]
@@ -270,7 +296,7 @@
             total = part if total is None else total + part
         total = total.astype(bf16)
         for q in range(per):
-            o_ref[q] = total[:, q * share : (q + 1) * share]
+            o_ref[q] = fold(total[:, q * share : (q + 1) * share])
 
     return pl.pallas_call(
         kernel,
@@ -280,8 +306,8 @@
             pl.BlockSpec((rows, tile), lambda i: (0, i)),
             pl.BlockSpec((8, tile), lambda i: (0, i)),
         ],
-        out_specs=pl.BlockSpec((per, count, share), lambda i: (i, 0, 0)),
-        out_shape=jax.ShapeDtypeStruct((owners, count, share), bf16),
+        out_specs=pl.BlockSpec((per, *folded(count, share)), lambda i: (i, 0, 0)),
+        out_shape=jax.ShapeDtypeStruct((owners, *folded(count, share)), bf16),
         compiler_params=params(),
         cost_estimate=cost(2 * count * rows * cols, rows * cols),
         name="out_product",
@@ -691,14 +717,15 @@
     else:
         tops = joined_max(place, weights, units, chunk, tile)
     away = rounded_weights(
-        place, weights, tops, paired, 0, 1, units, chunk, pick_tile(units // 2, 2048)
+        place, weights, tops, paired, 0, 1, units, chunk, pick_tile(units // 2, 1024)
     )
     gain = lax.dynamic_slice_in_dim(norm_gain, me * width_dev, width_dev, 0).astype(f32)[None]
     residual = jnp.transpose(residual_in, (1, 0, 2)).reshape(tokens, width_dev).astype(f32)
     projected, away, gain, residual = lax.optimization_barrier(
         (projected, away, gain, residual)
     )
-    hidden = (residual + jnp.sum(projected.astype(f32), axis=0)).astype(bf16)
+    projected = unfold(jnp.sum(projected.astype(f32), axis=0), tokens, width_dev)
+    hidden = (residual + projected).astype(bf16)
 
     states = [hidden]
     if parts == 2:

time: 139 us -> 138 us (level)
  waiting for transfers between devices: 17.4 us -> 14.8 us
  starting transfers between devices: 24.5 us -> 26.2 us
    ppermute x3, waiting for transfers between devices: 11.9 us -> 10.3 us  [exchange_halves(): received = lax.ppermute(send, 'wide', [(i, i ^ bit) for i in range(count)])]
  transfers between devices with their start and end apart: 12 -> 12, of which waited for: 7 -> 7; matrix products, arithmetic and copies ran while one was open for 3% -> 3% of each run, Pallas kernels for 29% -> 28%
where the time goes in v9:
time: 138 us; the launch traced here: 137 us
  Pallas kernels  54.1 us (39%)
  blocking collectives  33.6 us (24%)
  starting transfers between devices  26.2 us (19%)
  waiting for transfers between devices  14.8 us (11%)
  other arithmetic  4.54 us (3%)
  local copies, waits for them, and re-layouts  3.09 us (2%)
    all_to_all x1, blocking collectives, exchange_chips(): lax.all_to_all(value, 'wide', split_axis=0, concat_axis=0, tiled=True, ax...  22 us
    pallas_call x3, Pallas kernels, rounded_weights(): pl.pallas_call(kernel, grid_spec=pltpu.PrefetchScalarGridSpec(num_scalar_...  19.8 us
    pallas_call x2, Pallas kernels, gate_up_product(): pl.pallas_call(kernel, grid_spec=pltpu.PrefetchScalarGridSpec(num_scalar_...  13.6 us
    all_to_all x2, starting transfers between devices, exchange(): lax.all_to_all(value, 'wide', split_axis=0, concat_axis=0, tiled=True)  11.9 us
    all_to_all x1, blocking collectives, on_device(): both = lax.all_to_all(both, axes, split_axis=0, concat_axis=0, tiled=True)  11.6 us
    ppermute x3, waiting for transfers between devices, exchange_halves(): received = lax.ppermute(send, 'wide', [(i, i ^ bit) for i in range(count)])  10.3 us
    ppermute x3, starting transfers between devices, exchange_halves(): received = lax.ppermute(send, 'wide', [(i, i ^ bit) for i in range(count)])  5.72 us
    pallas_call x1, Pallas kernels, out_levels_of(): pl.pallas_call(kernel, grid=(cols // tile,), in_specs=[pl.BlockSpec((rows...  5.44 us
  transfers between devices with their start and end apart: 12, of which 7 were waited for; matrix products, arithmetic and copies ran while one was open for 3% of the time, Pallas kernels for 28%

profile of v9, /device:TPU:0, one launch (start us, length us, event | category | flops | bytes accessed | tf_op | source)
XLA Modules:
  0.0 137.3 jit_solution(1128814367995601249)
XLA Ops:
  0.6 4.0 %attention.1 = (bf16[3,1,8,8,128]{4,3,2,1,0:T(8,128)(2,1)}, bf16[16,1,3,512]{3,2,1,0:T(4,128)(2,1)}) custom-call(s32[16]{0:T(128)} %len_ref.1, bf16[3,1,8,8,128]{4,3,2,1,0:T(8,128)(2,1)} %q_ref.1, bf16[2,1,8,512,128]{4,3,2,1,0:T(8,128)(2,1)} %kv_ref.1, bf16[3,2,1,8,128]{4,3,2,1,0:T(8,128)(2,1)} %new_ref.1), custom_call_target="tpu_custom_call" | custom-call | flops 50331648 | bytes 2097152 | tf_op jit(solution)/shard_map/attention/pallas_call | solution.py:595
  4.6 7.4 %all-to-all-start = ((bf16[16,1,3,512]{3,2,1,0:T(4,128)(2,1)}), bf16[16,1,3,512]{3,2,1,0:T(4,128)(2,1)S(1)}, u32[]{:S(2)}, u32[]{:S(2)}) async-start(bf16[16,1,3,512]{3,2,1,0:T(4,128)(2,1)} %get-tuple-element.29), calls=%async_computation | async-start | bytes 131072 | tf_op jit(solution)/shard_map/all_to_all | solution.py:628
  12.0 5.4 %out_levels_of.1 = (f8e4m3fn[512,5120]{1,0:T(32,128)(4,1)}, f32[8,5120]{1,0:T(8,128)}) custom-call(bf16[512,5120]{1,0:T(8,128)(2,1)} %w_ref.1), custom_call_target="tpu_custom_call" | custom-call | flops 20971520 | bytes 7864320 | tf_op jit(solution)/shard_map/out_levels_of/pallas_call | solution.py:241
  17.5 1.5 %all-to-all-done = bf16[16,1,3,512]{3,2,1,0:T(4,128)(2,1)S(1)} async-done(((bf16[16,1,3,512]{3,2,1,0:T(4,128)(2,1)}), bf16[16,1,3,512]{3,2,1,0:T(4,128)(2,1)S(1)}, u32[]{:S(2)}, u32[]{:S(2)}) %all-to-all-start) | async-done | bytes 49184 | tf_op jit(solution)/shard_map/all_to_all | solution.py:628
  18.9 0.7 reshape.50.x_ref
  19.6 3.4 %out_product.1 = bf16[16,120,128]{2,1,0:T(8,128)(2,1)} custom-call(bf16[48,512]{1,0:T(8,128)(2,1)} %reshape.50.x_ref, f8e4m3fn[512,5120]{1,0:T(32,128)(4,1)} %get-tuple-element.33.l_ref, f32[8,5120]{1,0:T(8,128)} %get-tuple-element.34.s_ref), custom_call_target="tpu_custom_call" | custom-call | flops 251658240 | bytes 2621440 | tf_op jit(solution)/shard_map/out_product/pallas_call | solution.py:301
  23.0 4.6 %all-to-all-start.1 = ((bf16[16,120,128]{2,1,0:T(8,128)(2,1)}), bf16[16,120,128]{2,1,0:T(8,128)(2,1)S(1)}, u32[]{:S(2)}, u32[]{:S(2)}) async-start(bf16[16,120,128]{2,1,0:T(8,128)(2,1)} %out_product.1), calls=%async_computation.1 | async-start | bytes 983040 | tf_op jit(solution)/shard_map/all_to_all | solution.py:628
  28.3 3.7 %edge_max.1 = f32[8,8192]{1,0:T(8,128)} custom-call(s32[4]{0:T(128)} %pad_add_fusion.place_ref, bf16[320,16384]{1,0:T(8,128)(2,1)} %refs_3_.1, bf16[320,16384]{1,0:T(8,128)(2,1)} %refs_4_.1, bf16[320,16384]{1,0:T(8,128)(2,1)} %bitcast.44), custom_call_target="tpu_custom_call" | custom-call | flops 3145728 | bytes 3145728 | tf_op jit(solution)/shard_map/edge_max/pallas_call | solution.py:99
  32.4 0.8 dynamic-slice_convert_fusion
  33.8 7.2 %rounded_weights.3 = (bf16[320,4096]{1,0:T(8,128)(2,1)}, bf16[320,4096]{1,0:T(8,128)(2,1)}) custom-call(s32[4]{0:T(128)} %pad_add_fusion.place_ref, bf16[320,16384]{1,0:T(8,128)(2,1)} %refs_3_.1, bf16[320,16384]{1,0:T(8,128)(2,1)} %refs_4_.1, f32[8,8192]{1,0:T(8,128)S(1)} %collective-permute-done.refs_2_.refs_5_.refs_1_), custom_call_target="tpu_custom_call" | custom-call | flops 15728640 | bytes 10485760 | tf_op jit(solution)/shard_map/rounded_weights/pallas_call | solution.py:171
  41.5 1.6 %collective-permute-start.1 = (bf16[48,320]{1,0:T(8,128)(2,1)S(1)}, bf16[48,320]{1,0:T(8,128)(2,1)S(1)}, u32[]{:S(2)}, u32[]{:S(2)}) collective-permute-start(bf16[48,320]{1,0:T(8,128)(2,1)S(1)} %fusion.4.refs_0_.refs_1_), channel_id=1, source_target_pairs={{0,16},{16,0},{1,17},{17,1},{2,18},{18,2},{3,19},{19,3},{4,20},{20... | collective-permute-start | bytes 92168 | tf_op jit(solution)/shard_map/ppermute | solution.py:732
  43.1 2.5 %collective-permute-done.1.refs_1_.refs_2_ = bf16[48,320]{1,0:T(8,128)(2,1)S(1)} collective-permute-done((bf16[48,320]{1,0:T(8,128)(2,1)S(1)}, bf16[48,320]{1,0:T(8,128)(2,1)S(1)}, u32[]{:S(2)}, u32[]{:S(2)}) %collective-permute-start.1) | collective-permute-done | bytes 30752 | tf_op jit(solution)/shard_map/ppermute | solution.py:732
  45.6 5.6 %gate_up_product.3 = (bf16[8,96,768]{2,1,0:T(8,128)(2,1)}, bf16[8,96,384]{2,1,0:T(8,128)(2,1)}) custom-call(s32[4]{0:T(128)} %pad_add_fusion.place_ref, bf16[48,320]{1,0:T(8,128)(2,1)S(1)} %fusion.4.refs_0_.refs_1_, bf16[48,320]{1,0:T(8,128)(2,1)S(1)} %collective-permute-done.1.refs_1_.refs_2_, f32[1,320]{1,0:T(1,128)} %reshape.55.refs_2_, ...), custom_call_target="tpu_custom_call" | custom-call | flops 503316480 | bytes 5242880 | tf_op jit(solution)/shard_map/gate_up_product/pallas_call | solution.py:406
  51.7 8.0 %gate_up_product.2 = (bf16[8,96,768]{2,1,0:T(8,128)(2,1)}, bf16[8,96,384]{2,1,0:T(8,128)(2,1)}) custom-call(s32[4]{0:T(128)} %pad_add_fusion.place_ref, bf16[48,320]{1,0:T(8,128)(2,1)S(1)} %fusion.4.refs_0_.refs_1_, bf16[48,320]{1,0:T(8,128)(2,1)S(1)} %collective-permute-done.1.refs_1_.refs_2_, f32[1,320]{1,0:T(1,128)} %reshape.55.refs_2_, ...), custom_call_target="tpu_custom_call" | custom-call | flops 503316480 | bytes 5242880 | tf_op jit(solution)/shard_map/gate_up_product/pallas_call | solution.py:406
  59.7 1.3 add_convert_fusion.2
  61.0 1.0 add_convert_fusion.1
  62.0 4.6 %all-to-all-start.2 = ((bf16[4,2,96,384]{3,2,1,0:T(8,128)(2,1)}), bf16[4,2,96,384]{3,2,1,0:T(8,128)(2,1)S(1)}, u32[]{:S(2)}, u32[]{:S(2)}) async-start(bf16[4,2,96,384]{3,2,1,0:T(8,128)(2,1)} %bitcast.7), calls=%async_computation.2 | async-start | bytes 1179648 | tf_op jit(solution)/shard_map/all_to_all | solution.py:662
  66.5 1.5 %collective-permute-start.4 = (bf16[4,96,768]{2,1,0:T(8,128)(2,1)S(1)}, bf16[4,96,768]{2,1,0:T(8,128)(2,1)S(1)}, u32[]{:S(2)}, u32[]{:S(2)}) collective-permute-start(bf16[4,96,768]{2,1,0:T(8,128)(2,1)S(1)} %add_convert_fusion.2), channel_id=1, source_target_pairs={{0,2},{1,3},{2,0},{3,1},{4,6},{5,7},{6,4},{7,5},{8,10},{9,11},{10,... | collective-permute-start | bytes 1769480 | tf_op jit(solution)/shard_map/ppermute | solution.py:644
  68.0 6.2 %rounded_weights.5.w_ref = bf16[320,4096]{1,0:T(8,128)(2,1)} custom-call(s32[4]{0:T(128)} %pad_add_fusion.place_ref, bf16[320,16384]{1,0:T(8,128)(2,1)} %bitcast.45, f32[8,8192]{1,0:T(8,128)S(1)} %collective-permute-done.refs_2_.refs_5_.refs_1_), custom_call_target="tpu_custom_call" | custom-call | flops 7864320 | bytes 5242880 | tf_op jit(solution)/shard_map/rounded_weights/pallas_call | solution.py:171
  74.2 6.4 %rounded_weights.4.w_ref = bf16[320,4096]{1,0:T(8,128)(2,1)} custom-call(s32[4]{0:T(128)} %pad_add_fusion.place_ref, bf16[320,16384]{1,0:T(8,128)(2,1)} %bitcast.46, f32[8,8192]{1,0:T(8,128)S(1)} %collective-permute-done.refs_2_.refs_5_.refs_1_), custom_call_target="tpu_custom_call" | custom-call | flops 7864320 | bytes 5242880 | tf_op jit(solution)/shard_map/rounded_weights/pallas_call | solution.py:171
  80.6 0.9 collective-permute-done.4
  81.7 1.8 %collective-permute-start.5 = (bf16[2,96,768]{2,1,0:T(8,128)(2,1)S(1)}, bf16[2,96,768]{2,1,0:T(8,128)(2,1)S(1)}, u32[]{:S(2)}, u32[]{:S(2)}) collective-permute-start(bf16[2,96,768]{2,1,0:T(8,128)(2,1)S(1)} %slice.119), channel_id=1, source_target_pairs={{0,4},{1,5},{2,6},{3,7},{4,0},{5,1},{6,2},{7,3},{8,12},{9,13},{10,... | collective-permute-start | bytes 884744 | tf_op jit(solution)/shard_map/ppermute | solution.py:644
  83.6 1.5 %collective-permute-start.7 = (bf16[96,384]{1,0:T(8,128)(2,1)S(1)}, bf16[96,384]{1,0:T(8,128)(2,1)S(1)}, u32[]{:S(2)}, u32[]{:S(2)}) collective-permute-start(bf16[96,384]{1,0:T(8,128)(2,1)S(1)} %fusion.3), channel_id=1, source_target_pairs={{0,2},{1,3},{2,0},{3,1},{4,6},{5,7},{6,4},{7,5},{8,10},{9,11},{10,... | collective-permute-start | bytes 221192 | tf_op jit(solution)/shard_map/ppermute | solution.py:666
  85.2 4.4 %collective-permute-done.5 = bf16[2,96,768]{2,1,0:T(8,128)(2,1)S(1)} collective-permute-done((bf16[2,96,768]{2,1,0:T(8,128)(2,1)S(1)}, bf16[2,96,768]{2,1,0:T(8,128)(2,1)S(1)}, u32[]{:S(2)}, u32[]{:S(2)}) %collective-permute-start.5) | collective-permute-done | bytes 294944 | tf_op jit(solution)/shard_map/ppermute | solution.py:644
  89.6 2.4 %collective-permute-start.6 = (bf16[1,96,768]{2,1,0:T(8,128)(2,1)S(1)}, bf16[1,96,768]{2,1,0:T(8,128)(2,1)S(1)}, u32[]{:S(2)}, u32[]{:S(2)}) collective-permute-start(bf16[1,96,768]{2,1,0:T(8,128)(2,1)S(1)} %slice.121), channel_id=1, source_target_pairs={{0,8},{1,9},{2,10},{3,11},{4,12},{5,13},{6,14},{7,15},{8,0},{9,1},... | collective-permute-start | bytes 442376 | tf_op jit(solution)/shard_map/ppermute | solution.py:644
  92.3 5.1 %collective-permute-done.6 = bf16[1,96,768]{2,1,0:T(8,128)(2,1)S(1)} collective-permute-done((bf16[1,96,768]{2,1,0:T(8,128)(2,1)S(1)}, bf16[1,96,768]{2,1,0:T(8,128)(2,1)S(1)}, u32[]{:S(2)}, u32[]{:S(2)}) %collective-permute-start.6) | collective-permute-done | bytes 147488 | tf_op jit(solution)/shard_map/ppermute | solution.py:644
  97.7 22.0 %all_to_all.25.a_ref = bf16[8,96,512]{2,1,0:T(8,128)(2,1)S(1)} all-to-all(bf16[8,96,512]{2,1,0:T(8,128)(2,1)S(1)} %broadcast_in_dim.16), channel_id=1, replica_groups={{0,2,4,6,8,10,12,14},{1,3,5,7,9,11,13,15},{16,18,20,22,24,26,28,30},{17..., dimensions={0} | all-to-all | bytes 1572864 | tf_op jit(solution)/shard_map/all_to_all | solution.py:634
  119.7 2.0 %down_product.2.refs_0_ = f32[96,320]{1,0:T(8,128)S(1)} custom-call(s32[4]{0:T(128)S(1)} %copy-done.2, bf16[8,96,512]{2,1,0:T(8,128)(2,1)S(1)} %all_to_all.25.a_ref, bf16[320,4096]{1,0:T(8,128)(2,1)S(1)} %copy-done.1), custom_call_target="tpu_custom_call" | custom-call | flops 251658240 | bytes 2621440 | tf_op jit(solution)/shard_map/down_product/pallas_call | solution.py:502
  122.0 2.1 %down_product.3 = bf16[32,15,128]{2,1,0:T(8,128)(2,1)S(1)} custom-call(s32[4]{0:T(128)S(1)} %copy-done.2, bf16[8,96,512]{2,1,0:T(8,128)(2,1)S(1)} %collective-permute-done.8.a_ref, bf16[320,4096]{1,0:T(8,128)(2,1)S(1)} %copy-done, f32[96,320]{1,0:T(8,128)S(1)} %down_product.2.refs_0_, bf16[48,320]{1,0:T(8,128)(2,1)S(1)} %fusion.4.refs_0_.refs_1_, ...), custom_call_target="tpu_custom_call" | custom-call | flops 251658240 | bytes 2621440 | tf_op jit(solution)/shard_map/down_product/pallas_call | solution.py:502
  124.1 11.6 %all_to_all.26 = bf16[32,15,128]{2,1,0:T(8,128)(2,1)S(1)} all-to-all(bf16[32,15,128]{2,1,0:T(8,128)(2,1)S(1)} %down_product.3), channel_id=1, replica_groups=mesh['grp'=2,'wide'=16] {'grp','wide'}, dimensions={0} | all-to-all | bytes 245760 | tf_op jit(solution)/shard_map/all_to_all | solution.py:776
  135.9 0.7 reshape.53
  136.6 0.7 reshape.54
  (52 shorter events, 4.0 us)
Async XLA Ops:
  4.6 14.3 %all-to-all-start = ((bf16[16,1,3,512]{3,2,1,0:T(4,128)(2,1)}), bf16[16,1,3,512]{3,2,1,0:T(4,128)(2,1)S(1)}, u32[]{:S(2)}, u32[]{:S(2)}) async-start(bf16[16,1,3,512]{3,2,1,0:T(4,128)(2,1)} %get-tuple-element.29), calls=%async_computation | async-start | bytes 131072 | tf_op jit(solution)/shard_map/all_to_all | solution.py:628
  23.0 18.3 %all-to-all-start.1 = ((bf16[16,120,128]{2,1,0:T(8,128)(2,1)}), bf16[16,120,128]{2,1,0:T(8,128)(2,1)S(1)}, u32[]{:S(2)}, u32[]{:S(2)}) async-start(bf16[16,120,128]{2,1,0:T(8,128)(2,1)} %out_product.1), calls=%async_computation.1 | async-start | bytes 983040 | tf_op jit(solution)/shard_map/all_to_all | solution.py:628
  28.3 5.4 %copy-start.5 = (bf16[3,16,320]{2,1,0:T(8,128)(2,1)S(1)}, bf16[3,16,320]{2,1,0:T(8,128)(2,1)}, u32[]{:S(2)}) copy-start(bf16[3,16,320]{2,1,0:T(8,128)(2,1)} %param.10) | copy-start | bytes 92164
  32.0 1.8 %collective-permute-start = (f32[8,8192]{1,0:T(8,128)}, f32[8,8192]{1,0:T(8,128)S(1)}, u32[]{:S(2)}, u32[]{:S(2)}) collective-permute-start(f32[8,8192]{1,0:T(8,128)} %edge_max.1), channel_id=1, source_target_pairs={{0,1},{1,0},{2,3},{3,2},{4,5},{5,4},{6,7},{7,6},{8,9},{9,8},{10,11... | collective-permute-start | bytes 786440 | tf_op jit(solution)/shard_map/ppermute | solution.py:624
  41.5 4.0 %collective-permute-start.1 = (bf16[48,320]{1,0:T(8,128)(2,1)S(1)}, bf16[48,320]{1,0:T(8,128)(2,1)S(1)}, u32[]{:S(2)}, u32[]{:S(2)}) collective-permute-start(bf16[48,320]{1,0:T(8,128)(2,1)S(1)} %fusion.4.refs_0_.refs_1_), channel_id=1, source_target_pairs={{0,16},{16,0},{1,17},{17,1},{2,18},{18,2},{3,19},{19,3},{4,20},{20... | collective-permute-start | bytes 92168 | tf_op jit(solution)/shard_map/ppermute | solution.py:732
  51.1 8.5 %collective-permute-start.2 = (bf16[8,96,768]{2,1,0:T(8,128)(2,1)}, bf16[8,96,768]{2,1,0:T(8,128)(2,1)S(1)}, u32[]{:S(2)}, u32[]{:S(2)}) collective-permute-start(bf16[8,96,768]{2,1,0:T(8,128)(2,1)} %get-tuple-element.43), channel_id=1, source_target_pairs={{0,1},{1,0},{2,3},{3,2},{4,5},{5,4},{6,7},{7,6},{8,9},{9,8},{10,11... | collective-permute-start | bytes 3538952 | tf_op jit(solution)/shard_map/ppermute | solution.py:624
  51.1 9.8 %collective-permute-start.3 = (bf16[8,96,384]{2,1,0:T(8,128)(2,1)}, bf16[8,96,384]{2,1,0:T(8,128)(2,1)S(1)}, u32[]{:S(2)}, u32[]{:S(2)}) collective-permute-start(bf16[8,96,384]{2,1,0:T(8,128)(2,1)} %get-tuple-element.45), channel_id=1, source_target_pairs={{0,1},{1,0},{2,3},{3,2},{4,5},{5,4},{6,7},{7,6},{8,9},{9,8},{10,11... | collective-permute-start | bytes 1769480 | tf_op jit(solution)/shard_map/ppermute | solution.py:624
  59.7 1.3 copy-start.4
  62.0 21.6 %all-to-all-start.2 = ((bf16[4,2,96,384]{3,2,1,0:T(8,128)(2,1)}), bf16[4,2,96,384]{3,2,1,0:T(8,128)(2,1)S(1)}, u32[]{:S(2)}, u32[]{:S(2)}) async-start(bf16[4,2,96,384]{3,2,1,0:T(8,128)(2,1)} %bitcast.7), calls=%async_computation.2 | async-start | bytes 1179648 | tf_op jit(solution)/shard_map/all_to_all | solution.py:662
  66.5 15.0 %collective-permute-start.4 = (bf16[4,96,768]{2,1,0:T(8,128)(2,1)S(1)}, bf16[4,96,768]{2,1,0:T(8,128)(2,1)S(1)}, u32[]{:S(2)}, u32[]{:S(2)}) collective-permute-start(bf16[4,96,768]{2,1,0:T(8,128)(2,1)S(1)} %add_convert_fusion.2), channel_id=1, source_target_pairs={{0,2},{1,3},{2,0},{3,1},{4,6},{5,7},{6,4},{7,5},{8,10},{9,11},{10,... | collective-permute-start | bytes 1769480 | tf_op jit(solution)/shard_map/ppermute | solution.py:644
  74.2 7.3 %copy-start.3 = (bf16[8,96,768]{2,1,0:T(8,128)(2,1)S(1)}, bf16[8,96,768]{2,1,0:T(8,128)(2,1)}, u32[]{:S(2)}) copy-start(bf16[8,96,768]{2,1,0:T(8,128)(2,1)} %get-tuple-element.40) | copy-start | bytes 3538948
  81.7 7.8 %collective-permute-start.5 = (bf16[2,96,768]{2,1,0:T(8,128)(2,1)S(1)}, bf16[2,96,768]{2,1,0:T(8,128)(2,1)S(1)}, u32[]{:S(2)}, u32[]{:S(2)}) collective-permute-start(bf16[2,96,768]{2,1,0:T(8,128)(2,1)S(1)} %slice.119), channel_id=1, source_target_pairs={{0,4},{1,5},{2,6},{3,7},{4,0},{5,1},{6,2},{7,3},{8,12},{9,13},{10,... | collective-permute-start | bytes 884744 | tf_op jit(solution)/shard_map/ppermute | solution.py:644
  83.6 8.4 %collective-permute-start.7 = (bf16[96,384]{1,0:T(8,128)(2,1)S(1)}, bf16[96,384]{1,0:T(8,128)(2,1)S(1)}, u32[]{:S(2)}, u32[]{:S(2)}) collective-permute-start(bf16[96,384]{1,0:T(8,128)(2,1)S(1)} %fusion.3), channel_id=1, source_target_pairs={{0,2},{1,3},{2,0},{3,1},{4,6},{5,7},{6,4},{7,5},{8,10},{9,11},{10,... | collective-permute-start | bytes 221192 | tf_op jit(solution)/shard_map/ppermute | solution.py:666
  89.6 7.8 %collective-permute-start.6 = (bf16[1,96,768]{2,1,0:T(8,128)(2,1)S(1)}, bf16[1,96,768]{2,1,0:T(8,128)(2,1)S(1)}, u32[]{:S(2)}, u32[]{:S(2)}) collective-permute-start(bf16[1,96,768]{2,1,0:T(8,128)(2,1)S(1)} %slice.121), channel_id=1, source_target_pairs={{0,8},{1,9},{2,10},{3,11},{4,12},{5,13},{6,14},{7,15},{8,0},{9,1},... | collective-permute-start | bytes 442376 | tf_op jit(solution)/shard_map/ppermute | solution.py:644
  97.6 22.1 %copy-start.1 = (bf16[320,4096]{1,0:T(8,128)(2,1)S(1)}, bf16[320,4096]{1,0:T(8,128)(2,1)}, u32[]{:S(2)}) copy-start(bf16[320,4096]{1,0:T(8,128)(2,1)} %rounded_weights.4.w_ref) | copy-start | bytes 7864324
  97.6 22.1 %copy-start.2 = (s32[4]{0:T(128)S(1)}, s32[4]{0:T(128)}, u32[]{:S(2)}) copy-start(s32[4]{0:T(128)} %pad_add_fusion.place_ref) | copy-start | bytes 52
  119.7 2.3 %copy-start = (bf16[320,4096]{1,0:T(8,128)(2,1)S(1)}, bf16[320,4096]{1,0:T(8,128)(2,1)}, u32[]{:S(2)}) copy-start(bf16[320,4096]{1,0:T(8,128)(2,1)} %rounded_weights.5.w_ref) | copy-start | bytes 7864324
  119.7 2.3 %collective-permute-start.8 = (bf16[8,96,512]{2,1,0:T(8,128)(2,1)S(1)}, bf16[8,96,512]{2,1,0:T(8,128)(2,1)S(1)}, u32[]{:S(2)}, u32[]{:S(2)}) collective-permute-start(bf16[8,96,512]{2,1,0:T(8,128)(2,1)S(1)} %all_to_all.25.a_ref), channel_id=1, source_target_pairs={{0,1},{1,0},{2,3},{3,2},{4,5},{5,4},{6,7},{7,6},{8,9},{9,8},{10,11... | collective-permute-start | bytes 2359304 | tf_op jit(solution)/shard_map/ppermute | solution.py:624
